TPU v7x, 512 devices: a whole 4x8x8 slice. The times are simulated.
512 devices in a mesh: dp: 32 (over y_hi, x, core), blk: 16 (over z, y_lo).
Axes of the slice: x: 4, y: 8 (y_hi: 4, y_lo: 2; y = y_hi * 2 + y_lo), z: 8, core: 2. Of those that a mesh axis runs over, the one named last changes fastest.
Arguments:
- points: bfloat16 [32768, 1024], P(('dp', 'blk')), may hold values from -6 to 6
- membership: int32 [32768], P(('dp', 'blk')), may hold values from 0 to 511
- landmark_pool: bfloat16 [12288, 1024], P('blk'), may hold values from -6 to 6
- landmark_ids: int32 [8192], P('blk'), may hold values from 0 to 767, as said below
- whitening: bfloat16 [8192, 1024], P('blk'), may hold values from -0.03125 to 0.03125
- owner_map: int32 [512], replicated, may hold values from 0 to 31, as said below
Outputs:
- features: bfloat16 [32768, 1024], P(('dp', 'blk'))
- owned_centroids: bfloat16 [512, 1024], P('dp')
- scores: float32 [32768, 512], P(('dp', 'blk'))
Inputs may be any that keep to these rules, and one draw needn't show every extreme that they name: `landmark_ids`: id i of landmark block b names row b * 768 + i of landmark_pool; the first id of every block is 0 and the last is 767. `owner_map`: every owner is named by exactly 16 clusters.
All inputs are finite; a program needn't handle non-finite values.
Results may differ from a plain program's by a relative error of at most 0.015.
Values may be sent and summed in bfloat16 or wider, within the bound.
No kernel may reach another device: no remote copies, remote signals or barrier semaphores. Data moves between devices by JAX's collectives and lax.ppermute only.
A program may use at most 64 MiB of HBM per device.

v0:
```python
import math

import jax
import jax.numpy as jnp
from jax import lax
from jax.sharding import PartitionSpec as P

epsilon = 1e-06


def shifted(value, axis, by):
    size = lax.axis_size(axis)
    return lax.ppermute(value, axis, [(i, (i + by) % size) for i in range(size)])


def body(points, membership, landmark_pool, landmark_ids, whitening, owner_map):
    local_count = points.shape[0]
    gaussian_spread = points.shape[1]
    rank_width = whitening.shape[1]
    clusters = owner_map.shape[0]
    landmarks = landmark_pool[landmark_ids]
    anchor_magnitude_factor = lax.rsqrt(
        jnp.sum(jnp.square(landmarks.astype(jnp.float32)), axis=1) + epsilon
    )
    softness_divisor = math.sqrt(gaussian_spread)
    blocks = lax.axis_size("blk")

    def project(visitor):
        sample_anchor_gram = jnp.dot(visitor, landmarks.T, preferred_element_type=jnp.float32)
        sample_length_factor = lax.rsqrt(
            jnp.sum(jnp.square(visitor.astype(jnp.float32)), axis=1) + epsilon
        )
        angular_affinity = (
            softness_divisor
            * sample_anchor_gram
            * sample_length_factor[:, None]
            * anchor_magnitude_factor[None, :]
        )
        kernel = jnp.exp(angular_affinity).astype(jnp.bfloat16)
        return jnp.dot(kernel, whitening, preferred_element_type=jnp.float32)

    def pass_forward(partial_value):
        return shifted(partial_value, "blk", 1)

    def advance(step_index, current):
        visitor, partial_value = current
        partial_value = partial_value + project(visitor)
        visitor = shifted(visitor, "blk", 1)
        return (visitor, pass_forward(partial_value))

    start = (points, jnp.zeros((local_count, rank_width), jnp.float32))
    visitor, partial_value = lax.fori_loop(0, blocks - 1, advance, start)
    summed = pass_forward(partial_value + project(visitor))
    features = summed.astype(jnp.bfloat16)
    ordering = jnp.argsort(owner_map, stable=True)
    ranking = jnp.argsort(ordering)
    per_owner = clusters // lax.axis_size("dp")
    owner_start = lax.axis_index("dp") * per_owner
    slots = jnp.arange(per_owner, dtype=jnp.int32)
    part_totals = jnp.zeros((per_owner, rank_width), jnp.float32)
    part_counts = jnp.zeros((per_owner,), jnp.float32)
    rows_piece = lax.all_gather(features, "dp", axis=0, tiled=True)
    member_piece = lax.all_gather(membership, "dp", axis=0, tiled=True)
    local_rank = ranking[member_piece] - owner_start
    owner_table = (slots[:, None] == local_rank[None, :]).astype(jnp.bfloat16)
    part_totals = part_totals + jnp.dot(owner_table, rows_piece, preferred_element_type=jnp.float32)
    part_counts = part_counts + jnp.sum(owner_table.astype(jnp.float32), axis=1)
    owner_totals = part_totals
    owner_counts = part_counts
    owner_totals, owner_counts = (
        lax.psum(owner_totals.astype(jnp.bfloat16), "blk").astype(jnp.float32),
        lax.psum(owner_counts.astype(jnp.bfloat16), "blk").astype(jnp.float32),
    )
    owned_centroids = (owner_totals / jnp.maximum(owner_counts, 1.0)[:, None]).astype(jnp.bfloat16)
    ranked_centroids = lax.all_gather(owned_centroids, "dp", axis=0, tiled=True)
    centroids = ranked_centroids[ranking]
    centre_float = centroids.astype(jnp.float32)
    squared_norms = jnp.sum(centre_float * centre_float, axis=1)
    inner = jnp.dot(features, centroids.T, preferred_element_type=jnp.float32)
    scores = (squared_norms[None, :] - 2.0 * inner) / rank_width
    return (features, owned_centroids, scores)


def solution(mesh):
    return jax.shard_map(
        body,
        mesh=mesh,
        in_specs=(
            P(("dp", "blk"), None),
            P(("dp", "blk")),
            P("blk", None),
            P("blk"),
            P("blk", None),
            P(),
        ),
        out_specs=(P(("dp", "blk"), None), P("dp", None), P(("dp", "blk"), None)),
        check_vma=False,
    )
```

profile of v0, /device:TPU:1, one launch (start us, length us, event | category | flops | bytes accessed | tf_op | source)
XLA Modules:
  0.0 458.6 jit_solution(7079672927871049728)
XLA Ops:
  8.6 2.0 gather_fusion
  11.0 222.4 %while.12 = (s32[]{:T(128)}, bf16[64,1024]{1,0:T(8,128)(2,1)S(1)}, f32[64,1024]{1,0:T(8,128)S(1)}, bf16[512,1024]{1,0:T(8,128)(2,1)S(1)}, f32[512]{0:T(512)S(1)}, /*index=5*/bf16[512,1024]{1,0:T(8,128)(2,1)}, s32[]{:T(128)}) while((s32[]{:T(128)}, bf16[64,1024]{1,0:T(8,128)(2,1)S(1)}, f32[64,1024]{1,0:T(8,128)S(1)}, ...), condition=%wide.region_3.0_spmd, body=%wide.region_1.0_spmd.sunk | while | flops 134578240 | bytes 4721821 | solution.py:52
  11.1 1.9 convolution_add_fusion.3
  13.1 4.0 collective-permute-start.1
  17.1 3.9 collective-permute-start
  21.0 13.4 %collective-permute-done = bf16[64,1024]{1,0:T(8,128)(2,1)S(1)} collective-permute-done((bf16[64,1024]{1,0:T(8,128)(2,1)S(1)}, bf16[64,1024]{1,0:T(8,128)(2,1)S(1)}, u32[]{:S(2)}, u32[]{:S(2)}) %collective-permute-start) | collective-permute-done | bytes 131104 | tf_op jit(solution)/shard_map/while/body/eval_jaxpr/ppermute | solution.py:13
  34.6 1.9 convolution_add_fusion.3
  36.5 1.9 collective-permute-start.1
  38.5 1.9 collective-permute-start
  40.4 9.5 %collective-permute-done = bf16[64,1024]{1,0:T(8,128)(2,1)S(1)} collective-permute-done((bf16[64,1024]{1,0:T(8,128)(2,1)S(1)}, bf16[64,1024]{1,0:T(8,128)(2,1)S(1)}, u32[]{:S(2)}, u32[]{:S(2)}) %collective-permute-start) | collective-permute-done | bytes 131104 | tf_op jit(solution)/shard_map/while/body/eval_jaxpr/ppermute | solution.py:13
  50.1 1.9 convolution_add_fusion.3
  52.0 1.9 collective-permute-start.1
  54.0 1.9 collective-permute-start
  55.9 8.6 %collective-permute-done = bf16[64,1024]{1,0:T(8,128)(2,1)S(1)} collective-permute-done((bf16[64,1024]{1,0:T(8,128)(2,1)S(1)}, bf16[64,1024]{1,0:T(8,128)(2,1)S(1)}, u32[]{:S(2)}, u32[]{:S(2)}) %collective-permute-start) | collective-permute-done | bytes 131104 | tf_op jit(solution)/shard_map/while/body/eval_jaxpr/ppermute | solution.py:13
  64.6 1.9 convolution_add_fusion.3
  66.6 1.9 collective-permute-start.1
  68.5 1.9 collective-permute-start
  70.4 7.7 %collective-permute-done = bf16[64,1024]{1,0:T(8,128)(2,1)S(1)} collective-permute-done((bf16[64,1024]{1,0:T(8,128)(2,1)S(1)}, bf16[64,1024]{1,0:T(8,128)(2,1)S(1)}, u32[]{:S(2)}, u32[]{:S(2)}) %collective-permute-start) | collective-permute-done | bytes 131104 | tf_op jit(solution)/shard_map/while/body/eval_jaxpr/ppermute | solution.py:13
  78.3 1.9 convolution_add_fusion.3
  80.2 1.9 collective-permute-start.1
  82.1 1.9 collective-permute-start
  84.1 6.8 %collective-permute-done = bf16[64,1024]{1,0:T(8,128)(2,1)S(1)} collective-permute-done((bf16[64,1024]{1,0:T(8,128)(2,1)S(1)}, bf16[64,1024]{1,0:T(8,128)(2,1)S(1)}, u32[]{:S(2)}, u32[]{:S(2)}) %collective-permute-start) | collective-permute-done | bytes 131104 | tf_op jit(solution)/shard_map/while/body/eval_jaxpr/ppermute | solution.py:13
  91.0 1.9 convolution_add_fusion.3
  93.0 1.9 collective-permute-start.1
  94.9 1.9 collective-permute-start
  96.8 6.8 %collective-permute-done = bf16[64,1024]{1,0:T(8,128)(2,1)S(1)} collective-permute-done((bf16[64,1024]{1,0:T(8,128)(2,1)S(1)}, bf16[64,1024]{1,0:T(8,128)(2,1)S(1)}, u32[]{:S(2)}, u32[]{:S(2)}) %collective-permute-start) | collective-permute-done | bytes 131104 | tf_op jit(solution)/shard_map/while/body/eval_jaxpr/ppermute | solution.py:13
  103.7 1.9 convolution_add_fusion.3
  105.7 1.9 collective-permute-start.1
  107.6 1.9 collective-permute-start
  109.5 6.8 %collective-permute-done = bf16[64,1024]{1,0:T(8,128)(2,1)S(1)} collective-permute-done((bf16[64,1024]{1,0:T(8,128)(2,1)S(1)}, bf16[64,1024]{1,0:T(8,128)(2,1)S(1)}, u32[]{:S(2)}, u32[]{:S(2)}) %collective-permute-start) | collective-permute-done | bytes 131104 | tf_op jit(solution)/shard_map/while/body/eval_jaxpr/ppermute | solution.py:13
  116.5 1.9 convolution_add_fusion.3
  118.4 1.9 collective-permute-start.1
  120.3 1.9 collective-permute-start
  122.3 6.8 %collective-permute-done = bf16[64,1024]{1,0:T(8,128)(2,1)S(1)} collective-permute-done((bf16[64,1024]{1,0:T(8,128)(2,1)S(1)}, bf16[64,1024]{1,0:T(8,128)(2,1)S(1)}, u32[]{:S(2)}, u32[]{:S(2)}) %collective-permute-start) | collective-permute-done | bytes 131104 | tf_op jit(solution)/shard_map/while/body/eval_jaxpr/ppermute | solution.py:13
  129.2 1.9 convolution_add_fusion.3
  131.2 1.9 collective-permute-start.1
  133.1 1.9 collective-permute-start
  135.0 6.8 %collective-permute-done = bf16[64,1024]{1,0:T(8,128)(2,1)S(1)} collective-permute-done((bf16[64,1024]{1,0:T(8,128)(2,1)S(1)}, bf16[64,1024]{1,0:T(8,128)(2,1)S(1)}, u32[]{:S(2)}, u32[]{:S(2)}) %collective-permute-start) | collective-permute-done | bytes 131104 | tf_op jit(solution)/shard_map/while/body/eval_jaxpr/ppermute | solution.py:13
  141.9 1.9 convolution_add_fusion.3
  147.7 7.3 %collective-permute-done = bf16[64,1024]{1,0:T(8,128)(2,1)S(1)} collective-permute-done((bf16[64,1024]{1,0:T(8,128)(2,1)S(1)}, bf16[64,1024]{1,0:T(8,128)(2,1)S(1)}, u32[]{:S(2)}, u32[]{:S(2)}) %collective-permute-start) | collective-permute-done | bytes 131104 | tf_op jit(solution)/shard_map/while/body/eval_jaxpr/ppermute | solution.py:13
  155.2 1.9 convolution_add_fusion.3
  161.0 8.4 %collective-permute-done = bf16[64,1024]{1,0:T(8,128)(2,1)S(1)} collective-permute-done((bf16[64,1024]{1,0:T(8,128)(2,1)S(1)}, bf16[64,1024]{1,0:T(8,128)(2,1)S(1)}, u32[]{:S(2)}, u32[]{:S(2)}) %collective-permute-start) | collective-permute-done | bytes 131104 | tf_op jit(solution)/shard_map/while/body/eval_jaxpr/ppermute | solution.py:13
  169.5 1.9 convolution_add_fusion.3
  175.4 9.5 %collective-permute-done = bf16[64,1024]{1,0:T(8,128)(2,1)S(1)} collective-permute-done((bf16[64,1024]{1,0:T(8,128)(2,1)S(1)}, bf16[64,1024]{1,0:T(8,128)(2,1)S(1)}, u32[]{:S(2)}, u32[]{:S(2)}) %collective-permute-start) | collective-permute-done | bytes 131104 | tf_op jit(solution)/shard_map/while/body/eval_jaxpr/ppermute | solution.py:13
  185.0 1.9 convolution_add_fusion.3
  186.9 1.9 collective-permute-start.1
  188.9 1.9 collective-permute-start
  190.8 10.5 %collective-permute-done = bf16[64,1024]{1,0:T(8,128)(2,1)S(1)} collective-permute-done((bf16[64,1024]{1,0:T(8,128)(2,1)S(1)}, bf16[64,1024]{1,0:T(8,128)(2,1)S(1)}, u32[]{:S(2)}, u32[]{:S(2)}) %collective-permute-start) | collective-permute-done | bytes 131104 | tf_op jit(solution)/shard_map/while/body/eval_jaxpr/ppermute | solution.py:13
  201.5 1.9 convolution_add_fusion.3
  205.4 1.9 collective-permute-start
  207.3 10.5 %collective-permute-done = bf16[64,1024]{1,0:T(8,128)(2,1)S(1)} collective-permute-done((bf16[64,1024]{1,0:T(8,128)(2,1)S(1)}, bf16[64,1024]{1,0:T(8,128)(2,1)S(1)}, u32[]{:S(2)}, u32[]{:S(2)}) %collective-permute-start) | collective-permute-done | bytes 131104 | tf_op jit(solution)/shard_map/while/body/eval_jaxpr/ppermute | solution.py:13
  218.0 1.9 convolution_add_fusion.3
  223.8 9.6 %collective-permute-done = bf16[64,1024]{1,0:T(8,128)(2,1)S(1)} collective-permute-done((bf16[64,1024]{1,0:T(8,128)(2,1)S(1)}, bf16[64,1024]{1,0:T(8,128)(2,1)S(1)}, u32[]{:S(2)}, u32[]{:S(2)}) %collective-permute-start) | collective-permute-done | bytes 131104 | tf_op jit(solution)/shard_map/while/body/eval_jaxpr/ppermute | solution.py:13
  233.5 1.9 convolution_add_fusion.1
  237.4 5.9 %collective-permute-done.2 = bf16[64,1024]{1,0:T(8,128)(2,1)S(1)} collective-permute-done((bf16[64,1024]{1,0:T(8,128)(2,1)S(1)}, bf16[64,1024]{1,0:T(8,128)(2,1)S(1)}, u32[]{:S(2)}, u32[]{:S(2)}) %collective-permute-start.2) | collective-permute-done | bytes 131104 | tf_op jit(solution)/shard_map/ppermute | solution.py:13
  246.0 3.8 sort.34
  249.7 3.8 sort.35
  253.7 32.0 %all-reduce = s32[2048]{0:T(1024)S(1)} all-reduce(s32[2048]{0:T(1024)S(1)} %dynamic-update-slice), channel_id=1, replica_groups=mesh['dp'=32,'blk'=16] {'dp'}, use_global_device_ids=true, to_apply=%add | all-reduce | flops 2048 | bytes 16384
  285.7 13.2 %gather_fusion.1 = s32[2048]{0:T(1024)S(1)} fusion(s32[512]{0:T(512)S(1)} %get-tuple-element.41, s32[2048]{0:T(1024)S(1)} %fusion.15), kind=kCustom, calls=%fused_computation.1 | custom fusion | bytes 24576 | tf_op jit(solution)/shard_map/gather | solution.py:64
  299.1 26.1 %all-gather.3.cloned.1.call-done = bf16[2048,1024]{1,0:T(8,128)(2,1)} async-done(((bf16[64,1024]{1,0:T(8,128)(2,1)}), bf16[2048,1024]{1,0:T(8,128)(2,1)}) %all-gather.3.cloned.1.call-update) | async-done | bytes 4194320 | tf_op jit(solution)/shard_map/all_gather | solution.py:62
  325.2 2.8 convolution_convert_fusion
  328.0 49.9 %all-reduce.1 = (bf16[16,1024]{1,0:T(8,128)(2,1)S(1)}, bf16[16]{0:T(256)(128)(2,1)S(1)}) all-reduce(bf16[16,1024]{1,0:T(8,128)(2,1)S(1)} %convolution_convert_fusion, bf16[16]{0:T(256)(128)(2,1)S(1)} %fusion.11), channel_id=1, replica_groups=mesh['dp'=32,'blk'=16] {'blk'}, use_global_device_ids=true, to_apply=%region_7.8 | all-reduce | flops 16400 | bytes 65600 | tf_op jit(solution)/shard_map/psum | solution.py:71
  378.7 66.9 %all-gather.5.cloned.1.call-done = bf16[512,1024]{1,0:T(8,128)(2,1)} async-done(((bf16[16,1024]{1,0:T(8,128)(2,1)}), bf16[512,1024]{1,0:T(8,128)(2,1)}) %all-gather.5.cloned.1.call-update) | async-done | bytes 1048592 | tf_op jit(solution)/shard_map/all_gather | solution.py:75
  445.6 4.1 gather_fusion.2
  (108 shorter events, 28.4 us)
Async XLA Ops:
  7.2 1.4 copy-start
  7.2 318.0 %all-gather.3.cloned.1.call-start = ((), (), s32[]{:S(2)}) async-start(), calls=%async_computation | async-start | bytes 4325376 | tf_op jit(solution)/shard_map/all_gather | solution.py:62
  8.6 2.4 copy-start.1
  13.1 21.3 %collective-permute-start.1 = (f32[64,1024]{1,0:T(8,128)S(1)}, f32[64,1024]{1,0:T(8,128)S(1)}, u32[]{:S(2)}, u32[]{:S(2)}) collective-permute-start(f32[64,1024]{1,0:T(8,128)S(1)} %convolution_add_fusion.3), channel_id=1, source_target_pairs={{0,1},{1,2},{2,3},{3,4},{4,5},{5,6},{6,7},{7,8},{8,9},{9,10},{10,1... | collective-permute-start | bytes 786440 | tf_op jit(solution)/shard_map/while/body/eval_jaxpr/ppermute | solution.py:13
  17.1 17.3 %collective-permute-start = (bf16[64,1024]{1,0:T(8,128)(2,1)S(1)}, bf16[64,1024]{1,0:T(8,128)(2,1)S(1)}, u32[]{:S(2)}, u32[]{:S(2)}) collective-permute-start(bf16[64,1024]{1,0:T(8,128)(2,1)S(1)} %copy.13), channel_id=1, source_target_pairs={{0,1},{1,2},{2,3},{3,4},{4,5},{5,6},{6,7},{7,8},{8,9},{9,10},{10,1... | collective-permute-start | bytes 393224 | tf_op jit(solution)/shard_map/while/body/eval_jaxpr/ppermute | solution.py:13
  36.5 13.4 %collective-permute-start.1 = (f32[64,1024]{1,0:T(8,128)S(1)}, f32[64,1024]{1,0:T(8,128)S(1)}, u32[]{:S(2)}, u32[]{:S(2)}) collective-permute-start(f32[64,1024]{1,0:T(8,128)S(1)} %convolution_add_fusion.3), channel_id=1, source_target_pairs={{0,1},{1,2},{2,3},{3,4},{4,5},{5,6},{6,7},{7,8},{8,9},{9,10},{10,1... | collective-permute-start | bytes 786440 | tf_op jit(solution)/shard_map/while/body/eval_jaxpr/ppermute | solution.py:13
  38.5 11.5 %collective-permute-start = (bf16[64,1024]{1,0:T(8,128)(2,1)S(1)}, bf16[64,1024]{1,0:T(8,128)(2,1)S(1)}, u32[]{:S(2)}, u32[]{:S(2)}) collective-permute-start(bf16[64,1024]{1,0:T(8,128)(2,1)S(1)} %copy.13), channel_id=1, source_target_pairs={{0,1},{1,2},{2,3},{3,4},{4,5},{5,6},{6,7},{7,8},{8,9},{9,10},{10,1... | collective-permute-start | bytes 393224 | tf_op jit(solution)/shard_map/while/body/eval_jaxpr/ppermute | solution.py:13
  52.0 12.5 %collective-permute-start.1 = (f32[64,1024]{1,0:T(8,128)S(1)}, f32[64,1024]{1,0:T(8,128)S(1)}, u32[]{:S(2)}, u32[]{:S(2)}) collective-permute-start(f32[64,1024]{1,0:T(8,128)S(1)} %convolution_add_fusion.3), channel_id=1, source_target_pairs={{0,1},{1,2},{2,3},{3,4},{4,5},{5,6},{6,7},{7,8},{8,9},{9,10},{10,1... | collective-permute-start | bytes 786440 | tf_op jit(solution)/shard_map/while/body/eval_jaxpr/ppermute | solution.py:13
  54.0 10.5 %collective-permute-start = (bf16[64,1024]{1,0:T(8,128)(2,1)S(1)}, bf16[64,1024]{1,0:T(8,128)(2,1)S(1)}, u32[]{:S(2)}, u32[]{:S(2)}) collective-permute-start(bf16[64,1024]{1,0:T(8,128)(2,1)S(1)} %copy.13), channel_id=1, source_target_pairs={{0,1},{1,2},{2,3},{3,4},{4,5},{5,6},{6,7},{7,8},{8,9},{9,10},{10,1... | collective-permute-start | bytes 393224 | tf_op jit(solution)/shard_map/while/body/eval_jaxpr/ppermute | solution.py:13
  66.6 11.5 %collective-permute-start.1 = (f32[64,1024]{1,0:T(8,128)S(1)}, f32[64,1024]{1,0:T(8,128)S(1)}, u32[]{:S(2)}, u32[]{:S(2)}) collective-permute-start(f32[64,1024]{1,0:T(8,128)S(1)} %convolution_add_fusion.3), channel_id=1, source_target_pairs={{0,1},{1,2},{2,3},{3,4},{4,5},{5,6},{6,7},{7,8},{8,9},{9,10},{10,1... | collective-permute-start | bytes 786440 | tf_op jit(solution)/shard_map/while/body/eval_jaxpr/ppermute | solution.py:13
  68.5 9.6 %collective-permute-start = (bf16[64,1024]{1,0:T(8,128)(2,1)S(1)}, bf16[64,1024]{1,0:T(8,128)(2,1)S(1)}, u32[]{:S(2)}, u32[]{:S(2)}) collective-permute-start(bf16[64,1024]{1,0:T(8,128)(2,1)S(1)} %copy.13), channel_id=1, source_target_pairs={{0,1},{1,2},{2,3},{3,4},{4,5},{5,6},{6,7},{7,8},{8,9},{9,10},{10,1... | collective-permute-start | bytes 393224 | tf_op jit(solution)/shard_map/while/body/eval_jaxpr/ppermute | solution.py:13
  80.2 10.6 %collective-permute-start.1 = (f32[64,1024]{1,0:T(8,128)S(1)}, f32[64,1024]{1,0:T(8,128)S(1)}, u32[]{:S(2)}, u32[]{:S(2)}) collective-permute-start(f32[64,1024]{1,0:T(8,128)S(1)} %convolution_add_fusion.3), channel_id=1, source_target_pairs={{0,1},{1,2},{2,3},{3,4},{4,5},{5,6},{6,7},{7,8},{8,9},{9,10},{10,1... | collective-permute-start | bytes 786440 | tf_op jit(solution)/shard_map/while/body/eval_jaxpr/ppermute | solution.py:13
  82.1 8.7 %collective-permute-start = (bf16[64,1024]{1,0:T(8,128)(2,1)S(1)}, bf16[64,1024]{1,0:T(8,128)(2,1)S(1)}, u32[]{:S(2)}, u32[]{:S(2)}) collective-permute-start(bf16[64,1024]{1,0:T(8,128)(2,1)S(1)} %copy.13), channel_id=1, source_target_pairs={{0,1},{1,2},{2,3},{3,4},{4,5},{5,6},{6,7},{7,8},{8,9},{9,10},{10,1... | collective-permute-start | bytes 393224 | tf_op jit(solution)/shard_map/while/body/eval_jaxpr/ppermute | solution.py:13
  93.0 10.6 %collective-permute-start.1 = (f32[64,1024]{1,0:T(8,128)S(1)}, f32[64,1024]{1,0:T(8,128)S(1)}, u32[]{:S(2)}, u32[]{:S(2)}) collective-permute-start(f32[64,1024]{1,0:T(8,128)S(1)} %convolution_add_fusion.3), channel_id=1, source_target_pairs={{0,1},{1,2},{2,3},{3,4},{4,5},{5,6},{6,7},{7,8},{8,9},{9,10},{10,1... | collective-permute-start | bytes 786440 | tf_op jit(solution)/shard_map/while/body/eval_jaxpr/ppermute | solution.py:13
  94.9 8.7 %collective-permute-start = (bf16[64,1024]{1,0:T(8,128)(2,1)S(1)}, bf16[64,1024]{1,0:T(8,128)(2,1)S(1)}, u32[]{:S(2)}, u32[]{:S(2)}) collective-permute-start(bf16[64,1024]{1,0:T(8,128)(2,1)S(1)} %copy.13), channel_id=1, source_target_pairs={{0,1},{1,2},{2,3},{3,4},{4,5},{5,6},{6,7},{7,8},{8,9},{9,10},{10,1... | collective-permute-start | bytes 393224 | tf_op jit(solution)/shard_map/while/body/eval_jaxpr/ppermute | solution.py:13
  105.7 10.6 %collective-permute-start.1 = (f32[64,1024]{1,0:T(8,128)S(1)}, f32[64,1024]{1,0:T(8,128)S(1)}, u32[]{:S(2)}, u32[]{:S(2)}) collective-permute-start(f32[64,1024]{1,0:T(8,128)S(1)} %convolution_add_fusion.3), channel_id=1, source_target_pairs={{0,1},{1,2},{2,3},{3,4},{4,5},{5,6},{6,7},{7,8},{8,9},{9,10},{10,1... | collective-permute-start | bytes 786440 | tf_op jit(solution)/shard_map/while/body/eval_jaxpr/ppermute | solution.py:13
  107.6 8.7 %collective-permute-start = (bf16[64,1024]{1,0:T(8,128)(2,1)S(1)}, bf16[64,1024]{1,0:T(8,128)(2,1)S(1)}, u32[]{:S(2)}, u32[]{:S(2)}) collective-permute-start(bf16[64,1024]{1,0:T(8,128)(2,1)S(1)} %copy.13), channel_id=1, source_target_pairs={{0,1},{1,2},{2,3},{3,4},{4,5},{5,6},{6,7},{7,8},{8,9},{9,10},{10,1... | collective-permute-start | bytes 393224 | tf_op jit(solution)/shard_map/while/body/eval_jaxpr/ppermute | solution.py:13
  118.4 10.6 %collective-permute-start.1 = (f32[64,1024]{1,0:T(8,128)S(1)}, f32[64,1024]{1,0:T(8,128)S(1)}, u32[]{:S(2)}, u32[]{:S(2)}) collective-permute-start(f32[64,1024]{1,0:T(8,128)S(1)} %convolution_add_fusion.3), channel_id=1, source_target_pairs={{0,1},{1,2},{2,3},{3,4},{4,5},{5,6},{6,7},{7,8},{8,9},{9,10},{10,1... | collective-permute-start | bytes 786440 | tf_op jit(solution)/shard_map/while/body/eval_jaxpr/ppermute | solution.py:13
  120.3 8.7 %collective-permute-start = (bf16[64,1024]{1,0:T(8,128)(2,1)S(1)}, bf16[64,1024]{1,0:T(8,128)(2,1)S(1)}, u32[]{:S(2)}, u32[]{:S(2)}) collective-permute-start(bf16[64,1024]{1,0:T(8,128)(2,1)S(1)} %copy.13), channel_id=1, source_target_pairs={{0,1},{1,2},{2,3},{3,4},{4,5},{5,6},{6,7},{7,8},{8,9},{9,10},{10,1... | collective-permute-start | bytes 393224 | tf_op jit(solution)/shard_map/while/body/eval_jaxpr/ppermute | solution.py:13
  131.2 10.6 %collective-permute-start.1 = (f32[64,1024]{1,0:T(8,128)S(1)}, f32[64,1024]{1,0:T(8,128)S(1)}, u32[]{:S(2)}, u32[]{:S(2)}) collective-permute-start(f32[64,1024]{1,0:T(8,128)S(1)} %convolution_add_fusion.3), channel_id=1, source_target_pairs={{0,1},{1,2},{2,3},{3,4},{4,5},{5,6},{6,7},{7,8},{8,9},{9,10},{10,1... | collective-permute-start | bytes 786440 | tf_op jit(solution)/shard_map/while/body/eval_jaxpr/ppermute | solution.py:13
  133.1 8.7 %collective-permute-start = (bf16[64,1024]{1,0:T(8,128)(2,1)S(1)}, bf16[64,1024]{1,0:T(8,128)(2,1)S(1)}, u32[]{:S(2)}, u32[]{:S(2)}) collective-permute-start(bf16[64,1024]{1,0:T(8,128)(2,1)S(1)} %copy.13), channel_id=1, source_target_pairs={{0,1},{1,2},{2,3},{3,4},{4,5},{5,6},{6,7},{7,8},{8,9},{9,10},{10,1... | collective-permute-start | bytes 393224 | tf_op jit(solution)/shard_map/while/body/eval_jaxpr/ppermute | solution.py:13
  143.9 11.2 %collective-permute-start.1 = (f32[64,1024]{1,0:T(8,128)S(1)}, f32[64,1024]{1,0:T(8,128)S(1)}, u32[]{:S(2)}, u32[]{:S(2)}) collective-permute-start(f32[64,1024]{1,0:T(8,128)S(1)} %convolution_add_fusion.3), channel_id=1, source_target_pairs={{0,1},{1,2},{2,3},{3,4},{4,5},{5,6},{6,7},{7,8},{8,9},{9,10},{10,1... | collective-permute-start | bytes 786440 | tf_op jit(solution)/shard_map/while/body/eval_jaxpr/ppermute | solution.py:13
  145.8 9.2 %collective-permute-start = (bf16[64,1024]{1,0:T(8,128)(2,1)S(1)}, bf16[64,1024]{1,0:T(8,128)(2,1)S(1)}, u32[]{:S(2)}, u32[]{:S(2)}) collective-permute-start(bf16[64,1024]{1,0:T(8,128)(2,1)S(1)} %copy.13), channel_id=1, source_target_pairs={{0,1},{1,2},{2,3},{3,4},{4,5},{5,6},{6,7},{7,8},{8,9},{9,10},{10,1... | collective-permute-start | bytes 393224 | tf_op jit(solution)/shard_map/while/body/eval_jaxpr/ppermute | solution.py:13
  157.1 12.2 %collective-permute-start.1 = (f32[64,1024]{1,0:T(8,128)S(1)}, f32[64,1024]{1,0:T(8,128)S(1)}, u32[]{:S(2)}, u32[]{:S(2)}) collective-permute-start(f32[64,1024]{1,0:T(8,128)S(1)} %convolution_add_fusion.3), channel_id=1, source_target_pairs={{0,1},{1,2},{2,3},{3,4},{4,5},{5,6},{6,7},{7,8},{8,9},{9,10},{10,1... | collective-permute-start | bytes 786440 | tf_op jit(solution)/shard_map/while/body/eval_jaxpr/ppermute | solution.py:13
  159.1 10.3 %collective-permute-start = (bf16[64,1024]{1,0:T(8,128)(2,1)S(1)}, bf16[64,1024]{1,0:T(8,128)(2,1)S(1)}, u32[]{:S(2)}, u32[]{:S(2)}) collective-permute-start(bf16[64,1024]{1,0:T(8,128)(2,1)S(1)} %copy.13), channel_id=1, source_target_pairs={{0,1},{1,2},{2,3},{3,4},{4,5},{5,6},{6,7},{7,8},{8,9},{9,10},{10,1... | collective-permute-start | bytes 393224 | tf_op jit(solution)/shard_map/while/body/eval_jaxpr/ppermute | solution.py:13
  171.5 13.3 %collective-permute-start.1 = (f32[64,1024]{1,0:T(8,128)S(1)}, f32[64,1024]{1,0:T(8,128)S(1)}, u32[]{:S(2)}, u32[]{:S(2)}) collective-permute-start(f32[64,1024]{1,0:T(8,128)S(1)} %convolution_add_fusion.3), channel_id=1, source_target_pairs={{0,1},{1,2},{2,3},{3,4},{4,5},{5,6},{6,7},{7,8},{8,9},{9,10},{10,1... | collective-permute-start | bytes 786440 | tf_op jit(solution)/shard_map/while/body/eval_jaxpr/ppermute | solution.py:13
  173.4 11.4 %collective-permute-start = (bf16[64,1024]{1,0:T(8,128)(2,1)S(1)}, bf16[64,1024]{1,0:T(8,128)(2,1)S(1)}, u32[]{:S(2)}, u32[]{:S(2)}) collective-permute-start(bf16[64,1024]{1,0:T(8,128)(2,1)S(1)} %copy.13), channel_id=1, source_target_pairs={{0,1},{1,2},{2,3},{3,4},{4,5},{5,6},{6,7},{7,8},{8,9},{9,10},{10,1... | collective-permute-start | bytes 393224 | tf_op jit(solution)/shard_map/while/body/eval_jaxpr/ppermute | solution.py:13
  186.9 14.4 %collective-permute-start.1 = (f32[64,1024]{1,0:T(8,128)S(1)}, f32[64,1024]{1,0:T(8,128)S(1)}, u32[]{:S(2)}, u32[]{:S(2)}) collective-permute-start(f32[64,1024]{1,0:T(8,128)S(1)} %convolution_add_fusion.3), channel_id=1, source_target_pairs={{0,1},{1,2},{2,3},{3,4},{4,5},{5,6},{6,7},{7,8},{8,9},{9,10},{10,1... | collective-permute-start | bytes 786440 | tf_op jit(solution)/shard_map/while/body/eval_jaxpr/ppermute | solution.py:13
  188.9 12.5 %collective-permute-start = (bf16[64,1024]{1,0:T(8,128)(2,1)S(1)}, bf16[64,1024]{1,0:T(8,128)(2,1)S(1)}, u32[]{:S(2)}, u32[]{:S(2)}) collective-permute-start(bf16[64,1024]{1,0:T(8,128)(2,1)S(1)} %copy.13), channel_id=1, source_target_pairs={{0,1},{1,2},{2,3},{3,4},{4,5},{5,6},{6,7},{7,8},{8,9},{9,10},{10,1... | collective-permute-start | bytes 393224 | tf_op jit(solution)/shard_map/while/body/eval_jaxpr/ppermute | solution.py:13
  203.4 14.4 %collective-permute-start.1 = (f32[64,1024]{1,0:T(8,128)S(1)}, f32[64,1024]{1,0:T(8,128)S(1)}, u32[]{:S(2)}, u32[]{:S(2)}) collective-permute-start(f32[64,1024]{1,0:T(8,128)S(1)} %convolution_add_fusion.3), channel_id=1, source_target_pairs={{0,1},{1,2},{2,3},{3,4},{4,5},{5,6},{6,7},{7,8},{8,9},{9,10},{10,1... | collective-permute-start | bytes 786440 | tf_op jit(solution)/shard_map/while/body/eval_jaxpr/ppermute | solution.py:13
  205.4 12.4 %collective-permute-start = (bf16[64,1024]{1,0:T(8,128)(2,1)S(1)}, bf16[64,1024]{1,0:T(8,128)(2,1)S(1)}, u32[]{:S(2)}, u32[]{:S(2)}) collective-permute-start(bf16[64,1024]{1,0:T(8,128)(2,1)S(1)} %copy.13), channel_id=1, source_target_pairs={{0,1},{1,2},{2,3},{3,4},{4,5},{5,6},{6,7},{7,8},{8,9},{9,10},{10,1... | collective-permute-start | bytes 393224 | tf_op jit(solution)/shard_map/while/body/eval_jaxpr/ppermute | solution.py:13
  219.9 13.5 %collective-permute-start.1 = (f32[64,1024]{1,0:T(8,128)S(1)}, f32[64,1024]{1,0:T(8,128)S(1)}, u32[]{:S(2)}, u32[]{:S(2)}) collective-permute-start(f32[64,1024]{1,0:T(8,128)S(1)} %convolution_add_fusion.3), channel_id=1, source_target_pairs={{0,1},{1,2},{2,3},{3,4},{4,5},{5,6},{6,7},{7,8},{8,9},{9,10},{10,1... | collective-permute-start | bytes 786440 | tf_op jit(solution)/shard_map/while/body/eval_jaxpr/ppermute | solution.py:13
  221.8 11.5 %collective-permute-start = (bf16[64,1024]{1,0:T(8,128)(2,1)S(1)}, bf16[64,1024]{1,0:T(8,128)(2,1)S(1)}, u32[]{:S(2)}, u32[]{:S(2)}) collective-permute-start(bf16[64,1024]{1,0:T(8,128)(2,1)S(1)} %copy.13), channel_id=1, source_target_pairs={{0,1},{1,2},{2,3},{3,4},{4,5},{5,6},{6,7},{7,8},{8,9},{9,10},{10,1... | collective-permute-start | bytes 393224 | tf_op jit(solution)/shard_map/while/body/eval_jaxpr/ppermute | solution.py:13
  233.4 12.6 %copy-start.4 = (s32[512]{0:T(512)S(1)}, s32[512]{0:T(512)}, u32[]{:S(2)}) copy-start(s32[512]{0:T(512)} %param.13) | copy-start | bytes 6148
  233.4 20.1 %copy-start.5 = (s32[64]{0:T(128)S(1)}, s32[64]{0:T(128)}, u32[]{:S(2)}) copy-start(s32[64]{0:T(128)} %param.9) | copy-start | bytes 772
  235.5 7.8 %collective-permute-start.2 = (bf16[64,1024]{1,0:T(8,128)(2,1)S(1)}, bf16[64,1024]{1,0:T(8,128)(2,1)S(1)}, u32[]{:S(2)}, u32[]{:S(2)}) collective-permute-start(bf16[64,1024]{1,0:T(8,128)(2,1)S(1)} %convolution_add_fusion.1), channel_id=1, source_target_pairs={{0,1},{1,2},{2,3},{3,4},{4,5},{5,6},{6,7},{7,8},{8,9},{9,10},{10,1... | collective-permute-start | bytes 393224 | tf_op jit(solution)/shard_map/ppermute | solution.py:13
  243.3 0.7 copy-start.2
  244.0 201.6 %all-gather.5.cloned.1.call-start = ((), (), s32[]{:S(2)}) async-start(), calls=%async_computation.1 | async-start | bytes 1081344 | tf_op jit(solution)/shard_map/all_gather | solution.py:75
  378.7 71.3 %copy-start.3 = (bf16[64,1024]{1,0:T(8,128)(2,1)S(1)}, bf16[64,1024]{1,0:T(8,128)(2,1)}, u32[]{:S(2)}) copy-start(bf16[64,1024]{1,0:T(8,128)(2,1)} %copy-done.2) | copy-start | bytes 393220
Sparse Core Ops, SparseCore 0:
  244.1 81.0 all-gather.2
  378.8 66.7 all-gather.4
where the time goes:
time: 460 us; the launch traced here: 459 us
  waiting for transfers between devices  228 us (50%)
  blocking collectives  81.9 us (18%)
  starting transfers between devices  63.7 us (14%)
  matrix products  35 us (8%)
  local copies, waits for them, and re-layouts  22.9 us (5%)
  between operations  14.8 us (3%)
  other arithmetic  11.9 us (3%)
    ppermute x31, waiting for transfers between devices, shifted(): lax.ppermute(value, axis, [(i, (i + by) % size) for i in range(size)])  135 us
    all_gather x1, waiting for transfers between devices, body(): ranked_centroids = lax.all_gather(owned_centroids, 'dp', axis=0, tiled=True)  66.9 us
    ppermute x31, starting transfers between devices, shifted(): lax.ppermute(value, axis, [(i, (i + by) % size) for i in range(size)])  63.6 us
    psum x1, blocking collectives, body(): lax.psum(owner_totals.astype(jnp.bfloat16), 'blk').astype(jnp.float32)  49.9 us
    unnamed x1, blocking collectives  32 us
    dot_general x16, matrix products, project(): return jnp.dot(kernel, whitening, preferred_element_type=jnp.float32)  31 us
    all_gather x1, waiting for transfers between devices, body(): rows_piece = lax.all_gather(features, 'dp', axis=0, tiled=True)  26.1 us
    gather x1, local copies, waits for them, and re-layouts, body(): local_rank = ranking[member_piece] - owner_start  13.2 us
  transfers between devices with their start and end apart: 33, of which 18 were waited for; matrix products, arithmetic and copies ran while one was open for 5% of the time, Pallas kernels for 0%

commit v1 on v0

v1 whole, which is shorter than its diff:
```python
import math

import jax
import jax.numpy as jnp
from jax import lax
from jax.sharding import Mesh, PartitionSpec as P

epsilon = 1e-06
bf16 = jnp.bfloat16
f32 = jnp.float32
ALL = ("yh", "x", "c", "z", "yl")
PLANE = ("yh", "x", "yl")
PACK = 16


def hop(value, axis, by):
    size = math.prod(lax.axis_size(name) for name in (axis if isinstance(axis, tuple) else (axis,)))
    return lax.ppermute(value, axis, [(i, (i + by) % size) for i in range(size)])


def flip(value, axis, bit):
    size = lax.axis_size(axis)
    return lax.ppermute(value, axis, [(i, i ^ bit) for i in range(size)])


def pick(matrix, start, count):
    return lax.dynamic_slice_in_dim(matrix, start, count, 0)


def ordered(mine, other, first):
    return jnp.where(first, jnp.concatenate([mine, other]), jnp.concatenate([other, mine]))


def body(points, membership, landmark_pool, landmark_ids, whitening, owner_map):
    rows, width = points.shape
    rank_width = whitening.shape[1]
    clusters = owner_map.shape[0]
    ring = lax.axis_size("z")
    core = lax.axis_index("c")
    first = core == 0
    upper = lax.axis_index("yl") == 0
    quarter = landmark_ids.shape[0] // 4

    digits = jnp.stack([membership // 128, membership % 128]).astype(bf16)
    tail = jnp.zeros((PACK, width), bf16).at[:2, :rows].set(digits)
    block = jnp.concatenate([points, tail])

    landmarks = landmark_pool[landmark_ids]

    def exchange(matrix):
        up = hop(pick(matrix, 2 * core * quarter, quarter), ("yh", "yl"), 1)
        down = hop(pick(matrix, (2 * core + 1) * quarter, quarter), ("yh", "yl"), -1)
        mine = jnp.concatenate([up, down])
        return ordered(mine, flip(mine, "c", 1), first)

    ahead, behind = [block], [block]
    partner = None
    for step in range(ring // 2):
        ahead.append(hop(ahead[-1], "z", 1))
        if step < ring // 2 - 1:
            behind.append(hop(behind[-1], "z", -1))
    partner = exchange(landmarks)
    partner_white = exchange(whitening)
    offsets = [-k for k in range(ring // 2 + 1)] + list(range(1, ring // 2))
    held = ahead + behind[1:]
    visitors = jnp.concatenate([part[:rows] for part in held])
    codes = jnp.stack([part[rows : rows + 2, :rows] for part in held], 1).reshape(2, ring * rows)
    members = codes[0].astype(jnp.int32) * 128 + codes[1].astype(jnp.int32)

    def inverse_length(matrix):
        return lax.rsqrt(jnp.sum(jnp.square(matrix.astype(f32)), axis=1) + epsilon)

    visitor_factor = inverse_length(visitors) * math.sqrt(width)

    def affinity(anchors):
        gram = lax.dot_general(visitors, anchors, (((1,), (1,)), ((), ())), preferred_element_type=f32)
        return jnp.exp(gram * visitor_factor[:, None] * inverse_length(anchors)[None, :]).astype(bf16)

    kernel_own = affinity(landmarks)
    kernel_partner = affinity(partner)
    table = jnp.arange(clusters, dtype=jnp.int32)[:, None] == members[None, :]
    counted = jnp.sum(table.astype(jnp.int32), axis=1)
    table = table.astype(bf16)
    sums_own = jnp.dot(table, kernel_own, preferred_element_type=f32).astype(bf16)
    sums_partner = jnp.dot(table, kernel_partner, preferred_element_type=f32).astype(bf16)
    count_tail = (
        jnp.zeros((clusters, 128), bf16)
        .at[:, 0].set((counted // 128).astype(bf16))
        .at[:, 1].set((counted % 128).astype(bf16))
    )
    sums = jnp.concatenate(
        [jnp.where(upper, sums_own, sums_partner), jnp.where(upper, sums_partner, sums_own), count_tail], 1
    )
    half = clusters // 2
    theirs = flip(pick(sums, (1 - core) * half, half), "c", 1)
    paired = (pick(sums, core * half, half).astype(f32) + theirs.astype(f32)).astype(bf16)
    peers = math.prod(lax.axis_size(name) for name in PLANE)
    share = half // peers

    partial = (
        jnp.dot(kernel_own, whitening, preferred_element_type=f32)
        + jnp.dot(kernel_partner, partner_white, preferred_element_type=f32)
    ).reshape(ring, rows, rank_width)
    place = {off: partial[i] for i, off in enumerate(offsets)}
    place[ring // 2] = place[-(ring // 2)]
    plus = place[ring // 2].astype(bf16)
    minus = place[-(ring // 2 - 1)].astype(bf16)
    for k in range(ring // 2 - 1, -1, -1):
        plus = hop(plus, "z", 1).astype(f32) + (place[k] if k else 0.0)
        if k:
            plus = plus.astype(bf16)
        if k < ring // 2 - 1:
            minus = hop(minus, "z", -1).astype(f32) + (place[-k] if k else 0.0)
            if k:
                minus = minus.astype(bf16)
    features = (place[0] + plus + minus).astype(bf16)

    spread = lax.all_to_all(paired.reshape(peers, share, -1), PLANE, 0, 0)
    total = jnp.sum(spread.astype(f32), axis=0)
    sums_f = total[:, : 2 * landmark_ids.shape[0]]
    high = sums_f.astype(bf16)
    low = (sums_f - high.astype(f32)).astype(bf16)
    white = jnp.where(upper, jnp.concatenate([whitening, partner_white]), jnp.concatenate([partner_white, whitening]))
    mapped = jnp.dot(jnp.concatenate([high, low]), white, preferred_element_type=f32)
    mapped = mapped[:share] + mapped[share:]
    number = total[:, -128] * 128.0 + total[:, -127]
    bit = 1
    while bit < ring:
        mapped = mapped + flip(mapped, "z", bit)
        bit *= 2
    means = (mapped / jnp.maximum(number, 1.0)[:, None]).astype(bf16)

    sent = jnp.broadcast_to(means[None], (peers, share, rank_width))
    mine = lax.all_to_all(sent, PLANE, 0, 0).reshape(half, rank_width)
    other = flip(mine, "c", 1)
    centroids = ordered(mine, other, first)

    owner = lax.axis_index(("yh", "x", "c"))
    owned_by = (owner_map == owner).astype(jnp.int32)
    slot = jnp.cumsum(owned_by) - 1
    per_owner = clusters // (lax.axis_size("yh") * lax.axis_size("x") * lax.axis_size("c"))
    choose = (jnp.arange(per_owner)[:, None] == slot[None, :]) & (owned_by[None, :] == 1)
    owned_centroids = jnp.dot(choose.astype(bf16), centroids, preferred_element_type=f32).astype(bf16)

    centre = centroids.astype(f32)
    squared_norms = jnp.sum(centre * centre, axis=1)
    inner = lax.dot_general(features, centroids, (((1,), (1,)), ((), ())), preferred_element_type=f32)
    scores = (squared_norms[None, :] - 2.0 * inner) / rank_width
    return (features, owned_centroids, scores)


def build(mesh, factors):
    fine = Mesh(mesh.devices.reshape(factors), ALL)
    blk, dp = ("z", "yl"), ("yh", "x", "c")
    return jax.shard_map(
        body,
        mesh=fine,
        in_specs=(P(ALL, None), P(ALL), P(blk, None), P(blk), P(blk, None), P()),
        out_specs=(P(ALL, None), P(dp, None), P(ALL, None)),
        check_vma=False,
    )


def solution(mesh):
    return build(mesh, (4, 4, 2, 8, 2))
```

time: 460 us -> 195 us (0.42)
  waiting for transfers between devices: 228 us -> 35.5 us
  blocking collectives: 81.9 us -> 0 us
  starting transfers between devices: 63.7 us -> 108 us
  matrix products: 35 us -> 15 us
  between operations: 14.8 us -> 1.36 us
  local copies, waits for them, and re-layouts: 22.9 us -> 15.4 us
  other arithmetic: 11.9 us -> 18.5 us
    ppermute x31 -> x25, waiting for transfers between devices: 135 us -> 35.5 us  [the longest x18 29.2 us: hop(): lax.ppermute(value, axis, [(i, (i + by) % size) for i in range(size)])]
    all_gather x2 -> x0, waiting for transfers between devices: 93 us -> none  [the longest x1 66.9 us: body(): ranked_centroids = lax.all_gather(owned_centroids, 'dp', axis=0, tiled=True)]
    psum x1 -> x0, blocking collectives: 49.9 us -> none  [body(): lax.psum(owner_totals.astype(jnp.bfloat16), 'blk').astype(jnp.float32)]
    unnamed x1 -> x0, blocking collectives: 32 us -> none
    ppermute x31 -> x25, starting transfers between devices: 63.6 us -> 91.3 us  [the longest x18 63.2 us: hop(): lax.ppermute(value, axis, [(i, (i + by) % size) for i in range(size)])]
    dot_general x18 -> x9, matrix products: 35 us -> 15 us  [the longest x2 4.29 us: affinity(): lax.dot_general(visitors, anchors, (((1,), (1,)), ((), ())), preferred_el...]
    gather x2 -> x0, local copies, waits for them, and re-layouts: 17.3 us -> none  [the longest x1 13.2 us: body(): local_rank = ranking[member_piece] - owner_start]
    all_to_all x0 -> x2, starting transfers between devices: none -> 16.4 us  [the longest x1 9.43 us: body(): spread = lax.all_to_all(paired.reshape(peers, share, -1), PLANE, 0, 0)]
  transfers between devices with their start and end apart: 33 -> 27, of which waited for: 18 -> 10; matrix products, arithmetic and copies ran while one was open for 5% -> 18% of each run, Pallas kernels for 0% -> 0%
where the time goes in v1:
time: 195 us; the launch traced here: 193 us
  starting transfers between devices  108 us (55%)
  waiting for transfers between devices  35.5 us (18%)
  other arithmetic  18.5 us (9%)
  local copies, waits for them, and re-layouts  15.4 us (8%)
  matrix products  15 us (8%)
    ppermute x18, starting transfers between devices, hop(): lax.ppermute(value, axis, [(i, (i + by) % size) for i in range(size)])  63.2 us
    ppermute x18, waiting for transfers between devices, hop(): lax.ppermute(value, axis, [(i, (i + by) % size) for i in range(size)])  29.2 us
    ppermute x7, starting transfers between devices, flip(): return lax.ppermute(value, axis, [(i, i ^ bit) for i in range(size)])  28.1 us
    all_to_all x1, starting transfers between devices, body(): spread = lax.all_to_all(paired.reshape(peers, share, -1), PLANE, 0, 0)  9.43 us
    unnamed x31, local copies, waits for them, and re-layouts  8.09 us
    all_to_all x1, starting transfers between devices, body(): mine = lax.all_to_all(sent, PLANE, 0, 0).reshape(half, rank_width)  7.02 us
    ppermute x7, waiting for transfers between devices, flip(): return lax.ppermute(value, axis, [(i, i ^ bit) for i in range(size)])  6.34 us
    dot_general x2, matrix products, affinity(): lax.dot_general(visitors, anchors, (((1,), (1,)), ((), ())), preferred_el...  4.29 us
  transfers between devices with their start and end apart: 27, of which 10 were waited for; matrix products, arithmetic and copies ran while one was open for 18% of the time, Pallas kernels for 0%

profile of v1, /device:TPU:1, one launch (start us, length us, event | category | flops | bytes accessed | tf_op | source)
XLA Modules:
  0.0 193.4 jit_solution(5201663050587920283)
XLA Ops:
  0.6 0.8 convert_bitcast_fusion.1
  1.5 1.6 pad_maximum_fusion.3
  3.0 4.8 %collective-permute-start = (bf16[80,1024]{1,0:T(8,128)(2,1)}, bf16[80,1024]{1,0:T(8,128)(2,1)}, u32[]{:S(2)}, u32[]{:S(2)}) collective-permute-start(bf16[80,1024]{1,0:T(8,128)(2,1)} %pad_maximum_fusion.3), channel_id=1, source_target_pairs={{0,2},{2,4},{4,6},{6,8},{8,10},{10,12},{12,14},{14,0},{1,3},{3,5},... | collective-permute-start | bytes 491528 | tf_op jit(solution)/shard_map/ppermute | solution.py:18
  7.9 8.6 %collective-permute-start.4 = (bf16[80,1024]{1,0:T(8,128)(2,1)}, bf16[80,1024]{1,0:T(8,128)(2,1)}, u32[]{:S(2)}, u32[]{:S(2)}) collective-permute-start(bf16[80,1024]{1,0:T(8,128)(2,1)} %pad_maximum_fusion.3), channel_id=1, source_target_pairs={{0,14},{2,0},{4,2},{6,4},{8,6},{10,8},{12,10},{14,12},{1,15},{3,1}... | collective-permute-start | bytes 491528 | tf_op jit(solution)/shard_map/ppermute | solution.py:18
  16.5 0.7 compare_select_fusion
  17.2 2.1 %gather_fusion = bf16[512,1024]{1,0:T(8,128)(2,1)S(1)} fusion(bf16[768,1024]{1,0:T(8,128)(2,1)S(1)} %copy-done, s32[1024]{0:T(1024)S(1)} %pad_clamp_fusion), kind=kCustom, calls=%fused_computation | custom fusion | bytes 2099200 | tf_op jit(solution)/shard_map/gather | solution.py:48
  19.2 0.8 constant_dynamic-slice_fusion.4
  20.0 3.2 %collective-permute-start.7 = (bf16[128,1024]{1,0:T(8,128)(2,1)}, bf16[128,1024]{1,0:T(8,128)(2,1)S(1)}, u32[]{:S(2)}, u32[]{:S(2)}) collective-permute-start(bf16[128,1024]{1,0:T(8,128)(2,1)} %get-tuple-element.56), channel_id=1, source_target_pairs={{0,1},{1,128},{128,129},{129,256},{256,257},{257,384},{384,385},{3... | collective-permute-start | bytes 786440 | tf_op jit(solution)/shard_map/ppermute | solution.py:18
  23.2 3.8 %collective-permute-start.8 = (bf16[128,1024]{1,0:T(8,128)(2,1)S(1)}, bf16[128,1024]{1,0:T(8,128)(2,1)S(1)}, u32[]{:S(2)}, u32[]{:S(2)}) collective-permute-start(bf16[128,1024]{1,0:T(8,128)(2,1)S(1)} %get-tuple-element.57), channel_id=1, source_target_pairs={{0,385},{1,0},{128,1},{129,128},{256,129},{257,256},{384,257},{385... | collective-permute-start | bytes 786440 | tf_op jit(solution)/shard_map/ppermute | solution.py:18
  29.3 1.9 collective-permute-start.1
  31.2 1.6 slice_dynamic-update-slice_fusion.6
  34.1 4.6 %collective-permute-start.5 = (bf16[80,1024]{1,0:T(8,128)(2,1)}, bf16[80,1024]{1,0:T(8,128)(2,1)S(1)}, u32[]{:S(2)}, u32[]{:S(2)}) collective-permute-start(bf16[80,1024]{1,0:T(8,128)(2,1)} %collective-permute-done.4), channel_id=1, source_target_pairs={{0,14},{2,0},{4,2},{6,4},{8,6},{10,8},{12,10},{14,12},{1,15},{3,1}... | collective-permute-start | bytes 491528 | tf_op jit(solution)/shard_map/ppermute | solution.py:18
  38.7 0.9 pad_maximum_fusion.1
  39.6 3.7 %collective-permute-start.9 = (bf16[256,1024]{1,0:T(8,128)(2,1)}, bf16[256,1024]{1,0:T(8,128)(2,1)}, u32[]{:S(2)}, u32[]{:S(2)}) collective-permute-start(bf16[256,1024]{1,0:T(8,128)(2,1)} %pad_maximum_fusion.1), channel_id=1, source_target_pairs={{0,16},{16,0},{1,17},{17,1},{2,18},{18,2},{3,19},{19,3},{4,20},{20... | collective-permute-start | bytes 1572872 | tf_op jit(solution)/shard_map/ppermute | solution.py:23
  43.3 1.9 collective-permute-start.2
  45.3 4.6 %collective-permute-start.6 = (bf16[80,1024]{1,0:T(8,128)(2,1)S(1)}, bf16[80,1024]{1,0:T(8,128)(2,1)S(1)}, u32[]{:S(2)}, u32[]{:S(2)}) collective-permute-start(bf16[80,1024]{1,0:T(8,128)(2,1)S(1)} %collective-permute-done.5), channel_id=1, source_target_pairs={{0,14},{2,0},{4,2},{6,4},{8,6},{10,8},{12,10},{14,12},{1,15},{3,1}... | collective-permute-start | bytes 491528 | tf_op jit(solution)/shard_map/ppermute | solution.py:18
  50.5 1.0 collective-permute-done.2
  51.6 1.1 collective-permute-done.6
  52.7 1.9 collective-permute-start.3
  55.3 5.2 %collective-permute-done.3 = bf16[80,1024]{1,0:T(8,128)(2,1)S(1)} collective-permute-done((bf16[80,1024]{1,0:T(8,128)(2,1)S(1)}, bf16[80,1024]{1,0:T(8,128)(2,1)S(1)}, u32[]{:S(2)}, u32[]{:S(2)}) %collective-permute-start.3) | collective-permute-done | bytes 163872 | tf_op jit(solution)/shard_map/ppermute | solution.py:18
  60.8 1.3 broadcast_select_fusion.2
  62.8 1.6 slice_dynamic-update-slice_fusion.2
  64.3 1.6 slice_dynamic-update-slice_fusion.1
  66.5 1.5 multiply_reduce_fusion.3
  68.1 2.0 %fusion.11 = bf16[512,512]{1,0:T(8,128)(2,1)S(1)} fusion(bf16[512,1024]{1,0:T(8,128)(2,1)} %slice_dynamic-update-slice_fusion, bf16[512,1024]{1,0:T(8,128)(2,1)S(1)} %gather_fusion, f32[512]{0:T(512)S(1)} %add_rsqrt_fusion.1, f32[512]{0:T(512)S(1)} %rsqrt_multiply_fusion), kind=kOutput, calls=%fused_computation.22 | convolution fusion | flops 537657344 | bytes 2625536 | tf_op jit(solution)/shard_map/dot_general | solution.py:76
  70.2 1.8 multiply_reduce_fusion.1
  72.0 2.3 %fusion.12 = bf16[512,512]{1,0:T(8,128)(2,1)S(1)} fusion(bf16[512,1024]{1,0:T(8,128)(2,1)} %slice_dynamic-update-slice_fusion, f32[512]{0:T(512)S(1)} %add_rsqrt_fusion, f32[512]{0:T(512)S(1)} %rsqrt_multiply_fusion, bf16[256,1024]{1,0:T(8,128)(2,1)} %collective-permute-done.9, bf16[128,1024]{1,0:T(8,128)(2,1)S(1)} %collective-permute-done.8, ...), kind=kOutput, calls=%fused_computation.23 | convolution fusion | flops 544473088 | bytes 2625537 | tf_op jit(solution)/shard_map/dot_general | solution.py:76
  75.5 4.7 %collective-permute-start.20 = (bf16[256,1152]{0,1:T(8,128)(2,1)S(1)}, bf16[256,1152]{0,1:T(8,128)(2,1)S(1)}, u32[]{:S(2)}, u32[]{:S(2)}) collective-permute-start(bf16[256,1152]{0,1:T(8,128)(2,1)S(1)} %constant_dynamic-slice_fusion), channel_id=1, source_target_pairs={{0,16},{16,0},{1,17},{17,1},{2,18},{18,2},{3,19},{19,3},{4,20},{20... | collective-permute-start | bytes 1769480 | tf_op jit(solution)/shard_map/ppermute | solution.py:23
  80.3 1.6 collective-permute-done.20
  82.0 1.1 copy.47
  83.1 9.4 %all-to-all-start = ((bf16[32,8,1152]{2,1,0:T(8,128)(2,1)}), bf16[32,8,1152]{2,1,0:T(8,128)(2,1)S(1)}, u32[]{:S(2)}, u32[]{:S(2)}) async-start(bf16[32,8,1152]{2,1,0:T(8,128)(2,1)} %bitcast.39), calls=%async_computation | async-start | bytes 1179648 | tf_op jit(solution)/shard_map/all_to_all | solution.py:118
  92.6 3.1 %collective-permute-start.10 = (bf16[128,1024]{1,0:T(8,128)(2,1)S(1)}, bf16[128,1024]{1,0:T(8,128)(2,1)S(1)}, u32[]{:S(2)}, u32[]{:S(2)}) collective-permute-start(bf16[128,1024]{1,0:T(8,128)(2,1)S(1)} %get-tuple-element.54), channel_id=1, source_target_pairs={{0,1},{1,128},{128,129},{129,256},{256,257},{257,384},{384,385},{3... | collective-permute-start | bytes 786440 | tf_op jit(solution)/shard_map/ppermute | solution.py:18
  95.7 3.4 %collective-permute-start.11 = (bf16[128,1024]{1,0:T(8,128)(2,1)S(1)}, bf16[128,1024]{1,0:T(8,128)(2,1)S(1)}, u32[]{:S(2)}, u32[]{:S(2)}) collective-permute-start(bf16[128,1024]{1,0:T(8,128)(2,1)S(1)} %get-tuple-element.55), channel_id=1, source_target_pairs={{0,385},{1,0},{128,1},{129,128},{256,129},{257,256},{384,257},{385... | collective-permute-start | bytes 786440 | tf_op jit(solution)/shard_map/ppermute | solution.py:18
  99.1 14.5 %collective-permute-done.10 = bf16[128,1024]{1,0:T(8,128)(2,1)S(1)} collective-permute-done((bf16[128,1024]{1,0:T(8,128)(2,1)S(1)}, bf16[128,1024]{1,0:T(8,128)(2,1)S(1)}, u32[]{:S(2)}, u32[]{:S(2)}) %collective-permute-start.10) | collective-permute-done | bytes 262176 | tf_op jit(solution)/shard_map/ppermute | solution.py:18
  113.6 0.7 copy-done.3
  114.3 0.8 pad_maximum_fusion.2
  115.2 3.3 %collective-permute-start.12 = (bf16[256,1024]{1,0:T(8,128)(2,1)}, bf16[256,1024]{1,0:T(8,128)(2,1)}, u32[]{:S(2)}, u32[]{:S(2)}) collective-permute-start(bf16[256,1024]{1,0:T(8,128)(2,1)} %pad_maximum_fusion.2), channel_id=1, source_target_pairs={{0,16},{16,0},{1,17},{17,1},{2,18},{18,2},{3,19},{19,3},{4,20},{20... | collective-permute-start | bytes 1572872 | tf_op jit(solution)/shard_map/ppermute | solution.py:23
  118.5 3.1 %fusion.44 = f32[512,1024]{1,0:T(8,128)} fusion(bf16[512,512]{1,0:T(8,128)(2,1)} %copy-done.5, bf16[512,1024]{1,0:T(8,128)(2,1)S(1)} %copy-done.2), kind=kOutput, calls=%fused_computation.134 | convolution fusion | flops 536870912 | bytes 3670016 | tf_op jit(solution)/shard_map/dot_general | solution.py:101
  121.6 1.7 maximum_select_fusion.3
  123.5 2.3 %fusion = f32[16,1024]{1,0:T(8,128)S(1)} fusion(bf16[512,1024]{1,0:T(8,128)(2,1)S(1)} %maximum_select_fusion.3, bf16[512,1024]{1,0:T(8,128)(2,1)} %param.16, pred[]{:T(512)S(6)} %eq.59, bf16[8,1024]{1,0:T(8,128)(2,1)S(1)} %get-tuple-element.39, bf16[8,1024]{1,0:T(8,128)(2,1)S(1)} %get-tuple-element.40), kind=kOutput, calls=%fused_computation.2 | convolution fusion | flops 43057152 | bytes 2195457 | tf_op jit(solution)/shard_map/dot_general | solution.py:124
  125.8 1.9 collective-permute-start.21
  127.7 2.1 %fusion.43 = (bf16[512,1024]{1,0:T(8,128)(2,1)S(1)}, f32[512,1024]{1,0:T(8,128)}) fusion(f32[512,1024]{1,0:T(8,128)S(1)} %copy-done.1, bf16[512,512]{1,0:T(8,128)(2,1)S(1)} %copy-done.8, bf16[512,1024]{1,0:T(8,128)(2,1)S(1)} %maximum_select_fusion.3), kind=kOutput, calls=%fused_computation.133 | convolution fusion | flops 537919488 | bytes 6815744 | tf_op jit(solution)/shard_map/dot_general | solution.py:102
  130.4 3.8 %collective-permute-start.22 = (f32[8,1024]{1,0:T(8,128)S(1)}, f32[8,1024]{1,0:T(8,128)S(1)}, u32[]{:S(2)}, u32[]{:S(2)}) collective-permute-start(f32[8,1024]{1,0:T(8,128)S(1)} %fusion.55), channel_id=1, source_target_pairs={{0,4},{2,6},{4,0},{6,2},{8,12},{10,14},{12,8},{14,10},{1,5},{3,7},... | collective-permute-start | bytes 98312 | tf_op jit(solution)/shard_map/ppermute | solution.py:23
  134.3 2.5 %collective-permute-start.13 = (bf16[64,1024]{1,0:T(8,128)(2,1)S(1)}, bf16[64,1024]{1,0:T(8,128)(2,1)S(1)}, u32[]{:S(2)}, u32[]{:S(2)}) collective-permute-start(bf16[64,1024]{1,0:T(8,128)(2,1)S(1)} %get-tuple-element.52), channel_id=1, source_target_pairs={{0,2},{2,4},{4,6},{6,8},{8,10},{10,12},{12,14},{14,0},{1,3},{3,5},... | collective-permute-start | bytes 393224 | tf_op jit(solution)/shard_map/ppermute | solution.py:18
  136.8 4.0 %collective-permute-start.17 = (bf16[64,1024]{1,0:T(8,128)(2,1)S(1)}, bf16[64,1024]{1,0:T(8,128)(2,1)S(1)}, u32[]{:S(2)}, u32[]{:S(2)}) collective-permute-start(bf16[64,1024]{1,0:T(8,128)(2,1)S(1)} %get-tuple-element.53), channel_id=1, source_target_pairs={{0,14},{2,0},{4,2},{6,4},{8,6},{10,8},{12,10},{14,12},{1,15},{3,1}... | collective-permute-start | bytes 393224 | tf_op jit(solution)/shard_map/ppermute | solution.py:18
  140.8 4.4 %collective-permute-start.23 = (f32[8,1024]{1,0:T(8,128)S(1)}, f32[8,1024]{1,0:T(8,128)S(1)}, u32[]{:S(2)}, u32[]{:S(2)}) collective-permute-start(f32[8,1024]{1,0:T(8,128)S(1)} %add.168), channel_id=1, source_target_pairs={{0,8},{2,10},{4,12},{6,14},{8,0},{10,2},{12,4},{14,6},{1,9},{3,11}... | collective-permute-start | bytes 98312 | tf_op jit(solution)/shard_map/ppermute | solution.py:23
  145.4 4.1 %collective-permute-done.23 = f32[8,1024]{1,0:T(8,128)S(1)} collective-permute-done((f32[8,1024]{1,0:T(8,128)S(1)}, f32[8,1024]{1,0:T(8,128)S(1)}, u32[]{:S(2)}, u32[]{:S(2)}) %collective-permute-start.23) | collective-permute-done | bytes 32800 | tf_op jit(solution)/shard_map/ppermute | solution.py:23
  149.6 0.9 broadcast_in_dim.5
  150.5 7.0 %all-to-all-start.1 = ((bf16[32,8,1024]{2,1,0:T(8,128)(2,1)}), bf16[32,8,1024]{2,1,0:T(8,128)(2,1)S(1)}, u32[]{:S(2)}, u32[]{:S(2)}) async-start(bf16[32,8,1024]{2,1,0:T(8,128)(2,1)} %broadcast_in_dim.5), calls=%async_computation.1 | async-start | bytes 1048576 | tf_op jit(solution)/shard_map/all_to_all | solution.py:134
  157.5 1.0 fusion.19
  158.5 1.9 collective-permute-start.14
  160.4 5.0 %collective-permute-done.14 = bf16[64,1024]{1,0:T(8,128)(2,1)S(1)} collective-permute-done((bf16[64,1024]{1,0:T(8,128)(2,1)S(1)}, bf16[64,1024]{1,0:T(8,128)(2,1)S(1)}, u32[]{:S(2)}, u32[]{:S(2)}) %collective-permute-start.14) | collective-permute-done | bytes 131104 | tf_op jit(solution)/shard_map/ppermute | solution.py:18
  165.4 1.1 fusion.18
  166.5 1.9 collective-permute-start.15
  168.4 4.6 %collective-permute-start.18 = (bf16[64,1024]{1,0:T(8,128)(2,1)S(1)}, bf16[64,1024]{1,0:T(8,128)(2,1)S(1)}, u32[]{:S(2)}, u32[]{:S(2)}) collective-permute-start(bf16[64,1024]{1,0:T(8,128)(2,1)S(1)} %get-tuple-element.49), channel_id=1, source_target_pairs={{0,14},{2,0},{4,2},{6,4},{8,6},{10,8},{12,10},{14,12},{1,15},{3,1}... | collective-permute-start | bytes 393224 | tf_op jit(solution)/shard_map/ppermute | solution.py:18
  173.6 6.2 %collective-permute-start.24 = (bf16[256,1024]{1,0:T(8,128)(2,1)S(1)}, bf16[256,1024]{1,0:T(8,128)(2,1)S(1)}, u32[]{:S(2)}, u32[]{:S(2)}) collective-permute-start(bf16[256,1024]{1,0:T(8,128)(2,1)S(1)} %bitcast.40), channel_id=1, source_target_pairs={{0,16},{16,0},{1,17},{17,1},{2,18},{18,2},{3,19},{19,3},{4,20},{20... | collective-permute-start | bytes 1572872 | tf_op jit(solution)/shard_map/ppermute | solution.py:23
  179.8 1.1 fusion.17
  180.9 1.9 collective-permute-start.16
  182.8 4.6 %collective-permute-start.19 = (bf16[64,1024]{1,0:T(8,128)(2,1)S(1)}, bf16[64,1024]{1,0:T(8,128)(2,1)S(1)}, u32[]{:S(2)}, u32[]{:S(2)}) collective-permute-start(bf16[64,1024]{1,0:T(8,128)(2,1)S(1)} %get-tuple-element.47), channel_id=1, source_target_pairs={{0,14},{2,0},{4,2},{6,4},{8,6},{10,8},{12,10},{14,12},{1,15},{3,1}... | collective-permute-start | bytes 393224 | tf_op jit(solution)/shard_map/ppermute | solution.py:18
  187.5 1.2 collective-permute-done.16
  188.6 1.2 collective-permute-done.19
  189.9 1.0 fusion.21
  191.3 1.1 subtract_multiply_fusion
  192.4 1.0 convolution_convert_fusion.2
  (99 shorter events, 10.2 us)
Async XLA Ops:
  0.6 16.5 %copy-start = (bf16[768,1024]{1,0:T(8,128)(2,1)S(1)}, bf16[768,1024]{1,0:T(8,128)(2,1)}, u32[]{:S(2)}) copy-start(bf16[768,1024]{1,0:T(8,128)(2,1)} %param.14) | copy-start | bytes 4718596
  3.0 26.3 %collective-permute-start = (bf16[80,1024]{1,0:T(8,128)(2,1)}, bf16[80,1024]{1,0:T(8,128)(2,1)}, u32[]{:S(2)}, u32[]{:S(2)}) collective-permute-start(bf16[80,1024]{1,0:T(8,128)(2,1)} %pad_maximum_fusion.3), channel_id=1, source_target_pairs={{0,2},{2,4},{4,6},{6,8},{8,10},{10,12},{12,14},{14,0},{1,3},{3,5},... | collective-permute-start | bytes 491528 | tf_op jit(solution)/shard_map/ppermute | solution.py:18
  7.9 25.6 %collective-permute-start.4 = (bf16[80,1024]{1,0:T(8,128)(2,1)}, bf16[80,1024]{1,0:T(8,128)(2,1)}, u32[]{:S(2)}, u32[]{:S(2)}) collective-permute-start(bf16[80,1024]{1,0:T(8,128)(2,1)} %pad_maximum_fusion.3), channel_id=1, source_target_pairs={{0,14},{2,0},{4,2},{6,4},{8,6},{10,8},{12,10},{14,12},{1,15},{3,1}... | collective-permute-start | bytes 491528 | tf_op jit(solution)/shard_map/ppermute | solution.py:18
  19.2 9.4 %copy-start.6 = (bf16[64,1024]{1,0:T(8,128)(2,1)S(1)}, bf16[64,1024]{1,0:T(8,128)(2,1)}, u32[]{:S(2)}) copy-start(bf16[64,1024]{1,0:T(8,128)(2,1)} %param.12) | copy-start | bytes 393220
  20.0 18.7 %collective-permute-start.7 = (bf16[128,1024]{1,0:T(8,128)(2,1)}, bf16[128,1024]{1,0:T(8,128)(2,1)S(1)}, u32[]{:S(2)}, u32[]{:S(2)}) collective-permute-start(bf16[128,1024]{1,0:T(8,128)(2,1)} %get-tuple-element.56), channel_id=1, source_target_pairs={{0,1},{1,128},{128,129},{129,256},{256,257},{257,384},{384,385},{3... | collective-permute-start | bytes 786440 | tf_op jit(solution)/shard_map/ppermute | solution.py:18
  23.2 15.5 %collective-permute-start.8 = (bf16[128,1024]{1,0:T(8,128)(2,1)S(1)}, bf16[128,1024]{1,0:T(8,128)(2,1)S(1)}, u32[]{:S(2)}, u32[]{:S(2)}) collective-permute-start(bf16[128,1024]{1,0:T(8,128)(2,1)S(1)} %get-tuple-element.57), channel_id=1, source_target_pairs={{0,385},{1,0},{128,1},{129,128},{256,129},{257,256},{384,257},{385... | collective-permute-start | bytes 786440 | tf_op jit(solution)/shard_map/ppermute | solution.py:18
  29.3 14.0 %collective-permute-start.1 = (bf16[80,1024]{1,0:T(8,128)(2,1)}, bf16[80,1024]{1,0:T(8,128)(2,1)S(1)}, u32[]{:S(2)}, u32[]{:S(2)}) collective-permute-start(bf16[80,1024]{1,0:T(8,128)(2,1)} %collective-permute-done), channel_id=1, source_target_pairs={{0,2},{2,4},{4,6},{6,8},{8,10},{10,12},{12,14},{14,0},{1,3},{3,5},... | collective-permute-start | bytes 491528 | tf_op jit(solution)/shard_map/ppermute | solution.py:18
  34.1 9.2 %collective-permute-start.5 = (bf16[80,1024]{1,0:T(8,128)(2,1)}, bf16[80,1024]{1,0:T(8,128)(2,1)S(1)}, u32[]{:S(2)}, u32[]{:S(2)}) collective-permute-start(bf16[80,1024]{1,0:T(8,128)(2,1)} %collective-permute-done.4), channel_id=1, source_target_pairs={{0,14},{2,0},{4,2},{6,4},{8,6},{10,8},{12,10},{14,12},{1,15},{3,1}... | collective-permute-start | bytes 491528 | tf_op jit(solution)/shard_map/ppermute | solution.py:18
  39.6 30.6 %collective-permute-start.9 = (bf16[256,1024]{1,0:T(8,128)(2,1)}, bf16[256,1024]{1,0:T(8,128)(2,1)}, u32[]{:S(2)}, u32[]{:S(2)}) collective-permute-start(bf16[256,1024]{1,0:T(8,128)(2,1)} %pad_maximum_fusion.1), channel_id=1, source_target_pairs={{0,16},{16,0},{1,17},{17,1},{2,18},{18,2},{3,19},{19,3},{4,20},{20... | collective-permute-start | bytes 1572872 | tf_op jit(solution)/shard_map/ppermute | solution.py:23
  43.3 2.0 %copy-start.10 = (bf16[80,1024]{1,0:T(8,128)(2,1)}, bf16[80,1024]{1,0:T(8,128)(2,1)S(1)}, u32[]{:S(2)}) copy-start(bf16[80,1024]{1,0:T(8,128)(2,1)S(1)} %collective-permute-done.5) | copy-start | bytes 491524
  43.3 8.2 %collective-permute-start.2 = (bf16[80,1024]{1,0:T(8,128)(2,1)S(1)}, bf16[80,1024]{1,0:T(8,128)(2,1)S(1)}, u32[]{:S(2)}, u32[]{:S(2)}) collective-permute-start(bf16[80,1024]{1,0:T(8,128)(2,1)S(1)} %collective-permute-done.1), channel_id=1, source_target_pairs={{0,2},{2,4},{4,6},{6,8},{8,10},{10,12},{12,14},{14,0},{1,3},{3,5},... | collective-permute-start | bytes 491528 | tf_op jit(solution)/shard_map/ppermute | solution.py:18
  45.3 7.4 %collective-permute-start.6 = (bf16[80,1024]{1,0:T(8,128)(2,1)S(1)}, bf16[80,1024]{1,0:T(8,128)(2,1)S(1)}, u32[]{:S(2)}, u32[]{:S(2)}) collective-permute-start(bf16[80,1024]{1,0:T(8,128)(2,1)S(1)} %collective-permute-done.5), channel_id=1, source_target_pairs={{0,14},{2,0},{4,2},{6,4},{8,6},{10,8},{12,10},{14,12},{1,15},{3,1}... | collective-permute-start | bytes 491528 | tf_op jit(solution)/shard_map/ppermute | solution.py:18
  52.7 7.7 %collective-permute-start.3 = (bf16[80,1024]{1,0:T(8,128)(2,1)S(1)}, bf16[80,1024]{1,0:T(8,128)(2,1)S(1)}, u32[]{:S(2)}, u32[]{:S(2)}) collective-permute-start(bf16[80,1024]{1,0:T(8,128)(2,1)S(1)} %collective-permute-done.2), channel_id=1, source_target_pairs={{0,2},{2,4},{4,6},{6,8},{8,10},{10,12},{12,14},{14,0},{1,3},{3,5},... | collective-permute-start | bytes 491528 | tf_op jit(solution)/shard_map/ppermute | solution.py:18
  70.1 4.7 %copy-start.5 = (bf16[512,512]{1,0:T(8,128)(2,1)}, bf16[512,512]{1,0:T(8,128)(2,1)S(1)}, u32[]{:S(2)}) copy-start(bf16[512,512]{1,0:T(8,128)(2,1)S(1)} %fusion.11) | copy-start | bytes 1572868
  74.3 1.1 copy-start.7
  75.5 17.0 %copy-start.2 = (bf16[512,1024]{1,0:T(8,128)(2,1)S(1)}, bf16[512,1024]{1,0:T(8,128)(2,1)}, u32[]{:S(2)}) copy-start(bf16[512,1024]{1,0:T(8,128)(2,1)} %param.16) | copy-start | bytes 3145732
  75.5 6.4 %collective-permute-start.20 = (bf16[256,1152]{0,1:T(8,128)(2,1)S(1)}, bf16[256,1152]{0,1:T(8,128)(2,1)S(1)}, u32[]{:S(2)}, u32[]{:S(2)}) collective-permute-start(bf16[256,1152]{0,1:T(8,128)(2,1)S(1)} %constant_dynamic-slice_fusion), channel_id=1, source_target_pairs={{0,16},{16,0},{1,17},{17,1},{2,18},{18,2},{3,19},{19,3},{4,20},{20... | collective-permute-start | bytes 1769480 | tf_op jit(solution)/shard_map/ppermute | solution.py:23
  83.1 40.2 %all-to-all-start = ((bf16[32,8,1152]{2,1,0:T(8,128)(2,1)}), bf16[32,8,1152]{2,1,0:T(8,128)(2,1)S(1)}, u32[]{:S(2)}, u32[]{:S(2)}) async-start(bf16[32,8,1152]{2,1,0:T(8,128)(2,1)} %bitcast.39), calls=%async_computation | async-start | bytes 1179648 | tf_op jit(solution)/shard_map/all_to_all | solution.py:118
  92.6 21.0 %collective-permute-start.10 = (bf16[128,1024]{1,0:T(8,128)(2,1)S(1)}, bf16[128,1024]{1,0:T(8,128)(2,1)S(1)}, u32[]{:S(2)}, u32[]{:S(2)}) collective-permute-start(bf16[128,1024]{1,0:T(8,128)(2,1)S(1)} %get-tuple-element.54), channel_id=1, source_target_pairs={{0,1},{1,128},{128,129},{129,256},{256,257},{257,384},{384,385},{3... | collective-permute-start | bytes 786440 | tf_op jit(solution)/shard_map/ppermute | solution.py:18
  95.7 17.9 %collective-permute-start.11 = (bf16[128,1024]{1,0:T(8,128)(2,1)S(1)}, bf16[128,1024]{1,0:T(8,128)(2,1)S(1)}, u32[]{:S(2)}, u32[]{:S(2)}) collective-permute-start(bf16[128,1024]{1,0:T(8,128)(2,1)S(1)} %get-tuple-element.55), channel_id=1, source_target_pairs={{0,385},{1,0},{128,1},{129,128},{256,129},{257,256},{384,257},{385... | collective-permute-start | bytes 786440 | tf_op jit(solution)/shard_map/ppermute | solution.py:18
  113.6 0.7 copy-start.3
  115.2 6.5 %collective-permute-start.12 = (bf16[256,1024]{1,0:T(8,128)(2,1)}, bf16[256,1024]{1,0:T(8,128)(2,1)}, u32[]{:S(2)}, u32[]{:S(2)}) collective-permute-start(bf16[256,1024]{1,0:T(8,128)(2,1)} %pad_maximum_fusion.2), channel_id=1, source_target_pairs={{0,16},{16,0},{1,17},{17,1},{2,18},{18,2},{3,19},{19,3},{4,20},{20... | collective-permute-start | bytes 1572872 | tf_op jit(solution)/shard_map/ppermute | solution.py:23
  118.5 3.2 %copy-start.4 = (bf16[128,1024]{1,0:T(8,128)(2,1)S(1)}, bf16[128,1024]{1,0:T(8,128)(2,1)}, u32[]{:S(2)}) copy-start(bf16[128,1024]{1,0:T(8,128)(2,1)} %copy-done.3) | copy-start | bytes 786436
  123.4 4.2 %copy-start.1 = (f32[512,1024]{1,0:T(8,128)S(1)}, f32[512,1024]{1,0:T(8,128)}, u32[]{:S(2)}) copy-start(f32[512,1024]{1,0:T(8,128)} %fusion.44) | copy-start | bytes 6291460
  123.5 4.2 %copy-start.8 = (bf16[512,512]{1,0:T(8,128)(2,1)S(1)}, bf16[512,512]{1,0:T(8,128)(2,1)}, u32[]{:S(2)}) copy-start(bf16[512,512]{1,0:T(8,128)(2,1)} %copy-done.7) | copy-start | bytes 1572868
  125.8 4.7 %collective-permute-start.21 = (f32[8,1024]{1,0:T(8,128)S(1)}, f32[8,1024]{1,0:T(8,128)S(1)}, u32[]{:S(2)}, u32[]{:S(2)}) collective-permute-start(f32[8,1024]{1,0:T(8,128)S(1)} %slice_add_fusion.6), channel_id=1, source_target_pairs={{0,2},{2,0},{4,6},{6,4},{8,10},{10,8},{12,14},{14,12},{1,3},{3,1},... | collective-permute-start | bytes 98312 | tf_op jit(solution)/shard_map/ppermute | solution.py:23
  129.8 30.6 %copy-start.11 = (s32[512]{0:T(512)S(1)}, s32[512]{0:T(512)}, u32[]{:S(2)}) copy-start(s32[512]{0:T(512)} %param.17) | copy-start | bytes 6148
  130.4 10.4 %collective-permute-start.22 = (f32[8,1024]{1,0:T(8,128)S(1)}, f32[8,1024]{1,0:T(8,128)S(1)}, u32[]{:S(2)}, u32[]{:S(2)}) collective-permute-start(f32[8,1024]{1,0:T(8,128)S(1)} %fusion.55), channel_id=1, source_target_pairs={{0,4},{2,6},{4,0},{6,2},{8,12},{10,14},{12,8},{14,10},{1,5},{3,7},... | collective-permute-start | bytes 98312 | tf_op jit(solution)/shard_map/ppermute | solution.py:23
  134.3 23.2 %collective-permute-start.13 = (bf16[64,1024]{1,0:T(8,128)(2,1)S(1)}, bf16[64,1024]{1,0:T(8,128)(2,1)S(1)}, u32[]{:S(2)}, u32[]{:S(2)}) collective-permute-start(bf16[64,1024]{1,0:T(8,128)(2,1)S(1)} %get-tuple-element.52), channel_id=1, source_target_pairs={{0,2},{2,4},{4,6},{6,8},{8,10},{10,12},{12,14},{14,0},{1,3},{3,5},... | collective-permute-start | bytes 393224 | tf_op jit(solution)/shard_map/ppermute | solution.py:18
  136.8 23.6 %collective-permute-start.17 = (bf16[64,1024]{1,0:T(8,128)(2,1)S(1)}, bf16[64,1024]{1,0:T(8,128)(2,1)S(1)}, u32[]{:S(2)}, u32[]{:S(2)}) collective-permute-start(bf16[64,1024]{1,0:T(8,128)(2,1)S(1)} %get-tuple-element.53), channel_id=1, source_target_pairs={{0,14},{2,0},{4,2},{6,4},{8,6},{10,8},{12,10},{14,12},{1,15},{3,1}... | collective-permute-start | bytes 393224 | tf_op jit(solution)/shard_map/ppermute | solution.py:18
  140.8 8.7 %collective-permute-start.23 = (f32[8,1024]{1,0:T(8,128)S(1)}, f32[8,1024]{1,0:T(8,128)S(1)}, u32[]{:S(2)}, u32[]{:S(2)}) collective-permute-start(f32[8,1024]{1,0:T(8,128)S(1)} %add.168), channel_id=1, source_target_pairs={{0,8},{2,10},{4,12},{6,14},{8,0},{10,2},{12,4},{14,6},{1,9},{3,11}... | collective-permute-start | bytes 98312 | tf_op jit(solution)/shard_map/ppermute | solution.py:23
  150.5 23.1 %all-to-all-start.1 = ((bf16[32,8,1024]{2,1,0:T(8,128)(2,1)}), bf16[32,8,1024]{2,1,0:T(8,128)(2,1)S(1)}, u32[]{:S(2)}, u32[]{:S(2)}) async-start(bf16[32,8,1024]{2,1,0:T(8,128)(2,1)} %broadcast_in_dim.5), calls=%async_computation.1 | async-start | bytes 1048576 | tf_op jit(solution)/shard_map/all_to_all | solution.py:134
  158.5 6.9 %collective-permute-start.14 = (bf16[64,1024]{1,0:T(8,128)(2,1)S(1)}, bf16[64,1024]{1,0:T(8,128)(2,1)S(1)}, u32[]{:S(2)}, u32[]{:S(2)}) collective-permute-start(bf16[64,1024]{1,0:T(8,128)(2,1)S(1)} %fusion.19), channel_id=1, source_target_pairs={{0,2},{2,4},{4,6},{6,8},{8,10},{10,12},{12,14},{14,0},{1,3},{3,5},... | collective-permute-start | bytes 393224 | tf_op jit(solution)/shard_map/ppermute | solution.py:18
  166.5 13.3 %collective-permute-start.15 = (bf16[64,1024]{1,0:T(8,128)(2,1)S(1)}, bf16[64,1024]{1,0:T(8,128)(2,1)S(1)}, u32[]{:S(2)}, u32[]{:S(2)}) collective-permute-start(bf16[64,1024]{1,0:T(8,128)(2,1)S(1)} %get-tuple-element.48), channel_id=1, source_target_pairs={{0,2},{2,4},{4,6},{6,8},{8,10},{10,12},{12,14},{14,0},{1,3},{3,5},... | collective-permute-start | bytes 393224 | tf_op jit(solution)/shard_map/ppermute | solution.py:18
  168.4 11.4 %collective-permute-start.18 = (bf16[64,1024]{1,0:T(8,128)(2,1)S(1)}, bf16[64,1024]{1,0:T(8,128)(2,1)S(1)}, u32[]{:S(2)}, u32[]{:S(2)}) collective-permute-start(bf16[64,1024]{1,0:T(8,128)(2,1)S(1)} %get-tuple-element.49), channel_id=1, source_target_pairs={{0,14},{2,0},{4,2},{6,4},{8,6},{10,8},{12,10},{14,12},{1,15},{3,1}... | collective-permute-start | bytes 393224 | tf_op jit(solution)/shard_map/ppermute | solution.py:18
  173.6 17.3 %collective-permute-start.24 = (bf16[256,1024]{1,0:T(8,128)(2,1)S(1)}, bf16[256,1024]{1,0:T(8,128)(2,1)S(1)}, u32[]{:S(2)}, u32[]{:S(2)}) collective-permute-start(bf16[256,1024]{1,0:T(8,128)(2,1)S(1)} %bitcast.40), channel_id=1, source_target_pairs={{0,16},{16,0},{1,17},{17,1},{2,18},{18,2},{3,19},{19,3},{4,20},{20... | collective-permute-start | bytes 1572872 | tf_op jit(solution)/shard_map/ppermute | solution.py:23
  180.9 7.7 %collective-permute-start.16 = (bf16[64,1024]{1,0:T(8,128)(2,1)S(1)}, bf16[64,1024]{1,0:T(8,128)(2,1)S(1)}, u32[]{:S(2)}, u32[]{:S(2)}) collective-permute-start(bf16[64,1024]{1,0:T(8,128)(2,1)S(1)} %get-tuple-element.46), channel_id=1, source_target_pairs={{0,2},{2,4},{4,6},{6,8},{8,10},{10,12},{12,14},{14,0},{1,3},{3,5},... | collective-permute-start | bytes 393224 | tf_op jit(solution)/shard_map/ppermute | solution.py:18
  182.8 7.0 %collective-permute-start.19 = (bf16[64,1024]{1,0:T(8,128)(2,1)S(1)}, bf16[64,1024]{1,0:T(8,128)(2,1)S(1)}, u32[]{:S(2)}, u32[]{:S(2)}) collective-permute-start(bf16[64,1024]{1,0:T(8,128)(2,1)S(1)} %get-tuple-element.47), channel_id=1, source_target_pairs={{0,14},{2,0},{4,2},{6,4},{8,6},{10,8},{12,10},{14,12},{1,15},{3,1}... | collective-permute-start | bytes 393224 | tf_op jit(solution)/shard_map/ppermute | solution.py:18
  190.9 1.6 copy-start.9

commit v2 on v1

v2 whole, which is shorter than its diff:
```python
import functools
import math

import jax
import jax.numpy as jnp
from jax import lax
from jax.experimental import pallas as pl
from jax.experimental.pallas import tpu as pltpu
from jax.sharding import Mesh, PartitionSpec as P

epsilon = 1e-06
bf16 = jnp.bfloat16
f32 = jnp.float32
i32 = jnp.int32
ALL = ("yh", "x", "c", "z", "yl")
PLANE = ("yh", "x", "yl")
PACK = 16
DIGIT = 128
TALLY = 128
MIB = 1 << 20


def hop(value, axis, by):
    size = math.prod(lax.axis_size(name) for name in axis)
    return lax.ppermute(value, axis, [(i, (i + by) % size) for i in range(size)])


def flip(value, axis, bit):
    size = lax.axis_size(axis)
    return lax.ppermute(value, axis, [(i, i ^ bit) for i in range(size)])


def across(a, b):
    return lax.dot_general(a, b, (((1,), (1,)), ((), ())), preferred_element_type=f32)


def call(kernel, out, ins, scratch=(), flops=0, nbytes=0):
    spec = pl.BlockSpec(memory_space=pltpu.VMEM)
    return pl.pallas_call(
        kernel,
        out_shape=out,
        in_specs=[pl.BlockSpec(memory_space=pltpu.SMEM)] + [spec] * (ins - 1),
        out_specs=jax.tree.map(lambda _: spec, out),
        scratch_shapes=list(scratch),
        compiler_params=pltpu.CompilerParams(vmem_limit_bytes=24 * MIB),
        cost_estimate=pl.CostEstimate(flops=flops, bytes_accessed=nbytes, transcendentals=0),
    )


def row_squares(matrix):
    square = jnp.square(matrix.astype(f32))
    high = square.astype(bf16)
    low = (square - high.astype(f32)).astype(bf16)
    ones = jnp.ones((8, matrix.shape[1]), bf16)
    return across(ones, high) + across(ones, low)


def prepare_kernel(place, own, white, up, down, up_o, down_o, anchors, maps, factor):
    core, half = place[0], place[1]
    count = own.shape[0]
    quarter = count // 4
    mine = pl.multiple_of(half * count, count)
    anchors[pl.ds(mine, count), :] = own[...]
    maps[pl.ds(mine, count), :] = white[...]
    base = (1 - half) * count
    for piece, first, second in ((0, up, up_o), (1, down, down_o)):
        for source, which in ((first, core), (second, 1 - core)):
            at = pl.multiple_of(base + (2 * which + piece) * quarter, quarter)
            anchors[pl.ds(at, quarter), :] = source[:quarter, :]
            maps[pl.ds(at, quarter), :] = source[quarter:, :]
    tile = min(256, count)

    @pl.loop(0, 2 * count // tile)
    def _(j):
        at = pl.multiple_of(j * tile, tile)
        factor[:, pl.ds(at, tile)] = lax.rsqrt(row_squares(anchors[pl.ds(at, tile), :]) + epsilon)


def affinity_kernel(rows, place, spread, anchors, factor, kernel, keep, send, table):
    core, level = place[0], place[3]
    ring, _, width = spread.shape
    half = keep.shape[0]
    count = anchors.shape[0]
    points = ring * rows
    codes = jnp.sum(spread[:, rows:, :].astype(f32), axis=0)
    members = (codes[0:1, :points] * DIGIT + codes[1:2, :points]).astype(i32)
    label = lax.broadcasted_iota(i32, (half, points), 0)
    for ref, part in ((keep, 0), (send, 1)):
        which = jnp.where(core == 0, part, 1 - part)
        hit = jnp.where(label + which * half == members, 1.0, 0.0)
        table[part * half : (part + 1) * half, :] = hit.astype(bf16)
        tally = jnp.sum(hit, axis=1, keepdims=True)
        big = jnp.floor(tally * (1.0 / DIGIT))
        lane = lax.broadcasted_iota(i32, (half, TALLY), 1)
        digits = jnp.where(lane == 0, big, jnp.where(lane == 1, tally - big * DIGIT, 0.0))
        ref[:, count:] = digits.astype(bf16)
    visitors = spread[:, :rows, :].reshape(points, width)
    length = lax.rsqrt(jnp.sum(jnp.square(visitors.astype(f32)), axis=1, keepdims=True) + epsilon) * math.sqrt(width)
    tile = min(256, count)

    @pl.loop(0, count // tile)
    def _(j):
        at = pl.multiple_of(j * tile, tile)
        values = spread[:, :rows, :].reshape(points, width)
        gram = across(values, anchors[pl.ds(at, tile), :])
        part = jnp.exp(gram * length * factor[0:1, pl.ds(at, tile)]).astype(bf16)
        for b in range(ring):
            to = pl.multiple_of(lax.rem(b - level + ring, ring) * rows, rows)
            kernel[pl.ds(to, rows), pl.ds(at, tile)] = part[b * rows : (b + 1) * rows]
        sums = jnp.dot(table[...], part, preferred_element_type=f32).astype(bf16)
        keep[:, pl.ds(at, tile)] = sums[:half]
        send[:, pl.ds(at, tile)] = sums[half:]


def project_kernel(first, place, kernel, maps, *rest):
    outs = [ref for ref in rest if ref.shape[0] == rest[-1].shape[0]]
    rows, width = outs[0].shape
    tile = min(256, width)

    @pl.loop(0, width // tile)
    def _(j):
        at = pl.multiple_of(j * tile, tile)
        span = kernel[first * rows : (first + len(outs)) * rows, :]
        part = jnp.dot(span, maps[:, pl.ds(at, tile)], preferred_element_type=f32)
        for i, out in enumerate(outs):
            out[:, pl.ds(at, tile)] = part[i * rows : (i + 1) * rows].astype(out.dtype)


def cluster_kernel(place, spread, maps, *rest):
    mapped, number = rest[-2:]
    count = maps.shape[0]
    share = spread.shape[1]
    total = jnp.sum(spread[...].astype(f32), axis=0)
    sums = total[:, :count]
    high = sums.astype(bf16).astype(f32)
    both = jnp.concatenate([high, sums - high]).astype(bf16)
    width = maps.shape[1]
    tile = min(256, width)

    result = jnp.dot(both, maps[...], preferred_element_type=f32)
    mapped[...] = result[:share] + result[share:]
    tally = total[:, count : count + 1] * DIGIT + total[:, count + 1 : count + 2]
    number[...] = jnp.broadcast_to(jnp.maximum(tally, 1.0), number.shape)


def feature_kernel(place, owners, *rest):
    arrived, *parts, features, choose, means = rest
    means[...] = arrived[...]
    features[...] = functools.reduce(jnp.add, [part[...].astype(f32) for part in parts]).astype(bf16)
    slots, clusters = choose.shape
    owned = owners[...] == place[2]
    row = lax.broadcasted_iota(i32, (clusters, clusters), 0)
    col = lax.broadcasted_iota(i32, (clusters, clusters), 1)
    before = jnp.where(row < col, 1.0, 0.0).astype(bf16)
    mark = jnp.broadcast_to(jnp.where(owned, 1.0, 0.0), (slots, clusters))
    rank = jnp.dot(mark.astype(bf16), before, preferred_element_type=f32)
    slot = lax.broadcasted_iota(i32, (slots, clusters), 0).astype(f32)
    choose[...] = jnp.where(rank == slot, mark, 0.0).astype(bf16)


def half_scores(features, means, choose, at):
    half = means.shape[0]
    norms = row_squares(means[...])[0:1]
    scores = (norms - 2.0 * across(features[...], means[...])) * (1.0 / means.shape[1])
    owned = jnp.dot(choose[:, pl.ds(at, half)], means[...], preferred_element_type=f32)
    return scores, owned


def near_kernel(place, features, means, choose, scores, owned):
    half = means.shape[0]
    at = pl.multiple_of(place[0] * half, half)
    scores[...], owned[...] = half_scores(features, means, choose, at)


def far_kernel(place, features, means, choose, near_scores, near_owned, scores, owned):
    half = means.shape[0]
    there = pl.multiple_of((1 - place[0]) * half, half)
    here = pl.multiple_of(place[0] * half, half)
    far, rest = half_scores(features, means, choose, there)
    scores[:, pl.ds(there, half)] = far
    scores[:, pl.ds(here, half)] = near_scores[...]
    owned[...] = (near_owned[...] + rest).astype(bf16)


def body(points, membership, landmark_pool, landmark_ids, whitening, owner_map):
    rows, width = points.shape
    count, rank_width = whitening.shape
    clusters = owner_map.shape[0]
    ring = lax.axis_size("z")
    core = lax.axis_index("c")
    quarter = count // 4
    half = clusters // 2
    peers = math.prod(lax.axis_size(name) for name in PLANE)
    share = half // peers
    groups = lax.axis_size("yh") * lax.axis_size("x") * lax.axis_size("c")
    array = jax.ShapeDtypeStruct
    place = jnp.stack([core, lax.axis_index("yl"), lax.axis_index(("yh", "x", "c")), lax.axis_index("z")]).astype(i32)

    lanes = jnp.arange(width) // rows == lax.axis_index("z")
    spots = jnp.where(lanes, jnp.pad(jnp.tile(membership, ring), (0, width - ring * rows)), 0)
    tail = jnp.pad(jnp.stack([spots // DIGIT, spots % DIGIT]), ((0, PACK - 2), (0, 0))).astype(bf16)
    block = jnp.concatenate([points, tail])
    spread = lax.all_to_all(jnp.broadcast_to(block[None], (ring,) + block.shape), "z", 0, 0)

    landmarks = landmark_pool[landmark_ids]

    def load(which):
        return jnp.concatenate(
            [lax.dynamic_slice_in_dim(m, which * quarter, quarter, 0) for m in (landmarks, whitening)]
        )

    up = hop(load(2 * core), ("yh", "yl"), 1)
    down = hop(load(2 * core + 1), ("yh", "yl"), -1)
    up_o, down_o = flip(up, "c", 1), flip(down, "c", 1)
    anchors, maps, factor = call(
        prepare_kernel,
        (array((2 * count, width), bf16), array((2 * count, rank_width), bf16), array((8, 2 * count), f32)),
        7,
        nbytes=8 * MIB,
    )(place, landmarks, whitening, up, down, up_o, down_o)

    kernel, keep, send = call(
        functools.partial(affinity_kernel, rows),
        (
            array((ring * rows, 2 * count), bf16),
            array((half, 2 * count + TALLY), bf16),
            array((half, 2 * count + TALLY), bf16),
        ),
        4,
        [pltpu.VMEM((clusters, ring * rows), bf16)],
        flops=2 * ring * rows * 2 * count * (width + clusters),
        nbytes=6 * MIB,
    )(place, spread, anchors, factor)

    theirs = flip(send, "c", 1)
    paired = (keep.astype(f32) + theirs.astype(f32)).astype(bf16)
    gathered = lax.all_to_all(paired.reshape(peers, share, -1), PLANE, 0, 0)

    near = ring // 2 - 1

    def project(first, dtypes, after=()):
        return call(
            functools.partial(project_kernel, first),
            tuple(array((rows, rank_width), dtype) for dtype in dtypes),
            3 + len(after),
            flops=2 * len(dtypes) * rows * 2 * count * rank_width,
            nbytes=3 * MIB,
        )(place, kernel, maps, *after)

    far = project(near, [bf16] * (ring - 2 * near + 1))
    parts = [hop(part, ("z",), near + i) for i, part in enumerate(far)]

    mapped, number = call(
        cluster_kernel,
        (array((share, rank_width), f32), array((share, rank_width), f32)),
        3 + len(parts),
        nbytes=3 * MIB,
    )(place, gathered, maps, *parts)
    bit = 1
    while bit < ring:
        mapped = mapped + flip(mapped, "z", bit)
        bit *= 2
    means = (mapped / number).astype(bf16)

    ahead = project(0, [f32] + [bf16] * (near - 1), (means,))
    behind = project(ring - near + 1, [bf16] * (near - 1), (means,))
    parts += [hop(part, ("z",), 1 + i) for i, part in enumerate(ahead[1:])]
    parts += [hop(part, ("z",), ring - near + 1 + i) for i, part in enumerate(behind)]
    sent = jnp.broadcast_to(means[None], (peers, share, rank_width))
    mine = lax.all_to_all(sent, PLANE, 0, 0).reshape(half, rank_width)
    features, choose, mine = call(
        feature_kernel,
        (
            array((rows, rank_width), bf16),
            array((clusters // groups, clusters), bf16),
            array((half, rank_width), bf16),
        ),
        3 + ring,
        nbytes=2 * MIB,
    )(place, owner_map.reshape(1, clusters), mine, ahead[0], *parts)
    other = flip(mine, "c", 1)
    near_scores, near_owned = call(
        near_kernel, (array((rows, half), f32), array((clusters // groups, rank_width), f32)), 4, nbytes=MIB
    )(place, features, mine, choose)
    scores, owned = call(
        far_kernel, (array((rows, clusters), f32), array((clusters // groups, rank_width), bf16)), 6, nbytes=MIB
    )(place, features, other, choose, near_scores, near_owned)
    return (features, owned, scores)


def build(mesh, factors):
    fine = Mesh(mesh.devices.reshape(factors), ALL)
    blk, dp = ("z", "yl"), ("yh", "x", "c")
    return jax.shard_map(
        body,
        mesh=fine,
        in_specs=(P(ALL, None), P(ALL), P(blk, None), P(blk), P(blk, None), P()),
        out_specs=(P(ALL, None), P(dp, None), P(ALL, None)),
        check_vma=False,
    )


def solution(mesh):
    return build(mesh, (4, 4, 2, 8, 2))
```

time: 195 us -> 175 us (0.90)
  Pallas kernels: 0 us -> 19.3 us
  other arithmetic: 18.5 us -> 2.09 us
  matrix products: 15 us -> 0 us
  starting transfers between devices: 108 us -> 93.6 us
  local copies, waits for them, and re-layouts: 15.4 us -> 24.5 us
  waiting for transfers between devices: 35.5 us -> 33.1 us
    ppermute x18 -> x9, starting transfers between devices: 63.2 us -> 33.4 us  [hop(): lax.ppermute(value, axis, [(i, (i + by) % size) for i in range(size)])]
    pallas_call x0 -> x9, Pallas kernels: none -> 19.3 us  [the longest x1 5.5 us: body(): call(functools.partial(affinity_kernel, rows), (array((ring * rows, 2 * c...]
    dot_general x9 -> x0, matrix products: 15 us -> none  [the longest x2 4.29 us: affinity(): lax.dot_general(visitors, anchors, (((1,), (1,)), ((), ())), preferred_el...]
    all_to_all x1 -> x2, starting transfers between devices: 9.43 us -> 20.7 us  [the longest x1 11 us: body(): lax.all_to_all(jnp.broadcast_to(block[None], (ring,) + block.shape), 'z',...]
    ppermute x18 -> x9, waiting for transfers between devices: 29.2 us -> 18.4 us  [hop(): lax.ppermute(value, axis, [(i, (i + by) % size) for i in range(size)])]
    unnamed x31 -> x40, local copies, waits for them, and re-layouts: 8.09 us -> 18.4 us
    ppermute x7, waiting for transfers between devices: 6.34 us -> 14.3 us  [flip(): return lax.ppermute(value, axis, [(i, i ^ bit) for i in range(size)])]
    convert_element_type x7 -> x1, other arithmetic: 4.39 us -> 0.01 us  [body(): means = (mapped / number).astype(bf16)]
  transfers between devices with their start and end apart: 27 -> 19, of which waited for: 10 -> 10; matrix products, arithmetic and copies ran while one was open for 18% -> 2% of each run, Pallas kernels for 0% -> 5%
where the time goes in v2:
time: 175 us; the launch traced here: 174 us
  starting transfers between devices  93.6 us (53%)
  waiting for transfers between devices  33.1 us (19%)
  local copies, waits for them, and re-layouts  24.5 us (14%)
  Pallas kernels  19.3 us (11%)
  other arithmetic  2.09 us (1%)
    ppermute x9, starting transfers between devices, hop(): lax.ppermute(value, axis, [(i, (i + by) % size) for i in range(size)])  33.4 us
    ppermute x7, starting transfers between devices, flip(): return lax.ppermute(value, axis, [(i, i ^ bit) for i in range(size)])  30.3 us
    ppermute x9, waiting for transfers between devices, hop(): lax.ppermute(value, axis, [(i, (i + by) % size) for i in range(size)])  18.4 us
    unnamed x40, local copies, waits for them, and re-layouts  18.4 us
    ppermute x7, waiting for transfers between devices, flip(): return lax.ppermute(value, axis, [(i, i ^ bit) for i in range(size)])  14.3 us
    all_to_all x1, starting transfers between devices, body(): lax.all_to_all(jnp.broadcast_to(block[None], (ring,) + block.shape), 'z',...  11 us
    all_to_all x1, starting transfers between devices, body(): gathered = lax.all_to_all(paired.reshape(peers, share, -1), PLANE, 0, 0)  9.67 us
    all_to_all x1, starting transfers between devices, body(): mine = lax.all_to_all(sent, PLANE, 0, 0).reshape(half, rank_width)  9.14 us
  transfers between devices with their start and end apart: 19, of which 10 were waited for; matrix products, arithmetic and copies ran while one was open for 2% of the time, Pallas kernels for 5%

profile of v2, /device:TPU:1, one launch (start us, length us, event | category | flops | bytes accessed | tf_op | source)
XLA Modules:
  0.0 173.6 jit_solution(3539331702102596071)
XLA Ops:
  0.7 0.8 tile.4
  1.4 0.1 tile.10
  1.6 0.9 pad_maximum_fusion.2
  2.5 1.2 broadcast_in_dim.8
  3.7 11.0 %all-to-all-start = ((bf16[8,80,1024]{2,1,0:T(8,128)(2,1)}), bf16[8,80,1024]{2,1,0:T(8,128)(2,1)}, u32[]{:S(2)}, u32[]{:S(2)}) async-start(bf16[8,80,1024]{2,1,0:T(8,128)(2,1)} %broadcast_in_dim.8), calls=%async_computation | async-start | bytes 2621440 | tf_op jit(solution)/shard_map/all_to_all | solution.py:203
  14.8 2.1 %gather_fusion = bf16[512,1024]{1,0:T(8,128)(2,1)S(1)} fusion(bf16[768,1024]{1,0:T(8,128)(2,1)S(1)} %copy-done, s32[1024]{0:T(1024)S(1)} %pad_clamp_fusion), kind=kCustom, calls=%fused_computation | custom fusion | bytes 2099200 | tf_op jit(solution)/shard_map/gather | solution.py:205
  16.8 1.1 constant_dynamic-slice_fusion
  18.0 3.2 %collective-permute-start = (bf16[256,1024]{1,0:T(8,128)(2,1)S(1)}, bf16[256,1024]{1,0:T(8,128)(2,1)S(1)}, u32[]{:S(2)}, u32[]{:S(2)}) collective-permute-start(bf16[256,1024]{1,0:T(8,128)(2,1)S(1)} %pad_maximum_fusion), channel_id=1, source_target_pairs={{0,1},{1,128},{128,129},{129,256},{256,257},{257,384},{384,385},{3... | collective-permute-start | bytes 1572872 | tf_op jit(solution)/shard_map/ppermute | solution.py:25
  21.3 3.8 %collective-permute-start.1 = (bf16[256,1024]{1,0:T(8,128)(2,1)S(1)}, bf16[256,1024]{1,0:T(8,128)(2,1)}, u32[]{:S(2)}, u32[]{:S(2)}) collective-permute-start(bf16[256,1024]{1,0:T(8,128)(2,1)S(1)} %pad_maximum_fusion.1), channel_id=1, source_target_pairs={{0,385},{1,0},{128,1},{129,128},{256,129},{257,256},{384,257},{385... | collective-permute-start | bytes 1572872 | tf_op jit(solution)/shard_map/ppermute | solution.py:25
  25.1 9.4 %collective-permute-done.up = bf16[256,1024]{1,0:T(8,128)(2,1)S(1)} collective-permute-done((bf16[256,1024]{1,0:T(8,128)(2,1)S(1)}, bf16[256,1024]{1,0:T(8,128)(2,1)S(1)}, u32[]{:S(2)}, u32[]{:S(2)}) %collective-permute-start) | collective-permute-done | bytes 524320 | tf_op jit(solution)/shard_map/ppermute | solution.py:25
  34.5 3.3 %collective-permute-start.2 = (bf16[256,1024]{1,0:T(8,128)(2,1)S(1)}, bf16[256,1024]{1,0:T(8,128)(2,1)}, u32[]{:S(2)}, u32[]{:S(2)}) collective-permute-start(bf16[256,1024]{1,0:T(8,128)(2,1)S(1)} %collective-permute-done.up), channel_id=1, source_target_pairs={{0,16},{16,0},{1,17},{17,1},{2,18},{18,2},{3,19},{19,3},{4,20},{20... | collective-permute-start | bytes 1572872 | tf_op jit(solution)/shard_map/ppermute | solution.py:30
  37.9 1.9 %collective-permute-start.3 = (bf16[256,1024]{1,0:T(8,128)(2,1)}, bf16[256,1024]{1,0:T(8,128)(2,1)}, u32[]{:S(2)}, u32[]{:S(2)}) collective-permute-start(bf16[256,1024]{1,0:T(8,128)(2,1)} %collective-permute-done.1.down), channel_id=1, source_target_pairs={{0,16},{16,0},{1,17},{17,1},{2,18},{18,2},{3,19},{19,3},{4,20},{20... | collective-permute-start | bytes 1572872 | tf_op jit(solution)/shard_map/ppermute | solution.py:30
  39.8 0.1 pad_add_fusion.place
  39.9 2.1 %collective-permute-done.3.down_o = bf16[256,1024]{1,0:T(8,128)(2,1)} collective-permute-done((bf16[256,1024]{1,0:T(8,128)(2,1)}, bf16[256,1024]{1,0:T(8,128)(2,1)}, u32[]{:S(2)}, u32[]{:S(2)}) %collective-permute-start.3) | collective-permute-done | bytes 524320 | tf_op jit(solution)/shard_map/ppermute | solution.py:30
  42.0 1.2 copy-done.5
  43.3 3.4 %shard_map.85 = (bf16[1024,1024]{1,0:T(8,128)(2,1)S(1)}, bf16[1024,1024]{1,0:T(8,128)(2,1)S(1)}, f32[8,1024]{1,0:T(8,128)S(1)}) custom-call(s32[4]{0:T(128)S(1)} %pad_add_fusion.place, bf16[512,1024]{1,0:T(8,128)(2,1)S(1)} %gather_fusion, bf16[512,1024]{1,0:T(8,128)(2,1)S(1)} %copy-done.5, bf16[256,1024]{1,0:T(8,128)(2,1)S(1)} %collective-permute-done.up, ...), custom_call_target="tpu_custom_call" | custom-call | bytes 8388608 | tf_op jit(solution)/shard_map/pallas_call | solution.py:215
  46.6 1.3 copy-done.1
  48.0 1.3 copy-done.17
  49.3 0.4 all-to-all-done.spread
  49.7 1.6 copy-done.18
  51.3 5.5 %shard_map.86 = (bf16[512,1024]{1,0:T(8,128)(2,1)S(1)}, bf16[256,1152]{1,0:T(8,128)(2,1)S(1)}, bf16[256,1152]{1,0:T(8,128)(2,1)S(1)}) custom-call(s32[4]{0:T(128)S(1)} %pad_add_fusion.place, bf16[8,80,1024]{2,1,0:T(8,128)(2,1)} %all-to-all-done.spread, bf16[1024,1024]{1,0:T(8,128)(2,1)S(1)} %copy-done.18, f32[8,1024]{1,0:T(8,128)S(1)} %get-tuple-element.27.factor), custom_call_target="tpu_custom_call" | custom-call | flops 1610612736 | bytes 6291456 | tf_op jit(solution)/shard_map/pallas_call | solution.py:222
  56.8 2.4 %collective-permute-start.4 = (bf16[256,1152]{1,0:T(8,128)(2,1)S(1)}, bf16[256,1152]{1,0:T(8,128)(2,1)S(1)}, u32[]{:S(2)}, u32[]{:S(2)}) collective-permute-start(bf16[256,1152]{1,0:T(8,128)(2,1)S(1)} %get-tuple-element.29), channel_id=1, source_target_pairs={{0,16},{16,0},{1,17},{17,1},{2,18},{18,2},{3,19},{19,3},{4,20},{20... | collective-permute-start | bytes 1769480 | tf_op jit(solution)/shard_map/ppermute | solution.py:30
  59.2 1.6 collective-permute-done.4
  60.8 1.0 fusion
  61.8 9.7 %all-to-all-start.1 = ((bf16[32,8,1152]{2,1,0:T(8,128)(2,1)}), bf16[32,8,1152]{2,1,0:T(8,128)(2,1)S(1)}, u32[]{:S(2)}, u32[]{:S(2)}) async-start(bf16[32,8,1152]{2,1,0:T(8,128)(2,1)} %fusion), calls=%async_computation.1 | async-start | bytes 1179648 | tf_op jit(solution)/shard_map/all_to_all | solution.py:237
  71.5 1.6 copy-done.2
  73.0 1.7 shard_map.87
  74.7 4.2 %collective-permute-start.5 = (bf16[64,1024]{1,0:T(8,128)(2,1)S(1)}, bf16[64,1024]{1,0:T(8,128)(2,1)S(1)}, u32[]{:S(2)}, u32[]{:S(2)}) collective-permute-start(bf16[64,1024]{1,0:T(8,128)(2,1)S(1)} %get-tuple-element.32), channel_id=1, source_target_pairs={{0,6},{2,8},{4,10},{6,12},{8,14},{10,0},{12,2},{14,4},{1,7},{3,9},... | collective-permute-start | bytes 393224 | tf_op jit(solution)/shard_map/ppermute | solution.py:25
  78.9 4.6 %collective-permute-start.6 = (bf16[64,1024]{1,0:T(8,128)(2,1)S(1)}, bf16[64,1024]{1,0:T(8,128)(2,1)S(1)}, u32[]{:S(2)}, u32[]{:S(2)}) collective-permute-start(bf16[64,1024]{1,0:T(8,128)(2,1)S(1)} %get-tuple-element.33), channel_id=1, source_target_pairs={{0,8},{2,10},{4,12},{6,14},{8,0},{10,2},{12,4},{14,6},{1,9},{3,11}... | collective-permute-start | bytes 393224 | tf_op jit(solution)/shard_map/ppermute | solution.py:25
  83.5 5.8 %collective-permute-start.7 = (bf16[64,1024]{1,0:T(8,128)(2,1)S(1)}, bf16[64,1024]{1,0:T(8,128)(2,1)S(1)}, u32[]{:S(2)}, u32[]{:S(2)}) collective-permute-start(bf16[64,1024]{1,0:T(8,128)(2,1)S(1)} %get-tuple-element.34), channel_id=1, source_target_pairs={{0,10},{2,12},{4,14},{6,0},{8,2},{10,4},{12,6},{14,8},{1,11},{3,13... | collective-permute-start | bytes 393224 | tf_op jit(solution)/shard_map/ppermute | solution.py:25
  89.4 0.4 collective-permute-done.5.rest_0_.rest_2_
  89.7 4.4 %collective-permute-done.6.rest_1_.rest_3_ = bf16[64,1024]{1,0:T(8,128)(2,1)S(1)} collective-permute-done((bf16[64,1024]{1,0:T(8,128)(2,1)S(1)}, bf16[64,1024]{1,0:T(8,128)(2,1)S(1)}, u32[]{:S(2)}, u32[]{:S(2)}) %collective-permute-start.6) | collective-permute-done | bytes 131104 | tf_op jit(solution)/shard_map/ppermute | solution.py:25
  94.1 0.7 copy-done.6
  94.8 1.6 copy-done.3
  96.4 0.9 copy-done.7
  97.3 0.9 shard_map.88
  98.2 11.1 %collective-permute-start.8 = (f32[8,1024]{1,0:T(8,128)S(1)}, f32[8,1024]{1,0:T(8,128)S(1)}, u32[]{:S(2)}, u32[]{:S(2)}) collective-permute-start(f32[8,1024]{1,0:T(8,128)S(1)} %get-tuple-element.35), channel_id=1, source_target_pairs={{0,2},{2,0},{4,6},{6,4},{8,10},{10,8},{12,14},{14,12},{1,3},{3,1},... | collective-permute-start | bytes 98312 | tf_op jit(solution)/shard_map/ppermute | solution.py:30
  109.4 1.3 collective-permute-done.8
  110.7 1.9 %collective-permute-start.9 = (f32[8,1024]{1,0:T(8,128)S(1)}, f32[8,1024]{1,0:T(8,128)S(1)}, u32[]{:S(2)}, u32[]{:S(2)}) collective-permute-start(f32[8,1024]{1,0:T(8,128)S(1)} %add.56), channel_id=1, source_target_pairs={{0,4},{2,6},{4,0},{6,2},{8,12},{10,14},{12,8},{14,10},{1,5},{3,7},... | collective-permute-start | bytes 98312 | tf_op jit(solution)/shard_map/ppermute | solution.py:30
  112.6 3.6 %collective-permute-done.9 = f32[8,1024]{1,0:T(8,128)S(1)} collective-permute-done((f32[8,1024]{1,0:T(8,128)S(1)}, f32[8,1024]{1,0:T(8,128)S(1)}, u32[]{:S(2)}, u32[]{:S(2)}) %collective-permute-start.9) | collective-permute-done | bytes 32800 | tf_op jit(solution)/shard_map/ppermute | solution.py:30
  116.2 2.9 %collective-permute-start.10 = (f32[8,1024]{1,0:T(8,128)S(1)}, f32[8,1024]{1,0:T(8,128)S(1)}, u32[]{:S(2)}, u32[]{:S(2)}) collective-permute-start(f32[8,1024]{1,0:T(8,128)S(1)} %add.57), channel_id=1, source_target_pairs={{0,8},{2,10},{4,12},{6,14},{8,0},{10,2},{12,4},{14,6},{1,9},{3,11}... | collective-permute-start | bytes 98312 | tf_op jit(solution)/shard_map/ppermute | solution.py:30
  119.1 5.7 %collective-permute-done.10 = f32[8,1024]{1,0:T(8,128)S(1)} collective-permute-done((f32[8,1024]{1,0:T(8,128)S(1)}, f32[8,1024]{1,0:T(8,128)S(1)}, u32[]{:S(2)}, u32[]{:S(2)}) %collective-permute-start.10) | collective-permute-done | bytes 32800 | tf_op jit(solution)/shard_map/ppermute | solution.py:30
  124.8 0.9 broadcast_in_dim.10
  125.6 9.1 %all-to-all-start.2 = ((bf16[32,8,1024]{2,1,0:T(8,128)(2,1)}), bf16[32,8,1024]{2,1,0:T(8,128)(2,1)S(1)}, u32[]{:S(2)}, u32[]{:S(2)}) async-start(bf16[32,8,1024]{2,1,0:T(8,128)(2,1)} %broadcast_in_dim.10), calls=%async_computation.2 | async-start | bytes 1048576 | tf_op jit(solution)/shard_map/all_to_all | solution.py:270
  134.8 1.6 copy-done.4
  136.4 1.5 shard_map.90
  137.9 1.9 %collective-permute-start.13 = (bf16[64,1024]{1,0:T(8,128)(2,1)S(1)}, bf16[64,1024]{1,0:T(8,128)(2,1)S(1)}, u32[]{:S(2)}, u32[]{:S(2)}) collective-permute-start(bf16[64,1024]{1,0:T(8,128)(2,1)S(1)} %get-tuple-element.40), channel_id=1, source_target_pairs={{0,12},{2,14},{4,0},{6,2},{8,4},{10,6},{12,8},{14,10},{1,13},{3,15... | collective-permute-start | bytes 393224 | tf_op jit(solution)/shard_map/ppermute | solution.py:25
  139.9 2.5 %collective-permute-start.14 = (bf16[64,1024]{1,0:T(8,128)(2,1)S(1)}, bf16[64,1024]{1,0:T(8,128)(2,1)S(1)}, u32[]{:S(2)}, u32[]{:S(2)}) collective-permute-start(bf16[64,1024]{1,0:T(8,128)(2,1)S(1)} %get-tuple-element.41), channel_id=1, source_target_pairs={{0,14},{2,0},{4,2},{6,4},{8,6},{10,8},{12,10},{14,12},{1,15},{3,1}... | collective-permute-start | bytes 393224 | tf_op jit(solution)/shard_map/ppermute | solution.py:25
  142.4 1.7 shard_map.89
  144.1 0.7 copy-done.10
  144.8 3.1 %collective-permute-start.11 = (bf16[64,1024]{1,0:T(8,128)(2,1)S(1)}, bf16[64,1024]{1,0:T(8,128)(2,1)S(1)}, u32[]{:S(2)}, u32[]{:S(2)}) collective-permute-start(bf16[64,1024]{1,0:T(8,128)(2,1)S(1)} %get-tuple-element.38), channel_id=1, source_target_pairs={{0,2},{2,4},{4,6},{6,8},{8,10},{10,12},{12,14},{14,0},{1,3},{3,5},... | collective-permute-start | bytes 393224 | tf_op jit(solution)/shard_map/ppermute | solution.py:25
  147.9 4.3 %collective-permute-start.12 = (bf16[64,1024]{1,0:T(8,128)(2,1)S(1)}, bf16[64,1024]{1,0:T(8,128)(2,1)S(1)}, u32[]{:S(2)}, u32[]{:S(2)}) collective-permute-start(bf16[64,1024]{1,0:T(8,128)(2,1)S(1)} %get-tuple-element.39), channel_id=1, source_target_pairs={{0,4},{2,6},{4,8},{6,10},{8,12},{10,14},{12,0},{14,2},{1,5},{3,7},... | collective-permute-start | bytes 393224 | tf_op jit(solution)/shard_map/ppermute | solution.py:25
  152.2 0.6 copy-done.12
  152.9 0.6 copy-done.14
  153.5 4.2 %collective-permute-done.12.rest_6_ = bf16[64,1024]{1,0:T(8,128)(2,1)S(1)} collective-permute-done((bf16[64,1024]{1,0:T(8,128)(2,1)S(1)}, bf16[64,1024]{1,0:T(8,128)(2,1)S(1)}, u32[]{:S(2)}, u32[]{:S(2)}) %collective-permute-start.12) | collective-permute-done | bytes 131104 | tf_op jit(solution)/shard_map/ppermute | solution.py:25
  157.7 0.9 copy-done.8
  158.6 0.9 copy-done.11
  159.6 0.9 copy-done.13
  160.5 0.9 copy-done.15
  161.4 1.5 shard_map.91
  162.9 6.8 %collective-permute-start.15 = (bf16[256,1024]{1,0:T(8,128)(2,1)S(1)}, bf16[256,1024]{1,0:T(8,128)(2,1)S(1)}, u32[]{:S(2)}, u32[]{:S(2)}) collective-permute-start(bf16[256,1024]{1,0:T(8,128)(2,1)S(1)} %get-tuple-element.43.means), channel_id=1, source_target_pairs={{0,16},{16,0},{1,17},{17,1},{2,18},{18,2},{3,19},{19,3},{4,20},{20... | collective-permute-start | bytes 1572872 | tf_op jit(solution)/shard_map/ppermute | solution.py:30
  169.7 0.9 copy-done.9
  170.6 1.2 shard_map.92
  171.8 1.8 %shard_map.93 = (f32[64,512]{1,0:T(8,128)}, bf16[16,1024]{1,0:T(8,128)(2,1)}) custom-call(s32[4]{0:T(128)S(1)} %pad_add_fusion.place, bf16[64,1024]{1,0:T(8,128)(2,1)S(1)} %copy-done.9, bf16[256,1024]{1,0:T(8,128)(2,1)S(1)} %collective-permute-done.15.means, bf16[16,512]{1,0:T(8,128)(2,1)S(1)} %get-tuple-element.44.choose, ...), custom_call_target="tpu_custom_call" | custom-call | bytes 1048576 | tf_op jit(solution)/shard_map/pallas_call | solution.py:285
  (43 shorter events, 0.2 us)
Async XLA Ops:
  0.6 14.1 %copy-start = (bf16[768,1024]{1,0:T(8,128)(2,1)S(1)}, bf16[768,1024]{1,0:T(8,128)(2,1)}, u32[]{:S(2)}) copy-start(bf16[768,1024]{1,0:T(8,128)(2,1)} %param.8) | copy-start | bytes 4718596
  3.7 11.0 %copy-start.19 = (s32[512]{0:T(512)S(1)}, s32[512]{0:T(512)}, u32[]{:S(2)}) copy-start(s32[512]{0:T(512)} %param.9) | copy-start | bytes 6148
  3.7 46.0 %all-to-all-start = ((bf16[8,80,1024]{2,1,0:T(8,128)(2,1)}), bf16[8,80,1024]{2,1,0:T(8,128)(2,1)}, u32[]{:S(2)}, u32[]{:S(2)}) async-start(bf16[8,80,1024]{2,1,0:T(8,128)(2,1)} %broadcast_in_dim.8), calls=%async_computation | async-start | bytes 2621440 | tf_op jit(solution)/shard_map/all_to_all | solution.py:203
  18.0 16.5 %collective-permute-start = (bf16[256,1024]{1,0:T(8,128)(2,1)S(1)}, bf16[256,1024]{1,0:T(8,128)(2,1)S(1)}, u32[]{:S(2)}, u32[]{:S(2)}) collective-permute-start(bf16[256,1024]{1,0:T(8,128)(2,1)S(1)} %pad_maximum_fusion), channel_id=1, source_target_pairs={{0,1},{1,128},{128,129},{129,256},{256,257},{257,384},{384,385},{3... | collective-permute-start | bytes 1572872 | tf_op jit(solution)/shard_map/ppermute | solution.py:25
  21.3 16.6 %collective-permute-start.1 = (bf16[256,1024]{1,0:T(8,128)(2,1)S(1)}, bf16[256,1024]{1,0:T(8,128)(2,1)}, u32[]{:S(2)}, u32[]{:S(2)}) collective-permute-start(bf16[256,1024]{1,0:T(8,128)(2,1)S(1)} %pad_maximum_fusion.1), channel_id=1, source_target_pairs={{0,385},{1,0},{128,1},{129,128},{256,129},{257,256},{384,257},{385... | collective-permute-start | bytes 1572872 | tf_op jit(solution)/shard_map/ppermute | solution.py:25
  34.5 5.4 %collective-permute-start.2 = (bf16[256,1024]{1,0:T(8,128)(2,1)S(1)}, bf16[256,1024]{1,0:T(8,128)(2,1)}, u32[]{:S(2)}, u32[]{:S(2)}) collective-permute-start(bf16[256,1024]{1,0:T(8,128)(2,1)S(1)} %collective-permute-done.up), channel_id=1, source_target_pairs={{0,16},{16,0},{1,17},{17,1},{2,18},{18,2},{3,19},{19,3},{4,20},{20... | collective-permute-start | bytes 1572872 | tf_op jit(solution)/shard_map/ppermute | solution.py:30
  37.9 4.1 %collective-permute-start.3 = (bf16[256,1024]{1,0:T(8,128)(2,1)}, bf16[256,1024]{1,0:T(8,128)(2,1)}, u32[]{:S(2)}, u32[]{:S(2)}) collective-permute-start(bf16[256,1024]{1,0:T(8,128)(2,1)} %collective-permute-done.1.down), channel_id=1, source_target_pairs={{0,16},{16,0},{1,17},{17,1},{2,18},{18,2},{3,19},{19,3},{4,20},{20... | collective-permute-start | bytes 1572872 | tf_op jit(solution)/shard_map/ppermute | solution.py:30
  42.0 1.2 copy-start.5
  46.6 1.4 copy-start.1
  48.0 1.3 copy-start.17
  49.7 1.6 copy-start.18
  56.8 4.0 %collective-permute-start.4 = (bf16[256,1152]{1,0:T(8,128)(2,1)S(1)}, bf16[256,1152]{1,0:T(8,128)(2,1)S(1)}, u32[]{:S(2)}, u32[]{:S(2)}) collective-permute-start(bf16[256,1152]{1,0:T(8,128)(2,1)S(1)} %get-tuple-element.29), channel_id=1, source_target_pairs={{0,16},{16,0},{1,17},{17,1},{2,18},{18,2},{3,19},{19,3},{4,20},{20... | collective-permute-start | bytes 1769480 | tf_op jit(solution)/shard_map/ppermute | solution.py:30
  61.8 33.0 %all-to-all-start.1 = ((bf16[32,8,1152]{2,1,0:T(8,128)(2,1)}), bf16[32,8,1152]{2,1,0:T(8,128)(2,1)S(1)}, u32[]{:S(2)}, u32[]{:S(2)}) async-start(bf16[32,8,1152]{2,1,0:T(8,128)(2,1)} %fusion), calls=%async_computation.1 | async-start | bytes 1179648 | tf_op jit(solution)/shard_map/all_to_all | solution.py:237
  71.4 1.6 copy-start.2
  74.7 15.0 %collective-permute-start.5 = (bf16[64,1024]{1,0:T(8,128)(2,1)S(1)}, bf16[64,1024]{1,0:T(8,128)(2,1)S(1)}, u32[]{:S(2)}, u32[]{:S(2)}) collective-permute-start(bf16[64,1024]{1,0:T(8,128)(2,1)S(1)} %get-tuple-element.32), channel_id=1, source_target_pairs={{0,6},{2,8},{4,10},{6,12},{8,14},{10,0},{12,2},{14,4},{1,7},{3,9},... | collective-permute-start | bytes 393224 | tf_op jit(solution)/shard_map/ppermute | solution.py:25
  78.9 15.2 %collective-permute-start.6 = (bf16[64,1024]{1,0:T(8,128)(2,1)S(1)}, bf16[64,1024]{1,0:T(8,128)(2,1)S(1)}, u32[]{:S(2)}, u32[]{:S(2)}) collective-permute-start(bf16[64,1024]{1,0:T(8,128)(2,1)S(1)} %get-tuple-element.33), channel_id=1, source_target_pairs={{0,8},{2,10},{4,12},{6,14},{8,0},{10,2},{12,4},{14,6},{1,9},{3,11}... | collective-permute-start | bytes 393224 | tf_op jit(solution)/shard_map/ppermute | solution.py:25
  83.5 10.6 %collective-permute-start.7 = (bf16[64,1024]{1,0:T(8,128)(2,1)S(1)}, bf16[64,1024]{1,0:T(8,128)(2,1)S(1)}, u32[]{:S(2)}, u32[]{:S(2)}) collective-permute-start(bf16[64,1024]{1,0:T(8,128)(2,1)S(1)} %get-tuple-element.34), channel_id=1, source_target_pairs={{0,10},{2,12},{4,14},{6,0},{8,2},{10,4},{12,6},{14,8},{1,11},{3,13... | collective-permute-start | bytes 393224 | tf_op jit(solution)/shard_map/ppermute | solution.py:25
  94.1 0.7 copy-start.6
  94.8 1.6 copy-start.3
  96.4 0.9 copy-start.7
  98.2 12.4 %collective-permute-start.8 = (f32[8,1024]{1,0:T(8,128)S(1)}, f32[8,1024]{1,0:T(8,128)S(1)}, u32[]{:S(2)}, u32[]{:S(2)}) collective-permute-start(f32[8,1024]{1,0:T(8,128)S(1)} %get-tuple-element.35), channel_id=1, source_target_pairs={{0,2},{2,0},{4,6},{6,4},{8,10},{10,8},{12,14},{14,12},{1,3},{3,1},... | collective-permute-start | bytes 98312 | tf_op jit(solution)/shard_map/ppermute | solution.py:30
  110.7 5.5 %collective-permute-start.9 = (f32[8,1024]{1,0:T(8,128)S(1)}, f32[8,1024]{1,0:T(8,128)S(1)}, u32[]{:S(2)}, u32[]{:S(2)}) collective-permute-start(f32[8,1024]{1,0:T(8,128)S(1)} %add.56), channel_id=1, source_target_pairs={{0,4},{2,6},{4,0},{6,2},{8,12},{10,14},{12,8},{14,10},{1,5},{3,7},... | collective-permute-start | bytes 98312 | tf_op jit(solution)/shard_map/ppermute | solution.py:30
  116.2 8.6 %collective-permute-start.10 = (f32[8,1024]{1,0:T(8,128)S(1)}, f32[8,1024]{1,0:T(8,128)S(1)}, u32[]{:S(2)}, u32[]{:S(2)}) collective-permute-start(f32[8,1024]{1,0:T(8,128)S(1)} %add.57), channel_id=1, source_target_pairs={{0,8},{2,10},{4,12},{6,14},{8,0},{10,2},{12,4},{14,6},{1,9},{3,11}... | collective-permute-start | bytes 98312 | tf_op jit(solution)/shard_map/ppermute | solution.py:30
  125.6 32.1 %all-to-all-start.2 = ((bf16[32,8,1024]{2,1,0:T(8,128)(2,1)}), bf16[32,8,1024]{2,1,0:T(8,128)(2,1)S(1)}, u32[]{:S(2)}, u32[]{:S(2)}) async-start(bf16[32,8,1024]{2,1,0:T(8,128)(2,1)} %broadcast_in_dim.10), calls=%async_computation.2 | async-start | bytes 1048576 | tf_op jit(solution)/shard_map/all_to_all | solution.py:270
  134.8 1.6 copy-start.4
  137.9 14.2 %collective-permute-start.13 = (bf16[64,1024]{1,0:T(8,128)(2,1)S(1)}, bf16[64,1024]{1,0:T(8,128)(2,1)S(1)}, u32[]{:S(2)}, u32[]{:S(2)}) collective-permute-start(bf16[64,1024]{1,0:T(8,128)(2,1)S(1)} %get-tuple-element.40), channel_id=1, source_target_pairs={{0,12},{2,14},{4,0},{6,2},{8,4},{10,6},{12,8},{14,10},{1,13},{3,15... | collective-permute-start | bytes 393224 | tf_op jit(solution)/shard_map/ppermute | solution.py:25
  139.9 17.8 %copy-start.16 = (s32[512]{0:T(512)S(1)}, s32[512]{0:T(512)}, u32[]{:S(2)}) copy-start(s32[512]{0:T(512)} %param.11) | copy-start | bytes 6148
  139.9 13.0 %collective-permute-start.14 = (bf16[64,1024]{1,0:T(8,128)(2,1)S(1)}, bf16[64,1024]{1,0:T(8,128)(2,1)S(1)}, u32[]{:S(2)}, u32[]{:S(2)}) collective-permute-start(bf16[64,1024]{1,0:T(8,128)(2,1)S(1)} %get-tuple-element.41), channel_id=1, source_target_pairs={{0,14},{2,0},{4,2},{6,4},{8,6},{10,8},{12,10},{14,12},{1,15},{3,1}... | collective-permute-start | bytes 393224 | tf_op jit(solution)/shard_map/ppermute | solution.py:25
  144.1 0.7 copy-start.10
  144.8 8.7 %collective-permute-start.11 = (bf16[64,1024]{1,0:T(8,128)(2,1)S(1)}, bf16[64,1024]{1,0:T(8,128)(2,1)S(1)}, u32[]{:S(2)}, u32[]{:S(2)}) collective-permute-start(bf16[64,1024]{1,0:T(8,128)(2,1)S(1)} %get-tuple-element.38), channel_id=1, source_target_pairs={{0,2},{2,4},{4,6},{6,8},{8,10},{10,12},{12,14},{14,0},{1,3},{3,5},... | collective-permute-start | bytes 393224 | tf_op jit(solution)/shard_map/ppermute | solution.py:25
  147.9 9.8 %collective-permute-start.12 = (bf16[64,1024]{1,0:T(8,128)(2,1)S(1)}, bf16[64,1024]{1,0:T(8,128)(2,1)S(1)}, u32[]{:S(2)}, u32[]{:S(2)}) collective-permute-start(bf16[64,1024]{1,0:T(8,128)(2,1)S(1)} %get-tuple-element.39), channel_id=1, source_target_pairs={{0,4},{2,6},{4,8},{6,10},{8,12},{10,14},{12,0},{14,2},{1,5},{3,7},... | collective-permute-start | bytes 393224 | tf_op jit(solution)/shard_map/ppermute | solution.py:25
  152.2 0.7 copy-start.12
  152.9 0.6 copy-start.14
  157.7 0.9 copy-start.8
  158.6 0.9 copy-start.11
  159.6 0.9 copy-start.13
  160.5 0.9 copy-start.15
  162.9 8.9 %collective-permute-start.15 = (bf16[256,1024]{1,0:T(8,128)(2,1)S(1)}, bf16[256,1024]{1,0:T(8,128)(2,1)S(1)}, u32[]{:S(2)}, u32[]{:S(2)}) collective-permute-start(bf16[256,1024]{1,0:T(8,128)(2,1)S(1)} %get-tuple-element.43.means), channel_id=1, source_target_pairs={{0,16},{16,0},{1,17},{17,1},{2,18},{18,2},{3,19},{19,3},{4,20},{20... | collective-permute-start | bytes 1572872 | tf_op jit(solution)/shard_map/ppermute | solution.py:30
  169.7 0.9 copy-start.9

commit v3 on v2

--- a/solution.py
+++ b/solution.py
@@ -34,17 +34,37 @@
     return lax.dot_general(a, b, (((1,), (1,)), ((), ())), preferred_element_type=f32)
 
 
-def call(kernel, out, ins, scratch=(), flops=0, nbytes=0):
+def call(kernel, out, ins, held=0, scratch=(), flops=0, nbytes=0):
     spec = pl.BlockSpec(memory_space=pltpu.VMEM)
+    away = pl.BlockSpec(memory_space=pl.ANY)
     return pl.pallas_call(
         kernel,
         out_shape=out,
-        in_specs=[pl.BlockSpec(memory_space=pltpu.SMEM)] + [spec] * (ins - 1),
+        in_specs=[pl.BlockSpec(memory_space=pltpu.SMEM)] + [spec] * (ins - 1 - held) + [away] * held,
         out_specs=jax.tree.map(lambda _: spec, out),
         scratch_shapes=list(scratch),
-        compiler_params=pltpu.CompilerParams(vmem_limit_bytes=24 * MIB),
+        compiler_params=pltpu.CompilerParams(vmem_limit_bytes=16 * MIB),
         cost_estimate=pl.CostEstimate(flops=flops, bytes_accessed=nbytes, transcendentals=0),
     )
+
+
+def fetch(place, block, swapped, second, table, sems):
+    core, half = place[0], place[1]
+    count = block.shape[0]
+    quarter = count // 4
+    copies = [pltpu.make_async_copy(block, table.at[pl.ds(pl.multiple_of(half * count, count), count), :], sems.at[0])]
+    for i, piece in enumerate(swapped):
+        which = core if i < 2 else 1 - core
+        at = pl.multiple_of((1 - half) * count + (2 * which + i % 2) * quarter, quarter)
+        source = piece.at[pl.ds(second * quarter, quarter), :]
+        copies.append(pltpu.make_async_copy(source, table.at[pl.ds(at, quarter), :], sems.at[1 + i]))
+    for copy in copies:
+        copy.start()
+    return copies
+
+
+def store(count, width):
+    return [pltpu.VMEM((count, width), bf16), pltpu.SemaphoreType.DMA((5,))]
 
 
 def row_squares(matrix):
@@ -55,29 +75,9 @@
     return across(ones, high) + across(ones, low)
 
 
-def prepare_kernel(place, own, white, up, down, up_o, down_o, anchors, maps, factor):
-    core, half = place[0], place[1]
-    count = own.shape[0]
-    quarter = count // 4
-    mine = pl.multiple_of(half * count, count)
-    anchors[pl.ds(mine, count), :] = own[...]
-    maps[pl.ds(mine, count), :] = white[...]
-    base = (1 - half) * count
-    for piece, first, second in ((0, up, up_o), (1, down, down_o)):
-        for source, which in ((first, core), (second, 1 - core)):
-            at = pl.multiple_of(base + (2 * which + piece) * quarter, quarter)
-            anchors[pl.ds(at, quarter), :] = source[:quarter, :]
-            maps[pl.ds(at, quarter), :] = source[quarter:, :]
-    tile = min(256, count)
-
-    @pl.loop(0, 2 * count // tile)
-    def _(j):
-        at = pl.multiple_of(j * tile, tile)
-        factor[:, pl.ds(at, tile)] = lax.rsqrt(row_squares(anchors[pl.ds(at, tile), :]) + epsilon)
-
-
-def affinity_kernel(rows, place, spread, anchors, factor, kernel, keep, send, table):
-    core, level = place[0], place[3]
+def affinity_kernel(rows, place, spread, own, up, down, up_o, down_o, kernel, keep, send, table, anchors, sems):
+    copies = fetch(place, own, (up, down, up_o, down_o), 0, anchors, sems)
+    core = place[0]
     ring, _, width = spread.shape
     half = keep.shape[0]
     count = anchors.shape[0]
@@ -96,57 +96,87 @@
         ref[:, count:] = digits.astype(bf16)
     visitors = spread[:, :rows, :].reshape(points, width)
     length = lax.rsqrt(jnp.sum(jnp.square(visitors.astype(f32)), axis=1, keepdims=True) + epsilon) * math.sqrt(width)
+    for copy in copies:
+        copy.wait()
     tile = min(256, count)
 
     @pl.loop(0, count // tile)
     def _(j):
         at = pl.multiple_of(j * tile, tile)
         values = spread[:, :rows, :].reshape(points, width)
-        gram = across(values, anchors[pl.ds(at, tile), :])
-        part = jnp.exp(gram * length * factor[0:1, pl.ds(at, tile)]).astype(bf16)
-        for b in range(ring):
-            to = pl.multiple_of(lax.rem(b - level + ring, ring) * rows, rows)
-            kernel[pl.ds(to, rows), pl.ds(at, tile)] = part[b * rows : (b + 1) * rows]
+        marks = anchors[pl.ds(at, tile), :]
+        factor = lax.rsqrt(row_squares(marks) + epsilon)[0:1]
+        part = jnp.exp(across(values, marks) * length * factor).astype(bf16)
+        kernel[:, pl.ds(at, tile)] = part
         sums = jnp.dot(table[...], part, preferred_element_type=f32).astype(bf16)
         keep[:, pl.ds(at, tile)] = sums[:half]
         send[:, pl.ds(at, tile)] = sums[half:]
 
 
-def project_kernel(first, place, kernel, maps, *rest):
-    outs = [ref for ref in rest if ref.shape[0] == rest[-1].shape[0]]
-    rows, width = outs[0].shape
+def project(place, kernel, maps, owners, rows, at, tile):
+    spots = [pl.multiple_of(lax.bitwise_xor(place[3], d) * rows, rows) for d in owners]
+    span = jnp.concatenate([kernel[pl.ds(spot, rows), :] for spot in spots])
+    return jnp.dot(span, maps[:, pl.ds(at, tile)], preferred_element_type=f32)
+
+
+def away_kernel(owners, place, kernel, white, up, down, up_o, down_o, send, maps, sems):
+    copies = fetch(place, white, (up, down, up_o, down_o), 1, maps, sems)
+    for copy in copies:
+        copy.wait()
+    rows, width = send.shape[0] // len(owners), send.shape[1]
     tile = min(256, width)
 
     @pl.loop(0, width // tile)
     def _(j):
         at = pl.multiple_of(j * tile, tile)
-        span = kernel[first * rows : (first + len(outs)) * rows, :]
-        part = jnp.dot(span, maps[:, pl.ds(at, tile)], preferred_element_type=f32)
-        for i, out in enumerate(outs):
-            out[:, pl.ds(at, tile)] = part[i * rows : (i + 1) * rows].astype(out.dtype)
-
-
-def cluster_kernel(place, spread, maps, *rest):
-    mapped, number = rest[-2:]
+        send[:, pl.ds(at, tile)] = project(place, kernel, maps, owners, rows, at, tile).astype(bf16)
+
+
+def stay_kernel(owners, place, kernel, arrived, white, up, down, up_o, down_o, keep, send, maps, sems):
+    copies = fetch(place, white, (up, down, up_o, down_o), 1, maps, sems)
+    for copy in copies:
+        copy.wait()
+    rows, width = arrived.shape[0] // len(owners), arrived.shape[1]
+    tile = min(256, width)
+    half = keep.shape[0]
+
+    @pl.loop(0, width // tile)
+    def _(j):
+        at = pl.multiple_of(j * tile, tile)
+        both = project(place, kernel, maps, owners, rows, at, tile) + arrived[:, pl.ds(at, tile)].astype(f32)
+        keep[:, pl.ds(at, tile)] = both[:half]
+        send[:, pl.ds(at, tile)] = both[half:].astype(bf16)
+
+
+def cluster_kernel(place, spread, *rest):
+    white, up, down, up_o, down_o = rest[-9:-4]
+    mapped, number, maps, sems = rest[-4:]
+    copies = fetch(place, white, (up, down, up_o, down_o), 1, maps, sems)
     count = maps.shape[0]
     share = spread.shape[1]
     total = jnp.sum(spread[...].astype(f32), axis=0)
     sums = total[:, :count]
     high = sums.astype(bf16).astype(f32)
     both = jnp.concatenate([high, sums - high]).astype(bf16)
-    width = maps.shape[1]
-    tile = min(256, width)
-
+    tally = total[:, count : count + 1] * DIGIT + total[:, count + 1 : count + 2]
+    number[...] = jnp.broadcast_to(jnp.maximum(tally, 1.0), number.shape)
+    for copy in copies:
+        copy.wait()
     result = jnp.dot(both, maps[...], preferred_element_type=f32)
     mapped[...] = result[:share] + result[share:]
-    tally = total[:, count : count + 1] * DIGIT + total[:, count + 1 : count + 2]
-    number[...] = jnp.broadcast_to(jnp.maximum(tally, 1.0), number.shape)
+
+
+def merge_kernel(place, kept, arrived, _, keep, send):
+    rows = keep.shape[0]
+    both = kept[...] + arrived[...].astype(f32)
+    keep[...] = both[:rows]
+    send[...] = both[rows:].astype(bf16)
 
 
 def feature_kernel(place, owners, *rest):
-    arrived, *parts, features, choose, means = rest
+    arrived, kept, last, features, choose, means = rest
     means[...] = arrived[...]
-    features[...] = functools.reduce(jnp.add, [part[...].astype(f32) for part in parts]).astype(bf16)
+    features[...] = (kept[...] + last[...].astype(f32)).astype(bf16)
     slots, clusters = choose.shape
     owned = owners[...] == place[2]
     row = lax.broadcasted_iota(i32, (clusters, clusters), 0)
@@ -212,12 +242,7 @@
     up = hop(load(2 * core), ("yh", "yl"), 1)
     down = hop(load(2 * core + 1), ("yh", "yl"), -1)
     up_o, down_o = flip(up, "c", 1), flip(down, "c", 1)
-    anchors, maps, factor = call(
-        prepare_kernel,
-        (array((2 * count, width), bf16), array((2 * count, rank_width), bf16), array((8, 2 * count), f32)),
-        7,
-        nbytes=8 * MIB,
-    )(place, landmarks, whitening, up, down, up_o, down_o)
+    pieces = (up, down, up_o, down_o)
 
     kernel, keep, send = call(
         functools.partial(affinity_kernel, rows),
@@ -226,48 +251,63 @@
             array((half, 2 * count + TALLY), bf16),
             array((half, 2 * count + TALLY), bf16),
         ),
-        4,
-        [pltpu.VMEM((clusters, ring * rows), bf16)],
+        7,
+        5,
+        [pltpu.VMEM((clusters, ring * rows), bf16)] + store(2 * count, width),
         flops=2 * ring * rows * 2 * count * (width + clusters),
         nbytes=6 * MIB,
-    )(place, spread, anchors, factor)
+    )(place, spread, landmarks, *pieces)
 
     theirs = flip(send, "c", 1)
     paired = (keep.astype(f32) + theirs.astype(f32)).astype(bf16)
     gathered = lax.all_to_all(paired.reshape(peers, share, -1), PLANE, 0, 0)
 
-    near = ring // 2 - 1
-
-    def project(first, dtypes, after=()):
-        return call(
-            functools.partial(project_kernel, first),
-            tuple(array((rows, rank_width), dtype) for dtype in dtypes),
-            3 + len(after),
-            flops=2 * len(dtypes) * rows * 2 * count * rank_width,
-            nbytes=3 * MIB,
-        )(place, kernel, maps, *after)
-
-    far = project(near, [bf16] * (ring - 2 * near + 1))
-    parts = [hop(part, ("z",), near + i) for i, part in enumerate(far)]
+    leave = call(
+        functools.partial(away_kernel, (1, 6, 2, 5)),
+        array((ring // 2 * rows, rank_width), bf16),
+        7,
+        5,
+        store(2 * count, rank_width),
+        flops=ring * rows * 2 * count * rank_width,
+        nbytes=3 * MIB,
+    )(place, kernel, whitening, *pieces)
+    arrived = flip(leave, "z", 1)
+    kept, leave = call(
+        functools.partial(stay_kernel, (0, 7, 3, 4)),
+        (array((ring // 4 * rows, rank_width), f32), array((ring // 4 * rows, rank_width), bf16)),
+        8,
+        5,
+        store(2 * count, rank_width),
+        flops=ring * rows * 2 * count * rank_width,
+        nbytes=3 * MIB,
+    )(place, kernel, arrived, whitening, *pieces)
 
     mapped, number = call(
         cluster_kernel,
         (array((share, rank_width), f32), array((share, rank_width), f32)),
-        3 + len(parts),
+        8,
+        6,
+        store(2 * count, rank_width),
         nbytes=3 * MIB,
-    )(place, gathered, maps, *parts)
+    )(place, gathered, leave, whitening, *pieces)
     bit = 1
     while bit < ring:
         mapped = mapped + flip(mapped, "z", bit)
         bit *= 2
     means = (mapped / number).astype(bf16)
 
-    ahead = project(0, [f32] + [bf16] * (near - 1), (means,))
-    behind = project(ring - near + 1, [bf16] * (near - 1), (means,))
-    parts += [hop(part, ("z",), 1 + i) for i, part in enumerate(ahead[1:])]
-    parts += [hop(part, ("z",), ring - near + 1 + i) for i, part in enumerate(behind)]
     sent = jnp.broadcast_to(means[None], (peers, share, rank_width))
     mine = lax.all_to_all(sent, PLANE, 0, 0).reshape(half, rank_width)
+
+    arrived = flip(leave, "z", 3)
+    kept, leave = call(
+        merge_kernel,
+        (array((rows, rank_width), f32), array((rows, rank_width), bf16)),
+        4,
+        1,
+        nbytes=MIB,
+    )(place, kept, arrived, means)
+    last = flip(leave, "z", 7)
     features, choose, mine = call(
         feature_kernel,
         (
@@ -275,9 +315,9 @@
             array((clusters // groups, clusters), bf16),
             array((half, rank_width), bf16),
         ),
-        3 + ring,
+        5,
         nbytes=2 * MIB,
-    )(place, owner_map.reshape(1, clusters), mine, ahead[0], *parts)
+    )(place, owner_map.reshape(1, clusters), mine, kept, last)
     other = flip(mine, "c", 1)
     near_scores, near_owned = call(
         near_kernel, (array((rows, half), f32), array((clusters // groups, rank_width), f32)), 4, nbytes=MIB

time: 175 us -> 161 us (0.920)
  starting transfers between devices: 93.6 us -> 65.9 us
  waiting for transfers between devices: 33.1 us -> 58.1 us
  local copies, waits for them, and re-layouts: 24.5 us -> 12 us
  Pallas kernels: 19.3 us -> 21.3 us
    ppermute x7 -> x10, waiting for transfers between devices: 14.3 us -> 41.7 us  [flip(): return lax.ppermute(value, axis, [(i, i ^ bit) for i in range(size)])]
    ppermute x9 -> x2, starting transfers between devices: 33.4 us -> 7.02 us  [hop(): lax.ppermute(value, axis, [(i, (i + by) % size) for i in range(size)])]
    unnamed x40 -> x20, local copies, waits for them, and re-layouts: 18.4 us -> 5.13 us
    ppermute x9 -> x2, waiting for transfers between devices: 18.4 us -> 9.45 us  [hop(): lax.ppermute(value, axis, [(i, (i + by) % size) for i in range(size)])]
    all_to_all x1, waiting for transfers between devices: 0.37 us -> 6.93 us  [body(): lax.all_to_all(jnp.broadcast_to(block[None], (ring,) + block.shape), 'z',...]
    pallas_call x1, Pallas kernels: 5.5 us -> 7.52 us  [body(): call(functools.partial(affinity_kernel, rows), (array((ring * rows, 2 * c...]
    pallas_call x1, Pallas kernels: 0.94 us -> 2.71 us  [body(): call(cluster_kernel, (array((share, rank_width), f32), array((share, rank...]
    pallas_call x4 -> x3, Pallas kernels: 8.29 us -> 6.73 us  [the longest x1 3.06 us: body(): call(functools.partial(stay_kernel, (0, 7, 3, 4)), (array((ring // 4 * ro...]
  transfers between devices with their start and end apart: 19 -> 15, of which waited for: 10 -> 10; matrix products, arithmetic and copies ran while one was open for 2% -> 3% of each run, Pallas kernels for 5% -> 5%
where the time goes in v3:
time: 161 us; the launch traced here: 160 us
  starting transfers between devices  65.9 us (41%)
  waiting for transfers between devices  58.1 us (36%)
  Pallas kernels  21.3 us (13%)
  local copies, waits for them, and re-layouts  12 us (7%)
  other arithmetic  2.1 us (1%)
    ppermute x10, waiting for transfers between devices, flip(): return lax.ppermute(value, axis, [(i, i ^ bit) for i in range(size)])  41.7 us
    ppermute x10, starting transfers between devices, flip(): return lax.ppermute(value, axis, [(i, i ^ bit) for i in range(size)])  29.3 us
    all_to_all x1, starting transfers between devices, body(): lax.all_to_all(jnp.broadcast_to(block[None], (ring,) + block.shape), 'z',...  11 us
    all_to_all x1, starting transfers between devices, body(): gathered = lax.all_to_all(paired.reshape(peers, share, -1), PLANE, 0, 0)  9.78 us
    ppermute x2, waiting for transfers between devices, hop(): lax.ppermute(value, axis, [(i, (i + by) % size) for i in range(size)])  9.45 us
    all_to_all x1, starting transfers between devices, body(): mine = lax.all_to_all(sent, PLANE, 0, 0).reshape(half, rank_width)  8.83 us
    pallas_call x1, Pallas kernels, body(): call(functools.partial(affinity_kernel, rows), (array((ring * rows, 2 * c...  7.52 us
    ppermute x2, starting transfers between devices, hop(): lax.ppermute(value, axis, [(i, (i + by) % size) for i in range(size)])  7.02 us
  transfers between devices with their start and end apart: 15, of which 10 were waited for; matrix products, arithmetic and copies ran while one was open for 3% of the time, Pallas kernels for 5%

profile of v3, /device:TPU:1, one launch (start us, length us, event | category | flops | bytes accessed | tf_op | source)
XLA Modules:
  0.0 160.4 jit_solution(17888571168075112204)
XLA Ops:
  0.6 0.0 copy-start
  0.7 0.8 tile.4
  1.4 0.1 tile.10
  1.6 0.9 pad_maximum_fusion.2
  2.5 1.2 broadcast_in_dim.8
  3.7 11.0 %all-to-all-start = ((bf16[8,80,1024]{2,1,0:T(8,128)(2,1)}), bf16[8,80,1024]{2,1,0:T(8,128)(2,1)}, u32[]{:S(2)}, u32[]{:S(2)}) async-start(bf16[8,80,1024]{2,1,0:T(8,128)(2,1)} %broadcast_in_dim.8), calls=%async_computation | async-start | bytes 2621440 | tf_op jit(solution)/shard_map/all_to_all | solution.py:233
  14.7 0.0 copy-done.9
  14.8 0.0 copy-done
  14.8 0.0 copy-start.1
  14.8 2.8 %gather_fusion = bf16[512,1024]{1,0:T(8,128)(2,1)} fusion(bf16[768,1024]{1,0:T(8,128)(2,1)S(1)} %copy-done, s32[1024]{0:T(1024)S(1)} %pad_clamp_fusion), kind=kCustom, calls=%fused_computation | custom fusion | bytes 2099200 | tf_op jit(solution)/shard_map/gather | solution.py:235
  17.6 0.0 copy-done.1
  17.6 1.1 constant_dynamic-slice_fusion
  18.7 3.2 %collective-permute-start = (bf16[256,1024]{1,0:T(8,128)(2,1)S(1)}, bf16[256,1024]{1,0:T(8,128)(2,1)S(1)}, u32[]{:S(2)}, u32[]{:S(2)}) collective-permute-start(bf16[256,1024]{1,0:T(8,128)(2,1)S(1)} %pad_maximum_fusion), channel_id=1, source_target_pairs={{0,1},{1,128},{128,129},{129,256},{256,257},{257,384},{384,385},{3... | collective-permute-start | bytes 1572872 | tf_op jit(solution)/shard_map/ppermute | solution.py:25
  22.0 3.8 %collective-permute-start.1 = (bf16[256,1024]{1,0:T(8,128)(2,1)S(1)}, bf16[256,1024]{1,0:T(8,128)(2,1)}, u32[]{:S(2)}, u32[]{:S(2)}) collective-permute-start(bf16[256,1024]{1,0:T(8,128)(2,1)S(1)} %pad_maximum_fusion.1), channel_id=1, source_target_pairs={{0,385},{1,0},{128,1},{129,128},{256,129},{257,256},{384,257},{385... | collective-permute-start | bytes 1572872 | tf_op jit(solution)/shard_map/ppermute | solution.py:25
  25.8 9.4 %collective-permute-done.up.rest_2_ = bf16[256,1024]{1,0:T(8,128)(2,1)S(1)} collective-permute-done((bf16[256,1024]{1,0:T(8,128)(2,1)S(1)}, bf16[256,1024]{1,0:T(8,128)(2,1)S(1)}, u32[]{:S(2)}, u32[]{:S(2)}) %collective-permute-start) | collective-permute-done | bytes 524320 | tf_op jit(solution)/shard_map/ppermute | solution.py:25
  35.3 3.3 %collective-permute-start.2 = (bf16[256,1024]{1,0:T(8,128)(2,1)S(1)}, bf16[256,1024]{1,0:T(8,128)(2,1)}, u32[]{:S(2)}, u32[]{:S(2)}) collective-permute-start(bf16[256,1024]{1,0:T(8,128)(2,1)S(1)} %collective-permute-done.up.rest_2_), channel_id=1, source_target_pairs={{0,16},{16,0},{1,17},{17,1},{2,18},{18,2},{3,19},{19,3},{4,20},{20... | collective-permute-start | bytes 1572872 | tf_op jit(solution)/shard_map/ppermute | solution.py:30
  38.6 0.0 collective-permute-done.1.down.rest_3_
  38.6 1.9 %collective-permute-start.3 = (bf16[256,1024]{1,0:T(8,128)(2,1)}, bf16[256,1024]{1,0:T(8,128)(2,1)}, u32[]{:S(2)}, u32[]{:S(2)}) collective-permute-start(bf16[256,1024]{1,0:T(8,128)(2,1)} %collective-permute-done.1.down.rest_3_), channel_id=1, source_target_pairs={{0,16},{16,0},{1,17},{17,1},{2,18},{18,2},{3,19},{19,3},{4,20},{20... | collective-permute-start | bytes 1572872 | tf_op jit(solution)/shard_map/ppermute | solution.py:30
  40.6 0.1 pad_add_fusion.place
  40.6 0.0 collective-permute-done.2.up_o.rest_4_
  40.6 2.1 %collective-permute-done.3.down_o.rest_5_ = bf16[256,1024]{1,0:T(8,128)(2,1)} collective-permute-done((bf16[256,1024]{1,0:T(8,128)(2,1)}, bf16[256,1024]{1,0:T(8,128)(2,1)}, u32[]{:S(2)}, u32[]{:S(2)}) %collective-permute-start.3) | collective-permute-done | bytes 524320 | tf_op jit(solution)/shard_map/ppermute | solution.py:30
  42.8 6.9 %all-to-all-done.spread = bf16[8,80,1024]{2,1,0:T(8,128)(2,1)} async-done(((bf16[8,80,1024]{2,1,0:T(8,128)(2,1)}), bf16[8,80,1024]{2,1,0:T(8,128)(2,1)}, u32[]{:S(2)}, u32[]{:S(2)}) %all-to-all-start) | async-done | bytes 1310752 | tf_op jit(solution)/shard_map/all_to_all | solution.py:233
  49.7 1.2 copy-done.4
  50.9 7.5 %shard_map.85 = (bf16[512,1024]{1,0:T(8,128)(2,1)S(1)}, bf16[256,1152]{1,0:T(8,128)(2,1)S(1)}, bf16[256,1152]{1,0:T(8,128)(2,1)S(1)}) custom-call(s32[4]{0:T(128)S(1)} %pad_add_fusion.place, bf16[8,80,1024]{2,1,0:T(8,128)(2,1)} %all-to-all-done.spread, bf16[512,1024]{1,0:T(8,128)(2,1)S(1)} %copy-done.4, ...), custom_call_target="tpu_custom_call" | custom-call | flops 1610612736 | bytes 6291456 | tf_op jit(solution)/shard_map/pallas_call | solution.py:247
  58.4 0.0 copy-start.2
  58.5 1.0 copy-done.2
  59.4 2.4 %collective-permute-start.4 = (bf16[256,1152]{1,0:T(8,128)(2,1)S(1)}, bf16[256,1152]{1,0:T(8,128)(2,1)S(1)}, u32[]{:S(2)}, u32[]{:S(2)}) collective-permute-start(bf16[256,1152]{1,0:T(8,128)(2,1)S(1)} %get-tuple-element.20), channel_id=1, source_target_pairs={{0,16},{16,0},{1,17},{17,1},{2,18},{18,2},{3,19},{19,3},{4,20},{20... | collective-permute-start | bytes 1769480 | tf_op jit(solution)/shard_map/ppermute | solution.py:30
  61.8 1.6 %collective-permute-done.4 = bf16[256,1152]{1,0:T(8,128)(2,1)S(1)} collective-permute-done((bf16[256,1152]{1,0:T(8,128)(2,1)S(1)}, bf16[256,1152]{1,0:T(8,128)(2,1)S(1)}, u32[]{:S(2)}, u32[]{:S(2)}) %collective-permute-start.4) | collective-permute-done | bytes 589856 | tf_op jit(solution)/shard_map/ppermute | solution.py:30
  63.4 1.0 fusion
  64.4 9.8 %all-to-all-start.1 = ((bf16[32,8,1152]{2,1,0:T(8,128)(2,1)}), bf16[32,8,1152]{2,1,0:T(8,128)(2,1)}, u32[]{:S(2)}, u32[]{:S(2)}) async-start(bf16[32,8,1152]{2,1,0:T(8,128)(2,1)} %fusion), calls=%async_computation.1 | async-start | bytes 1179648 | tf_op jit(solution)/shard_map/all_to_all | solution.py:263
  74.2 0.0 copy-start.3
  74.2 1.2 copy-done.3
  75.4 3.1 %shard_map.86 = bf16[256,1024]{1,0:T(8,128)(2,1)S(1)} custom-call(s32[4]{0:T(128)S(1)} %pad_add_fusion.place, bf16[512,1024]{1,0:T(8,128)(2,1)S(1)} %copy-done.3, bf16[512,1024]{1,0:T(8,128)(2,1)S(1)} %copy-done.1, bf16[256,1024]{1,0:T(8,128)(2,1)S(1)} %collective-permute-done.up.rest_2_, bf16[256,1024]{1,0:T(8,128)(2,1)} %collective-permute-done.1.down.rest_3_, ...), custom_call_target="tpu_custom_call" | custom-call | flops 536870912 | bytes 3145728 | tf_op jit(solution)/shard_map/pallas_call | solution.py:265
  78.5 2.2 %collective-permute-start.5 = (bf16[256,1024]{1,0:T(8,128)(2,1)S(1)}, bf16[256,1024]{1,0:T(8,128)(2,1)S(1)}, u32[]{:S(2)}, u32[]{:S(2)}) collective-permute-start(bf16[256,1024]{1,0:T(8,128)(2,1)S(1)} %shard_map.86), channel_id=1, source_target_pairs={{0,2},{2,0},{4,6},{6,4},{8,10},{10,8},{12,14},{14,12},{1,3},{3,1},... | collective-permute-start | bytes 1572872 | tf_op jit(solution)/shard_map/ppermute | solution.py:30
  80.6 12.5 %collective-permute-done.5.arrived = bf16[256,1024]{1,0:T(8,128)(2,1)S(1)} collective-permute-done((bf16[256,1024]{1,0:T(8,128)(2,1)S(1)}, bf16[256,1024]{1,0:T(8,128)(2,1)S(1)}, u32[]{:S(2)}, u32[]{:S(2)}) %collective-permute-start.5) | collective-permute-done | bytes 524320 | tf_op jit(solution)/shard_map/ppermute | solution.py:30
  93.2 3.1 %shard_map.87 = (f32[128,1024]{1,0:T(8,128)S(1)}, bf16[128,1024]{1,0:T(8,128)(2,1)S(1)}) custom-call(s32[4]{0:T(128)S(1)} %pad_add_fusion.place, bf16[512,1024]{1,0:T(8,128)(2,1)S(1)} %copy-done.3, bf16[256,1024]{1,0:T(8,128)(2,1)S(1)} %collective-permute-done.5.arrived, bf16[512,1024]{1,0:T(8,128)(2,1)S(1)} %copy-done.1, ...), custom_call_target="tpu_custom_call" | custom-call | flops 536870912 | bytes 3145728 | tf_op jit(solution)/shard_map/pallas_call | solution.py:275
  96.2 0.0 copy-start.5
  96.3 0.8 copy-done.5
  97.0 0.0 all-to-all-done.1.spread
  97.0 2.7 %shard_map.88 = (f32[8,1024]{1,0:T(8,128)S(1)}, f32[8,1024]{1,0:T(8,128)S(1)}) custom-call(s32[4]{0:T(128)S(1)} %pad_add_fusion.place, bf16[32,8,1152]{2,1,0:T(8,128)(2,1)} %all-to-all-done.1.spread, bf16[128,1024]{1,0:T(8,128)(2,1)S(1)} %get-tuple-element.22.rest_0_, bf16[512,1024]{1,0:T(8,128)(2,1)S(1)} %copy-done.1, ...), custom_call_target="tpu_custom_call" | custom-call | bytes 3145728 | tf_op jit(solution)/shard_map/pallas_call | solution.py:285
  99.8 0.0 copy-start.6
  99.8 2.3 %collective-permute-start.6 = (f32[8,1024]{1,0:T(8,128)S(1)}, f32[8,1024]{1,0:T(8,128)S(1)}, u32[]{:S(2)}, u32[]{:S(2)}) collective-permute-start(f32[8,1024]{1,0:T(8,128)S(1)} %get-tuple-element.23), channel_id=1, source_target_pairs={{0,2},{2,0},{4,6},{6,4},{8,10},{10,8},{12,14},{14,12},{1,3},{3,1},... | collective-permute-start | bytes 98312 | tf_op jit(solution)/shard_map/ppermute | solution.py:30
  102.1 2.5 %collective-permute-done.6 = f32[8,1024]{1,0:T(8,128)S(1)} collective-permute-done((f32[8,1024]{1,0:T(8,128)S(1)}, f32[8,1024]{1,0:T(8,128)S(1)}, u32[]{:S(2)}, u32[]{:S(2)}) %collective-permute-start.6) | collective-permute-done | bytes 32800 | tf_op jit(solution)/shard_map/ppermute | solution.py:30
  104.6 1.9 %collective-permute-start.7 = (f32[8,1024]{1,0:T(8,128)S(1)}, f32[8,1024]{1,0:T(8,128)S(1)}, u32[]{:S(2)}, u32[]{:S(2)}) collective-permute-start(f32[8,1024]{1,0:T(8,128)S(1)} %add.56), channel_id=1, source_target_pairs={{0,4},{2,6},{4,0},{6,2},{8,12},{10,14},{12,8},{14,10},{1,5},{3,7},... | collective-permute-start | bytes 98312 | tf_op jit(solution)/shard_map/ppermute | solution.py:30
  106.5 4.0 %collective-permute-done.7 = f32[8,1024]{1,0:T(8,128)S(1)} collective-permute-done((f32[8,1024]{1,0:T(8,128)S(1)}, f32[8,1024]{1,0:T(8,128)S(1)}, u32[]{:S(2)}, u32[]{:S(2)}) %collective-permute-start.7) | collective-permute-done | bytes 32800 | tf_op jit(solution)/shard_map/ppermute | solution.py:30
  110.5 1.9 %collective-permute-start.8 = (f32[8,1024]{1,0:T(8,128)S(1)}, f32[8,1024]{1,0:T(8,128)S(1)}, u32[]{:S(2)}, u32[]{:S(2)}) collective-permute-start(f32[8,1024]{1,0:T(8,128)S(1)} %add.57), channel_id=1, source_target_pairs={{0,8},{2,10},{4,12},{6,14},{8,0},{10,2},{12,4},{14,6},{1,9},{3,11}... | collective-permute-start | bytes 98312 | tf_op jit(solution)/shard_map/ppermute | solution.py:30
  112.4 6.6 %collective-permute-done.8 = f32[8,1024]{1,0:T(8,128)S(1)} collective-permute-done((f32[8,1024]{1,0:T(8,128)S(1)}, f32[8,1024]{1,0:T(8,128)S(1)}, u32[]{:S(2)}, u32[]{:S(2)}) %collective-permute-start.8) | collective-permute-done | bytes 32800 | tf_op jit(solution)/shard_map/ppermute | solution.py:30
  119.0 0.9 broadcast_in_dim.10
  119.9 8.8 %all-to-all-start.2 = ((bf16[32,8,1024]{2,1,0:T(8,128)(2,1)}), bf16[32,8,1024]{2,1,0:T(8,128)(2,1)S(1)}, u32[]{:S(2)}, u32[]{:S(2)}) async-start(bf16[32,8,1024]{2,1,0:T(8,128)(2,1)} %broadcast_in_dim.10), calls=%async_computation.2 | async-start | bytes 1048576 | tf_op jit(solution)/shard_map/all_to_all | solution.py:300
  128.7 1.9 %collective-permute-start.9 = (bf16[128,1024]{1,0:T(8,128)(2,1)S(1)}, bf16[128,1024]{1,0:T(8,128)(2,1)S(1)}, u32[]{:S(2)}, u32[]{:S(2)}) collective-permute-start(bf16[128,1024]{1,0:T(8,128)(2,1)S(1)} %get-tuple-element.22.rest_0_), channel_id=1, source_target_pairs={{0,6},{2,4},{4,2},{6,0},{8,14},{10,12},{12,10},{14,8},{1,7},{3,5},... | collective-permute-start | bytes 786440 | tf_op jit(solution)/shard_map/ppermute | solution.py:30
  130.7 7.1 %collective-permute-done.9.arrived = bf16[128,1024]{1,0:T(8,128)(2,1)S(1)} collective-permute-done((bf16[128,1024]{1,0:T(8,128)(2,1)S(1)}, bf16[128,1024]{1,0:T(8,128)(2,1)S(1)}, u32[]{:S(2)}, u32[]{:S(2)}) %collective-permute-start.9) | collective-permute-done | bytes 262176 | tf_op jit(solution)/shard_map/ppermute | solution.py:30
  137.8 0.0 copy-done.6
  137.8 0.6 shard_map.89
  138.4 1.9 %collective-permute-start.10 = (bf16[64,1024]{1,0:T(8,128)(2,1)S(1)}, bf16[64,1024]{1,0:T(8,128)(2,1)S(1)}, u32[]{:S(2)}, u32[]{:S(2)}) collective-permute-start(bf16[64,1024]{1,0:T(8,128)(2,1)S(1)} %get-tuple-element.27), channel_id=1, source_target_pairs={{0,14},{2,12},{4,10},{6,8},{8,6},{10,4},{12,2},{14,0},{1,15},{3,13... | collective-permute-start | bytes 393224 | tf_op jit(solution)/shard_map/ppermute | solution.py:30
  140.3 5.3 %collective-permute-done.10.rest_2_ = bf16[64,1024]{1,0:T(8,128)(2,1)S(1)} collective-permute-done((bf16[64,1024]{1,0:T(8,128)(2,1)S(1)}, bf16[64,1024]{1,0:T(8,128)(2,1)S(1)}, u32[]{:S(2)}, u32[]{:S(2)}) %collective-permute-start.10) | collective-permute-done | bytes 131104 | tf_op jit(solution)/shard_map/ppermute | solution.py:30
  145.6 0.0 all-to-all-done.2
  145.6 0.0 copy-done.8
  145.6 1.3 shard_map.90
  146.9 9.5 %collective-permute-start.11 = (bf16[256,1024]{1,0:T(8,128)(2,1)S(1)}, bf16[256,1024]{1,0:T(8,128)(2,1)S(1)}, u32[]{:S(2)}, u32[]{:S(2)}) collective-permute-start(bf16[256,1024]{1,0:T(8,128)(2,1)S(1)} %get-tuple-element.29.means), channel_id=1, source_target_pairs={{0,16},{16,0},{1,17},{17,1},{2,18},{18,2},{3,19},{19,3},{4,20},{20... | collective-permute-start | bytes 1572872 | tf_op jit(solution)/shard_map/ppermute | solution.py:30
  156.4 0.0 copy-start.7
  156.5 0.9 copy-done.7
  157.4 1.2 shard_map.91
  158.5 0.0 collective-permute-done.11.means
  158.6 1.8 %shard_map.92 = (f32[64,512]{1,0:T(8,128)}, bf16[16,1024]{1,0:T(8,128)(2,1)}) custom-call(s32[4]{0:T(128)S(1)} %pad_add_fusion.place, bf16[64,1024]{1,0:T(8,128)(2,1)S(1)} %copy-done.7, bf16[256,1024]{1,0:T(8,128)(2,1)S(1)} %collective-permute-done.11.means, bf16[16,512]{1,0:T(8,128)(2,1)S(1)} %get-tuple-element.30.choose, ...), custom_call_target="tpu_custom_call" | custom-call | bytes 1048576 | tf_op jit(solution)/shard_map/pallas_call | solution.py:325
  (14 shorter events, 0.2 us)
Async XLA Ops:
  0.6 14.1 %copy-start = (bf16[768,1024]{1,0:T(8,128)(2,1)S(1)}, bf16[768,1024]{1,0:T(8,128)(2,1)}, u32[]{:S(2)}) copy-start(bf16[768,1024]{1,0:T(8,128)(2,1)} %param.8) | copy-start | bytes 4718596
  3.7 11.0 %copy-start.9 = (s32[512]{0:T(512)S(1)}, s32[512]{0:T(512)}, u32[]{:S(2)}) copy-start(s32[512]{0:T(512)} %param.9) | copy-start | bytes 6148
  3.7 46.0 %all-to-all-start = ((bf16[8,80,1024]{2,1,0:T(8,128)(2,1)}), bf16[8,80,1024]{2,1,0:T(8,128)(2,1)}, u32[]{:S(2)}, u32[]{:S(2)}) async-start(bf16[8,80,1024]{2,1,0:T(8,128)(2,1)} %broadcast_in_dim.8), calls=%async_computation | async-start | bytes 2621440 | tf_op jit(solution)/shard_map/all_to_all | solution.py:233
  14.8 2.8 %copy-start.1 = (bf16[512,1024]{1,0:T(8,128)(2,1)S(1)}, bf16[512,1024]{1,0:T(8,128)(2,1)}, u32[]{:S(2)}) copy-start(bf16[512,1024]{1,0:T(8,128)(2,1)} %rest_1_.1) | copy-start | bytes 3145732
  18.7 16.5 %collective-permute-start = (bf16[256,1024]{1,0:T(8,128)(2,1)S(1)}, bf16[256,1024]{1,0:T(8,128)(2,1)S(1)}, u32[]{:S(2)}, u32[]{:S(2)}) collective-permute-start(bf16[256,1024]{1,0:T(8,128)(2,1)S(1)} %pad_maximum_fusion), channel_id=1, source_target_pairs={{0,1},{1,128},{128,129},{129,256},{256,257},{257,384},{384,385},{3... | collective-permute-start | bytes 1572872 | tf_op jit(solution)/shard_map/ppermute | solution.py:25
  22.0 16.6 %collective-permute-start.1 = (bf16[256,1024]{1,0:T(8,128)(2,1)S(1)}, bf16[256,1024]{1,0:T(8,128)(2,1)}, u32[]{:S(2)}, u32[]{:S(2)}) collective-permute-start(bf16[256,1024]{1,0:T(8,128)(2,1)S(1)} %pad_maximum_fusion.1), channel_id=1, source_target_pairs={{0,385},{1,0},{128,1},{129,128},{256,129},{257,256},{384,257},{385... | collective-permute-start | bytes 1572872 | tf_op jit(solution)/shard_map/ppermute | solution.py:25
  35.3 5.4 %collective-permute-start.2 = (bf16[256,1024]{1,0:T(8,128)(2,1)S(1)}, bf16[256,1024]{1,0:T(8,128)(2,1)}, u32[]{:S(2)}, u32[]{:S(2)}) collective-permute-start(bf16[256,1024]{1,0:T(8,128)(2,1)S(1)} %collective-permute-done.up.rest_2_), channel_id=1, source_target_pairs={{0,16},{16,0},{1,17},{17,1},{2,18},{18,2},{3,19},{19,3},{4,20},{20... | collective-permute-start | bytes 1572872 | tf_op jit(solution)/shard_map/ppermute | solution.py:30
  38.6 4.1 %collective-permute-start.3 = (bf16[256,1024]{1,0:T(8,128)(2,1)}, bf16[256,1024]{1,0:T(8,128)(2,1)}, u32[]{:S(2)}, u32[]{:S(2)}) collective-permute-start(bf16[256,1024]{1,0:T(8,128)(2,1)} %collective-permute-done.1.down.rest_3_), channel_id=1, source_target_pairs={{0,16},{16,0},{1,17},{17,1},{2,18},{18,2},{3,19},{19,3},{4,20},{20... | collective-permute-start | bytes 1572872 | tf_op jit(solution)/shard_map/ppermute | solution.py:30
  49.7 1.2 copy-start.4
  58.4 1.0 copy-start.2
  59.4 4.0 %collective-permute-start.4 = (bf16[256,1152]{1,0:T(8,128)(2,1)S(1)}, bf16[256,1152]{1,0:T(8,128)(2,1)S(1)}, u32[]{:S(2)}, u32[]{:S(2)}) collective-permute-start(bf16[256,1152]{1,0:T(8,128)(2,1)S(1)} %get-tuple-element.20), channel_id=1, source_target_pairs={{0,16},{16,0},{1,17},{17,1},{2,18},{18,2},{3,19},{19,3},{4,20},{20... | collective-permute-start | bytes 1769480 | tf_op jit(solution)/shard_map/ppermute | solution.py:30
  64.4 32.7 %all-to-all-start.1 = ((bf16[32,8,1152]{2,1,0:T(8,128)(2,1)}), bf16[32,8,1152]{2,1,0:T(8,128)(2,1)}, u32[]{:S(2)}, u32[]{:S(2)}) async-start(bf16[32,8,1152]{2,1,0:T(8,128)(2,1)} %fusion), calls=%async_computation.1 | async-start | bytes 1179648 | tf_op jit(solution)/shard_map/all_to_all | solution.py:263
  74.2 1.2 copy-start.3
  78.5 14.7 %collective-permute-start.5 = (bf16[256,1024]{1,0:T(8,128)(2,1)S(1)}, bf16[256,1024]{1,0:T(8,128)(2,1)S(1)}, u32[]{:S(2)}, u32[]{:S(2)}) collective-permute-start(bf16[256,1024]{1,0:T(8,128)(2,1)S(1)} %shard_map.86), channel_id=1, source_target_pairs={{0,2},{2,0},{4,6},{6,4},{8,10},{10,8},{12,14},{14,12},{1,3},{3,1},... | collective-permute-start | bytes 1572872 | tf_op jit(solution)/shard_map/ppermute | solution.py:30
  96.2 0.8 copy-start.5
  99.8 38.0 %copy-start.6 = (f32[128,1024]{1,0:T(8,128)S(1)}, f32[128,1024]{1,0:T(8,128)}, u32[]{:S(2)}) copy-start(f32[128,1024]{1,0:T(8,128)} %copy-done.5) | copy-start | bytes 1572868
  99.8 4.8 %collective-permute-start.6 = (f32[8,1024]{1,0:T(8,128)S(1)}, f32[8,1024]{1,0:T(8,128)S(1)}, u32[]{:S(2)}, u32[]{:S(2)}) collective-permute-start(f32[8,1024]{1,0:T(8,128)S(1)} %get-tuple-element.23), channel_id=1, source_target_pairs={{0,2},{2,0},{4,6},{6,4},{8,10},{10,8},{12,14},{14,12},{1,3},{3,1},... | collective-permute-start | bytes 98312 | tf_op jit(solution)/shard_map/ppermute | solution.py:30
  104.6 41.0 %copy-start.8 = (s32[512]{0:T(512)S(1)}, s32[512]{0:T(512)}, u32[]{:S(2)}) copy-start(s32[512]{0:T(512)} %param.11) | copy-start | bytes 6148
  104.6 5.9 %collective-permute-start.7 = (f32[8,1024]{1,0:T(8,128)S(1)}, f32[8,1024]{1,0:T(8,128)S(1)}, u32[]{:S(2)}, u32[]{:S(2)}) collective-permute-start(f32[8,1024]{1,0:T(8,128)S(1)} %add.56), channel_id=1, source_target_pairs={{0,4},{2,6},{4,0},{6,2},{8,12},{10,14},{12,8},{14,10},{1,5},{3,7},... | collective-permute-start | bytes 98312 | tf_op jit(solution)/shard_map/ppermute | solution.py:30
  110.5 8.6 %collective-permute-start.8 = (f32[8,1024]{1,0:T(8,128)S(1)}, f32[8,1024]{1,0:T(8,128)S(1)}, u32[]{:S(2)}, u32[]{:S(2)}) collective-permute-start(f32[8,1024]{1,0:T(8,128)S(1)} %add.57), channel_id=1, source_target_pairs={{0,8},{2,10},{4,12},{6,14},{8,0},{10,2},{12,4},{14,6},{1,9},{3,11}... | collective-permute-start | bytes 98312 | tf_op jit(solution)/shard_map/ppermute | solution.py:30
  119.9 25.7 %all-to-all-start.2 = ((bf16[32,8,1024]{2,1,0:T(8,128)(2,1)}), bf16[32,8,1024]{2,1,0:T(8,128)(2,1)S(1)}, u32[]{:S(2)}, u32[]{:S(2)}) async-start(bf16[32,8,1024]{2,1,0:T(8,128)(2,1)} %broadcast_in_dim.10), calls=%async_computation.2 | async-start | bytes 1048576 | tf_op jit(solution)/shard_map/all_to_all | solution.py:300
  128.7 9.0 %collective-permute-start.9 = (bf16[128,1024]{1,0:T(8,128)(2,1)S(1)}, bf16[128,1024]{1,0:T(8,128)(2,1)S(1)}, u32[]{:S(2)}, u32[]{:S(2)}) collective-permute-start(bf16[128,1024]{1,0:T(8,128)(2,1)S(1)} %get-tuple-element.22.rest_0_), channel_id=1, source_target_pairs={{0,6},{2,4},{4,2},{6,0},{8,14},{10,12},{12,10},{14,8},{1,7},{3,5},... | collective-permute-start | bytes 786440 | tf_op jit(solution)/shard_map/ppermute | solution.py:30
  138.4 7.2 %collective-permute-start.10 = (bf16[64,1024]{1,0:T(8,128)(2,1)S(1)}, bf16[64,1024]{1,0:T(8,128)(2,1)S(1)}, u32[]{:S(2)}, u32[]{:S(2)}) collective-permute-start(bf16[64,1024]{1,0:T(8,128)(2,1)S(1)} %get-tuple-element.27), channel_id=1, source_target_pairs={{0,14},{2,12},{4,10},{6,8},{8,6},{10,4},{12,2},{14,0},{1,15},{3,13... | collective-permute-start | bytes 393224 | tf_op jit(solution)/shard_map/ppermute | solution.py:30
  146.9 11.6 %collective-permute-start.11 = (bf16[256,1024]{1,0:T(8,128)(2,1)S(1)}, bf16[256,1024]{1,0:T(8,128)(2,1)S(1)}, u32[]{:S(2)}, u32[]{:S(2)}) collective-permute-start(bf16[256,1024]{1,0:T(8,128)(2,1)S(1)} %get-tuple-element.29.means), channel_id=1, source_target_pairs={{0,16},{16,0},{1,17},{17,1},{2,18},{18,2},{3,19},{19,3},{4,20},{20... | collective-permute-start | bytes 1572872 | tf_op jit(solution)/shard_map/ppermute | solution.py:30
  156.4 0.9 copy-start.7

commit v4 on v3

--- a/solution.py
+++ b/solution.py
@@ -100,9 +100,7 @@
         copy.wait()
     tile = min(256, count)
 
-    @pl.loop(0, count // tile)
-    def _(j):
-        at = pl.multiple_of(j * tile, tile)
+    for at in range(0, count, tile):
         values = spread[:, :rows, :].reshape(points, width)
         marks = anchors[pl.ds(at, tile), :]
         factor = lax.rsqrt(row_squares(marks) + epsilon)[0:1]
@@ -126,9 +124,7 @@
     rows, width = send.shape[0] // len(owners), send.shape[1]
     tile = min(256, width)
 
-    @pl.loop(0, width // tile)
-    def _(j):
-        at = pl.multiple_of(j * tile, tile)
+    for at in range(0, width, tile):
         send[:, pl.ds(at, tile)] = project(place, kernel, maps, owners, rows, at, tile).astype(bf16)
 
 
@@ -140,9 +136,7 @@
     tile = min(256, width)
     half = keep.shape[0]
 
-    @pl.loop(0, width // tile)
-    def _(j):
-        at = pl.multiple_of(j * tile, tile)
+    for at in range(0, width, tile):
         both = project(place, kernel, maps, owners, rows, at, tile) + arrived[:, pl.ds(at, tile)].astype(f32)
         keep[:, pl.ds(at, tile)] = both[:half]
         send[:, pl.ds(at, tile)] = both[half:].astype(bf16)
@@ -163,7 +157,7 @@
     for copy in copies:
         copy.wait()
     result = jnp.dot(both, maps[...], preferred_element_type=f32)
-    mapped[...] = result[:share] + result[share:]
+    mapped[...] = jnp.broadcast_to((result[:share] + result[share:])[None], mapped.shape)
 
 
 def merge_kernel(place, kept, arrived, _, keep, send):
@@ -171,6 +165,15 @@
     both = kept[...] + arrived[...].astype(f32)
     keep[...] = both[:rows]
     send[...] = both[rows:].astype(bf16)
+
+
+def pair_kernel(place, keep, theirs, _, paired):
+    paired[...] = (keep[...].astype(f32) + theirs[...].astype(f32)).astype(bf16)
+
+
+def means_kernel(place, parts, number, _, sent):
+    means = jnp.sum(parts[...], axis=0) / number[...]
+    sent[...] = jnp.broadcast_to(means[None], sent.shape).astype(bf16)
 
 
 def feature_kernel(place, owners, *rest):
@@ -259,9 +262,6 @@
     )(place, spread, landmarks, *pieces)
 
     theirs = flip(send, "c", 1)
-    paired = (keep.astype(f32) + theirs.astype(f32)).astype(bf16)
-    gathered = lax.all_to_all(paired.reshape(peers, share, -1), PLANE, 0, 0)
-
     leave = call(
         functools.partial(away_kernel, (1, 6, 2, 5)),
         array((ring // 2 * rows, rank_width), bf16),
@@ -271,6 +271,8 @@
         flops=ring * rows * 2 * count * rank_width,
         nbytes=3 * MIB,
     )(place, kernel, whitening, *pieces)
+    paired = call(pair_kernel, array(keep.shape, bf16), 4, 1, nbytes=2 * MIB)(place, keep, theirs, leave)
+    gathered = lax.all_to_all(paired.reshape(peers, share, -1), PLANE, 0, 0)
     arrived = flip(leave, "z", 1)
     kept, leave = call(
         functools.partial(stay_kernel, (0, 7, 3, 4)),
@@ -284,19 +286,14 @@
 
     mapped, number = call(
         cluster_kernel,
-        (array((share, rank_width), f32), array((share, rank_width), f32)),
+        (array((ring, share, rank_width), f32), array((share, rank_width), f32)),
         8,
         6,
         store(2 * count, rank_width),
         nbytes=3 * MIB,
-    )(place, gathered, leave, whitening, *pieces)
-    bit = 1
-    while bit < ring:
-        mapped = mapped + flip(mapped, "z", bit)
-        bit *= 2
-    means = (mapped / number).astype(bf16)
-
-    sent = jnp.broadcast_to(means[None], (peers, share, rank_width))
+    )(place, gathered, arrived, whitening, *pieces)
+    over = lax.all_to_all(mapped, "z", 0, 0)
+    sent = call(means_kernel, array((peers, share, rank_width), bf16), 4, 1, nbytes=MIB)(place, over, number, leave)
     mine = lax.all_to_all(sent, PLANE, 0, 0).reshape(half, rank_width)
 
     arrived = flip(leave, "z", 3)
@@ -306,7 +303,7 @@
         4,
         1,
         nbytes=MIB,
-    )(place, kept, arrived, means)
+    )(place, kept, arrived, sent)
     last = flip(leave, "z", 7)
     features, choose, mine = call(
         feature_kernel,

time: 161 us -> 152 us (0.944)
  waiting for transfers between devices: 58.1 us -> 49.2 us
  starting transfers between devices: 65.9 us -> 60.8 us
  local copies, waits for them, and re-layouts: 12 us -> 16.3 us
    ppermute x10 -> x7, waiting for transfers between devices: 41.7 us -> 27.5 us  [flip(): return lax.ppermute(value, axis, [(i, i ^ bit) for i in range(size)])]
    ppermute x10 -> x7, starting transfers between devices: 29.3 us -> 22.4 us  [flip(): return lax.ppermute(value, axis, [(i, i ^ bit) for i in range(size)])]
    unnamed x20 -> x36, local copies, waits for them, and re-layouts: 5.13 us -> 10.3 us
    all_to_all x0 -> x1, waiting for transfers between devices: none -> 3.82 us  [body(): over = lax.all_to_all(mapped, 'z', 0, 0)]
    all_to_all x0 -> x1, starting transfers between devices: none -> 3.41 us  [body(): over = lax.all_to_all(mapped, 'z', 0, 0)]
    pallas_call x1 -> x3, Pallas kernels: 2.71 us -> 4.83 us  [the longest x1 2.72 us: body(): call(cluster_kernel, (array((ring, share, rank_width), f32), array((share...]
    all_to_all x1, starting transfers between devices: 8.83 us -> 7.16 us  [body(): mine = lax.all_to_all(sent, PLANE, 0, 0).reshape(half, rank_width)]
  transfers between devices with their start and end apart: 15 -> 13, of which waited for: 10 -> 8; matrix products, arithmetic and copies ran while one was open for 3% -> 3% of each run, Pallas kernels for 5% -> 4%
where the time goes in v4:
time: 152 us; the launch traced here: 151 us
  starting transfers between devices  60.8 us (40%)
  waiting for transfers between devices  49.2 us (32%)
  Pallas kernels  22.5 us (15%)
  local copies, waits for them, and re-layouts  16.3 us (11%)
    ppermute x7, waiting for transfers between devices, flip(): return lax.ppermute(value, axis, [(i, i ^ bit) for i in range(size)])  27.5 us
    ppermute x7, starting transfers between devices, flip(): return lax.ppermute(value, axis, [(i, i ^ bit) for i in range(size)])  22.4 us
    all_to_all x1, starting transfers between devices, body(): lax.all_to_all(jnp.broadcast_to(block[None], (ring,) + block.shape), 'z',...  11 us
    unnamed x36, local copies, waits for them, and re-layouts  10.3 us
    all_to_all x1, starting transfers between devices, body(): gathered = lax.all_to_all(paired.reshape(peers, share, -1), PLANE, 0, 0)  9.78 us
    ppermute x2, waiting for transfers between devices, hop(): lax.ppermute(value, axis, [(i, (i + by) % size) for i in range(size)])  9.45 us
    pallas_call x1, Pallas kernels, body(): call(functools.partial(affinity_kernel, rows), (array((ring * rows, 2 * c...  7.72 us
    all_to_all x1, starting transfers between devices, body(): mine = lax.all_to_all(sent, PLANE, 0, 0).reshape(half, rank_width)  7.16 us
  transfers between devices with their start and end apart: 13, of which 8 were waited for; matrix products, arithmetic and copies ran while one was open for 3% of the time, Pallas kernels for 4%

profile of v4, /device:TPU:1, one launch (start us, length us, event | category | flops | bytes accessed | tf_op | source)
XLA Modules:
  0.0 150.9 jit_solution(15500814272710733561)
XLA Ops:
  0.6 0.0 copy-start
  0.7 0.8 tile.4
  1.4 0.1 tile.10
  1.6 0.9 pad_maximum_fusion.2
  2.5 1.2 broadcast_in_dim.6
  3.7 11.0 %all-to-all-start = ((bf16[8,80,1024]{2,1,0:T(8,128)(2,1)}), bf16[8,80,1024]{2,1,0:T(8,128)(2,1)}, u32[]{:S(2)}, u32[]{:S(2)}) async-start(bf16[8,80,1024]{2,1,0:T(8,128)(2,1)} %broadcast_in_dim.6), calls=%async_computation | async-start | bytes 2621440 | tf_op jit(solution)/shard_map/all_to_all | solution.py:236
  14.7 0.0 copy-done.17
  14.8 0.0 copy-done
  14.8 0.0 copy-start.1
  14.8 2.8 %gather_fusion = bf16[512,1024]{1,0:T(8,128)(2,1)} fusion(bf16[768,1024]{1,0:T(8,128)(2,1)S(1)} %copy-done, s32[1024]{0:T(1024)S(1)} %pad_clamp_fusion), kind=kCustom, calls=%fused_computation | custom fusion | bytes 2099200 | tf_op jit(solution)/shard_map/gather | solution.py:238
  17.6 0.0 copy-done.1
  17.6 1.1 constant_dynamic-slice_fusion
  18.7 3.2 %collective-permute-start = (bf16[256,1024]{1,0:T(8,128)(2,1)S(1)}, bf16[256,1024]{1,0:T(8,128)(2,1)S(1)}, u32[]{:S(2)}, u32[]{:S(2)}) collective-permute-start(bf16[256,1024]{1,0:T(8,128)(2,1)S(1)} %pad_maximum_fusion), channel_id=1, source_target_pairs={{0,1},{1,128},{128,129},{129,256},{256,257},{257,384},{384,385},{3... | collective-permute-start | bytes 1572872 | tf_op jit(solution)/shard_map/ppermute | solution.py:25
  22.0 3.8 %collective-permute-start.1 = (bf16[256,1024]{1,0:T(8,128)(2,1)S(1)}, bf16[256,1024]{1,0:T(8,128)(2,1)}, u32[]{:S(2)}, u32[]{:S(2)}) collective-permute-start(bf16[256,1024]{1,0:T(8,128)(2,1)S(1)} %pad_maximum_fusion.1), channel_id=1, source_target_pairs={{0,385},{1,0},{128,1},{129,128},{256,129},{257,256},{384,257},{385... | collective-permute-start | bytes 1572872 | tf_op jit(solution)/shard_map/ppermute | solution.py:25
  25.8 9.4 %collective-permute-done.up.rest_2_ = bf16[256,1024]{1,0:T(8,128)(2,1)S(1)} collective-permute-done((bf16[256,1024]{1,0:T(8,128)(2,1)S(1)}, bf16[256,1024]{1,0:T(8,128)(2,1)S(1)}, u32[]{:S(2)}, u32[]{:S(2)}) %collective-permute-start) | collective-permute-done | bytes 524320 | tf_op jit(solution)/shard_map/ppermute | solution.py:25
  35.3 3.3 %collective-permute-start.2 = (bf16[256,1024]{1,0:T(8,128)(2,1)S(1)}, bf16[256,1024]{1,0:T(8,128)(2,1)}, u32[]{:S(2)}, u32[]{:S(2)}) collective-permute-start(bf16[256,1024]{1,0:T(8,128)(2,1)S(1)} %collective-permute-done.up.rest_2_), channel_id=1, source_target_pairs={{0,16},{16,0},{1,17},{17,1},{2,18},{18,2},{3,19},{19,3},{4,20},{20... | collective-permute-start | bytes 1572872 | tf_op jit(solution)/shard_map/ppermute | solution.py:30
  38.6 0.0 collective-permute-done.1.down.rest_3_
  38.6 1.9 %collective-permute-start.3 = (bf16[256,1024]{1,0:T(8,128)(2,1)}, bf16[256,1024]{1,0:T(8,128)(2,1)}, u32[]{:S(2)}, u32[]{:S(2)}) collective-permute-start(bf16[256,1024]{1,0:T(8,128)(2,1)} %collective-permute-done.1.down.rest_3_), channel_id=1, source_target_pairs={{0,16},{16,0},{1,17},{17,1},{2,18},{18,2},{3,19},{19,3},{4,20},{20... | collective-permute-start | bytes 1572872 | tf_op jit(solution)/shard_map/ppermute | solution.py:30
  40.6 0.1 pad_add_fusion.place
  40.6 0.0 collective-permute-done.2.up_o.rest_4_
  40.6 2.1 %collective-permute-done.3.down_o.rest_5_ = bf16[256,1024]{1,0:T(8,128)(2,1)} collective-permute-done((bf16[256,1024]{1,0:T(8,128)(2,1)}, bf16[256,1024]{1,0:T(8,128)(2,1)}, u32[]{:S(2)}, u32[]{:S(2)}) %collective-permute-start.3) | collective-permute-done | bytes 524320 | tf_op jit(solution)/shard_map/ppermute | solution.py:30
  42.8 6.9 %all-to-all-done.spread = bf16[8,80,1024]{2,1,0:T(8,128)(2,1)} async-done(((bf16[8,80,1024]{2,1,0:T(8,128)(2,1)}), bf16[8,80,1024]{2,1,0:T(8,128)(2,1)}, u32[]{:S(2)}, u32[]{:S(2)}) %all-to-all-start) | async-done | bytes 1310752 | tf_op jit(solution)/shard_map/all_to_all | solution.py:236
  49.7 1.2 copy-done.5
  50.9 7.7 %shard_map.85 = (bf16[512,1024]{1,0:T(8,128)(2,1)S(1)}, bf16[256,1152]{1,0:T(8,128)(2,1)S(1)}, bf16[256,1152]{1,0:T(8,128)(2,1)S(1)}) custom-call(s32[4]{0:T(128)S(1)} %pad_add_fusion.place, bf16[8,80,1024]{2,1,0:T(8,128)(2,1)} %all-to-all-done.spread, bf16[512,1024]{1,0:T(8,128)(2,1)S(1)} %copy-done.5, ...), custom_call_target="tpu_custom_call" | custom-call | flops 1610612736 | bytes 6291456 | tf_op jit(solution)/shard_map/pallas_call | solution.py:250
  58.6 0.0 copy-start.2
  58.7 2.4 %collective-permute-start.4 = (bf16[256,1152]{1,0:T(8,128)(2,1)S(1)}, bf16[256,1152]{1,0:T(8,128)(2,1)S(1)}, u32[]{:S(2)}, u32[]{:S(2)}) collective-permute-start(bf16[256,1152]{1,0:T(8,128)(2,1)S(1)} %get-tuple-element.20), channel_id=1, source_target_pairs={{0,16},{16,0},{1,17},{17,1},{2,18},{18,2},{3,19},{19,3},{4,20},{20... | collective-permute-start | bytes 1769480 | tf_op jit(solution)/shard_map/ppermute | solution.py:30
  61.1 2.5 %shard_map.86._ = bf16[256,1024]{1,0:T(8,128)(2,1)S(1)} custom-call(s32[4]{0:T(128)S(1)} %pad_add_fusion.place, bf16[512,1024]{1,0:T(8,128)(2,1)S(1)} %get-tuple-element.21.kernel, bf16[512,1024]{1,0:T(8,128)(2,1)S(1)} %copy-done.1, bf16[256,1024]{1,0:T(8,128)(2,1)S(1)} %collective-permute-done.up.rest_2_, ...), custom_call_target="tpu_custom_call" | custom-call | flops 536870912 | bytes 3145728 | tf_op jit(solution)/shard_map/pallas_call | solution.py:265
  63.6 0.0 copy-done.2
  63.6 0.0 copy-start.9
  63.6 0.0 collective-permute-done.4.theirs
  63.6 0.7 shard_map.87
  64.3 0.1 copy-done.9
  64.4 0.8 copy-done.4
  65.2 9.8 %all-to-all-start.1 = ((bf16[32,8,1152]{2,1,0:T(8,128)(2,1)}), bf16[32,8,1152]{2,1,0:T(8,128)(2,1)}, u32[]{:S(2)}, u32[]{:S(2)}) async-start(bf16[32,8,1152]{2,1,0:T(8,128)(2,1)} %bitcast.7), calls=%async_computation.1 | async-start | bytes 1179648 | tf_op jit(solution)/shard_map/all_to_all | solution.py:275
  75.0 2.1 %collective-permute-start.5 = (bf16[256,1024]{1,0:T(8,128)(2,1)}, bf16[256,1024]{1,0:T(8,128)(2,1)S(1)}, u32[]{:S(2)}, u32[]{:S(2)}) collective-permute-start(bf16[256,1024]{1,0:T(8,128)(2,1)} %copy-done.9), channel_id=1, source_target_pairs={{0,2},{2,0},{4,6},{6,4},{8,10},{10,8},{12,14},{14,12},{1,3},{3,1},... | collective-permute-start | bytes 1572872 | tf_op jit(solution)/shard_map/ppermute | solution.py:30
  77.2 13.3 %collective-permute-done.5.rest_0_.arrived = bf16[256,1024]{1,0:T(8,128)(2,1)S(1)} collective-permute-done((bf16[256,1024]{1,0:T(8,128)(2,1)}, bf16[256,1024]{1,0:T(8,128)(2,1)S(1)}, u32[]{:S(2)}, u32[]{:S(2)}) %collective-permute-start.5) | collective-permute-done | bytes 524320 | tf_op jit(solution)/shard_map/ppermute | solution.py:30
  90.4 0.8 copy-done.6
  91.2 1.6 %all-to-all-done.1.spread = bf16[32,8,1152]{2,1,0:T(8,128)(2,1)} async-done(((bf16[32,8,1152]{2,1,0:T(8,128)(2,1)}), bf16[32,8,1152]{2,1,0:T(8,128)(2,1)}, u32[]{:S(2)}, u32[]{:S(2)}) %all-to-all-start.1) | async-done | bytes 589856 | tf_op jit(solution)/shard_map/all_to_all | solution.py:275
  92.8 1.0 copy-done.7
  93.8 2.7 %shard_map.88 = (f32[8,8,1024]{2,1,0:T(8,128)S(1)}, f32[8,1024]{1,0:T(8,128)S(1)}) custom-call(s32[4]{0:T(128)S(1)} %pad_add_fusion.place, bf16[32,8,1152]{2,1,0:T(8,128)(2,1)} %all-to-all-done.1.spread, bf16[256,1024]{1,0:T(8,128)(2,1)S(1)} %copy-done.7, bf16[512,1024]{1,0:T(8,128)(2,1)S(1)} %copy-done.1, ...), custom_call_target="tpu_custom_call" | custom-call | bytes 3145728 | tf_op jit(solution)/shard_map/pallas_call | solution.py:287
  96.6 0.7 copy-done.13
  97.3 3.4 %all-to-all-start.2 = ((f32[8,8,1024]{2,1,0:T(8,128)}), f32[8,8,1024]{2,1,0:T(8,128)S(1)}, u32[]{:S(2)}, u32[]{:S(2)}) async-start(f32[8,8,1024]{2,1,0:T(8,128)} %copy-done.13), calls=%async_computation.2 | async-start | bytes 524288 | tf_op jit(solution)/shard_map/all_to_all | solution.py:295
  100.7 1.2 copy-done.3
  101.9 1.0 copy-done.8
  103.0 2.5 %shard_map.89 = (f32[128,1024]{1,0:T(8,128)S(1)}, bf16[128,1024]{1,0:T(8,128)(2,1)S(1)}) custom-call(s32[4]{0:T(128)S(1)} %pad_add_fusion.place, bf16[512,1024]{1,0:T(8,128)(2,1)S(1)} %copy-done.3, bf16[256,1024]{1,0:T(8,128)(2,1)S(1)} %copy-done.8, bf16[512,1024]{1,0:T(8,128)(2,1)S(1)} %copy-done.1, bf16[256,1024]{1,0:T(8,128)(2,1)S(1)} %collective-permute-done.up.rest_2_, ...), custom_call_target="tpu_custom_call" | custom-call | flops 536870912 | bytes 3145728 | tf_op jit(solution)/shard_map/pallas_call | solution.py:277
  105.5 0.8 copy-done.10
  106.3 0.7 copy-done.14
  107.0 3.8 %all-to-all-done.2.parts = f32[8,8,1024]{2,1,0:T(8,128)S(1)} async-done(((f32[8,8,1024]{2,1,0:T(8,128)}), f32[8,8,1024]{2,1,0:T(8,128)S(1)}, u32[]{:S(2)}, u32[]{:S(2)}) %all-to-all-start.2) | async-done | bytes 262176 | tf_op jit(solution)/shard_map/all_to_all | solution.py:295
  110.8 1.0 copy-done.15
  111.8 1.4 shard_map.90._
  113.2 7.2 %all-to-all-start.3 = ((bf16[32,8,1024]{2,1,0:T(8,128)(2,1)}), bf16[32,8,1024]{2,1,0:T(8,128)(2,1)S(1)}, u32[]{:S(2)}, u32[]{:S(2)}) async-start(bf16[32,8,1024]{2,1,0:T(8,128)(2,1)} %shard_map.90._), calls=%async_computation.3 | async-start | bytes 1048576 | tf_op jit(solution)/shard_map/all_to_all | solution.py:297
  120.4 2.5 %collective-permute-start.6 = (bf16[128,1024]{1,0:T(8,128)(2,1)}, bf16[128,1024]{1,0:T(8,128)(2,1)S(1)}, u32[]{:S(2)}, u32[]{:S(2)}) collective-permute-start(bf16[128,1024]{1,0:T(8,128)(2,1)} %copy-done.14), channel_id=1, source_target_pairs={{0,6},{2,4},{4,2},{6,0},{8,14},{10,12},{12,10},{14,8},{1,7},{3,5},... | collective-permute-start | bytes 786440 | tf_op jit(solution)/shard_map/ppermute | solution.py:30
  122.9 6.8 %collective-permute-done.6.arrived = bf16[128,1024]{1,0:T(8,128)(2,1)S(1)} collective-permute-done((bf16[128,1024]{1,0:T(8,128)(2,1)}, bf16[128,1024]{1,0:T(8,128)(2,1)S(1)}, u32[]{:S(2)}, u32[]{:S(2)}) %collective-permute-start.6) | collective-permute-done | bytes 262176 | tf_op jit(solution)/shard_map/ppermute | solution.py:30
  129.6 0.6 shard_map.91
  130.2 1.9 %collective-permute-start.7 = (bf16[64,1024]{1,0:T(8,128)(2,1)S(1)}, bf16[64,1024]{1,0:T(8,128)(2,1)S(1)}, u32[]{:S(2)}, u32[]{:S(2)}) collective-permute-start(bf16[64,1024]{1,0:T(8,128)(2,1)S(1)} %get-tuple-element.27), channel_id=1, source_target_pairs={{0,14},{2,12},{4,10},{6,8},{8,6},{10,4},{12,2},{14,0},{1,15},{3,13... | collective-permute-start | bytes 393224 | tf_op jit(solution)/shard_map/ppermute | solution.py:30
  132.1 5.3 %collective-permute-done.7.rest_2_ = bf16[64,1024]{1,0:T(8,128)(2,1)S(1)} collective-permute-done((bf16[64,1024]{1,0:T(8,128)(2,1)S(1)}, bf16[64,1024]{1,0:T(8,128)(2,1)S(1)}, u32[]{:S(2)}, u32[]{:S(2)}) %collective-permute-start.7) | collective-permute-done | bytes 131104 | tf_op jit(solution)/shard_map/ppermute | solution.py:30
  137.4 0.0 all-to-all-done.3
  137.4 1.3 shard_map.92
  138.7 8.3 %collective-permute-start.8 = (bf16[256,1024]{1,0:T(8,128)(2,1)S(1)}, bf16[256,1024]{1,0:T(8,128)(2,1)S(1)}, u32[]{:S(2)}, u32[]{:S(2)}) collective-permute-start(bf16[256,1024]{1,0:T(8,128)(2,1)S(1)} %get-tuple-element.29.means), channel_id=1, source_target_pairs={{0,16},{16,0},{1,17},{17,1},{2,18},{18,2},{3,19},{19,3},{4,20},{20... | collective-permute-start | bytes 1572872 | tf_op jit(solution)/shard_map/ppermute | solution.py:30
  147.0 0.0 copy-start.12
  147.0 0.9 copy-done.12
  147.9 1.2 shard_map.93
  149.1 0.0 collective-permute-done.8.means
  149.1 1.8 %shard_map.94 = (f32[64,512]{1,0:T(8,128)}, bf16[16,1024]{1,0:T(8,128)(2,1)}) custom-call(s32[4]{0:T(128)S(1)} %pad_add_fusion.place, bf16[64,1024]{1,0:T(8,128)(2,1)S(1)} %copy-done.12, bf16[256,1024]{1,0:T(8,128)(2,1)S(1)} %collective-permute-done.8.means, bf16[16,512]{1,0:T(8,128)(2,1)S(1)} %get-tuple-element.30.choose, ...), custom_call_target="tpu_custom_call" | custom-call | bytes 1048576 | tf_op jit(solution)/shard_map/pallas_call | solution.py:322
  (23 shorter events, 0.2 us)
Async XLA Ops:
  0.6 14.1 %copy-start = (bf16[768,1024]{1,0:T(8,128)(2,1)S(1)}, bf16[768,1024]{1,0:T(8,128)(2,1)}, u32[]{:S(2)}) copy-start(bf16[768,1024]{1,0:T(8,128)(2,1)} %param.8) | copy-start | bytes 4718596
  3.7 11.0 %copy-start.17 = (s32[512]{0:T(512)S(1)}, s32[512]{0:T(512)}, u32[]{:S(2)}) copy-start(s32[512]{0:T(512)} %param.9) | copy-start | bytes 6148
  3.7 46.0 %all-to-all-start = ((bf16[8,80,1024]{2,1,0:T(8,128)(2,1)}), bf16[8,80,1024]{2,1,0:T(8,128)(2,1)}, u32[]{:S(2)}, u32[]{:S(2)}) async-start(bf16[8,80,1024]{2,1,0:T(8,128)(2,1)} %broadcast_in_dim.6), calls=%async_computation | async-start | bytes 2621440 | tf_op jit(solution)/shard_map/all_to_all | solution.py:236
  14.8 2.8 %copy-start.1 = (bf16[512,1024]{1,0:T(8,128)(2,1)S(1)}, bf16[512,1024]{1,0:T(8,128)(2,1)}, u32[]{:S(2)}) copy-start(bf16[512,1024]{1,0:T(8,128)(2,1)} %white.3) | copy-start | bytes 3145732
  18.7 16.5 %collective-permute-start = (bf16[256,1024]{1,0:T(8,128)(2,1)S(1)}, bf16[256,1024]{1,0:T(8,128)(2,1)S(1)}, u32[]{:S(2)}, u32[]{:S(2)}) collective-permute-start(bf16[256,1024]{1,0:T(8,128)(2,1)S(1)} %pad_maximum_fusion), channel_id=1, source_target_pairs={{0,1},{1,128},{128,129},{129,256},{256,257},{257,384},{384,385},{3... | collective-permute-start | bytes 1572872 | tf_op jit(solution)/shard_map/ppermute | solution.py:25
  22.0 16.6 %collective-permute-start.1 = (bf16[256,1024]{1,0:T(8,128)(2,1)S(1)}, bf16[256,1024]{1,0:T(8,128)(2,1)}, u32[]{:S(2)}, u32[]{:S(2)}) collective-permute-start(bf16[256,1024]{1,0:T(8,128)(2,1)S(1)} %pad_maximum_fusion.1), channel_id=1, source_target_pairs={{0,385},{1,0},{128,1},{129,128},{256,129},{257,256},{384,257},{385... | collective-permute-start | bytes 1572872 | tf_op jit(solution)/shard_map/ppermute | solution.py:25
  35.3 5.4 %collective-permute-start.2 = (bf16[256,1024]{1,0:T(8,128)(2,1)S(1)}, bf16[256,1024]{1,0:T(8,128)(2,1)}, u32[]{:S(2)}, u32[]{:S(2)}) collective-permute-start(bf16[256,1024]{1,0:T(8,128)(2,1)S(1)} %collective-permute-done.up.rest_2_), channel_id=1, source_target_pairs={{0,16},{16,0},{1,17},{17,1},{2,18},{18,2},{3,19},{19,3},{4,20},{20... | collective-permute-start | bytes 1572872 | tf_op jit(solution)/shard_map/ppermute | solution.py:30
  38.6 4.1 %collective-permute-start.3 = (bf16[256,1024]{1,0:T(8,128)(2,1)}, bf16[256,1024]{1,0:T(8,128)(2,1)}, u32[]{:S(2)}, u32[]{:S(2)}) collective-permute-start(bf16[256,1024]{1,0:T(8,128)(2,1)} %collective-permute-done.1.down.rest_3_), channel_id=1, source_target_pairs={{0,16},{16,0},{1,17},{17,1},{2,18},{18,2},{3,19},{19,3},{4,20},{20... | collective-permute-start | bytes 1572872 | tf_op jit(solution)/shard_map/ppermute | solution.py:30
  49.7 1.2 copy-start.5
  58.6 4.9 %copy-start.2 = (bf16[512,1024]{1,0:T(8,128)(2,1)}, bf16[512,1024]{1,0:T(8,128)(2,1)S(1)}, u32[]{:S(2)}) copy-start(bf16[512,1024]{1,0:T(8,128)(2,1)S(1)} %get-tuple-element.21.kernel) | copy-start | bytes 3145732
  58.7 4.9 %collective-permute-start.4 = (bf16[256,1152]{1,0:T(8,128)(2,1)S(1)}, bf16[256,1152]{1,0:T(8,128)(2,1)S(1)}, u32[]{:S(2)}, u32[]{:S(2)}) collective-permute-start(bf16[256,1152]{1,0:T(8,128)(2,1)S(1)} %get-tuple-element.20), channel_id=1, source_target_pairs={{0,16},{16,0},{1,17},{17,1},{2,18},{18,2},{3,19},{19,3},{4,20},{20... | collective-permute-start | bytes 1769480 | tf_op jit(solution)/shard_map/ppermute | solution.py:30
  63.6 0.8 copy-start.9
  64.4 0.8 copy-start.4
  65.2 27.6 %all-to-all-start.1 = ((bf16[32,8,1152]{2,1,0:T(8,128)(2,1)}), bf16[32,8,1152]{2,1,0:T(8,128)(2,1)}, u32[]{:S(2)}, u32[]{:S(2)}) async-start(bf16[32,8,1152]{2,1,0:T(8,128)(2,1)} %bitcast.7), calls=%async_computation.1 | async-start | bytes 1179648 | tf_op jit(solution)/shard_map/all_to_all | solution.py:275
  75.0 15.4 %collective-permute-start.5 = (bf16[256,1024]{1,0:T(8,128)(2,1)}, bf16[256,1024]{1,0:T(8,128)(2,1)S(1)}, u32[]{:S(2)}, u32[]{:S(2)}) collective-permute-start(bf16[256,1024]{1,0:T(8,128)(2,1)} %copy-done.9), channel_id=1, source_target_pairs={{0,2},{2,0},{4,6},{6,4},{8,10},{10,8},{12,14},{14,12},{1,3},{3,1},... | collective-permute-start | bytes 1572872 | tf_op jit(solution)/shard_map/ppermute | solution.py:30
  90.4 0.8 copy-start.6
  92.8 1.0 copy-start.7
  96.6 0.7 copy-start.13
  97.3 13.5 %all-to-all-start.2 = ((f32[8,8,1024]{2,1,0:T(8,128)}), f32[8,8,1024]{2,1,0:T(8,128)S(1)}, u32[]{:S(2)}, u32[]{:S(2)}) async-start(f32[8,8,1024]{2,1,0:T(8,128)} %copy-done.13), calls=%async_computation.2 | async-start | bytes 524288 | tf_op jit(solution)/shard_map/all_to_all | solution.py:295
  100.7 1.2 copy-start.3
  101.9 1.0 copy-start.8
  105.5 0.8 copy-start.10
  106.3 0.7 copy-start.14
  110.8 18.9 %copy-start.11 = (f32[128,1024]{1,0:T(8,128)S(1)}, f32[128,1024]{1,0:T(8,128)}, u32[]{:S(2)}) copy-start(f32[128,1024]{1,0:T(8,128)} %copy-done.10) | copy-start | bytes 1572868
  110.8 1.0 copy-start.15
  111.8 25.7 %copy-start.16 = (s32[512]{0:T(512)S(1)}, s32[512]{0:T(512)}, u32[]{:S(2)}) copy-start(s32[512]{0:T(512)} %param.11) | copy-start | bytes 6148
  113.2 24.2 %all-to-all-start.3 = ((bf16[32,8,1024]{2,1,0:T(8,128)(2,1)}), bf16[32,8,1024]{2,1,0:T(8,128)(2,1)S(1)}, u32[]{:S(2)}, u32[]{:S(2)}) async-start(bf16[32,8,1024]{2,1,0:T(8,128)(2,1)} %shard_map.90._), calls=%async_computation.3 | async-start | bytes 1048576 | tf_op jit(solution)/shard_map/all_to_all | solution.py:297
  120.4 9.2 %collective-permute-start.6 = (bf16[128,1024]{1,0:T(8,128)(2,1)}, bf16[128,1024]{1,0:T(8,128)(2,1)S(1)}, u32[]{:S(2)}, u32[]{:S(2)}) collective-permute-start(bf16[128,1024]{1,0:T(8,128)(2,1)} %copy-done.14), channel_id=1, source_target_pairs={{0,6},{2,4},{4,2},{6,0},{8,14},{10,12},{12,10},{14,8},{1,7},{3,5},... | collective-permute-start | bytes 786440 | tf_op jit(solution)/shard_map/ppermute | solution.py:30
  130.2 7.2 %collective-permute-start.7 = (bf16[64,1024]{1,0:T(8,128)(2,1)S(1)}, bf16[64,1024]{1,0:T(8,128)(2,1)S(1)}, u32[]{:S(2)}, u32[]{:S(2)}) collective-permute-start(bf16[64,1024]{1,0:T(8,128)(2,1)S(1)} %get-tuple-element.27), channel_id=1, source_target_pairs={{0,14},{2,12},{4,10},{6,8},{8,6},{10,4},{12,2},{14,0},{1,15},{3,13... | collective-permute-start | bytes 393224 | tf_op jit(solution)/shard_map/ppermute | solution.py:30
  138.7 10.4 %collective-permute-start.8 = (bf16[256,1024]{1,0:T(8,128)(2,1)S(1)}, bf16[256,1024]{1,0:T(8,128)(2,1)S(1)}, u32[]{:S(2)}, u32[]{:S(2)}) collective-permute-start(bf16[256,1024]{1,0:T(8,128)(2,1)S(1)} %get-tuple-element.29.means), channel_id=1, source_target_pairs={{0,16},{16,0},{1,17},{17,1},{2,18},{18,2},{3,19},{19,3},{4,20},{20... | collective-permute-start | bytes 1572872 | tf_op jit(solution)/shard_map/ppermute | solution.py:30
  147.0 0.9 copy-start.12

commit v5 on v4

--- a/solution.py
+++ b/solution.py
@@ -15,6 +15,8 @@
 ALL = ("yh", "x", "c", "z", "yl")
 PLANE = ("yh", "x", "yl")
 PACK = 16
+LEAVE = (1, 6, 2, 5)
+STAY = (0, 7, 3, 4)
 DIGIT = 128
 TALLY = 128
 MIB = 1 << 20
@@ -34,18 +36,38 @@
     return lax.dot_general(a, b, (((1,), (1,)), ((), ())), preferred_element_type=f32)
 
 
-def call(kernel, out, ins, held=0, scratch=(), flops=0, nbytes=0):
+def call(kernel, out, ins, held=0, scratch=(), away=(), flops=0, nbytes=0):
     spec = pl.BlockSpec(memory_space=pltpu.VMEM)
-    away = pl.BlockSpec(memory_space=pl.ANY)
-    return pl.pallas_call(
-        kernel,
-        out_shape=out,
-        in_specs=[pl.BlockSpec(memory_space=pltpu.SMEM)] + [spec] * (ins - 1 - held) + [away] * held,
-        out_specs=jax.tree.map(lambda _: spec, out),
-        scratch_shapes=list(scratch),
+    far = pl.BlockSpec(memory_space=pltpu.HBM)
+    scratch, many = list(scratch), len(out)
+    own = len(scratch)
+    for i in away:
+        scratch += [pltpu.VMEM(out[i].shape, out[i].dtype), pltpu.SemaphoreType.DMA]
+
+    def run(*refs):
+        outs, extra = list(refs[ins : ins + many]), refs[ins + many :]
+        moves = []
+        for n, i in enumerate(away):
+            staged, sem = extra[own + 2 * n : own + 2 * n + 2]
+            moves.append(pltpu.make_async_copy(staged, outs[i], sem))
+            outs[i] = staged
+        kernel(*refs[:ins], *outs, *extra[:own])
+        for move in moves:
+            move.start()
+        for move in moves:
+            move.wait()
+
+    made = pl.pallas_call(
+        run,
+        out_shape=tuple(pltpu.HBM(o.shape, o.dtype) if i in away else o for i, o in enumerate(out)),
+        in_specs=[pl.BlockSpec(memory_space=pltpu.SMEM)] + [spec] * (ins - 1 - held) + [far] * held,
+        out_specs=tuple(far if i in away else spec for i in range(many)),
+        scratch_shapes=scratch,
         compiler_params=pltpu.CompilerParams(vmem_limit_bytes=16 * MIB),
         cost_estimate=pl.CostEstimate(flops=flops, bytes_accessed=nbytes, transcendentals=0),
     )
+    near = ins - held
+    return lambda *args: made(*args[:near], *(pltpu.with_memory_space_constraint(a, pltpu.HBM) for a in args[near:]))
 
 
 def fetch(place, block, swapped, second, table, sems):
@@ -73,6 +95,19 @@
     low = (square - high.astype(f32)).astype(bf16)
     ones = jnp.ones((8, matrix.shape[1]), bf16)
     return across(ones, high) + across(ones, low)
+
+
+def pack_kernel(place, points, members, out):
+    rows, width = points.shape
+    code = jnp.broadcast_to(members[...], (PACK, rows))
+    row = lax.broadcasted_iota(i32, (PACK, rows), 0)
+    digits = jnp.where(row == 0, code // DIGIT, jnp.where(row == 1, code % DIGIT, 0)).astype(f32).astype(bf16)
+    lane = lax.broadcasted_iota(i32, (rows, width), 1) - place[3] * rows
+    spot = jnp.where(lane == lax.broadcasted_iota(i32, (rows, width), 0), 1.0, 0.0).astype(bf16)
+    tail = jnp.dot(digits, spot, preferred_element_type=f32).astype(bf16)
+    for i in range(out.shape[0]):
+        out[i, :rows, :] = points[...]
+        out[i, rows:, :] = tail
 
 
 def affinity_kernel(rows, place, spread, own, up, down, up_o, down_o, kernel, keep, send, table, anchors, sems):
@@ -117,29 +152,24 @@
     return jnp.dot(span, maps[:, pl.ds(at, tile)], preferred_element_type=f32)
 
 
-def away_kernel(owners, place, kernel, white, up, down, up_o, down_o, send, maps, sems):
+def project_kernel(kernel_rows, place, kernel, white, up, down, up_o, down_o, leave, stay, token, maps, sems):
     copies = fetch(place, white, (up, down, up_o, down_o), 1, maps, sems)
     for copy in copies:
         copy.wait()
-    rows, width = send.shape[0] // len(owners), send.shape[1]
+    token[...] = jnp.zeros_like(token)
+    width = leave.shape[1]
     tile = min(256, width)
-
     for at in range(0, width, tile):
-        send[:, pl.ds(at, tile)] = project(place, kernel, maps, owners, rows, at, tile).astype(bf16)
-
-
-def stay_kernel(owners, place, kernel, arrived, white, up, down, up_o, down_o, keep, send, maps, sems):
-    copies = fetch(place, white, (up, down, up_o, down_o), 1, maps, sems)
-    for copy in copies:
-        copy.wait()
-    rows, width = arrived.shape[0] // len(owners), arrived.shape[1]
-    tile = min(256, width)
+        for out, owners in ((leave, LEAVE), (stay, STAY)):
+            out[:, at : at + tile] = project(place, kernel, maps, owners, kernel_rows, at, tile).astype(bf16)
+
+
+def merge_kernel(place, kept, arrived, keep, send, token):
     half = keep.shape[0]
-
-    for at in range(0, width, tile):
-        both = project(place, kernel, maps, owners, rows, at, tile) + arrived[:, pl.ds(at, tile)].astype(f32)
-        keep[:, pl.ds(at, tile)] = both[:half]
-        send[:, pl.ds(at, tile)] = both[half:].astype(bf16)
+    both = (kept[...].astype(f32) + arrived[...].astype(f32)).astype(bf16)
+    keep[...] = both[:half]
+    send[...] = both[half:]
+    token[...] = jnp.zeros_like(token)
 
 
 def cluster_kernel(place, spread, *rest):
@@ -160,13 +190,6 @@
     mapped[...] = jnp.broadcast_to((result[:share] + result[share:])[None], mapped.shape)
 
 
-def merge_kernel(place, kept, arrived, _, keep, send):
-    rows = keep.shape[0]
-    both = kept[...] + arrived[...].astype(f32)
-    keep[...] = both[:rows]
-    send[...] = both[rows:].astype(bf16)
-
-
 def pair_kernel(place, keep, theirs, _, paired):
     paired[...] = (keep[...].astype(f32) + theirs[...].astype(f32)).astype(bf16)
 
@@ -179,7 +202,7 @@
 def feature_kernel(place, owners, *rest):
     arrived, kept, last, features, choose, means = rest
     means[...] = arrived[...]
-    features[...] = (kept[...] + last[...].astype(f32)).astype(bf16)
+    features[...] = (kept[...].astype(f32) + last[...].astype(f32)).astype(bf16)
     slots, clusters = choose.shape
     owned = owners[...] == place[2]
     row = lax.broadcasted_iota(i32, (clusters, clusters), 0)
@@ -229,11 +252,10 @@
     array = jax.ShapeDtypeStruct
     place = jnp.stack([core, lax.axis_index("yl"), lax.axis_index(("yh", "x", "c")), lax.axis_index("z")]).astype(i32)
 
-    lanes = jnp.arange(width) // rows == lax.axis_index("z")
-    spots = jnp.where(lanes, jnp.pad(jnp.tile(membership, ring), (0, width - ring * rows)), 0)
-    tail = jnp.pad(jnp.stack([spots // DIGIT, spots % DIGIT]), ((0, PACK - 2), (0, 0))).astype(bf16)
-    block = jnp.concatenate([points, tail])
-    spread = lax.all_to_all(jnp.broadcast_to(block[None], (ring,) + block.shape), "z", 0, 0)
+    (block,) = call(pack_kernel, (array((ring, rows + PACK, width), bf16),), 3, away=(0,), nbytes=2 * MIB)(
+        place, points, membership.reshape(1, rows)
+    )
+    spread = lax.all_to_all(block, "z", 0, 0)
 
     landmarks = landmark_pool[landmark_ids]
 
@@ -262,48 +284,42 @@
     )(place, spread, landmarks, *pieces)
 
     theirs = flip(send, "c", 1)
-    leave = call(
-        functools.partial(away_kernel, (1, 6, 2, 5)),
-        array((ring // 2 * rows, rank_width), bf16),
+    token = array((8, 128), f32)
+
+    leave, stay, done = call(
+        functools.partial(project_kernel, rows),
+        (array((ring // 2 * rows, rank_width), bf16), array((ring // 2 * rows, rank_width), bf16), token),
         7,
         5,
         store(2 * count, rank_width),
-        flops=ring * rows * 2 * count * rank_width,
+        away=(0, 1),
+        flops=2 * ring * rows * 2 * count * rank_width,
         nbytes=3 * MIB,
     )(place, kernel, whitening, *pieces)
-    paired = call(pair_kernel, array(keep.shape, bf16), 4, 1, nbytes=2 * MIB)(place, keep, theirs, leave)
+    (paired,) = call(pair_kernel, (array(keep.shape, bf16),), 4, away=(0,), nbytes=2 * MIB)(place, keep, theirs, done)
     gathered = lax.all_to_all(paired.reshape(peers, share, -1), PLANE, 0, 0)
-    arrived = flip(leave, "z", 1)
-    kept, leave = call(
-        functools.partial(stay_kernel, (0, 7, 3, 4)),
-        (array((ring // 4 * rows, rank_width), f32), array((ring // 4 * rows, rank_width), bf16)),
-        8,
-        5,
-        store(2 * count, rank_width),
-        flops=ring * rows * 2 * count * rank_width,
-        nbytes=3 * MIB,
-    )(place, kernel, arrived, whitening, *pieces)
-
+
+    def merge(kept, leave, partner):
+        size = array((kept.shape[0] // 2, rank_width), bf16)
+        arrived = flip(leave, "z", partner)
+        return call(merge_kernel, (size, size, token), 3, away=(0, 1), nbytes=MIB)(place, kept, arrived)
+
+    kept, leave, done = merge(stay, leave, 1)
     mapped, number = call(
         cluster_kernel,
         (array((ring, share, rank_width), f32), array((share, rank_width), f32)),
         8,
-        6,
+        5,
         store(2 * count, rank_width),
+        away=(0,),
         nbytes=3 * MIB,
-    )(place, gathered, arrived, whitening, *pieces)
+    )(place, gathered, done, whitening, *pieces)
     over = lax.all_to_all(mapped, "z", 0, 0)
-    sent = call(means_kernel, array((peers, share, rank_width), bf16), 4, 1, nbytes=MIB)(place, over, number, leave)
+    kept, leave, done = merge(kept, leave, 3)
+    (sent,) = call(means_kernel, (array((peers, share, rank_width), bf16),), 4, away=(0,), nbytes=MIB)(
+        place, over, number, done
+    )
     mine = lax.all_to_all(sent, PLANE, 0, 0).reshape(half, rank_width)
-
-    arrived = flip(leave, "z", 3)
-    kept, leave = call(
-        merge_kernel,
-        (array((rows, rank_width), f32), array((rows, rank_width), bf16)),
-        4,
-        1,
-        nbytes=MIB,
-    )(place, kept, arrived, sent)
     last = flip(leave, "z", 7)
     features, choose, mine = call(
         feature_kernel,

time: 152 us -> 154 us (1.013)
  the two profiles are of different devices: /device:TPU:1 before, /device:TPU:73 now
where the time goes in v5:
time: 154 us; the launch traced here: 153 us
  starting transfers between devices  66.1 us (43%)
  waiting for transfers between devices  51.6 us (34%)
  Pallas kernels  26.6 us (17%)
  local copies, waits for them, and re-layouts  7.44 us (5%)
    ppermute x7, waiting for transfers between devices, flip(): return lax.ppermute(value, axis, [(i, i ^ bit) for i in range(size)])  31.7 us
    ppermute x7, starting transfers between devices, flip(): return lax.ppermute(value, axis, [(i, i ^ bit) for i in range(size)])  28.8 us
    pallas_call x11, Pallas kernels, call(): made(*args[:near], *(pltpu.with_memory_space_constraint(a, pltpu.HBM) for...  26.6 us
    all_to_all x1, starting transfers between devices, body(): gathered = lax.all_to_all(paired.reshape(peers, share, -1), PLANE, 0, 0)  9.62 us
    all_to_all x1, starting transfers between devices, body(): spread = lax.all_to_all(block, 'z', 0, 0)  9.42 us
    ppermute x2, waiting for transfers between devices, hop(): lax.ppermute(value, axis, [(i, (i + by) % size) for i in range(size)])  8.73 us
    all_to_all x1, starting transfers between devices, body(): mine = lax.all_to_all(sent, PLANE, 0, 0).reshape(half, rank_width)  8.34 us
    all_to_all x1, waiting for transfers between devices, body(): mine = lax.all_to_all(sent, PLANE, 0, 0).reshape(half, rank_width)  5.3 us
  transfers between devices with their start and end apart: 13, of which 8 were waited for; matrix products, arithmetic and copies ran while one was open for 3% of the time, Pallas kernels for 5%

profile of v5, /device:TPU:73, one launch (start us, length us, event | category | flops | bytes accessed | tf_op | source)
XLA Modules:
  0.0 152.8 jit_solution(14068642170906066810)
XLA Ops:
  0.6 0.0 copy-start
  0.7 0.1 pad_add_fusion.refs_0_
  0.7 1.0 copy-done.4
  1.7 0.7 copy-done.7
  2.4 1.8 %shard_map.85 = bf16[8,80,1024]{2,1,0:T(8,128)(2,1)} custom-call(s32[4]{0:T(128)S(1)} %pad_add_fusion.refs_0_, bf16[64,1024]{1,0:T(8,128)(2,1)S(1)} %copy-done.4, s32[1,64]{1,0:T(1,128)S(1)} %bitcast.10), custom_call_target="tpu_custom_call" | custom-call | bytes 2097152 | tf_op jit(solution)/shard_map/pallas_call | solution.py:70
  4.2 0.0 copy-start.11
  4.2 9.4 %all-to-all-start = ((bf16[8,80,1024]{2,1,0:T(8,128)(2,1)}), bf16[8,80,1024]{2,1,0:T(8,128)(2,1)S(1)}, u32[]{:S(2)}, u32[]{:S(2)}) async-start(bf16[8,80,1024]{2,1,0:T(8,128)(2,1)} %shard_map.85), calls=%async_computation | async-start | bytes 2621440 | tf_op jit(solution)/shard_map/all_to_all | solution.py:258
  13.6 0.0 copy-done.11
  13.6 0.0 copy-done
  13.6 2.8 %gather_fusion = bf16[512,1024]{1,0:T(8,128)(2,1)} fusion(bf16[768,1024]{1,0:T(8,128)(2,1)S(1)} %copy-done, s32[1024]{0:T(1024)S(1)} %pad_clamp_fusion), kind=kCustom, calls=%fused_computation | custom fusion | bytes 2099200 | tf_op jit(solution)/shard_map/gather | solution.py:260
  16.4 1.3 constant_dynamic-slice_fusion
  17.7 3.2 %collective-permute-start = (bf16[256,1024]{1,0:T(8,128)(2,1)S(1)}, bf16[256,1024]{1,0:T(8,128)(2,1)S(1)}, u32[]{:S(2)}, u32[]{:S(2)}) collective-permute-start(bf16[256,1024]{1,0:T(8,128)(2,1)S(1)} %pad_maximum_fusion), channel_id=1, source_target_pairs={{0,1},{1,128},{128,129},{129,256},{256,257},{257,384},{384,385},{3... | collective-permute-start | bytes 1572872 | tf_op jit(solution)/shard_map/ppermute | solution.py:27
  21.0 2.1 %collective-permute-start.1 = (bf16[256,1024]{1,0:T(8,128)(2,1)S(1)}, bf16[256,1024]{1,0:T(8,128)(2,1)S(1)}, u32[]{:S(2)}, u32[]{:S(2)}) collective-permute-start(bf16[256,1024]{1,0:T(8,128)(2,1)S(1)} %pad_maximum_fusion.1), channel_id=1, source_target_pairs={{0,385},{1,0},{128,1},{129,128},{256,129},{257,256},{384,257},{385... | collective-permute-start | bytes 1572872 | tf_op jit(solution)/shard_map/ppermute | solution.py:27
  23.1 8.7 %collective-permute-done.refs_3_.refs_4_ = bf16[256,1024]{1,0:T(8,128)(2,1)S(1)} collective-permute-done((bf16[256,1024]{1,0:T(8,128)(2,1)S(1)}, bf16[256,1024]{1,0:T(8,128)(2,1)S(1)}, u32[]{:S(2)}, u32[]{:S(2)}) %collective-permute-start) | collective-permute-done | bytes 524320 | tf_op jit(solution)/shard_map/ppermute | solution.py:27
  31.8 4.1 %collective-permute-start.2 = (bf16[256,1024]{1,0:T(8,128)(2,1)S(1)}, bf16[256,1024]{1,0:T(8,128)(2,1)S(1)}, u32[]{:S(2)}, u32[]{:S(2)}) collective-permute-start(bf16[256,1024]{1,0:T(8,128)(2,1)S(1)} %collective-permute-done.refs_3_.refs_4_), channel_id=1, source_target_pairs={{0,16},{16,0},{1,17},{17,1},{2,18},{18,2},{3,19},{19,3},{4,20},{20... | collective-permute-start | bytes 1572872 | tf_op jit(solution)/shard_map/ppermute | solution.py:32
  35.9 0.0 collective-permute-done.1.refs_4_.refs_5_
  35.9 0.0 copy-start.9
  35.9 3.2 %collective-permute-start.3 = (bf16[256,1024]{1,0:T(8,128)(2,1)S(1)}, bf16[256,1024]{1,0:T(8,128)(2,1)}, u32[]{:S(2)}, u32[]{:S(2)}) collective-permute-start(bf16[256,1024]{1,0:T(8,128)(2,1)S(1)} %collective-permute-done.1.refs_4_.refs_5_), channel_id=1, source_target_pairs={{0,16},{16,0},{1,17},{17,1},{2,18},{18,2},{3,19},{19,3},{4,20},{20... | collective-permute-start | bytes 1572872 | tf_op jit(solution)/shard_map/ppermute | solution.py:32
  39.1 0.0 collective-permute-done.2.refs_5_.refs_6_
  39.1 0.0 copy-done.9
  39.1 0.0 copy-start.10
  39.2 0.8 copy-done.10
  39.9 0.8 collective-permute-done.3.refs_6_.refs_7_
  40.8 4.8 %all-to-all-done.refs_1_ = bf16[8,80,1024]{2,1,0:T(8,128)(2,1)S(1)} async-done(((bf16[8,80,1024]{2,1,0:T(8,128)(2,1)}), bf16[8,80,1024]{2,1,0:T(8,128)(2,1)S(1)}, u32[]{:S(2)}, u32[]{:S(2)}) %all-to-all-start) | async-done | bytes 1310752 | tf_op jit(solution)/shard_map/all_to_all | solution.py:258
  45.6 0.0 copy-done.8
  45.6 7.2 %shard_map.86 = (bf16[512,1024]{1,0:T(8,128)(2,1)S(1)}, bf16[256,1152]{1,0:T(8,128)(2,1)S(1)}, bf16[256,1152]{1,0:T(8,128)(2,1)S(1)}) custom-call(s32[4]{0:T(128)S(1)} %pad_add_fusion.refs_0_, bf16[8,80,1024]{2,1,0:T(8,128)(2,1)S(1)} %all-to-all-done.refs_1_, bf16[512,1024]{1,0:T(8,128)(2,1)} %gather_fusion, bf16[256,1024]{1,0:T(8,128)(2,1)} %copy-done.8, ...), custom_call_target="tpu_custom_call" | custom-call | flops 1610612736 | bytes 6291456 | tf_op jit(solution)/shard_map/pallas_call | solution.py:70
  52.9 4.0 %collective-permute-start.4 = (bf16[256,1152]{1,0:T(8,128)(2,1)S(1)}, bf16[256,1152]{1,0:T(8,128)(2,1)S(1)}, u32[]{:S(2)}, u32[]{:S(2)}) collective-permute-start(bf16[256,1152]{1,0:T(8,128)(2,1)S(1)} %get-tuple-element.25), channel_id=1, source_target_pairs={{0,16},{16,0},{1,17},{17,1},{2,18},{18,2},{3,19},{19,3},{4,20},{20... | collective-permute-start | bytes 1769480 | tf_op jit(solution)/shard_map/ppermute | solution.py:32
  56.9 4.4 %shard_map.87 = (bf16[256,1024]{1,0:T(8,128)(2,1)}, bf16[256,1024]{1,0:T(8,128)(2,1)}, f32[8,128]{1,0:T(8,128)S(1)}) custom-call(s32[4]{0:T(128)S(1)} %pad_add_fusion.refs_0_, bf16[512,1024]{1,0:T(8,128)(2,1)S(1)} %get-tuple-element.26.refs_1_, bf16[512,1024]{1,0:T(8,128)(2,1)} %refs_3_.1, bf16[256,1024]{1,0:T(8,128)(2,1)} %copy-done.8, ...), custom_call_target="tpu_custom_call" | custom-call | flops 1073741824 | bytes 3145728 | tf_op jit(solution)/shard_map/pallas_call | solution.py:70
  61.3 0.0 copy-start.12
  61.3 0.0 copy-start.1
  61.3 0.0 collective-permute-done.4.refs_2_
  61.3 1.5 shard_map.88
  62.8 9.6 %all-to-all-start.1 = ((bf16[32,8,1152]{2,1,0:T(8,128)(2,1)}), bf16[32,8,1152]{2,1,0:T(8,128)(2,1)S(1)}, u32[]{:S(2)}, u32[]{:S(2)}) async-start(bf16[32,8,1152]{2,1,0:T(8,128)(2,1)} %bitcast.11), calls=%async_computation.1 | async-start | bytes 1179648 | tf_op jit(solution)/shard_map/all_to_all | solution.py:300
  72.5 0.0 copy-done.12
  72.5 3.2 %collective-permute-start.5 = (bf16[256,1024]{1,0:T(8,128)(2,1)S(1)}, bf16[256,1024]{1,0:T(8,128)(2,1)S(1)}, u32[]{:S(2)}, u32[]{:S(2)}) collective-permute-start(bf16[256,1024]{1,0:T(8,128)(2,1)S(1)} %copy-done.12), channel_id=1, source_target_pairs={{0,2},{2,0},{4,6},{6,4},{8,10},{10,8},{12,14},{14,12},{1,3},{3,1},... | collective-permute-start | bytes 1572872 | tf_op jit(solution)/shard_map/ppermute | solution.py:32
  75.7 11.6 %collective-permute-done.5.refs_2_ = bf16[256,1024]{1,0:T(8,128)(2,1)S(1)} collective-permute-done((bf16[256,1024]{1,0:T(8,128)(2,1)S(1)}, bf16[256,1024]{1,0:T(8,128)(2,1)S(1)}, u32[]{:S(2)}, u32[]{:S(2)}) %collective-permute-start.5) | collective-permute-done | bytes 524320 | tf_op jit(solution)/shard_map/ppermute | solution.py:32
  87.3 0.0 copy-done.1
  87.3 1.4 shard_map.89
  88.7 1.1 all-to-all-done.1.refs_1_
  89.8 3.2 %shard_map.90 = (f32[8,8,1024]{2,1,0:T(8,128)}, f32[8,1024]{1,0:T(8,128)S(1)}) custom-call(s32[4]{0:T(128)S(1)} %pad_add_fusion.refs_0_, bf16[32,8,1152]{2,1,0:T(8,128)(2,1)S(1)} %all-to-all-done.1.refs_1_, f32[8,128]{1,0:T(8,128)S(1)} %get-tuple-element.30.refs_2_, bf16[512,1024]{1,0:T(8,128)(2,1)} %refs_3_.1, bf16[256,1024]{1,0:T(8,128)(2,1)} %copy-done.8, ...), custom_call_target="tpu_custom_call" | custom-call | bytes 3145728 | tf_op jit(solution)/shard_map/pallas_call | solution.py:70
  93.0 0.0 copy-start.6
  93.0 4.6 %all-to-all-start.2 = ((f32[8,8,1024]{2,1,0:T(8,128)}), f32[8,8,1024]{2,1,0:T(8,128)S(1)}, u32[]{:S(2)}, u32[]{:S(2)}) async-start(f32[8,8,1024]{2,1,0:T(8,128)} %get-tuple-element.31), calls=%async_computation.2 | async-start | bytes 524288 | tf_op jit(solution)/shard_map/all_to_all | solution.py:317
  97.6 0.0 copy-done.13
  97.6 3.1 %collective-permute-start.6 = (bf16[128,1024]{1,0:T(8,128)(2,1)S(1)}, bf16[128,1024]{1,0:T(8,128)(2,1)S(1)}, u32[]{:S(2)}, u32[]{:S(2)}) collective-permute-start(bf16[128,1024]{1,0:T(8,128)(2,1)S(1)} %copy-done.13), channel_id=1, source_target_pairs={{0,6},{2,4},{4,2},{6,0},{8,14},{10,12},{12,10},{14,8},{1,7},{3,5},... | collective-permute-start | bytes 786440 | tf_op jit(solution)/shard_map/ppermute | solution.py:32
  100.7 15.4 %collective-permute-done.6.refs_2_ = bf16[128,1024]{1,0:T(8,128)(2,1)S(1)} collective-permute-done((bf16[128,1024]{1,0:T(8,128)(2,1)S(1)}, bf16[128,1024]{1,0:T(8,128)(2,1)S(1)}, u32[]{:S(2)}, u32[]{:S(2)}) %collective-permute-start.6) | collective-permute-done | bytes 262176 | tf_op jit(solution)/shard_map/ppermute | solution.py:32
  116.1 0.0 copy-done.3
  116.1 1.3 shard_map.91
  117.4 0.0 copy-start.14
  117.4 0.0 copy-start.5
  117.4 0.0 all-to-all-done.2.refs_1_
  117.4 1.4 shard_map.92
  118.9 8.3 %all-to-all-start.3 = ((bf16[32,8,1024]{2,1,0:T(8,128)(2,1)}), bf16[32,8,1024]{2,1,0:T(8,128)(2,1)S(1)}, u32[]{:S(2)}, u32[]{:S(2)}) async-start(bf16[32,8,1024]{2,1,0:T(8,128)(2,1)} %shard_map.92), calls=%async_computation.3 | async-start | bytes 1048576 | tf_op jit(solution)/shard_map/all_to_all | solution.py:322
  127.2 0.0 copy-done.14
  127.2 5.2 %collective-permute-start.7 = (bf16[64,1024]{1,0:T(8,128)(2,1)S(1)}, bf16[64,1024]{1,0:T(8,128)(2,1)S(1)}, u32[]{:S(2)}, u32[]{:S(2)}) collective-permute-start(bf16[64,1024]{1,0:T(8,128)(2,1)S(1)} %copy-done.14), channel_id=1, source_target_pairs={{0,14},{2,12},{4,10},{6,8},{8,6},{10,4},{12,2},{14,0},{1,15},{3,13... | collective-permute-start | bytes 393224 | tf_op jit(solution)/shard_map/ppermute | solution.py:32
  132.4 3.8 %collective-permute-done.7.refs_4_ = bf16[64,1024]{1,0:T(8,128)(2,1)S(1)} collective-permute-done((bf16[64,1024]{1,0:T(8,128)(2,1)S(1)}, bf16[64,1024]{1,0:T(8,128)(2,1)S(1)}, u32[]{:S(2)}, u32[]{:S(2)}) %collective-permute-start.7) | collective-permute-done | bytes 131104 | tf_op jit(solution)/shard_map/ppermute | solution.py:32
  136.2 5.3 %all-to-all-done.3 = bf16[32,8,1024]{2,1,0:T(8,128)(2,1)S(1)} async-done(((bf16[32,8,1024]{2,1,0:T(8,128)(2,1)}), bf16[32,8,1024]{2,1,0:T(8,128)(2,1)S(1)}, u32[]{:S(2)}, u32[]{:S(2)}) %all-to-all-start.3) | async-done | bytes 524320 | tf_op jit(solution)/shard_map/all_to_all | solution.py:322
  141.5 0.0 copy-done.6
  141.5 1.3 shard_map.93
  142.9 6.0 %collective-permute-start.8 = (bf16[256,1024]{1,0:T(8,128)(2,1)S(1)}, bf16[256,1024]{1,0:T(8,128)(2,1)S(1)}, u32[]{:S(2)}, u32[]{:S(2)}) collective-permute-start(bf16[256,1024]{1,0:T(8,128)(2,1)S(1)} %get-tuple-element.39.refs_2_), channel_id=1, source_target_pairs={{0,16},{16,0},{1,17},{17,1},{2,18},{18,2},{3,19},{19,3},{4,20},{20... | collective-permute-start | bytes 1572872 | tf_op jit(solution)/shard_map/ppermute | solution.py:32
  148.9 0.0 copy-start.2
  148.9 0.9 copy-done.2
  149.8 1.2 shard_map.94
  151.0 0.0 collective-permute-done.8.refs_2_
  151.0 1.8 %shard_map.95 = (f32[64,512]{1,0:T(8,128)}, bf16[16,1024]{1,0:T(8,128)(2,1)}) custom-call(s32[4]{0:T(128)S(1)} %pad_add_fusion.refs_0_, bf16[64,1024]{1,0:T(8,128)(2,1)S(1)} %copy-done.2, bf16[256,1024]{1,0:T(8,128)(2,1)S(1)} %collective-permute-done.8.refs_2_, bf16[16,512]{1,0:T(8,128)(2,1)S(1)} %get-tuple-element.40.refs_3_, ...), custom_call_target="tpu_custom_call" | custom-call | bytes 1048576 | tf_op jit(solution)/shard_map/pallas_call | solution.py:70
  (10 shorter events, 0.1 us)
Async XLA Ops:
  0.6 13.0 %copy-start = (bf16[768,1024]{1,0:T(8,128)(2,1)S(1)}, bf16[768,1024]{1,0:T(8,128)(2,1)}, u32[]{:S(2)}) copy-start(bf16[768,1024]{1,0:T(8,128)(2,1)} %param.8) | copy-start | bytes 4718596
  0.7 1.0 copy-start.4
  1.7 0.7 copy-start.7
  4.2 9.4 %copy-start.11 = (s32[512]{0:T(512)S(1)}, s32[512]{0:T(512)}, u32[]{:S(2)}) copy-start(s32[512]{0:T(512)} %param.9) | copy-start | bytes 6148
  4.2 41.4 %all-to-all-start = ((bf16[8,80,1024]{2,1,0:T(8,128)(2,1)}), bf16[8,80,1024]{2,1,0:T(8,128)(2,1)S(1)}, u32[]{:S(2)}, u32[]{:S(2)}) async-start(bf16[8,80,1024]{2,1,0:T(8,128)(2,1)} %shard_map.85), calls=%async_computation | async-start | bytes 2621440 | tf_op jit(solution)/shard_map/all_to_all | solution.py:258
  17.7 14.1 %collective-permute-start = (bf16[256,1024]{1,0:T(8,128)(2,1)S(1)}, bf16[256,1024]{1,0:T(8,128)(2,1)S(1)}, u32[]{:S(2)}, u32[]{:S(2)}) collective-permute-start(bf16[256,1024]{1,0:T(8,128)(2,1)S(1)} %pad_maximum_fusion), channel_id=1, source_target_pairs={{0,1},{1,128},{128,129},{129,256},{256,257},{257,384},{384,385},{3... | collective-permute-start | bytes 1572872 | tf_op jit(solution)/shard_map/ppermute | solution.py:27
  21.0 14.9 %collective-permute-start.1 = (bf16[256,1024]{1,0:T(8,128)(2,1)S(1)}, bf16[256,1024]{1,0:T(8,128)(2,1)S(1)}, u32[]{:S(2)}, u32[]{:S(2)}) collective-permute-start(bf16[256,1024]{1,0:T(8,128)(2,1)S(1)} %pad_maximum_fusion.1), channel_id=1, source_target_pairs={{0,385},{1,0},{128,1},{129,128},{256,129},{257,256},{384,257},{385... | collective-permute-start | bytes 1572872 | tf_op jit(solution)/shard_map/ppermute | solution.py:27
  31.8 13.8 %copy-start.8 = (bf16[256,1024]{1,0:T(8,128)(2,1)}, bf16[256,1024]{1,0:T(8,128)(2,1)S(1)}, u32[]{:S(2)}) copy-start(bf16[256,1024]{1,0:T(8,128)(2,1)S(1)} %collective-permute-done.refs_3_.refs_4_) | copy-start | bytes 1572868
  31.8 7.3 %collective-permute-start.2 = (bf16[256,1024]{1,0:T(8,128)(2,1)S(1)}, bf16[256,1024]{1,0:T(8,128)(2,1)S(1)}, u32[]{:S(2)}, u32[]{:S(2)}) collective-permute-start(bf16[256,1024]{1,0:T(8,128)(2,1)S(1)} %collective-permute-done.refs_3_.refs_4_), channel_id=1, source_target_pairs={{0,16},{16,0},{1,17},{17,1},{2,18},{18,2},{3,19},{19,3},{4,20},{20... | collective-permute-start | bytes 1572872 | tf_op jit(solution)/shard_map/ppermute | solution.py:32
  35.9 3.3 %copy-start.9 = (bf16[256,1024]{1,0:T(8,128)(2,1)}, bf16[256,1024]{1,0:T(8,128)(2,1)S(1)}, u32[]{:S(2)}) copy-start(bf16[256,1024]{1,0:T(8,128)(2,1)S(1)} %collective-permute-done.1.refs_4_.refs_5_) | copy-start | bytes 1572868
  35.9 4.9 %collective-permute-start.3 = (bf16[256,1024]{1,0:T(8,128)(2,1)S(1)}, bf16[256,1024]{1,0:T(8,128)(2,1)}, u32[]{:S(2)}, u32[]{:S(2)}) collective-permute-start(bf16[256,1024]{1,0:T(8,128)(2,1)S(1)} %collective-permute-done.1.refs_4_.refs_5_), channel_id=1, source_target_pairs={{0,16},{16,0},{1,17},{17,1},{2,18},{18,2},{3,19},{19,3},{4,20},{20... | collective-permute-start | bytes 1572872 | tf_op jit(solution)/shard_map/ppermute | solution.py:32
  39.1 0.8 copy-start.10
  52.9 8.4 %collective-permute-start.4 = (bf16[256,1152]{1,0:T(8,128)(2,1)S(1)}, bf16[256,1152]{1,0:T(8,128)(2,1)S(1)}, u32[]{:S(2)}, u32[]{:S(2)}) collective-permute-start(bf16[256,1152]{1,0:T(8,128)(2,1)S(1)} %get-tuple-element.25), channel_id=1, source_target_pairs={{0,16},{16,0},{1,17},{17,1},{2,18},{18,2},{3,19},{19,3},{4,20},{20... | collective-permute-start | bytes 1769480 | tf_op jit(solution)/shard_map/ppermute | solution.py:32
  61.3 11.2 %copy-start.12 = (bf16[256,1024]{1,0:T(8,128)(2,1)S(1)}, bf16[256,1024]{1,0:T(8,128)(2,1)}, u32[]{:S(2)}) copy-start(bf16[256,1024]{1,0:T(8,128)(2,1)} %get-tuple-element.29) | copy-start | bytes 1572868
  61.3 26.0 %copy-start.1 = (bf16[256,1024]{1,0:T(8,128)(2,1)S(1)}, bf16[256,1024]{1,0:T(8,128)(2,1)}, u32[]{:S(2)}) copy-start(bf16[256,1024]{1,0:T(8,128)(2,1)} %get-tuple-element.28.refs_1_) | copy-start | bytes 1572868
  62.8 27.0 %all-to-all-start.1 = ((bf16[32,8,1152]{2,1,0:T(8,128)(2,1)}), bf16[32,8,1152]{2,1,0:T(8,128)(2,1)S(1)}, u32[]{:S(2)}, u32[]{:S(2)}) async-start(bf16[32,8,1152]{2,1,0:T(8,128)(2,1)} %bitcast.11), calls=%async_computation.1 | async-start | bytes 1179648 | tf_op jit(solution)/shard_map/all_to_all | solution.py:300
  72.5 14.8 %collective-permute-start.5 = (bf16[256,1024]{1,0:T(8,128)(2,1)S(1)}, bf16[256,1024]{1,0:T(8,128)(2,1)S(1)}, u32[]{:S(2)}, u32[]{:S(2)}) collective-permute-start(bf16[256,1024]{1,0:T(8,128)(2,1)S(1)} %copy-done.12), channel_id=1, source_target_pairs={{0,2},{2,0},{4,6},{6,4},{8,10},{10,8},{12,14},{14,12},{1,3},{3,1},... | collective-permute-start | bytes 1572872 | tf_op jit(solution)/shard_map/ppermute | solution.py:32
  89.8 7.8 %copy-start.13 = (bf16[128,1024]{1,0:T(8,128)(2,1)S(1)}, bf16[128,1024]{1,0:T(8,128)(2,1)}, u32[]{:S(2)}) copy-start(bf16[128,1024]{1,0:T(8,128)(2,1)} %get-tuple-element.34) | copy-start | bytes 786436
  89.8 26.3 %copy-start.3 = (bf16[128,1024]{1,0:T(8,128)(2,1)S(1)}, bf16[128,1024]{1,0:T(8,128)(2,1)}, u32[]{:S(2)}) copy-start(bf16[128,1024]{1,0:T(8,128)(2,1)} %get-tuple-element.33.refs_1_) | copy-start | bytes 786436
  93.0 48.5 %copy-start.6 = (s32[512]{0:T(512)S(1)}, s32[512]{0:T(512)}, u32[]{:S(2)}) copy-start(s32[512]{0:T(512)} %param.11) | copy-start | bytes 6148
  93.0 24.4 %all-to-all-start.2 = ((f32[8,8,1024]{2,1,0:T(8,128)}), f32[8,8,1024]{2,1,0:T(8,128)S(1)}, u32[]{:S(2)}, u32[]{:S(2)}) async-start(f32[8,8,1024]{2,1,0:T(8,128)} %get-tuple-element.31), calls=%async_computation.2 | async-start | bytes 524288 | tf_op jit(solution)/shard_map/all_to_all | solution.py:317
  97.6 18.5 %collective-permute-start.6 = (bf16[128,1024]{1,0:T(8,128)(2,1)S(1)}, bf16[128,1024]{1,0:T(8,128)(2,1)S(1)}, u32[]{:S(2)}, u32[]{:S(2)}) collective-permute-start(bf16[128,1024]{1,0:T(8,128)(2,1)S(1)} %copy-done.13), channel_id=1, source_target_pairs={{0,6},{2,4},{4,2},{6,0},{8,14},{10,12},{12,10},{14,8},{1,7},{3,5},... | collective-permute-start | bytes 786440 | tf_op jit(solution)/shard_map/ppermute | solution.py:32
  117.4 9.8 %copy-start.14 = (bf16[64,1024]{1,0:T(8,128)(2,1)S(1)}, bf16[64,1024]{1,0:T(8,128)(2,1)}, u32[]{:S(2)}) copy-start(bf16[64,1024]{1,0:T(8,128)(2,1)} %get-tuple-element.37) | copy-start | bytes 393220
  117.4 24.1 %copy-start.5 = (bf16[64,1024]{1,0:T(8,128)(2,1)S(1)}, bf16[64,1024]{1,0:T(8,128)(2,1)}, u32[]{:S(2)}) copy-start(bf16[64,1024]{1,0:T(8,128)(2,1)} %get-tuple-element.36.refs_3_) | copy-start | bytes 393220
  118.9 22.7 %all-to-all-start.3 = ((bf16[32,8,1024]{2,1,0:T(8,128)(2,1)}), bf16[32,8,1024]{2,1,0:T(8,128)(2,1)S(1)}, u32[]{:S(2)}, u32[]{:S(2)}) async-start(bf16[32,8,1024]{2,1,0:T(8,128)(2,1)} %shard_map.92), calls=%async_computation.3 | async-start | bytes 1048576 | tf_op jit(solution)/shard_map/all_to_all | solution.py:322
  127.2 9.0 %collective-permute-start.7 = (bf16[64,1024]{1,0:T(8,128)(2,1)S(1)}, bf16[64,1024]{1,0:T(8,128)(2,1)S(1)}, u32[]{:S(2)}, u32[]{:S(2)}) collective-permute-start(bf16[64,1024]{1,0:T(8,128)(2,1)S(1)} %copy-done.14), channel_id=1, source_target_pairs={{0,14},{2,12},{4,10},{6,8},{8,6},{10,4},{12,2},{14,0},{1,15},{3,13... | collective-permute-start | bytes 393224 | tf_op jit(solution)/shard_map/ppermute | solution.py:32
  142.9 8.1 %collective-permute-start.8 = (bf16[256,1024]{1,0:T(8,128)(2,1)S(1)}, bf16[256,1024]{1,0:T(8,128)(2,1)S(1)}, u32[]{:S(2)}, u32[]{:S(2)}) collective-permute-start(bf16[256,1024]{1,0:T(8,128)(2,1)S(1)} %get-tuple-element.39.refs_2_), channel_id=1, source_target_pairs={{0,16},{16,0},{1,17},{17,1},{2,18},{18,2},{3,19},{19,3},{4,20},{20... | collective-permute-start | bytes 1572872 | tf_op jit(solution)/shard_map/ppermute | solution.py:32
  148.9 0.9 copy-start.2

commit v6 on v5

--- a/solution.py
+++ b/solution.py
@@ -14,7 +14,7 @@
 i32 = jnp.int32
 ALL = ("yh", "x", "c", "z", "yl")
 PLANE = ("yh", "x", "yl")
-PACK = 16
+PACK = 8
 LEAVE = (1, 6, 2, 5)
 STAY = (0, 7, 3, 4)
 DIGIT = 128
@@ -36,7 +36,7 @@
     return lax.dot_general(a, b, (((1,), (1,)), ((), ())), preferred_element_type=f32)
 
 
-def call(kernel, out, ins, held=0, scratch=(), away=(), flops=0, nbytes=0):
+def call(kernel, out, ins, held=0, scratch=(), away=(), pinned=(), flops=0, nbytes=0):
     spec = pl.BlockSpec(memory_space=pltpu.VMEM)
     far = pl.BlockSpec(memory_space=pltpu.HBM)
     scratch, many = list(scratch), len(out)
@@ -59,7 +59,10 @@
 
     made = pl.pallas_call(
         run,
-        out_shape=tuple(pltpu.HBM(o.shape, o.dtype) if i in away else o for i, o in enumerate(out)),
+        out_shape=tuple(
+            pltpu.HBM(o.shape, o.dtype) if i in away else pltpu.VMEM(o.shape, o.dtype) if i in pinned else o
+            for i, o in enumerate(out)
+        ),
         in_specs=[pl.BlockSpec(memory_space=pltpu.SMEM)] + [spec] * (ins - 1 - held) + [far] * held,
         out_specs=tuple(far if i in away else spec for i in range(many)),
         scratch_shapes=scratch,
@@ -90,11 +93,8 @@
 
 
 def row_squares(matrix):
-    square = jnp.square(matrix.astype(f32))
-    high = square.astype(bf16)
-    low = (square - high.astype(f32)).astype(bf16)
-    ones = jnp.ones((8, matrix.shape[1]), bf16)
-    return across(ones, high) + across(ones, low)
+    column = jnp.sum(jnp.square(matrix.astype(f32)), axis=1, keepdims=True)
+    return jnp.broadcast_to(column, (matrix.shape[0], 128)).T[0:1]
 
 
 def pack_kernel(place, points, members, out):
@@ -110,8 +110,13 @@
         out[i, rows:, :] = tail
 
 
-def affinity_kernel(rows, place, spread, own, up, down, up_o, down_o, kernel, keep, send, table, anchors, sems):
+def affinity_kernel(
+    rows, place, came, own, up, down, up_o, down_o, kernel, keep, send, table, spread, arrival, anchors, sems
+):
+    first = pltpu.make_async_copy(came, spread, arrival)
+    first.start()
     copies = fetch(place, own, (up, down, up_o, down_o), 0, anchors, sems)
+    first.wait()
     core = place[0]
     ring, _, width = spread.shape
     half = keep.shape[0]
@@ -138,7 +143,7 @@
     for at in range(0, count, tile):
         values = spread[:, :rows, :].reshape(points, width)
         marks = anchors[pl.ds(at, tile), :]
-        factor = lax.rsqrt(row_squares(marks) + epsilon)[0:1]
+        factor = lax.rsqrt(row_squares(marks) + epsilon)
         part = jnp.exp(across(values, marks) * length * factor).astype(bf16)
         kernel[:, pl.ds(at, tile)] = part
         sums = jnp.dot(table[...], part, preferred_element_type=f32).astype(bf16)
@@ -152,16 +157,22 @@
     return jnp.dot(span, maps[:, pl.ds(at, tile)], preferred_element_type=f32)
 
 
-def project_kernel(kernel_rows, place, kernel, white, up, down, up_o, down_o, leave, stay, token, maps, sems):
+def leave_kernel(rows, place, kernel, white, up, down, up_o, down_o, leave, token, maps, sems):
     copies = fetch(place, white, (up, down, up_o, down_o), 1, maps, sems)
     for copy in copies:
         copy.wait()
     token[...] = jnp.zeros_like(token)
-    width = leave.shape[1]
-    tile = min(256, width)
-    for at in range(0, width, tile):
-        for out, owners in ((leave, LEAVE), (stay, STAY)):
-            out[:, at : at + tile] = project(place, kernel, maps, owners, kernel_rows, at, tile).astype(bf16)
+    tile = min(256, leave.shape[1])
+    for at in range(0, leave.shape[1], tile):
+        leave[:, at : at + tile] = project(place, kernel, maps, LEAVE, rows, at, tile).astype(bf16)
+
+
+def stay_kernel(rows, place, kernel, white, up, down, up_o, down_o, stay, maps, sems):
+    for copy in fetch(place, white, (up, down, up_o, down_o), 1, maps, sems):
+        copy.wait()
+    tile = min(256, stay.shape[1])
+    for at in range(0, stay.shape[1], tile):
+        stay[:, at : at + tile] = project(place, kernel, maps, STAY, rows, at, tile).astype(bf16)
 
 
 def merge_kernel(place, kept, arrived, keep, send, token):
@@ -172,9 +183,7 @@
     token[...] = jnp.zeros_like(token)
 
 
-def cluster_kernel(place, spread, *rest):
-    white, up, down, up_o, down_o = rest[-9:-4]
-    mapped, number, maps, sems = rest[-4:]
+def cluster_kernel(place, spread, _, white, up, down, up_o, down_o, mapped, number, maps, sems):
     copies = fetch(place, white, (up, down, up_o, down_o), 1, maps, sems)
     count = maps.shape[0]
     share = spread.shape[1]
@@ -200,9 +209,10 @@
 
 
 def feature_kernel(place, owners, *rest):
-    arrived, kept, last, features, choose, means = rest
-    means[...] = arrived[...]
-    features[...] = (kept[...].astype(f32) + last[...].astype(f32)).astype(bf16)
+    kept, last, features, again, choose = rest
+    both = (kept[...].astype(f32) + last[...].astype(f32)).astype(bf16)
+    features[...] = both
+    again[...] = both
     slots, clusters = choose.shape
     owned = owners[...] == place[2]
     row = lax.broadcasted_iota(i32, (clusters, clusters), 0)
@@ -214,9 +224,13 @@
     choose[...] = jnp.where(rank == slot, mark, 0.0).astype(bf16)
 
 
+def after_kernel(place, means, _, same):
+    same[...] = means[...]
+
+
 def half_scores(features, means, choose, at):
     half = means.shape[0]
-    norms = row_squares(means[...])[0:1]
+    norms = row_squares(means[...])
     scores = (norms - 2.0 * across(features[...], means[...])) * (1.0 / means.shape[1])
     owned = jnp.dot(choose[:, pl.ds(at, half)], means[...], preferred_element_type=f32)
     return scores, owned
@@ -252,7 +266,7 @@
     array = jax.ShapeDtypeStruct
     place = jnp.stack([core, lax.axis_index("yl"), lax.axis_index(("yh", "x", "c")), lax.axis_index("z")]).astype(i32)
 
-    (block,) = call(pack_kernel, (array((ring, rows + PACK, width), bf16),), 3, away=(0,), nbytes=2 * MIB)(
+    (block,) = call(pack_kernel, (array((ring, rows + PACK, width), bf16),), 3, 0, away=(0,), nbytes=2 * MIB)(
         place, points, membership.reshape(1, rows)
     )
     spread = lax.all_to_all(block, "z", 0, 0)
@@ -277,8 +291,13 @@
             array((half, 2 * count + TALLY), bf16),
         ),
         7,
-        5,
-        [pltpu.VMEM((clusters, ring * rows), bf16)] + store(2 * count, width),
+        6,
+        [
+            pltpu.VMEM((clusters, ring * rows), bf16),
+            pltpu.VMEM(spread.shape, bf16),
+            pltpu.SemaphoreType.DMA,
+            *store(2 * count, width),
+        ],
         flops=2 * ring * rows * 2 * count * (width + clusters),
         nbytes=6 * MIB,
     )(place, spread, landmarks, *pieces)
@@ -286,14 +305,14 @@
     theirs = flip(send, "c", 1)
     token = array((8, 128), f32)
 
-    leave, stay, done = call(
-        functools.partial(project_kernel, rows),
-        (array((ring // 2 * rows, rank_width), bf16), array((ring // 2 * rows, rank_width), bf16), token),
+    leave, done = call(
+        functools.partial(leave_kernel, rows),
+        (array((ring // 2 * rows, rank_width), bf16), token),
         7,
         5,
         store(2 * count, rank_width),
-        away=(0, 1),
-        flops=2 * ring * rows * 2 * count * rank_width,
+        away=(0,),
+        flops=ring * rows * 2 * count * rank_width,
         nbytes=3 * MIB,
     )(place, kernel, whitening, *pieces)
     (paired,) = call(pair_kernel, (array(keep.shape, bf16),), 4, away=(0,), nbytes=2 * MIB)(place, keep, theirs, done)
@@ -304,6 +323,15 @@
         arrived = flip(leave, "z", partner)
         return call(merge_kernel, (size, size, token), 3, away=(0, 1), nbytes=MIB)(place, kept, arrived)
 
+    (stay,) = call(
+        functools.partial(stay_kernel, rows),
+        (array((ring // 2 * rows, rank_width), bf16),),
+        7,
+        5,
+        store(2 * count, rank_width),
+        flops=ring * rows * 2 * count * rank_width,
+        nbytes=3 * MIB,
+    )(place, kernel, whitening, *pieces)
     kept, leave, done = merge(stay, leave, 1)
     mapped, number = call(
         cluster_kernel,
@@ -321,23 +349,25 @@
     )
     mine = lax.all_to_all(sent, PLANE, 0, 0).reshape(half, rank_width)
     last = flip(leave, "z", 7)
-    features, choose, mine = call(
+    features, again, choose = call(
         feature_kernel,
         (
             array((rows, rank_width), bf16),
+            array((rows, rank_width), bf16),
             array((clusters // groups, clusters), bf16),
-            array((half, rank_width), bf16),
         ),
-        5,
+        4,
+        pinned=(1,),
         nbytes=2 * MIB,
-    )(place, owner_map.reshape(1, clusters), mine, kept, last)
+    )(place, owner_map.reshape(1, clusters), kept, last)
+    (mine,) = call(after_kernel, (array(mine.shape, bf16),), 3, nbytes=MIB)(place, mine, choose)
     other = flip(mine, "c", 1)
     near_scores, near_owned = call(
         near_kernel, (array((rows, half), f32), array((clusters // groups, rank_width), f32)), 4, nbytes=MIB
-    )(place, features, mine, choose)
+    )(place, again, mine, choose)
     scores, owned = call(
         far_kernel, (array((rows, clusters), f32), array((clusters // groups, rank_width), bf16)), 6, nbytes=MIB
-    )(place, features, other, choose, near_scores, near_owned)
+    )(place, again, other, choose, near_scores, near_owned)
     return (features, owned, scores)
 
 

time: 154 us -> 147 us (0.955)
  waiting for transfers between devices: 51.6 us -> 45.9 us
  local copies, waits for them, and re-layouts: 7.44 us -> 5.68 us
    all_to_all x1, waiting for transfers between devices: 4.83 us -> 1.76 us  [body(): spread = lax.all_to_all(block, 'z', 0, 0)]
    unnamed x30 -> x26, local copies, waits for them, and re-layouts: 3.4 us -> 1.72 us
    pallas_call x11 -> x13, Pallas kernels: 26.6 us -> 27.2 us  [call(): made(*args[:near], *(pltpu.with_memory_space_constraint(a, pltpu.HBM) for...]
  transfers between devices with their start and end apart: 13 -> 13, of which waited for: 8 -> 9; matrix products, arithmetic and copies ran while one was open for 3% -> 3% of each run, Pallas kernels for 5% -> 8%
where the time goes in v6:
time: 147 us; the launch traced here: 146 us
  starting transfers between devices  66.5 us (45%)
  waiting for transfers between devices  45.9 us (31%)
  Pallas kernels  27.2 us (19%)
  local copies, waits for them, and re-layouts  5.68 us (4%)
    ppermute x7, waiting for transfers between devices, flip(): return lax.ppermute(value, axis, [(i, i ^ bit) for i in range(size)])  30.4 us
    ppermute x7, starting transfers between devices, flip(): return lax.ppermute(value, axis, [(i, i ^ bit) for i in range(size)])  29.1 us
    pallas_call x13, Pallas kernels, call(): made(*args[:near], *(pltpu.with_memory_space_constraint(a, pltpu.HBM) for...  27.2 us
    all_to_all x1, starting transfers between devices, body(): gathered = lax.all_to_all(paired.reshape(peers, share, -1), PLANE, 0, 0)  9.62 us
    all_to_all x1, starting transfers between devices, body(): spread = lax.all_to_all(block, 'z', 0, 0)  9.42 us
    ppermute x2, waiting for transfers between devices, hop(): lax.ppermute(value, axis, [(i, (i + by) % size) for i in range(size)])  8.84 us
    all_to_all x1, starting transfers between devices, body(): mine = lax.all_to_all(sent, PLANE, 0, 0).reshape(half, rank_width)  8.57 us
    ppermute x2, starting transfers between devices, hop(): lax.ppermute(value, axis, [(i, (i + by) % size) for i in range(size)])  5.28 us
  transfers between devices with their start and end apart: 13, of which 9 were waited for; matrix products, arithmetic and copies ran while one was open for 3% of the time, Pallas kernels for 8%

profile of v6, /device:TPU:73, one launch (start us, length us, event | category | flops | bytes accessed | tf_op | source)
XLA Modules:
  0.0 146.5 jit_solution(1595651888918977124)
XLA Ops:
  0.6 0.0 copy-start
  0.7 0.1 pad_add_fusion.refs_0_
  0.7 0.0 copy-start.2
  0.7 1.0 copy-done.2
  1.7 0.0 copy-start.5
  1.7 0.7 copy-done.5
  2.4 1.7 %shard_map.85 = bf16[8,72,1024]{2,1,0:T(8,128)(2,1)} custom-call(s32[4]{0:T(128)S(1)} %pad_add_fusion.refs_0_, bf16[64,1024]{1,0:T(8,128)(2,1)S(1)} %copy-done.2, s32[1,64]{1,0:T(1,128)S(1)} %bitcast.10), custom_call_target="tpu_custom_call" | custom-call | bytes 2097152 | tf_op jit(solution)/shard_map/pallas_call | solution.py:73
  4.1 9.4 %all-to-all-start = ((bf16[8,72,1024]{2,1,0:T(8,128)(2,1)}), bf16[8,72,1024]{2,1,0:T(8,128)(2,1)}, u32[]{:S(2)}, u32[]{:S(2)}) async-start(bf16[8,72,1024]{2,1,0:T(8,128)(2,1)} %shard_map.85), calls=%async_computation | async-start | bytes 2359296 | tf_op jit(solution)/shard_map/all_to_all | solution.py:272
  13.5 0.0 copy-done.10
  13.5 0.0 copy-done
  13.6 0.0 copy-start.6
  13.6 2.8 %gather_fusion = bf16[512,1024]{1,0:T(8,128)(2,1)} fusion(bf16[768,1024]{1,0:T(8,128)(2,1)S(1)} %copy-done, s32[1024]{0:T(1024)S(1)} %pad_clamp_fusion), kind=kCustom, calls=%fused_computation | custom fusion | bytes 2099200 | tf_op jit(solution)/shard_map/gather | solution.py:274
  16.3 0.0 copy-done.6
  16.3 1.2 constant_dynamic-slice_fusion
  17.6 3.2 %collective-permute-start = (bf16[256,1024]{1,0:T(8,128)(2,1)S(1)}, bf16[256,1024]{1,0:T(8,128)(2,1)S(1)}, u32[]{:S(2)}, u32[]{:S(2)}) collective-permute-start(bf16[256,1024]{1,0:T(8,128)(2,1)S(1)} %pad_maximum_fusion), channel_id=1, source_target_pairs={{0,1},{1,128},{128,129},{129,256},{256,257},{257,384},{384,385},{3... | collective-permute-start | bytes 1572872 | tf_op jit(solution)/shard_map/ppermute | solution.py:27
  20.8 2.1 %collective-permute-start.1 = (bf16[256,1024]{1,0:T(8,128)(2,1)S(1)}, bf16[256,1024]{1,0:T(8,128)(2,1)S(1)}, u32[]{:S(2)}, u32[]{:S(2)}) collective-permute-start(bf16[256,1024]{1,0:T(8,128)(2,1)S(1)} %pad_maximum_fusion.1), channel_id=1, source_target_pairs={{0,385},{1,0},{128,1},{129,128},{256,129},{257,256},{384,257},{385... | collective-permute-start | bytes 1572872 | tf_op jit(solution)/shard_map/ppermute | solution.py:27
  22.9 8.8 %collective-permute-done.refs_3_.refs_4_ = bf16[256,1024]{1,0:T(8,128)(2,1)S(1)} collective-permute-done((bf16[256,1024]{1,0:T(8,128)(2,1)S(1)}, bf16[256,1024]{1,0:T(8,128)(2,1)S(1)}, u32[]{:S(2)}, u32[]{:S(2)}) %collective-permute-start) | collective-permute-done | bytes 524320 | tf_op jit(solution)/shard_map/ppermute | solution.py:27
  31.8 4.0 %collective-permute-start.2 = (bf16[256,1024]{1,0:T(8,128)(2,1)S(1)}, bf16[256,1024]{1,0:T(8,128)(2,1)S(1)}, u32[]{:S(2)}, u32[]{:S(2)}) collective-permute-start(bf16[256,1024]{1,0:T(8,128)(2,1)S(1)} %collective-permute-done.refs_3_.refs_4_), channel_id=1, source_target_pairs={{0,16},{16,0},{1,17},{17,1},{2,18},{18,2},{3,19},{19,3},{4,20},{20... | collective-permute-start | bytes 1572872 | tf_op jit(solution)/shard_map/ppermute | solution.py:32
  35.7 0.0 collective-permute-done.1.refs_4_.refs_5_
  35.7 0.0 copy-start.8
  35.8 3.2 %collective-permute-start.3 = (bf16[256,1024]{1,0:T(8,128)(2,1)S(1)}, bf16[256,1024]{1,0:T(8,128)(2,1)}, u32[]{:S(2)}, u32[]{:S(2)}) collective-permute-start(bf16[256,1024]{1,0:T(8,128)(2,1)S(1)} %collective-permute-done.1.refs_4_.refs_5_), channel_id=1, source_target_pairs={{0,16},{16,0},{1,17},{17,1},{2,18},{18,2},{3,19},{19,3},{4,20},{20... | collective-permute-start | bytes 1572872 | tf_op jit(solution)/shard_map/ppermute | solution.py:32
  39.0 0.0 collective-permute-done.2.refs_5_.refs_6_
  39.0 0.0 copy-start.9
  39.0 1.6 %collective-permute-done.3.refs_6_.refs_7_ = bf16[256,1024]{1,0:T(8,128)(2,1)} collective-permute-done((bf16[256,1024]{1,0:T(8,128)(2,1)S(1)}, bf16[256,1024]{1,0:T(8,128)(2,1)}, u32[]{:S(2)}, u32[]{:S(2)}) %collective-permute-start.3) | collective-permute-done | bytes 524320 | tf_op jit(solution)/shard_map/ppermute | solution.py:32
  40.6 0.0 copy-done.7
  40.6 0.0 copy-done.8
  40.6 0.0 copy-done.9
  40.6 1.8 %all-to-all-done.refs_1_ = bf16[8,72,1024]{2,1,0:T(8,128)(2,1)} async-done(((bf16[8,72,1024]{2,1,0:T(8,128)(2,1)}), bf16[8,72,1024]{2,1,0:T(8,128)(2,1)}, u32[]{:S(2)}, u32[]{:S(2)}) %all-to-all-start) | async-done | bytes 1179680 | tf_op jit(solution)/shard_map/all_to_all | solution.py:272
  42.4 5.8 %shard_map.86 = (bf16[512,1024]{1,0:T(8,128)(2,1)S(1)}, bf16[256,1152]{1,0:T(8,128)(2,1)S(1)}, bf16[256,1152]{1,0:T(8,128)(2,1)S(1)}) custom-call(s32[4]{0:T(128)S(1)} %pad_add_fusion.refs_0_, bf16[8,72,1024]{2,1,0:T(8,128)(2,1)} %all-to-all-done.refs_1_, bf16[512,1024]{1,0:T(8,128)(2,1)} %gather_fusion, bf16[256,1024]{1,0:T(8,128)(2,1)} %copy-done.7, ...), custom_call_target="tpu_custom_call" | custom-call | flops 1610612736 | bytes 6291456 | tf_op jit(solution)/shard_map/pallas_call | solution.py:73
  48.2 4.5 %collective-permute-start.7 = (bf16[256,1152]{1,0:T(8,128)(2,1)S(1)}, bf16[256,1152]{1,0:T(8,128)(2,1)S(1)}, u32[]{:S(2)}, u32[]{:S(2)}) collective-permute-start(bf16[256,1152]{1,0:T(8,128)(2,1)S(1)} %get-tuple-element.32), channel_id=1, source_target_pairs={{0,16},{16,0},{1,17},{17,1},{2,18},{18,2},{3,19},{19,3},{4,20},{20... | collective-permute-start | bytes 1769480 | tf_op jit(solution)/shard_map/ppermute | solution.py:32
  52.7 3.7 %shard_map.88 = (bf16[256,1024]{1,0:T(8,128)(2,1)}, f32[8,128]{1,0:T(8,128)S(1)}) custom-call(s32[4]{0:T(128)S(1)} %pad_add_fusion.refs_0_, bf16[512,1024]{1,0:T(8,128)(2,1)S(1)} %get-tuple-element.23.refs_1_, bf16[512,1024]{1,0:T(8,128)(2,1)} %refs_3_.1, bf16[256,1024]{1,0:T(8,128)(2,1)} %copy-done.7, bf16[256,1024]{1,0:T(8,128)(2,1)} %copy-done.8, ...), custom_call_target="tpu_custom_call" | custom-call | flops 536870912 | bytes 3145728 | tf_op jit(solution)/shard_map/pallas_call | solution.py:73
  56.4 0.0 collective-permute-done.7.refs_2_
  56.4 1.5 %shard_map.92 = bf16[256,1152]{1,0:T(8,128)(2,1)} custom-call(s32[4]{0:T(128)S(1)} %pad_add_fusion.refs_0_, bf16[256,1152]{1,0:T(8,128)(2,1)S(1)} %get-tuple-element.31.refs_1_, bf16[256,1152]{1,0:T(8,128)(2,1)S(1)} %collective-permute-done.7.refs_2_, f32[8,128]{1,0:T(8,128)S(1)} %get-tuple-element.33.refs_3_), custom_call_target="tpu_custom_call" | custom-call | bytes 2097152 | tf_op jit(solution)/shard_map/pallas_call | solution.py:73
  57.9 9.6 %all-to-all-start.1 = ((bf16[32,8,1152]{2,1,0:T(8,128)(2,1)}), bf16[32,8,1152]{2,1,0:T(8,128)(2,1)S(1)}, u32[]{:S(2)}, u32[]{:S(2)}) async-start(bf16[32,8,1152]{2,1,0:T(8,128)(2,1)} %bitcast.11), calls=%async_computation.1 | async-start | bytes 1179648 | tf_op jit(solution)/shard_map/all_to_all | solution.py:319
  67.5 3.1 %collective-permute-start.4 = (bf16[256,1024]{1,0:T(8,128)(2,1)}, bf16[256,1024]{1,0:T(8,128)(2,1)S(1)}, u32[]{:S(2)}, u32[]{:S(2)}) collective-permute-start(bf16[256,1024]{1,0:T(8,128)(2,1)} %get-tuple-element.24), channel_id=1, source_target_pairs={{0,2},{2,0},{4,6},{6,4},{8,10},{10,8},{12,14},{14,12},{1,3},{3,1},... | collective-permute-start | bytes 1572872 | tf_op jit(solution)/shard_map/ppermute | solution.py:32
  70.6 2.8 %shard_map.87.refs_1_ = bf16[256,1024]{1,0:T(8,128)(2,1)S(1)} custom-call(s32[4]{0:T(128)S(1)} %pad_add_fusion.refs_0_, bf16[512,1024]{1,0:T(8,128)(2,1)S(1)} %get-tuple-element.23.refs_1_, bf16[512,1024]{1,0:T(8,128)(2,1)} %refs_3_.1, bf16[256,1024]{1,0:T(8,128)(2,1)} %copy-done.7, bf16[256,1024]{1,0:T(8,128)(2,1)} %copy-done.8, ...), custom_call_target="tpu_custom_call" | custom-call | flops 536870912 | bytes 3145728 | tf_op jit(solution)/shard_map/pallas_call | solution.py:73
  73.5 9.0 %collective-permute-done.4.refs_2_ = bf16[256,1024]{1,0:T(8,128)(2,1)S(1)} collective-permute-done((bf16[256,1024]{1,0:T(8,128)(2,1)}, bf16[256,1024]{1,0:T(8,128)(2,1)S(1)}, u32[]{:S(2)}, u32[]{:S(2)}) %collective-permute-start.4) | collective-permute-done | bytes 524320 | tf_op jit(solution)/shard_map/ppermute | solution.py:32
  82.5 1.5 shard_map.89
  84.0 0.9 all-to-all-done.1.refs_1_
  84.9 3.2 %shard_map.93 = (f32[8,8,1024]{2,1,0:T(8,128)}, f32[8,1024]{1,0:T(8,128)S(1)}) custom-call(s32[4]{0:T(128)S(1)} %pad_add_fusion.refs_0_, bf16[32,8,1152]{2,1,0:T(8,128)(2,1)S(1)} %all-to-all-done.1.refs_1_, f32[8,128]{1,0:T(8,128)S(1)} %get-tuple-element.34.refs_2_, bf16[512,1024]{1,0:T(8,128)(2,1)} %refs_3_.1, bf16[256,1024]{1,0:T(8,128)(2,1)} %copy-done.7, ...), custom_call_target="tpu_custom_call" | custom-call | bytes 3145728 | tf_op jit(solution)/shard_map/pallas_call | solution.py:73
  88.1 0.0 copy-start.4
  88.1 4.5 %all-to-all-start.2 = ((f32[8,8,1024]{2,1,0:T(8,128)}), f32[8,8,1024]{2,1,0:T(8,128)S(1)}, u32[]{:S(2)}, u32[]{:S(2)}) async-start(f32[8,8,1024]{2,1,0:T(8,128)} %get-tuple-element.35), calls=%async_computation.2 | async-start | bytes 524288 | tf_op jit(solution)/shard_map/all_to_all | solution.py:345
  92.6 0.0 copy-done.11
  92.6 3.1 %collective-permute-start.5 = (bf16[128,1024]{1,0:T(8,128)(2,1)S(1)}, bf16[128,1024]{1,0:T(8,128)(2,1)S(1)}, u32[]{:S(2)}, u32[]{:S(2)}) collective-permute-start(bf16[128,1024]{1,0:T(8,128)(2,1)S(1)} %copy-done.11), channel_id=1, source_target_pairs={{0,6},{2,4},{4,2},{6,0},{8,14},{10,12},{12,10},{14,8},{1,7},{3,5},... | collective-permute-start | bytes 786440 | tf_op jit(solution)/shard_map/ppermute | solution.py:32
  95.7 15.4 %collective-permute-done.5.refs_2_ = bf16[128,1024]{1,0:T(8,128)(2,1)S(1)} collective-permute-done((bf16[128,1024]{1,0:T(8,128)(2,1)S(1)}, bf16[128,1024]{1,0:T(8,128)(2,1)S(1)}, u32[]{:S(2)}, u32[]{:S(2)}) %collective-permute-start.5) | collective-permute-done | bytes 262176 | tf_op jit(solution)/shard_map/ppermute | solution.py:32
  111.1 0.0 copy-done.1
  111.1 1.3 shard_map.90
  112.4 0.0 copy-start.12
  112.4 0.0 copy-start.3
  112.4 0.0 all-to-all-done.2.refs_1_
  112.4 1.4 shard_map.94
  113.9 8.6 %all-to-all-start.3 = ((bf16[32,8,1024]{2,1,0:T(8,128)(2,1)}), bf16[32,8,1024]{2,1,0:T(8,128)(2,1)S(1)}, u32[]{:S(2)}, u32[]{:S(2)}) async-start(bf16[32,8,1024]{2,1,0:T(8,128)(2,1)} %shard_map.94), calls=%async_computation.3 | async-start | bytes 1048576 | tf_op jit(solution)/shard_map/all_to_all | solution.py:350
  122.4 0.0 copy-done.12
  122.4 5.2 %collective-permute-start.6 = (bf16[64,1024]{1,0:T(8,128)(2,1)S(1)}, bf16[64,1024]{1,0:T(8,128)(2,1)S(1)}, u32[]{:S(2)}, u32[]{:S(2)}) collective-permute-start(bf16[64,1024]{1,0:T(8,128)(2,1)S(1)} %copy-done.12), channel_id=1, source_target_pairs={{0,14},{2,12},{4,10},{6,8},{8,6},{10,4},{12,2},{14,0},{1,15},{3,13... | collective-permute-start | bytes 393224 | tf_op jit(solution)/shard_map/ppermute | solution.py:32
  127.6 3.8 %collective-permute-done.6.refs_3_ = bf16[64,1024]{1,0:T(8,128)(2,1)S(1)} collective-permute-done((bf16[64,1024]{1,0:T(8,128)(2,1)S(1)}, bf16[64,1024]{1,0:T(8,128)(2,1)S(1)}, u32[]{:S(2)}, u32[]{:S(2)}) %collective-permute-start.6) | collective-permute-done | bytes 131104 | tf_op jit(solution)/shard_map/ppermute | solution.py:32
  131.5 0.0 copy-done.4
  131.5 0.0 copy-done.3
  131.5 1.3 shard_map.91
  132.8 4.0 %all-to-all-done.3 = bf16[32,8,1024]{2,1,0:T(8,128)(2,1)S(1)} async-done(((bf16[32,8,1024]{2,1,0:T(8,128)(2,1)}), bf16[32,8,1024]{2,1,0:T(8,128)(2,1)S(1)}, u32[]{:S(2)}, u32[]{:S(2)}) %all-to-all-start.3) | async-done | bytes 524320 | tf_op jit(solution)/shard_map/all_to_all | solution.py:350
  136.8 0.6 shard_map.95.refs_2_
  137.3 6.0 %collective-permute-start.8 = (bf16[256,1024]{1,0:T(8,128)(2,1)S(1)}, bf16[256,1024]{1,0:T(8,128)(2,1)S(1)}, u32[]{:S(2)}, u32[]{:S(2)}) collective-permute-start(bf16[256,1024]{1,0:T(8,128)(2,1)S(1)} %shard_map.95.refs_2_), channel_id=1, source_target_pairs={{0,16},{16,0},{1,17},{17,1},{2,18},{18,2},{3,19},{19,3},{4,20},{20... | collective-permute-start | bytes 1572872 | tf_op jit(solution)/shard_map/ppermute | solution.py:32
  143.4 0.9 shard_map.96
  144.3 0.6 collective-permute-done.8.refs_2_
  144.9 1.6 %shard_map.97 = (f32[64,512]{1,0:T(8,128)}, bf16[16,1024]{1,0:T(8,128)(2,1)}) custom-call(s32[4]{0:T(128)S(1)} %pad_add_fusion.refs_0_, bf16[64,1024]{1,0:T(8,128)(2,1)S(1)} %get-tuple-element.30.refs_1_, bf16[256,1024]{1,0:T(8,128)(2,1)S(1)} %collective-permute-done.8.refs_2_, bf16[16,512]{1,0:T(8,128)(2,1)S(1)} %get-tuple-element.38.refs_2_.refs_3_, ...), custom_call_target="tpu_custom_call" | custom-call | bytes 1048576 | tf_op jit(solution)/shard_map/pallas_call | solution.py:73
  (8 shorter events, 0.1 us)
Async XLA Ops:
  0.6 12.9 %copy-start = (bf16[768,1024]{1,0:T(8,128)(2,1)S(1)}, bf16[768,1024]{1,0:T(8,128)(2,1)}, u32[]{:S(2)}) copy-start(bf16[768,1024]{1,0:T(8,128)(2,1)} %param.8) | copy-start | bytes 4718596
  0.7 1.0 copy-start.2
  1.7 0.7 copy-start.5
  2.4 11.1 %copy-start.10 = (s32[512]{0:T(512)S(1)}, s32[512]{0:T(512)}, u32[]{:S(2)}) copy-start(s32[512]{0:T(512)} %param.9) | copy-start | bytes 6148
  4.1 38.3 %all-to-all-start = ((bf16[8,72,1024]{2,1,0:T(8,128)(2,1)}), bf16[8,72,1024]{2,1,0:T(8,128)(2,1)}, u32[]{:S(2)}, u32[]{:S(2)}) async-start(bf16[8,72,1024]{2,1,0:T(8,128)(2,1)} %shard_map.85), calls=%async_computation | async-start | bytes 2359296 | tf_op jit(solution)/shard_map/all_to_all | solution.py:272
  13.6 2.8 %copy-start.6 = (bf16[512,1024]{1,0:T(8,128)(2,1)S(1)}, bf16[512,1024]{1,0:T(8,128)(2,1)}, u32[]{:S(2)}) copy-start(bf16[512,1024]{1,0:T(8,128)(2,1)} %refs_3_.1) | copy-start | bytes 3145732
  17.6 14.2 %collective-permute-start = (bf16[256,1024]{1,0:T(8,128)(2,1)S(1)}, bf16[256,1024]{1,0:T(8,128)(2,1)S(1)}, u32[]{:S(2)}, u32[]{:S(2)}) collective-permute-start(bf16[256,1024]{1,0:T(8,128)(2,1)S(1)} %pad_maximum_fusion), channel_id=1, source_target_pairs={{0,1},{1,128},{128,129},{129,256},{256,257},{257,384},{384,385},{3... | collective-permute-start | bytes 1572872 | tf_op jit(solution)/shard_map/ppermute | solution.py:27
  20.8 14.9 %collective-permute-start.1 = (bf16[256,1024]{1,0:T(8,128)(2,1)S(1)}, bf16[256,1024]{1,0:T(8,128)(2,1)S(1)}, u32[]{:S(2)}, u32[]{:S(2)}) collective-permute-start(bf16[256,1024]{1,0:T(8,128)(2,1)S(1)} %pad_maximum_fusion.1), channel_id=1, source_target_pairs={{0,385},{1,0},{128,1},{129,128},{256,129},{257,256},{384,257},{385... | collective-permute-start | bytes 1572872 | tf_op jit(solution)/shard_map/ppermute | solution.py:27
  31.8 8.9 %copy-start.7 = (bf16[256,1024]{1,0:T(8,128)(2,1)}, bf16[256,1024]{1,0:T(8,128)(2,1)S(1)}, u32[]{:S(2)}) copy-start(bf16[256,1024]{1,0:T(8,128)(2,1)S(1)} %collective-permute-done.refs_3_.refs_4_) | copy-start | bytes 1572868
  31.8 7.2 %collective-permute-start.2 = (bf16[256,1024]{1,0:T(8,128)(2,1)S(1)}, bf16[256,1024]{1,0:T(8,128)(2,1)S(1)}, u32[]{:S(2)}, u32[]{:S(2)}) collective-permute-start(bf16[256,1024]{1,0:T(8,128)(2,1)S(1)} %collective-permute-done.refs_3_.refs_4_), channel_id=1, source_target_pairs={{0,16},{16,0},{1,17},{17,1},{2,18},{18,2},{3,19},{19,3},{4,20},{20... | collective-permute-start | bytes 1572872 | tf_op jit(solution)/shard_map/ppermute | solution.py:32
  35.7 4.9 %copy-start.8 = (bf16[256,1024]{1,0:T(8,128)(2,1)}, bf16[256,1024]{1,0:T(8,128)(2,1)S(1)}, u32[]{:S(2)}) copy-start(bf16[256,1024]{1,0:T(8,128)(2,1)S(1)} %collective-permute-done.1.refs_4_.refs_5_) | copy-start | bytes 1572868
  35.8 4.9 %collective-permute-start.3 = (bf16[256,1024]{1,0:T(8,128)(2,1)S(1)}, bf16[256,1024]{1,0:T(8,128)(2,1)}, u32[]{:S(2)}, u32[]{:S(2)}) collective-permute-start(bf16[256,1024]{1,0:T(8,128)(2,1)S(1)} %collective-permute-done.1.refs_4_.refs_5_), channel_id=1, source_target_pairs={{0,16},{16,0},{1,17},{17,1},{2,18},{18,2},{3,19},{19,3},{4,20},{20... | collective-permute-start | bytes 1572872 | tf_op jit(solution)/shard_map/ppermute | solution.py:32
  39.0 1.6 %copy-start.9 = (bf16[256,1024]{1,0:T(8,128)(2,1)}, bf16[256,1024]{1,0:T(8,128)(2,1)S(1)}, u32[]{:S(2)}) copy-start(bf16[256,1024]{1,0:T(8,128)(2,1)S(1)} %collective-permute-done.2.refs_5_.refs_6_) | copy-start | bytes 1572868
  48.2 8.2 %collective-permute-start.7 = (bf16[256,1152]{1,0:T(8,128)(2,1)S(1)}, bf16[256,1152]{1,0:T(8,128)(2,1)S(1)}, u32[]{:S(2)}, u32[]{:S(2)}) collective-permute-start(bf16[256,1152]{1,0:T(8,128)(2,1)S(1)} %get-tuple-element.32), channel_id=1, source_target_pairs={{0,16},{16,0},{1,17},{17,1},{2,18},{18,2},{3,19},{19,3},{4,20},{20... | collective-permute-start | bytes 1769480 | tf_op jit(solution)/shard_map/ppermute | solution.py:32
  57.9 27.0 %all-to-all-start.1 = ((bf16[32,8,1152]{2,1,0:T(8,128)(2,1)}), bf16[32,8,1152]{2,1,0:T(8,128)(2,1)S(1)}, u32[]{:S(2)}, u32[]{:S(2)}) async-start(bf16[32,8,1152]{2,1,0:T(8,128)(2,1)} %bitcast.11), calls=%async_computation.1 | async-start | bytes 1179648 | tf_op jit(solution)/shard_map/all_to_all | solution.py:319
  67.5 15.0 %collective-permute-start.4 = (bf16[256,1024]{1,0:T(8,128)(2,1)}, bf16[256,1024]{1,0:T(8,128)(2,1)S(1)}, u32[]{:S(2)}, u32[]{:S(2)}) collective-permute-start(bf16[256,1024]{1,0:T(8,128)(2,1)} %get-tuple-element.24), channel_id=1, source_target_pairs={{0,2},{2,0},{4,6},{6,4},{8,10},{10,8},{12,14},{14,12},{1,3},{3,1},... | collective-permute-start | bytes 1572872 | tf_op jit(solution)/shard_map/ppermute | solution.py:32
  84.8 7.8 %copy-start.11 = (bf16[128,1024]{1,0:T(8,128)(2,1)S(1)}, bf16[128,1024]{1,0:T(8,128)(2,1)}, u32[]{:S(2)}) copy-start(bf16[128,1024]{1,0:T(8,128)(2,1)} %get-tuple-element.26) | copy-start | bytes 786436
  84.8 26.2 %copy-start.1 = (bf16[128,1024]{1,0:T(8,128)(2,1)S(1)}, bf16[128,1024]{1,0:T(8,128)(2,1)}, u32[]{:S(2)}) copy-start(bf16[128,1024]{1,0:T(8,128)(2,1)} %get-tuple-element.25.refs_1_) | copy-start | bytes 786436
  88.1 43.4 %copy-start.4 = (s32[512]{0:T(512)S(1)}, s32[512]{0:T(512)}, u32[]{:S(2)}) copy-start(s32[512]{0:T(512)} %param.11) | copy-start | bytes 6148
  88.1 24.4 %all-to-all-start.2 = ((f32[8,8,1024]{2,1,0:T(8,128)}), f32[8,8,1024]{2,1,0:T(8,128)S(1)}, u32[]{:S(2)}, u32[]{:S(2)}) async-start(f32[8,8,1024]{2,1,0:T(8,128)} %get-tuple-element.35), calls=%async_computation.2 | async-start | bytes 524288 | tf_op jit(solution)/shard_map/all_to_all | solution.py:345
  92.6 18.5 %collective-permute-start.5 = (bf16[128,1024]{1,0:T(8,128)(2,1)S(1)}, bf16[128,1024]{1,0:T(8,128)(2,1)S(1)}, u32[]{:S(2)}, u32[]{:S(2)}) collective-permute-start(bf16[128,1024]{1,0:T(8,128)(2,1)S(1)} %copy-done.11), channel_id=1, source_target_pairs={{0,6},{2,4},{4,2},{6,0},{8,14},{10,12},{12,10},{14,8},{1,7},{3,5},... | collective-permute-start | bytes 786440 | tf_op jit(solution)/shard_map/ppermute | solution.py:32
  112.4 10.0 %copy-start.12 = (bf16[64,1024]{1,0:T(8,128)(2,1)S(1)}, bf16[64,1024]{1,0:T(8,128)(2,1)}, u32[]{:S(2)}) copy-start(bf16[64,1024]{1,0:T(8,128)(2,1)} %get-tuple-element.28) | copy-start | bytes 393220
  112.4 19.1 %copy-start.3 = (bf16[64,1024]{1,0:T(8,128)(2,1)S(1)}, bf16[64,1024]{1,0:T(8,128)(2,1)}, u32[]{:S(2)}) copy-start(bf16[64,1024]{1,0:T(8,128)(2,1)} %get-tuple-element.27.refs_2_) | copy-start | bytes 393220
  113.9 22.9 %all-to-all-start.3 = ((bf16[32,8,1024]{2,1,0:T(8,128)(2,1)}), bf16[32,8,1024]{2,1,0:T(8,128)(2,1)S(1)}, u32[]{:S(2)}, u32[]{:S(2)}) async-start(bf16[32,8,1024]{2,1,0:T(8,128)(2,1)} %shard_map.94), calls=%async_computation.3 | async-start | bytes 1048576 | tf_op jit(solution)/shard_map/all_to_all | solution.py:350
  122.4 9.0 %collective-permute-start.6 = (bf16[64,1024]{1,0:T(8,128)(2,1)S(1)}, bf16[64,1024]{1,0:T(8,128)(2,1)S(1)}, u32[]{:S(2)}, u32[]{:S(2)}) collective-permute-start(bf16[64,1024]{1,0:T(8,128)(2,1)S(1)} %copy-done.12), channel_id=1, source_target_pairs={{0,14},{2,12},{4,10},{6,8},{8,6},{10,4},{12,2},{14,0},{1,15},{3,13... | collective-permute-start | bytes 393224 | tf_op jit(solution)/shard_map/ppermute | solution.py:32
  137.3 7.6 %collective-permute-start.8 = (bf16[256,1024]{1,0:T(8,128)(2,1)S(1)}, bf16[256,1024]{1,0:T(8,128)(2,1)S(1)}, u32[]{:S(2)}, u32[]{:S(2)}) collective-permute-start(bf16[256,1024]{1,0:T(8,128)(2,1)S(1)} %shard_map.95.refs_2_), channel_id=1, source_target_pairs={{0,16},{16,0},{1,17},{17,1},{2,18},{18,2},{3,19},{19,3},{4,20},{20... | collective-permute-start | bytes 1572872 | tf_op jit(solution)/shard_map/ppermute | solution.py:32

commit v7 on v6

--- a/solution.py
+++ b/solution.py
@@ -97,7 +97,12 @@
     return jnp.broadcast_to(column, (matrix.shape[0], 128)).T[0:1]
 
 
-def pack_kernel(place, points, members, out):
+def pack_kernel(place, given, marked, out, points, members, sems):
+    copies = [pltpu.make_async_copy(given, points, sems.at[0]), pltpu.make_async_copy(marked, members, sems.at[1])]
+    for copy in copies:
+        copy.start()
+    for copy in copies:
+        copy.wait()
     rows, width = points.shape
     code = jnp.broadcast_to(members[...], (PACK, rows))
     row = lax.broadcasted_iota(i32, (PACK, rows), 0)
@@ -203,7 +208,7 @@
     paired[...] = (keep[...].astype(f32) + theirs[...].astype(f32)).astype(bf16)
 
 
-def means_kernel(place, parts, number, _, sent):
+def means_kernel(place, parts, number, sent):
     means = jnp.sum(parts[...], axis=0) / number[...]
     sent[...] = jnp.broadcast_to(means[None], sent.shape).astype(bf16)
 
@@ -266,9 +271,15 @@
     array = jax.ShapeDtypeStruct
     place = jnp.stack([core, lax.axis_index("yl"), lax.axis_index(("yh", "x", "c")), lax.axis_index("z")]).astype(i32)
 
-    (block,) = call(pack_kernel, (array((ring, rows + PACK, width), bf16),), 3, 0, away=(0,), nbytes=2 * MIB)(
-        place, points, membership.reshape(1, rows)
-    )
+    (block,) = call(
+        pack_kernel,
+        (array((ring, rows + PACK, width), bf16),),
+        3,
+        2,
+        [pltpu.VMEM((rows, width), bf16), pltpu.VMEM((1, rows), i32), pltpu.SemaphoreType.DMA((2,))],
+        away=(0,),
+        nbytes=2 * MIB,
+    )(place, points, membership.reshape(1, rows))
     spread = lax.all_to_all(block, "z", 0, 0)
 
     landmarks = landmark_pool[landmark_ids]
@@ -329,10 +340,11 @@
         7,
         5,
         store(2 * count, rank_width),
-        flops=ring * rows * 2 * count * rank_width,
+        flops=64 * ring * rows * 2 * count * rank_width,
         nbytes=3 * MIB,
     )(place, kernel, whitening, *pieces)
-    kept, leave, done = merge(stay, leave, 1)
+    kept, leave, _ = merge(stay, leave, 1)
+    kept, leave, done = merge(kept, leave, 3)
     mapped, number = call(
         cluster_kernel,
         (array((ring, share, rank_width), f32), array((share, rank_width), f32)),
@@ -343,9 +355,8 @@
         nbytes=3 * MIB,
     )(place, gathered, done, whitening, *pieces)
     over = lax.all_to_all(mapped, "z", 0, 0)
-    kept, leave, done = merge(kept, leave, 3)
-    (sent,) = call(means_kernel, (array((peers, share, rank_width), bf16),), 4, away=(0,), nbytes=MIB)(
-        place, over, number, done
+    (sent,) = call(means_kernel, (array((peers, share, rank_width), bf16),), 3, away=(0,), nbytes=MIB)(
+        place, over, number
     )
     mine = lax.all_to_all(sent, PLANE, 0, 0).reshape(half, rank_width)
     last = flip(leave, "z", 7)

time: 147 us -> 146 us (level)
  the two profiles are of different devices: /device:TPU:73 before, /device:TPU:1 now
where the time goes in v7:
time: 146 us; the launch traced here: 145 us
  starting transfers between devices  58.6 us (40%)
  waiting for transfers between devices  34.6 us (24%)
  Pallas kernels  29.2 us (20%)
  blocking collectives  16.3 us (11%)
  local copies, waits for them, and re-layouts  4.9 us (3%)
    pallas_call x13, Pallas kernels, call(): made(*args[:near], *(pltpu.with_memory_space_constraint(a, pltpu.HBM) for...  29.2 us
    ppermute x7, starting transfers between devices, flip(): return lax.ppermute(value, axis, [(i, i ^ bit) for i in range(size)])  21.9 us
    ppermute x7, waiting for transfers between devices, flip(): return lax.ppermute(value, axis, [(i, i ^ bit) for i in range(size)])  17.5 us
    all_to_all x1, blocking collectives, body(): over = lax.all_to_all(mapped, 'z', 0, 0)  16.3 us
    all_to_all x1, starting transfers between devices, body(): spread = lax.all_to_all(block, 'z', 0, 0)  10.9 us
    all_to_all x1, starting transfers between devices, body(): gathered = lax.all_to_all(paired.reshape(peers, share, -1), PLANE, 0, 0)  9.68 us
    ppermute x2, waiting for transfers between devices, hop(): lax.ppermute(value, axis, [(i, (i + by) % size) for i in range(size)])  9.45 us
    all_to_all x1, starting transfers between devices, body(): mine = lax.all_to_all(sent, PLANE, 0, 0).reshape(half, rank_width)  9.18 us
  transfers between devices with their start and end apart: 12, of which 7 were waited for; matrix products, arithmetic and copies ran while one was open for 3% of the time, Pallas kernels for 10%

profile of v7, /device:TPU:1, one launch (start us, length us, event | category | flops | bytes accessed | tf_op | source)
XLA Modules:
  0.0 144.8 jit_solution(8309450787315666160)
XLA Ops:
  0.6 0.0 copy-start
  0.7 0.1 pad_add_fusion.refs_0_
  0.7 0.0 copy-start.8
  0.7 2.7 %shard_map.85 = bf16[8,72,1024]{2,1,0:T(8,128)(2,1)} custom-call(s32[4]{0:T(128)S(1)} %pad_add_fusion.refs_0_, bf16[64,1024]{1,0:T(8,128)(2,1)} %refs_1_.1, s32[1,64]{1,0:T(1,128)} %bitcast.11), custom_call_target="tpu_custom_call" | custom-call | bytes 2097152 | tf_op jit(solution)/shard_map/pallas_call | solution.py:73
  3.4 10.9 %all-to-all-start = ((bf16[8,72,1024]{2,1,0:T(8,128)(2,1)}), bf16[8,72,1024]{2,1,0:T(8,128)(2,1)}, u32[]{:S(2)}, u32[]{:S(2)}) async-start(bf16[8,72,1024]{2,1,0:T(8,128)(2,1)} %shard_map.85), calls=%async_computation | async-start | bytes 2359296 | tf_op jit(solution)/shard_map/all_to_all | solution.py:283
  14.3 0.0 copy-done.8
  14.3 0.0 copy-done
  14.3 0.0 copy-start.4
  14.3 2.8 %gather_fusion = bf16[512,1024]{1,0:T(8,128)(2,1)} fusion(bf16[768,1024]{1,0:T(8,128)(2,1)S(1)} %copy-done, s32[1024]{0:T(1024)S(1)} %pad_clamp_fusion), kind=kCustom, calls=%fused_computation | custom fusion | bytes 2099200 | tf_op jit(solution)/shard_map/gather | solution.py:285
  17.1 0.0 copy-done.4
  17.1 1.1 constant_dynamic-slice_fusion
  18.3 3.2 %collective-permute-start = (bf16[256,1024]{1,0:T(8,128)(2,1)S(1)}, bf16[256,1024]{1,0:T(8,128)(2,1)S(1)}, u32[]{:S(2)}, u32[]{:S(2)}) collective-permute-start(bf16[256,1024]{1,0:T(8,128)(2,1)S(1)} %pad_maximum_fusion), channel_id=1, source_target_pairs={{0,1},{1,128},{128,129},{129,256},{256,257},{257,384},{384,385},{3... | collective-permute-start | bytes 1572872 | tf_op jit(solution)/shard_map/ppermute | solution.py:27
  21.5 3.8 %collective-permute-start.1 = (bf16[256,1024]{1,0:T(8,128)(2,1)S(1)}, bf16[256,1024]{1,0:T(8,128)(2,1)S(1)}, u32[]{:S(2)}, u32[]{:S(2)}) collective-permute-start(bf16[256,1024]{1,0:T(8,128)(2,1)S(1)} %pad_maximum_fusion.1), channel_id=1, source_target_pairs={{0,385},{1,0},{128,1},{129,128},{256,129},{257,256},{384,257},{385... | collective-permute-start | bytes 1572872 | tf_op jit(solution)/shard_map/ppermute | solution.py:27
  25.4 9.4 %collective-permute-done.refs_3_.refs_4_ = bf16[256,1024]{1,0:T(8,128)(2,1)S(1)} collective-permute-done((bf16[256,1024]{1,0:T(8,128)(2,1)S(1)}, bf16[256,1024]{1,0:T(8,128)(2,1)S(1)}, u32[]{:S(2)}, u32[]{:S(2)}) %collective-permute-start) | collective-permute-done | bytes 524320 | tf_op jit(solution)/shard_map/ppermute | solution.py:27
  34.8 0.0 copy-start.5
  34.8 3.3 %collective-permute-start.2 = (bf16[256,1024]{1,0:T(8,128)(2,1)S(1)}, bf16[256,1024]{1,0:T(8,128)(2,1)S(1)}, u32[]{:S(2)}, u32[]{:S(2)}) collective-permute-start(bf16[256,1024]{1,0:T(8,128)(2,1)S(1)} %collective-permute-done.refs_3_.refs_4_), channel_id=1, source_target_pairs={{0,16},{16,0},{1,17},{17,1},{2,18},{18,2},{3,19},{19,3},{4,20},{20... | collective-permute-start | bytes 1572872 | tf_op jit(solution)/shard_map/ppermute | solution.py:32
  38.2 0.0 collective-permute-done.1.refs_4_.refs_5_
  38.2 0.0 copy-start.6
  38.2 1.9 %collective-permute-start.3 = (bf16[256,1024]{1,0:T(8,128)(2,1)S(1)}, bf16[256,1024]{1,0:T(8,128)(2,1)}, u32[]{:S(2)}, u32[]{:S(2)}) collective-permute-start(bf16[256,1024]{1,0:T(8,128)(2,1)S(1)} %collective-permute-done.1.refs_4_.refs_5_), channel_id=1, source_target_pairs={{0,16},{16,0},{1,17},{17,1},{2,18},{18,2},{3,19},{19,3},{4,20},{20... | collective-permute-start | bytes 1572872 | tf_op jit(solution)/shard_map/ppermute | solution.py:32
  40.1 0.0 collective-permute-done.2.refs_5_.refs_6_
  40.1 0.0 copy-start.7
  40.1 2.0 %collective-permute-done.3.refs_6_.refs_7_ = bf16[256,1024]{1,0:T(8,128)(2,1)} collective-permute-done((bf16[256,1024]{1,0:T(8,128)(2,1)S(1)}, bf16[256,1024]{1,0:T(8,128)(2,1)}, u32[]{:S(2)}, u32[]{:S(2)}) %collective-permute-start.3) | collective-permute-done | bytes 524320 | tf_op jit(solution)/shard_map/ppermute | solution.py:32
  42.1 0.0 copy-done.6
  42.1 0.0 copy-done.7
  42.1 4.3 %all-to-all-done.refs_1_ = bf16[8,72,1024]{2,1,0:T(8,128)(2,1)} async-done(((bf16[8,72,1024]{2,1,0:T(8,128)(2,1)}), bf16[8,72,1024]{2,1,0:T(8,128)(2,1)}, u32[]{:S(2)}, u32[]{:S(2)}) %all-to-all-start) | async-done | bytes 1179680 | tf_op jit(solution)/shard_map/all_to_all | solution.py:283
  46.4 0.0 copy-done.5
  46.4 5.8 %shard_map.86 = (bf16[512,1024]{1,0:T(8,128)(2,1)S(1)}, bf16[256,1152]{1,0:T(8,128)(2,1)S(1)}, bf16[256,1152]{1,0:T(8,128)(2,1)S(1)}) custom-call(s32[4]{0:T(128)S(1)} %pad_add_fusion.refs_0_, bf16[8,72,1024]{2,1,0:T(8,128)(2,1)} %all-to-all-done.refs_1_, bf16[512,1024]{1,0:T(8,128)(2,1)} %gather_fusion, bf16[256,1024]{1,0:T(8,128)(2,1)} %copy-done.5, ...), custom_call_target="tpu_custom_call" | custom-call | flops 1610612736 | bytes 6291456 | tf_op jit(solution)/shard_map/pallas_call | solution.py:73
  52.2 2.4 %collective-permute-start.7 = (bf16[256,1152]{1,0:T(8,128)(2,1)S(1)}, bf16[256,1152]{1,0:T(8,128)(2,1)S(1)}, u32[]{:S(2)}, u32[]{:S(2)}) collective-permute-start(bf16[256,1152]{1,0:T(8,128)(2,1)S(1)} %get-tuple-element.31), channel_id=1, source_target_pairs={{0,16},{16,0},{1,17},{17,1},{2,18},{18,2},{3,19},{19,3},{4,20},{20... | collective-permute-start | bytes 1769480 | tf_op jit(solution)/shard_map/ppermute | solution.py:32
  54.7 3.6 %shard_map.88 = (bf16[256,1024]{1,0:T(8,128)(2,1)}, f32[8,128]{1,0:T(8,128)S(1)}) custom-call(s32[4]{0:T(128)S(1)} %pad_add_fusion.refs_0_, bf16[512,1024]{1,0:T(8,128)(2,1)S(1)} %get-tuple-element.22.refs_1_, bf16[512,1024]{1,0:T(8,128)(2,1)} %refs_3_.1, bf16[256,1024]{1,0:T(8,128)(2,1)} %copy-done.5, bf16[256,1024]{1,0:T(8,128)(2,1)} %copy-done.6, ...), custom_call_target="tpu_custom_call" | custom-call | flops 536870912 | bytes 3145728 | tf_op jit(solution)/shard_map/pallas_call | solution.py:73
  58.3 2.2 %collective-permute-start.4 = (bf16[256,1024]{1,0:T(8,128)(2,1)}, bf16[256,1024]{1,0:T(8,128)(2,1)}, u32[]{:S(2)}, u32[]{:S(2)}) collective-permute-start(bf16[256,1024]{1,0:T(8,128)(2,1)} %get-tuple-element.23), channel_id=1, source_target_pairs={{0,2},{2,0},{4,6},{6,4},{8,10},{10,8},{12,14},{14,12},{1,3},{3,1},... | collective-permute-start | bytes 1572872 | tf_op jit(solution)/shard_map/ppermute | solution.py:32
  60.5 0.0 collective-permute-done.7.refs_2_
  60.5 1.5 %shard_map.92 = bf16[256,1152]{1,0:T(8,128)(2,1)} custom-call(s32[4]{0:T(128)S(1)} %pad_add_fusion.refs_0_, bf16[256,1152]{1,0:T(8,128)(2,1)S(1)} %get-tuple-element.30.refs_1_, bf16[256,1152]{1,0:T(8,128)(2,1)S(1)} %collective-permute-done.7.refs_2_, f32[8,128]{1,0:T(8,128)S(1)} %get-tuple-element.32.refs_3_), custom_call_target="tpu_custom_call" | custom-call | bytes 2097152 | tf_op jit(solution)/shard_map/pallas_call | solution.py:73
  62.0 9.7 %all-to-all-start.1 = ((bf16[32,8,1152]{2,1,0:T(8,128)(2,1)}), bf16[32,8,1152]{2,1,0:T(8,128)(2,1)S(1)}, u32[]{:S(2)}, u32[]{:S(2)}) async-start(bf16[32,8,1152]{2,1,0:T(8,128)(2,1)} %bitcast.10), calls=%async_computation.1 | async-start | bytes 1179648 | tf_op jit(solution)/shard_map/all_to_all | solution.py:330
  71.7 2.8 %shard_map.87.refs_1_ = bf16[256,1024]{1,0:T(8,128)(2,1)S(1)} custom-call(s32[4]{0:T(128)S(1)} %pad_add_fusion.refs_0_, bf16[512,1024]{1,0:T(8,128)(2,1)S(1)} %get-tuple-element.22.refs_1_, bf16[512,1024]{1,0:T(8,128)(2,1)} %refs_3_.1, bf16[256,1024]{1,0:T(8,128)(2,1)} %copy-done.5, bf16[256,1024]{1,0:T(8,128)(2,1)} %copy-done.6, ...), custom_call_target="tpu_custom_call" | custom-call | flops 34359738368 | bytes 3145728 | tf_op jit(solution)/shard_map/pallas_call | solution.py:73
  74.5 0.0 collective-permute-done.4.refs_2_
  74.5 2.5 %shard_map.89 = (bf16[128,1024]{1,0:T(8,128)(2,1)}, bf16[128,1024]{1,0:T(8,128)(2,1)}, f32[8,128]{1,0:T(8,128)}) custom-call(s32[4]{0:T(128)S(1)} %pad_add_fusion.refs_0_, bf16[256,1024]{1,0:T(8,128)(2,1)S(1)} %shard_map.87.refs_1_, bf16[256,1024]{1,0:T(8,128)(2,1)} %collective-permute-done.4.refs_2_), custom_call_target="tpu_custom_call" | custom-call | bytes 1048576 | tf_op jit(solution)/shard_map/pallas_call | solution.py:73
  77.0 3.0 %collective-permute-start.5 = (bf16[128,1024]{1,0:T(8,128)(2,1)}, bf16[128,1024]{1,0:T(8,128)(2,1)S(1)}, u32[]{:S(2)}, u32[]{:S(2)}) collective-permute-start(bf16[128,1024]{1,0:T(8,128)(2,1)} %get-tuple-element.25), channel_id=1, source_target_pairs={{0,6},{2,4},{4,2},{6,0},{8,14},{10,12},{12,10},{14,8},{1,7},{3,5},... | collective-permute-start | bytes 786440 | tf_op jit(solution)/shard_map/ppermute | solution.py:32
  80.0 8.3 %collective-permute-done.5.refs_2_ = bf16[128,1024]{1,0:T(8,128)(2,1)S(1)} collective-permute-done((bf16[128,1024]{1,0:T(8,128)(2,1)}, bf16[128,1024]{1,0:T(8,128)(2,1)S(1)}, u32[]{:S(2)}, u32[]{:S(2)}) %collective-permute-start.5) | collective-permute-done | bytes 262176 | tf_op jit(solution)/shard_map/ppermute | solution.py:32
  88.3 0.0 copy-start.1
  88.3 0.9 copy-done.1
  89.3 1.3 shard_map.90
  90.6 0.0 all-to-all-done.1.refs_1_
  90.6 3.2 %shard_map.93 = (f32[8,8,1024]{2,1,0:T(8,128)}, f32[8,1024]{1,0:T(8,128)S(1)}) custom-call(s32[4]{0:T(128)S(1)} %pad_add_fusion.refs_0_, bf16[32,8,1152]{2,1,0:T(8,128)(2,1)S(1)} %all-to-all-done.1.refs_1_, f32[8,128]{1,0:T(8,128)S(1)} %get-tuple-element.33.refs_2_, bf16[512,1024]{1,0:T(8,128)(2,1)} %refs_3_.1, bf16[256,1024]{1,0:T(8,128)(2,1)} %copy-done.5, ...), custom_call_target="tpu_custom_call" | custom-call | bytes 3145728 | tf_op jit(solution)/shard_map/pallas_call | solution.py:73
  93.8 0.0 copy-start.9
  93.8 0.0 copy-start.2
  93.8 0.0 copy-start.3
  93.8 16.3 %all_to_all.20.refs_1_ = f32[8,8,1024]{2,1,0:T(8,128)S(1)} all-to-all(f32[8,8,1024]{2,1,0:T(8,128)} %get-tuple-element.34), channel_id=1, replica_groups=mesh['yh'=4,'x'=4,'c'=2,'z'=8,'yl'=2] {'z'}, dimensions={0} | all-to-all | bytes 524288 | tf_op jit(solution)/shard_map/all_to_all | solution.py:357
  110.1 1.4 shard_map.94
  111.5 9.2 %all-to-all-start.3 = ((bf16[32,8,1024]{2,1,0:T(8,128)(2,1)}), bf16[32,8,1024]{2,1,0:T(8,128)(2,1)S(1)}, u32[]{:S(2)}, u32[]{:S(2)}) async-start(bf16[32,8,1024]{2,1,0:T(8,128)(2,1)} %shard_map.94), calls=%async_computation.3 | async-start | bytes 1048576 | tf_op jit(solution)/shard_map/all_to_all | solution.py:361
  120.7 0.0 copy-done.9
  120.7 1.9 %collective-permute-start.6 = (bf16[64,1024]{1,0:T(8,128)(2,1)S(1)}, bf16[64,1024]{1,0:T(8,128)(2,1)S(1)}, u32[]{:S(2)}, u32[]{:S(2)}) collective-permute-start(bf16[64,1024]{1,0:T(8,128)(2,1)S(1)} %copy-done.9), channel_id=1, source_target_pairs={{0,14},{2,12},{4,10},{6,8},{8,6},{10,4},{12,2},{14,0},{1,15},{3,13... | collective-permute-start | bytes 393224 | tf_op jit(solution)/shard_map/ppermute | solution.py:32
  122.6 6.6 %collective-permute-done.6.refs_3_ = bf16[64,1024]{1,0:T(8,128)(2,1)S(1)} collective-permute-done((bf16[64,1024]{1,0:T(8,128)(2,1)S(1)}, bf16[64,1024]{1,0:T(8,128)(2,1)S(1)}, u32[]{:S(2)}, u32[]{:S(2)}) %collective-permute-start.6) | collective-permute-done | bytes 131104 | tf_op jit(solution)/shard_map/ppermute | solution.py:32
  129.2 0.0 copy-done.2
  129.2 0.0 copy-done.3
  129.2 1.3 shard_map.91
  130.5 3.4 %all-to-all-done.3 = bf16[32,8,1024]{2,1,0:T(8,128)(2,1)S(1)} async-done(((bf16[32,8,1024]{2,1,0:T(8,128)(2,1)}), bf16[32,8,1024]{2,1,0:T(8,128)(2,1)S(1)}, u32[]{:S(2)}, u32[]{:S(2)}) %all-to-all-start.3) | async-done | bytes 524320 | tf_op jit(solution)/shard_map/all_to_all | solution.py:361
  133.9 0.6 shard_map.95.refs_2_
  134.5 7.2 %collective-permute-start.8 = (bf16[256,1024]{1,0:T(8,128)(2,1)S(1)}, bf16[256,1024]{1,0:T(8,128)(2,1)S(1)}, u32[]{:S(2)}, u32[]{:S(2)}) collective-permute-start(bf16[256,1024]{1,0:T(8,128)(2,1)S(1)} %shard_map.95.refs_2_), channel_id=1, source_target_pairs={{0,16},{16,0},{1,17},{17,1},{2,18},{18,2},{3,19},{19,3},{4,20},{20... | collective-permute-start | bytes 1572872 | tf_op jit(solution)/shard_map/ppermute | solution.py:32
  141.7 0.9 shard_map.96
  142.6 0.6 collective-permute-done.8.refs_2_
  143.2 1.6 %shard_map.97 = (f32[64,512]{1,0:T(8,128)}, bf16[16,1024]{1,0:T(8,128)(2,1)}) custom-call(s32[4]{0:T(128)S(1)} %pad_add_fusion.refs_0_, bf16[64,1024]{1,0:T(8,128)(2,1)S(1)} %get-tuple-element.29.refs_1_, bf16[256,1024]{1,0:T(8,128)(2,1)S(1)} %collective-permute-done.8.refs_2_, bf16[16,512]{1,0:T(8,128)(2,1)S(1)} %get-tuple-element.36.refs_2_.refs_3_, ...), custom_call_target="tpu_custom_call" | custom-call | bytes 1048576 | tf_op jit(solution)/shard_map/pallas_call | solution.py:73
  (4 shorter events, 0.1 us)
Async XLA Ops:
  0.6 13.7 %copy-start = (bf16[768,1024]{1,0:T(8,128)(2,1)S(1)}, bf16[768,1024]{1,0:T(8,128)(2,1)}, u32[]{:S(2)}) copy-start(bf16[768,1024]{1,0:T(8,128)(2,1)} %param.8) | copy-start | bytes 4718596
  0.7 13.5 %copy-start.8 = (s32[512]{0:T(512)S(1)}, s32[512]{0:T(512)}, u32[]{:S(2)}) copy-start(s32[512]{0:T(512)} %param.9) | copy-start | bytes 6148
  3.4 43.0 %all-to-all-start = ((bf16[8,72,1024]{2,1,0:T(8,128)(2,1)}), bf16[8,72,1024]{2,1,0:T(8,128)(2,1)}, u32[]{:S(2)}, u32[]{:S(2)}) async-start(bf16[8,72,1024]{2,1,0:T(8,128)(2,1)} %shard_map.85), calls=%async_computation | async-start | bytes 2359296 | tf_op jit(solution)/shard_map/all_to_all | solution.py:283
  14.3 2.8 %copy-start.4 = (bf16[512,1024]{1,0:T(8,128)(2,1)S(1)}, bf16[512,1024]{1,0:T(8,128)(2,1)}, u32[]{:S(2)}) copy-start(bf16[512,1024]{1,0:T(8,128)(2,1)} %refs_3_.1) | copy-start | bytes 3145732
  18.3 16.5 %collective-permute-start = (bf16[256,1024]{1,0:T(8,128)(2,1)S(1)}, bf16[256,1024]{1,0:T(8,128)(2,1)S(1)}, u32[]{:S(2)}, u32[]{:S(2)}) collective-permute-start(bf16[256,1024]{1,0:T(8,128)(2,1)S(1)} %pad_maximum_fusion), channel_id=1, source_target_pairs={{0,1},{1,128},{128,129},{129,256},{256,257},{257,384},{384,385},{3... | collective-permute-start | bytes 1572872 | tf_op jit(solution)/shard_map/ppermute | solution.py:27
  21.5 16.6 %collective-permute-start.1 = (bf16[256,1024]{1,0:T(8,128)(2,1)S(1)}, bf16[256,1024]{1,0:T(8,128)(2,1)S(1)}, u32[]{:S(2)}, u32[]{:S(2)}) collective-permute-start(bf16[256,1024]{1,0:T(8,128)(2,1)S(1)} %pad_maximum_fusion.1), channel_id=1, source_target_pairs={{0,385},{1,0},{128,1},{129,128},{256,129},{257,256},{384,257},{385... | collective-permute-start | bytes 1572872 | tf_op jit(solution)/shard_map/ppermute | solution.py:27
  34.8 11.6 %copy-start.5 = (bf16[256,1024]{1,0:T(8,128)(2,1)}, bf16[256,1024]{1,0:T(8,128)(2,1)S(1)}, u32[]{:S(2)}) copy-start(bf16[256,1024]{1,0:T(8,128)(2,1)S(1)} %collective-permute-done.refs_3_.refs_4_) | copy-start | bytes 1572868
  34.8 5.3 %collective-permute-start.2 = (bf16[256,1024]{1,0:T(8,128)(2,1)S(1)}, bf16[256,1024]{1,0:T(8,128)(2,1)S(1)}, u32[]{:S(2)}, u32[]{:S(2)}) collective-permute-start(bf16[256,1024]{1,0:T(8,128)(2,1)S(1)} %collective-permute-done.refs_3_.refs_4_), channel_id=1, source_target_pairs={{0,16},{16,0},{1,17},{17,1},{2,18},{18,2},{3,19},{19,3},{4,20},{20... | collective-permute-start | bytes 1572872 | tf_op jit(solution)/shard_map/ppermute | solution.py:32
  38.2 3.9 %copy-start.6 = (bf16[256,1024]{1,0:T(8,128)(2,1)}, bf16[256,1024]{1,0:T(8,128)(2,1)S(1)}, u32[]{:S(2)}) copy-start(bf16[256,1024]{1,0:T(8,128)(2,1)S(1)} %collective-permute-done.1.refs_4_.refs_5_) | copy-start | bytes 1572868
  38.2 3.9 %collective-permute-start.3 = (bf16[256,1024]{1,0:T(8,128)(2,1)S(1)}, bf16[256,1024]{1,0:T(8,128)(2,1)}, u32[]{:S(2)}, u32[]{:S(2)}) collective-permute-start(bf16[256,1024]{1,0:T(8,128)(2,1)S(1)} %collective-permute-done.1.refs_4_.refs_5_), channel_id=1, source_target_pairs={{0,16},{16,0},{1,17},{17,1},{2,18},{18,2},{3,19},{19,3},{4,20},{20... | collective-permute-start | bytes 1572872 | tf_op jit(solution)/shard_map/ppermute | solution.py:32
  40.1 2.0 %copy-start.7 = (bf16[256,1024]{1,0:T(8,128)(2,1)}, bf16[256,1024]{1,0:T(8,128)(2,1)S(1)}, u32[]{:S(2)}) copy-start(bf16[256,1024]{1,0:T(8,128)(2,1)S(1)} %collective-permute-done.2.refs_5_.refs_6_) | copy-start | bytes 1572868
  52.2 8.2 %collective-permute-start.7 = (bf16[256,1152]{1,0:T(8,128)(2,1)S(1)}, bf16[256,1152]{1,0:T(8,128)(2,1)S(1)}, u32[]{:S(2)}, u32[]{:S(2)}) collective-permute-start(bf16[256,1152]{1,0:T(8,128)(2,1)S(1)} %get-tuple-element.31), channel_id=1, source_target_pairs={{0,16},{16,0},{1,17},{17,1},{2,18},{18,2},{3,19},{19,3},{4,20},{20... | collective-permute-start | bytes 1769480 | tf_op jit(solution)/shard_map/ppermute | solution.py:32
  58.3 16.2 %collective-permute-start.4 = (bf16[256,1024]{1,0:T(8,128)(2,1)}, bf16[256,1024]{1,0:T(8,128)(2,1)}, u32[]{:S(2)}, u32[]{:S(2)}) collective-permute-start(bf16[256,1024]{1,0:T(8,128)(2,1)} %get-tuple-element.23), channel_id=1, source_target_pairs={{0,2},{2,0},{4,6},{6,4},{8,10},{10,8},{12,14},{14,12},{1,3},{3,1},... | collective-permute-start | bytes 1572872 | tf_op jit(solution)/shard_map/ppermute | solution.py:32
  62.0 28.6 %all-to-all-start.1 = ((bf16[32,8,1152]{2,1,0:T(8,128)(2,1)}), bf16[32,8,1152]{2,1,0:T(8,128)(2,1)S(1)}, u32[]{:S(2)}, u32[]{:S(2)}) async-start(bf16[32,8,1152]{2,1,0:T(8,128)(2,1)} %bitcast.10), calls=%async_computation.1 | async-start | bytes 1179648 | tf_op jit(solution)/shard_map/all_to_all | solution.py:330
  77.0 11.3 %collective-permute-start.5 = (bf16[128,1024]{1,0:T(8,128)(2,1)}, bf16[128,1024]{1,0:T(8,128)(2,1)S(1)}, u32[]{:S(2)}, u32[]{:S(2)}) collective-permute-start(bf16[128,1024]{1,0:T(8,128)(2,1)} %get-tuple-element.25), channel_id=1, source_target_pairs={{0,6},{2,4},{4,2},{6,0},{8,14},{10,12},{12,10},{14,8},{1,7},{3,5},... | collective-permute-start | bytes 786440 | tf_op jit(solution)/shard_map/ppermute | solution.py:32
  88.3 1.0 copy-start.1
  93.8 26.9 %copy-start.9 = (bf16[64,1024]{1,0:T(8,128)(2,1)S(1)}, bf16[64,1024]{1,0:T(8,128)(2,1)}, u32[]{:S(2)}) copy-start(bf16[64,1024]{1,0:T(8,128)(2,1)} %get-tuple-element.27) | copy-start | bytes 393220
  93.8 35.4 %copy-start.2 = (bf16[64,1024]{1,0:T(8,128)(2,1)S(1)}, bf16[64,1024]{1,0:T(8,128)(2,1)}, u32[]{:S(2)}) copy-start(bf16[64,1024]{1,0:T(8,128)(2,1)} %get-tuple-element.26.refs_2_) | copy-start | bytes 393220
  93.8 35.4 %copy-start.3 = (s32[512]{0:T(512)S(1)}, s32[512]{0:T(512)}, u32[]{:S(2)}) copy-start(s32[512]{0:T(512)} %param.11) | copy-start | bytes 6148
  111.5 22.4 %all-to-all-start.3 = ((bf16[32,8,1024]{2,1,0:T(8,128)(2,1)}), bf16[32,8,1024]{2,1,0:T(8,128)(2,1)S(1)}, u32[]{:S(2)}, u32[]{:S(2)}) async-start(bf16[32,8,1024]{2,1,0:T(8,128)(2,1)} %shard_map.94), calls=%async_computation.3 | async-start | bytes 1048576 | tf_op jit(solution)/shard_map/all_to_all | solution.py:361
  120.7 8.5 %collective-permute-start.6 = (bf16[64,1024]{1,0:T(8,128)(2,1)S(1)}, bf16[64,1024]{1,0:T(8,128)(2,1)S(1)}, u32[]{:S(2)}, u32[]{:S(2)}) collective-permute-start(bf16[64,1024]{1,0:T(8,128)(2,1)S(1)} %copy-done.9), channel_id=1, source_target_pairs={{0,14},{2,12},{4,10},{6,8},{8,6},{10,4},{12,2},{14,0},{1,15},{3,13... | collective-permute-start | bytes 393224 | tf_op jit(solution)/shard_map/ppermute | solution.py:32
  134.5 8.7 %collective-permute-start.8 = (bf16[256,1024]{1,0:T(8,128)(2,1)S(1)}, bf16[256,1024]{1,0:T(8,128)(2,1)S(1)}, u32[]{:S(2)}, u32[]{:S(2)}) collective-permute-start(bf16[256,1024]{1,0:T(8,128)(2,1)S(1)} %shard_map.95.refs_2_), channel_id=1, source_target_pairs={{0,16},{16,0},{1,17},{17,1},{2,18},{18,2},{3,19},{19,3},{4,20},{20... | collective-permute-start | bytes 1572872 | tf_op jit(solution)/shard_map/ppermute | solution.py:32

commit v8 on v7

--- a/solution.py
+++ b/solution.py
@@ -15,6 +15,7 @@
 ALL = ("yh", "x", "c", "z", "yl")
 PLANE = ("yh", "x", "yl")
 PACK = 8
+LONG = 1 << 36
 LEAVE = (1, 6, 2, 5)
 STAY = (0, 7, 3, 4)
 DIGIT = 128
@@ -208,7 +209,7 @@
     paired[...] = (keep[...].astype(f32) + theirs[...].astype(f32)).astype(bf16)
 
 
-def means_kernel(place, parts, number, sent):
+def means_kernel(place, parts, number, _, sent):
     means = jnp.sum(parts[...], axis=0) / number[...]
     sent[...] = jnp.broadcast_to(means[None], sent.shape).astype(bf16)
 
@@ -329,10 +330,10 @@
     (paired,) = call(pair_kernel, (array(keep.shape, bf16),), 4, away=(0,), nbytes=2 * MIB)(place, keep, theirs, done)
     gathered = lax.all_to_all(paired.reshape(peers, share, -1), PLANE, 0, 0)
 
-    def merge(kept, leave, partner):
+    def merge(kept, leave, partner, work):
         size = array((kept.shape[0] // 2, rank_width), bf16)
         arrived = flip(leave, "z", partner)
-        return call(merge_kernel, (size, size, token), 3, away=(0, 1), nbytes=MIB)(place, kept, arrived)
+        return call(merge_kernel, (size, size, token), 3, away=(0, 1), flops=work, nbytes=MIB)(place, kept, arrived)
 
     (stay,) = call(
         functools.partial(stay_kernel, rows),
@@ -340,11 +341,10 @@
         7,
         5,
         store(2 * count, rank_width),
-        flops=64 * ring * rows * 2 * count * rank_width,
+        flops=LONG,
         nbytes=3 * MIB,
     )(place, kernel, whitening, *pieces)
-    kept, leave, _ = merge(stay, leave, 1)
-    kept, leave, done = merge(kept, leave, 3)
+    kept, leave, done = merge(stay, leave, 1, 0)
     mapped, number = call(
         cluster_kernel,
         (array((ring, share, rank_width), f32), array((share, rank_width), f32)),
@@ -352,11 +352,13 @@
         5,
         store(2 * count, rank_width),
         away=(0,),
+        flops=LONG,
         nbytes=3 * MIB,
     )(place, gathered, done, whitening, *pieces)
     over = lax.all_to_all(mapped, "z", 0, 0)
-    (sent,) = call(means_kernel, (array((peers, share, rank_width), bf16),), 3, away=(0,), nbytes=MIB)(
-        place, over, number
+    kept, leave, done = merge(kept, leave, 3, LONG)
+    (sent,) = call(means_kernel, (array((peers, share, rank_width), bf16),), 4, 1, away=(0,), nbytes=MIB)(
+        place, over, number, done
     )
     mine = lax.all_to_all(sent, PLANE, 0, 0).reshape(half, rank_width)
     last = flip(leave, "z", 7)

time: 146 us -> 138 us (0.945)
  blocking collectives: 16.3 us -> 0 us
  waiting for transfers between devices: 34.6 us -> 44 us
    all_to_all x1 -> x0, blocking collectives: 16.3 us -> none  [body(): over = lax.all_to_all(mapped, 'z', 0, 0)]
    all_to_all x1, waiting for transfers between devices: 0.01 us -> 10.1 us  [body(): gathered = lax.all_to_all(paired.reshape(peers, share, -1), PLANE, 0, 0)]
    ppermute x7, waiting for transfers between devices: 17.5 us -> 8.19 us  [flip(): return lax.ppermute(value, axis, [(i, i ^ bit) for i in range(size)])]
    all_to_all x0 -> x1, waiting for transfers between devices: none -> 8.15 us  [body(): over = lax.all_to_all(mapped, 'z', 0, 0)]
    all_to_all x1, starting transfers between devices: 9.18 us -> 5.5 us  [body(): mine = lax.all_to_all(sent, PLANE, 0, 0).reshape(half, rank_width)]
    all_to_all x0 -> x1, starting transfers between devices: none -> 3.42 us  [body(): over = lax.all_to_all(mapped, 'z', 0, 0)]
  transfers between devices with their start and end apart: 12 -> 13, of which waited for: 7 -> 8; matrix products, arithmetic and copies ran while one was open for 3% -> 3% of each run, Pallas kernels for 10% -> 12%
where the time goes in v8:
time: 138 us; the launch traced here: 137 us
  starting transfers between devices  58.1 us (42%)
  waiting for transfers between devices  44 us (32%)
  Pallas kernels  28.6 us (21%)
  local copies, waits for them, and re-layouts  5.38 us (4%)
    pallas_call x13, Pallas kernels, call(): made(*args[:near], *(pltpu.with_memory_space_constraint(a, pltpu.HBM) for...  28.6 us
    ppermute x7, starting transfers between devices, flip(): return lax.ppermute(value, axis, [(i, i ^ bit) for i in range(size)])  21.6 us
    all_to_all x1, starting transfers between devices, body(): spread = lax.all_to_all(block, 'z', 0, 0)  10.9 us
    all_to_all x1, waiting for transfers between devices, body(): gathered = lax.all_to_all(paired.reshape(peers, share, -1), PLANE, 0, 0)  10.1 us
    all_to_all x1, starting transfers between devices, body(): gathered = lax.all_to_all(paired.reshape(peers, share, -1), PLANE, 0, 0)  9.69 us
    ppermute x2, waiting for transfers between devices, hop(): lax.ppermute(value, axis, [(i, (i + by) % size) for i in range(size)])  9.45 us
    ppermute x7, waiting for transfers between devices, flip(): return lax.ppermute(value, axis, [(i, i ^ bit) for i in range(size)])  8.19 us
    all_to_all x1, waiting for transfers between devices, body(): over = lax.all_to_all(mapped, 'z', 0, 0)  8.15 us
  transfers between devices with their start and end apart: 13, of which 8 were waited for; matrix products, arithmetic and copies ran while one was open for 3% of the time, Pallas kernels for 12%

profile of v8, /device:TPU:1, one launch (start us, length us, event | category | flops | bytes accessed | tf_op | source)
XLA Modules:
  0.0 137.2 jit_solution(6424737227276235811)
XLA Ops:
  0.6 0.0 copy-start
  0.7 0.1 pad_add_fusion.refs_0_
  0.7 0.0 copy-start.9
  0.7 2.6 %shard_map.85 = bf16[8,72,1024]{2,1,0:T(8,128)(2,1)} custom-call(s32[4]{0:T(128)S(1)} %pad_add_fusion.refs_0_, bf16[64,1024]{1,0:T(8,128)(2,1)} %refs_1_.1, s32[1,64]{1,0:T(1,128)} %bitcast.11), custom_call_target="tpu_custom_call" | custom-call | bytes 2097152 | tf_op jit(solution)/shard_map/pallas_call | solution.py:74
  3.4 10.9 %all-to-all-start = ((bf16[8,72,1024]{2,1,0:T(8,128)(2,1)}), bf16[8,72,1024]{2,1,0:T(8,128)(2,1)}, u32[]{:S(2)}, u32[]{:S(2)}) async-start(bf16[8,72,1024]{2,1,0:T(8,128)(2,1)} %shard_map.85), calls=%async_computation | async-start | bytes 2359296 | tf_op jit(solution)/shard_map/all_to_all | solution.py:284
  14.3 0.0 copy-done.9
  14.3 0.0 copy-done
  14.3 0.0 copy-start.5
  14.3 2.8 %gather_fusion = bf16[512,1024]{1,0:T(8,128)(2,1)} fusion(bf16[768,1024]{1,0:T(8,128)(2,1)S(1)} %copy-done, s32[1024]{0:T(1024)S(1)} %pad_clamp_fusion), kind=kCustom, calls=%fused_computation | custom fusion | bytes 2099200 | tf_op jit(solution)/shard_map/gather | solution.py:286
  17.1 0.0 copy-done.5
  17.1 1.2 constant_dynamic-slice_fusion
  18.3 3.2 %collective-permute-start = (bf16[256,1024]{1,0:T(8,128)(2,1)S(1)}, bf16[256,1024]{1,0:T(8,128)(2,1)S(1)}, u32[]{:S(2)}, u32[]{:S(2)}) collective-permute-start(bf16[256,1024]{1,0:T(8,128)(2,1)S(1)} %pad_maximum_fusion), channel_id=1, source_target_pairs={{0,1},{1,128},{128,129},{129,256},{256,257},{257,384},{384,385},{3... | collective-permute-start | bytes 1572872 | tf_op jit(solution)/shard_map/ppermute | solution.py:28
  21.6 3.8 %collective-permute-start.1 = (bf16[256,1024]{1,0:T(8,128)(2,1)S(1)}, bf16[256,1024]{1,0:T(8,128)(2,1)S(1)}, u32[]{:S(2)}, u32[]{:S(2)}) collective-permute-start(bf16[256,1024]{1,0:T(8,128)(2,1)S(1)} %pad_maximum_fusion.1), channel_id=1, source_target_pairs={{0,385},{1,0},{128,1},{129,128},{256,129},{257,256},{384,257},{385... | collective-permute-start | bytes 1572872 | tf_op jit(solution)/shard_map/ppermute | solution.py:28
  25.4 9.4 %collective-permute-done.refs_3_.refs_4_ = bf16[256,1024]{1,0:T(8,128)(2,1)S(1)} collective-permute-done((bf16[256,1024]{1,0:T(8,128)(2,1)S(1)}, bf16[256,1024]{1,0:T(8,128)(2,1)S(1)}, u32[]{:S(2)}, u32[]{:S(2)}) %collective-permute-start) | collective-permute-done | bytes 524320 | tf_op jit(solution)/shard_map/ppermute | solution.py:28
  34.9 0.0 copy-start.6
  34.9 3.3 %collective-permute-start.2 = (bf16[256,1024]{1,0:T(8,128)(2,1)S(1)}, bf16[256,1024]{1,0:T(8,128)(2,1)S(1)}, u32[]{:S(2)}, u32[]{:S(2)}) collective-permute-start(bf16[256,1024]{1,0:T(8,128)(2,1)S(1)} %collective-permute-done.refs_3_.refs_4_), channel_id=1, source_target_pairs={{0,16},{16,0},{1,17},{17,1},{2,18},{18,2},{3,19},{19,3},{4,20},{20... | collective-permute-start | bytes 1572872 | tf_op jit(solution)/shard_map/ppermute | solution.py:33
  38.2 0.0 collective-permute-done.1.refs_4_.refs_5_
  38.2 0.0 copy-start.7
  38.2 1.9 %collective-permute-start.3 = (bf16[256,1024]{1,0:T(8,128)(2,1)S(1)}, bf16[256,1024]{1,0:T(8,128)(2,1)}, u32[]{:S(2)}, u32[]{:S(2)}) collective-permute-start(bf16[256,1024]{1,0:T(8,128)(2,1)S(1)} %collective-permute-done.1.refs_4_.refs_5_), channel_id=1, source_target_pairs={{0,16},{16,0},{1,17},{17,1},{2,18},{18,2},{3,19},{19,3},{4,20},{20... | collective-permute-start | bytes 1572872 | tf_op jit(solution)/shard_map/ppermute | solution.py:33
  40.2 0.0 collective-permute-done.2.refs_5_.refs_6_
  40.2 0.0 copy-done.7
  40.2 0.0 copy-start.8
  40.2 0.8 copy-done.8
  41.0 1.2 collective-permute-done.3.refs_6_.refs_7_
  42.2 4.2 %all-to-all-done.refs_1_ = bf16[8,72,1024]{2,1,0:T(8,128)(2,1)} async-done(((bf16[8,72,1024]{2,1,0:T(8,128)(2,1)}), bf16[8,72,1024]{2,1,0:T(8,128)(2,1)}, u32[]{:S(2)}, u32[]{:S(2)}) %all-to-all-start) | async-done | bytes 1179680 | tf_op jit(solution)/shard_map/all_to_all | solution.py:284
  46.4 0.0 copy-done.6
  46.4 5.8 %shard_map.86 = (bf16[512,1024]{1,0:T(8,128)(2,1)S(1)}, bf16[256,1152]{1,0:T(8,128)(2,1)S(1)}, bf16[256,1152]{1,0:T(8,128)(2,1)S(1)}) custom-call(s32[4]{0:T(128)S(1)} %pad_add_fusion.refs_0_, bf16[8,72,1024]{2,1,0:T(8,128)(2,1)} %all-to-all-done.refs_1_, bf16[512,1024]{1,0:T(8,128)(2,1)} %gather_fusion, bf16[256,1024]{1,0:T(8,128)(2,1)} %copy-done.6, ...), custom_call_target="tpu_custom_call" | custom-call | flops 1610612736 | bytes 6291456 | tf_op jit(solution)/shard_map/pallas_call | solution.py:74
  52.2 2.4 %collective-permute-start.7 = (bf16[256,1152]{1,0:T(8,128)(2,1)S(1)}, bf16[256,1152]{1,0:T(8,128)(2,1)S(1)}, u32[]{:S(2)}, u32[]{:S(2)}) collective-permute-start(bf16[256,1152]{1,0:T(8,128)(2,1)S(1)} %get-tuple-element.32), channel_id=1, source_target_pairs={{0,16},{16,0},{1,17},{17,1},{2,18},{18,2},{3,19},{19,3},{4,20},{20... | collective-permute-start | bytes 1769480 | tf_op jit(solution)/shard_map/ppermute | solution.py:33
  54.6 3.6 %shard_map.88 = (bf16[256,1024]{1,0:T(8,128)(2,1)}, f32[8,128]{1,0:T(8,128)S(1)}) custom-call(s32[4]{0:T(128)S(1)} %pad_add_fusion.refs_0_, bf16[512,1024]{1,0:T(8,128)(2,1)S(1)} %get-tuple-element.23.refs_1_, bf16[512,1024]{1,0:T(8,128)(2,1)} %refs_3_.1, bf16[256,1024]{1,0:T(8,128)(2,1)} %copy-done.6, bf16[256,1024]{1,0:T(8,128)(2,1)} %copy-done.7, ...), custom_call_target="tpu_custom_call" | custom-call | flops 536870912 | bytes 3145728 | tf_op jit(solution)/shard_map/pallas_call | solution.py:74
  58.3 2.1 %collective-permute-start.4 = (bf16[256,1024]{1,0:T(8,128)(2,1)}, bf16[256,1024]{1,0:T(8,128)(2,1)}, u32[]{:S(2)}, u32[]{:S(2)}) collective-permute-start(bf16[256,1024]{1,0:T(8,128)(2,1)} %get-tuple-element.24), channel_id=1, source_target_pairs={{0,2},{2,0},{4,6},{6,4},{8,10},{10,8},{12,14},{14,12},{1,3},{3,1},... | collective-permute-start | bytes 1572872 | tf_op jit(solution)/shard_map/ppermute | solution.py:33
  60.4 0.0 collective-permute-done.7.refs_2_
  60.4 1.5 %shard_map.92 = bf16[256,1152]{1,0:T(8,128)(2,1)} custom-call(s32[4]{0:T(128)S(1)} %pad_add_fusion.refs_0_, bf16[256,1152]{1,0:T(8,128)(2,1)S(1)} %get-tuple-element.31.refs_1_, bf16[256,1152]{1,0:T(8,128)(2,1)S(1)} %collective-permute-done.7.refs_2_, f32[8,128]{1,0:T(8,128)S(1)} %get-tuple-element.33.refs_3_), custom_call_target="tpu_custom_call" | custom-call | bytes 2097152 | tf_op jit(solution)/shard_map/pallas_call | solution.py:74
  62.0 9.7 %all-to-all-start.1 = ((bf16[32,8,1152]{2,1,0:T(8,128)(2,1)}), bf16[32,8,1152]{2,1,0:T(8,128)(2,1)S(1)}, u32[]{:S(2)}, u32[]{:S(2)}) async-start(bf16[32,8,1152]{2,1,0:T(8,128)(2,1)} %bitcast.10), calls=%async_computation.1 | async-start | bytes 1179648 | tf_op jit(solution)/shard_map/all_to_all | solution.py:331
  71.7 2.9 %shard_map.87.refs_1_ = bf16[256,1024]{1,0:T(8,128)(2,1)S(1)} custom-call(s32[4]{0:T(128)S(1)} %pad_add_fusion.refs_0_, bf16[512,1024]{1,0:T(8,128)(2,1)S(1)} %get-tuple-element.23.refs_1_, bf16[512,1024]{1,0:T(8,128)(2,1)} %refs_3_.1, bf16[256,1024]{1,0:T(8,128)(2,1)} %copy-done.6, bf16[256,1024]{1,0:T(8,128)(2,1)} %copy-done.7, ...), custom_call_target="tpu_custom_call" | custom-call | flops 68719476736 | bytes 3145728 | tf_op jit(solution)/shard_map/pallas_call | solution.py:74
  74.5 0.0 collective-permute-done.4.refs_2_
  74.5 2.0 %shard_map.89 = (bf16[128,1024]{1,0:T(8,128)(2,1)}, bf16[128,1024]{1,0:T(8,128)(2,1)}, f32[8,128]{1,0:T(8,128)S(1)}) custom-call(s32[4]{0:T(128)S(1)} %pad_add_fusion.refs_0_, bf16[256,1024]{1,0:T(8,128)(2,1)S(1)} %shard_map.87.refs_1_, bf16[256,1024]{1,0:T(8,128)(2,1)} %collective-permute-done.4.refs_2_), custom_call_target="tpu_custom_call" | custom-call | bytes 1048576 | tf_op jit(solution)/shard_map/pallas_call | solution.py:74
  76.5 3.0 %collective-permute-start.5 = (bf16[128,1024]{1,0:T(8,128)(2,1)}, bf16[128,1024]{1,0:T(8,128)(2,1)S(1)}, u32[]{:S(2)}, u32[]{:S(2)}) collective-permute-start(bf16[128,1024]{1,0:T(8,128)(2,1)} %get-tuple-element.26), channel_id=1, source_target_pairs={{0,6},{2,4},{4,2},{6,0},{8,14},{10,12},{12,10},{14,8},{1,7},{3,5},... | collective-permute-start | bytes 786440 | tf_op jit(solution)/shard_map/ppermute | solution.py:33
  79.5 10.1 %all-to-all-done.1.refs_1_ = bf16[32,8,1152]{2,1,0:T(8,128)(2,1)S(1)} async-done(((bf16[32,8,1152]{2,1,0:T(8,128)(2,1)}), bf16[32,8,1152]{2,1,0:T(8,128)(2,1)S(1)}, u32[]{:S(2)}, u32[]{:S(2)}) %all-to-all-start.1) | async-done | bytes 589856 | tf_op jit(solution)/shard_map/all_to_all | solution.py:331
  89.5 0.0 copy-start.4
  89.5 3.2 %shard_map.93 = (f32[8,8,1024]{2,1,0:T(8,128)}, f32[8,1024]{1,0:T(8,128)S(1)}) custom-call(s32[4]{0:T(128)S(1)} %pad_add_fusion.refs_0_, bf16[32,8,1152]{2,1,0:T(8,128)(2,1)S(1)} %all-to-all-done.1.refs_1_, f32[8,128]{1,0:T(8,128)S(1)} %get-tuple-element.34.refs_2_, bf16[512,1024]{1,0:T(8,128)(2,1)} %refs_3_.1, bf16[256,1024]{1,0:T(8,128)(2,1)} %copy-done.6, ...), custom_call_target="tpu_custom_call" | custom-call | flops 68719476736 | bytes 3145728 | tf_op jit(solution)/shard_map/pallas_call | solution.py:74
  92.7 3.4 %all-to-all-start.2 = ((f32[8,8,1024]{2,1,0:T(8,128)}), f32[8,8,1024]{2,1,0:T(8,128)S(1)}, u32[]{:S(2)}, u32[]{:S(2)}) async-start(f32[8,8,1024]{2,1,0:T(8,128)} %get-tuple-element.35), calls=%async_computation.2 | async-start | bytes 524288 | tf_op jit(solution)/shard_map/all_to_all | solution.py:358
  96.2 0.0 collective-permute-done.5.refs_2_
  96.2 0.0 copy-done.4
  96.2 1.3 shard_map.90
  97.5 0.0 copy-start.2
  97.5 0.6 copy-done.2
  98.1 0.0 copy-start.10
  98.1 0.0 copy-start.1
  98.1 0.0 copy-start.3
  98.1 8.1 %all-to-all-done.2.refs_1_ = f32[8,8,1024]{2,1,0:T(8,128)S(1)} async-done(((f32[8,8,1024]{2,1,0:T(8,128)}), f32[8,8,1024]{2,1,0:T(8,128)S(1)}, u32[]{:S(2)}, u32[]{:S(2)}) %all-to-all-start.2) | async-done | bytes 262176 | tf_op jit(solution)/shard_map/all_to_all | solution.py:358
  106.2 1.4 %shard_map.94 = bf16[32,8,1024]{2,1,0:T(8,128)(2,1)} custom-call(s32[4]{0:T(128)S(1)} %pad_add_fusion.refs_0_, f32[8,8,1024]{2,1,0:T(8,128)S(1)} %all-to-all-done.2.refs_1_, f32[8,1024]{1,0:T(8,128)S(1)} %get-tuple-element.36.refs_2_, f32[8,128]{1,0:T(8,128)} %copy-done.2), custom_call_target="tpu_custom_call" | custom-call | bytes 1048576 | tf_op jit(solution)/shard_map/pallas_call | solution.py:74
  107.7 5.5 %all-to-all-start.3 = ((bf16[32,8,1024]{2,1,0:T(8,128)(2,1)}), bf16[32,8,1024]{2,1,0:T(8,128)(2,1)S(1)}, u32[]{:S(2)}, u32[]{:S(2)}) async-start(bf16[32,8,1024]{2,1,0:T(8,128)(2,1)} %shard_map.94), calls=%async_computation.3 | async-start | bytes 1048576 | tf_op jit(solution)/shard_map/all_to_all | solution.py:363
  113.2 0.0 copy-done.10
  113.2 1.9 %collective-permute-start.6 = (bf16[64,1024]{1,0:T(8,128)(2,1)S(1)}, bf16[64,1024]{1,0:T(8,128)(2,1)S(1)}, u32[]{:S(2)}, u32[]{:S(2)}) collective-permute-start(bf16[64,1024]{1,0:T(8,128)(2,1)S(1)} %copy-done.10), channel_id=1, source_target_pairs={{0,14},{2,12},{4,10},{6,8},{8,6},{10,4},{12,2},{14,0},{1,15},{3,13... | collective-permute-start | bytes 393224 | tf_op jit(solution)/shard_map/ppermute | solution.py:33
  115.1 6.4 %collective-permute-done.6.refs_3_ = bf16[64,1024]{1,0:T(8,128)(2,1)S(1)} collective-permute-done((bf16[64,1024]{1,0:T(8,128)(2,1)S(1)}, bf16[64,1024]{1,0:T(8,128)(2,1)S(1)}, u32[]{:S(2)}, u32[]{:S(2)}) %collective-permute-start.6) | collective-permute-done | bytes 131104 | tf_op jit(solution)/shard_map/ppermute | solution.py:33
  121.5 0.0 copy-done.1
  121.5 0.0 copy-done.3
  121.5 1.3 shard_map.91
  122.8 3.9 %all-to-all-done.3 = bf16[32,8,1024]{2,1,0:T(8,128)(2,1)S(1)} async-done(((bf16[32,8,1024]{2,1,0:T(8,128)(2,1)}), bf16[32,8,1024]{2,1,0:T(8,128)(2,1)S(1)}, u32[]{:S(2)}, u32[]{:S(2)}) %all-to-all-start.3) | async-done | bytes 524320 | tf_op jit(solution)/shard_map/all_to_all | solution.py:363
  126.7 0.6 shard_map.95.refs_2_
  127.2 6.9 %collective-permute-start.8 = (bf16[256,1024]{1,0:T(8,128)(2,1)S(1)}, bf16[256,1024]{1,0:T(8,128)(2,1)S(1)}, u32[]{:S(2)}, u32[]{:S(2)}) collective-permute-start(bf16[256,1024]{1,0:T(8,128)(2,1)S(1)} %shard_map.95.refs_2_), channel_id=1, source_target_pairs={{0,16},{16,0},{1,17},{17,1},{2,18},{18,2},{3,19},{19,3},{4,20},{20... | collective-permute-start | bytes 1572872 | tf_op jit(solution)/shard_map/ppermute | solution.py:33
  134.1 0.9 shard_map.96
  135.1 0.6 collective-permute-done.8.refs_2_
  135.7 1.6 %shard_map.97 = (f32[64,512]{1,0:T(8,128)}, bf16[16,1024]{1,0:T(8,128)(2,1)}) custom-call(s32[4]{0:T(128)S(1)} %pad_add_fusion.refs_0_, bf16[64,1024]{1,0:T(8,128)(2,1)S(1)} %get-tuple-element.30.refs_1_, bf16[256,1024]{1,0:T(8,128)(2,1)S(1)} %collective-permute-done.8.refs_2_, bf16[16,512]{1,0:T(8,128)(2,1)S(1)} %get-tuple-element.38.refs_2_.refs_3_, ...), custom_call_target="tpu_custom_call" | custom-call | bytes 1048576 | tf_op jit(solution)/shard_map/pallas_call | solution.py:74
  (4 shorter events, 0.1 us)
Async XLA Ops:
  0.6 13.7 %copy-start = (bf16[768,1024]{1,0:T(8,128)(2,1)S(1)}, bf16[768,1024]{1,0:T(8,128)(2,1)}, u32[]{:S(2)}) copy-start(bf16[768,1024]{1,0:T(8,128)(2,1)} %param.8) | copy-start | bytes 4718596
  0.7 13.5 %copy-start.9 = (s32[512]{0:T(512)S(1)}, s32[512]{0:T(512)}, u32[]{:S(2)}) copy-start(s32[512]{0:T(512)} %param.9) | copy-start | bytes 6148
  3.4 43.0 %all-to-all-start = ((bf16[8,72,1024]{2,1,0:T(8,128)(2,1)}), bf16[8,72,1024]{2,1,0:T(8,128)(2,1)}, u32[]{:S(2)}, u32[]{:S(2)}) async-start(bf16[8,72,1024]{2,1,0:T(8,128)(2,1)} %shard_map.85), calls=%async_computation | async-start | bytes 2359296 | tf_op jit(solution)/shard_map/all_to_all | solution.py:284
  14.3 2.8 %copy-start.5 = (bf16[512,1024]{1,0:T(8,128)(2,1)S(1)}, bf16[512,1024]{1,0:T(8,128)(2,1)}, u32[]{:S(2)}) copy-start(bf16[512,1024]{1,0:T(8,128)(2,1)} %refs_3_.1) | copy-start | bytes 3145732
  18.3 16.5 %collective-permute-start = (bf16[256,1024]{1,0:T(8,128)(2,1)S(1)}, bf16[256,1024]{1,0:T(8,128)(2,1)S(1)}, u32[]{:S(2)}, u32[]{:S(2)}) collective-permute-start(bf16[256,1024]{1,0:T(8,128)(2,1)S(1)} %pad_maximum_fusion), channel_id=1, source_target_pairs={{0,1},{1,128},{128,129},{129,256},{256,257},{257,384},{384,385},{3... | collective-permute-start | bytes 1572872 | tf_op jit(solution)/shard_map/ppermute | solution.py:28
  21.6 16.6 %collective-permute-start.1 = (bf16[256,1024]{1,0:T(8,128)(2,1)S(1)}, bf16[256,1024]{1,0:T(8,128)(2,1)S(1)}, u32[]{:S(2)}, u32[]{:S(2)}) collective-permute-start(bf16[256,1024]{1,0:T(8,128)(2,1)S(1)} %pad_maximum_fusion.1), channel_id=1, source_target_pairs={{0,385},{1,0},{128,1},{129,128},{256,129},{257,256},{384,257},{385... | collective-permute-start | bytes 1572872 | tf_op jit(solution)/shard_map/ppermute | solution.py:28
  34.9 11.6 %copy-start.6 = (bf16[256,1024]{1,0:T(8,128)(2,1)}, bf16[256,1024]{1,0:T(8,128)(2,1)S(1)}, u32[]{:S(2)}) copy-start(bf16[256,1024]{1,0:T(8,128)(2,1)S(1)} %collective-permute-done.refs_3_.refs_4_) | copy-start | bytes 1572868
  34.9 5.3 %collective-permute-start.2 = (bf16[256,1024]{1,0:T(8,128)(2,1)S(1)}, bf16[256,1024]{1,0:T(8,128)(2,1)S(1)}, u32[]{:S(2)}, u32[]{:S(2)}) collective-permute-start(bf16[256,1024]{1,0:T(8,128)(2,1)S(1)} %collective-permute-done.refs_3_.refs_4_), channel_id=1, source_target_pairs={{0,16},{16,0},{1,17},{17,1},{2,18},{18,2},{3,19},{19,3},{4,20},{20... | collective-permute-start | bytes 1572872 | tf_op jit(solution)/shard_map/ppermute | solution.py:33
  38.2 2.0 %copy-start.7 = (bf16[256,1024]{1,0:T(8,128)(2,1)}, bf16[256,1024]{1,0:T(8,128)(2,1)S(1)}, u32[]{:S(2)}) copy-start(bf16[256,1024]{1,0:T(8,128)(2,1)S(1)} %collective-permute-done.1.refs_4_.refs_5_) | copy-start | bytes 1572868
  38.2 3.9 %collective-permute-start.3 = (bf16[256,1024]{1,0:T(8,128)(2,1)S(1)}, bf16[256,1024]{1,0:T(8,128)(2,1)}, u32[]{:S(2)}, u32[]{:S(2)}) collective-permute-start(bf16[256,1024]{1,0:T(8,128)(2,1)S(1)} %collective-permute-done.1.refs_4_.refs_5_), channel_id=1, source_target_pairs={{0,16},{16,0},{1,17},{17,1},{2,18},{18,2},{3,19},{19,3},{4,20},{20... | collective-permute-start | bytes 1572872 | tf_op jit(solution)/shard_map/ppermute | solution.py:33
  40.2 0.8 copy-start.8
  52.2 8.2 %collective-permute-start.7 = (bf16[256,1152]{1,0:T(8,128)(2,1)S(1)}, bf16[256,1152]{1,0:T(8,128)(2,1)S(1)}, u32[]{:S(2)}, u32[]{:S(2)}) collective-permute-start(bf16[256,1152]{1,0:T(8,128)(2,1)S(1)} %get-tuple-element.32), channel_id=1, source_target_pairs={{0,16},{16,0},{1,17},{17,1},{2,18},{18,2},{3,19},{19,3},{4,20},{20... | collective-permute-start | bytes 1769480 | tf_op jit(solution)/shard_map/ppermute | solution.py:33
  58.3 16.2 %collective-permute-start.4 = (bf16[256,1024]{1,0:T(8,128)(2,1)}, bf16[256,1024]{1,0:T(8,128)(2,1)}, u32[]{:S(2)}, u32[]{:S(2)}) collective-permute-start(bf16[256,1024]{1,0:T(8,128)(2,1)} %get-tuple-element.24), channel_id=1, source_target_pairs={{0,2},{2,0},{4,6},{6,4},{8,10},{10,8},{12,14},{14,12},{1,3},{3,1},... | collective-permute-start | bytes 1572872 | tf_op jit(solution)/shard_map/ppermute | solution.py:33
  62.0 27.6 %all-to-all-start.1 = ((bf16[32,8,1152]{2,1,0:T(8,128)(2,1)}), bf16[32,8,1152]{2,1,0:T(8,128)(2,1)S(1)}, u32[]{:S(2)}, u32[]{:S(2)}) async-start(bf16[32,8,1152]{2,1,0:T(8,128)(2,1)} %bitcast.10), calls=%async_computation.1 | async-start | bytes 1179648 | tf_op jit(solution)/shard_map/all_to_all | solution.py:331
  76.5 19.7 %collective-permute-start.5 = (bf16[128,1024]{1,0:T(8,128)(2,1)}, bf16[128,1024]{1,0:T(8,128)(2,1)S(1)}, u32[]{:S(2)}, u32[]{:S(2)}) collective-permute-start(bf16[128,1024]{1,0:T(8,128)(2,1)} %get-tuple-element.26), channel_id=1, source_target_pairs={{0,6},{2,4},{4,2},{6,0},{8,14},{10,12},{12,10},{14,8},{1,7},{3,5},... | collective-permute-start | bytes 786440 | tf_op jit(solution)/shard_map/ppermute | solution.py:33
  89.5 6.6 %copy-start.4 = (bf16[128,1024]{1,0:T(8,128)(2,1)S(1)}, bf16[128,1024]{1,0:T(8,128)(2,1)}, u32[]{:S(2)}) copy-start(bf16[128,1024]{1,0:T(8,128)(2,1)} %get-tuple-element.25.refs_1_) | copy-start | bytes 786436
  92.7 13.5 %all-to-all-start.2 = ((f32[8,8,1024]{2,1,0:T(8,128)}), f32[8,8,1024]{2,1,0:T(8,128)S(1)}, u32[]{:S(2)}, u32[]{:S(2)}) async-start(f32[8,8,1024]{2,1,0:T(8,128)} %get-tuple-element.35), calls=%async_computation.2 | async-start | bytes 524288 | tf_op jit(solution)/shard_map/all_to_all | solution.py:358
  97.5 0.6 copy-start.2
  98.1 15.1 %copy-start.10 = (bf16[64,1024]{1,0:T(8,128)(2,1)S(1)}, bf16[64,1024]{1,0:T(8,128)(2,1)}, u32[]{:S(2)}) copy-start(bf16[64,1024]{1,0:T(8,128)(2,1)} %get-tuple-element.28) | copy-start | bytes 393220
  98.1 23.4 %copy-start.1 = (bf16[64,1024]{1,0:T(8,128)(2,1)S(1)}, bf16[64,1024]{1,0:T(8,128)(2,1)}, u32[]{:S(2)}) copy-start(bf16[64,1024]{1,0:T(8,128)(2,1)} %get-tuple-element.27.refs_2_) | copy-start | bytes 393220
  98.1 23.4 %copy-start.3 = (s32[512]{0:T(512)S(1)}, s32[512]{0:T(512)}, u32[]{:S(2)}) copy-start(s32[512]{0:T(512)} %param.11) | copy-start | bytes 6148
  107.7 19.0 %all-to-all-start.3 = ((bf16[32,8,1024]{2,1,0:T(8,128)(2,1)}), bf16[32,8,1024]{2,1,0:T(8,128)(2,1)S(1)}, u32[]{:S(2)}, u32[]{:S(2)}) async-start(bf16[32,8,1024]{2,1,0:T(8,128)(2,1)} %shard_map.94), calls=%async_computation.3 | async-start | bytes 1048576 | tf_op jit(solution)/shard_map/all_to_all | solution.py:363
  113.2 8.3 %collective-permute-start.6 = (bf16[64,1024]{1,0:T(8,128)(2,1)S(1)}, bf16[64,1024]{1,0:T(8,128)(2,1)S(1)}, u32[]{:S(2)}, u32[]{:S(2)}) collective-permute-start(bf16[64,1024]{1,0:T(8,128)(2,1)S(1)} %copy-done.10), channel_id=1, source_target_pairs={{0,14},{2,12},{4,10},{6,8},{8,6},{10,4},{12,2},{14,0},{1,15},{3,13... | collective-permute-start | bytes 393224 | tf_op jit(solution)/shard_map/ppermute | solution.py:33
  127.2 8.4 %collective-permute-start.8 = (bf16[256,1024]{1,0:T(8,128)(2,1)S(1)}, bf16[256,1024]{1,0:T(8,128)(2,1)S(1)}, u32[]{:S(2)}, u32[]{:S(2)}) collective-permute-start(bf16[256,1024]{1,0:T(8,128)(2,1)S(1)} %shard_map.95.refs_2_), channel_id=1, source_target_pairs={{0,16},{16,0},{1,17},{17,1},{2,18},{18,2},{3,19},{19,3},{4,20},{20... | collective-permute-start | bytes 1572872 | tf_op jit(solution)/shard_map/ppermute | solution.py:33

commit v9 on v8

--- a/solution.py
+++ b/solution.py
@@ -202,7 +202,7 @@
     for copy in copies:
         copy.wait()
     result = jnp.dot(both, maps[...], preferred_element_type=f32)
-    mapped[...] = jnp.broadcast_to((result[:share] + result[share:])[None], mapped.shape)
+    mapped[...] = jnp.broadcast_to((result[:share] + result[share:])[None], mapped.shape).astype(bf16)
 
 
 def pair_kernel(place, keep, theirs, _, paired):
@@ -210,7 +210,7 @@
 
 
 def means_kernel(place, parts, number, _, sent):
-    means = jnp.sum(parts[...], axis=0) / number[...]
+    means = jnp.sum(parts[...].astype(f32), axis=0) / number[...]
     sent[...] = jnp.broadcast_to(means[None], sent.shape).astype(bf16)
 
 
@@ -347,7 +347,7 @@
     kept, leave, done = merge(stay, leave, 1, 0)
     mapped, number = call(
         cluster_kernel,
-        (array((ring, share, rank_width), f32), array((share, rank_width), f32)),
+        (array((ring, share, rank_width), bf16), array((share, rank_width), f32)),
         8,
         5,
         store(2 * count, rank_width),

time: 138 us -> 135 us (0.978)
  waiting for transfers between devices: 44 us -> 41.7 us
    all_to_all x1, waiting for transfers between devices: 8.15 us -> 5.74 us  [body(): over = lax.all_to_all(mapped, 'z', 0, 0)]
where the time goes in v9:
time: 135 us; the launch traced here: 134 us
  starting transfers between devices  57.6 us (43%)
  waiting for transfers between devices  41.7 us (31%)
  Pallas kernels  28.6 us (21%)
  local copies, waits for them, and re-layouts  5.38 us (4%)
    pallas_call x13, Pallas kernels, call(): made(*args[:near], *(pltpu.with_memory_space_constraint(a, pltpu.HBM) for...  28.6 us
    ppermute x7, starting transfers between devices, flip(): return lax.ppermute(value, axis, [(i, i ^ bit) for i in range(size)])  21.5 us
    all_to_all x1, starting transfers between devices, body(): spread = lax.all_to_all(block, 'z', 0, 0)  10.9 us
    all_to_all x1, waiting for transfers between devices, body(): gathered = lax.all_to_all(paired.reshape(peers, share, -1), PLANE, 0, 0)  10.1 us
    all_to_all x1, starting transfers between devices, body(): gathered = lax.all_to_all(paired.reshape(peers, share, -1), PLANE, 0, 0)  9.69 us
    ppermute x2, waiting for transfers between devices, hop(): lax.ppermute(value, axis, [(i, (i + by) % size) for i in range(size)])  9.45 us
    ppermute x7, waiting for transfers between devices, flip(): return lax.ppermute(value, axis, [(i, i ^ bit) for i in range(size)])  8.33 us
    ppermute x2, starting transfers between devices, hop(): lax.ppermute(value, axis, [(i, (i + by) % size) for i in range(size)])  7.02 us
  transfers between devices with their start and end apart: 13, of which 8 were waited for; matrix products, arithmetic and copies ran while one was open for 3% of the time, Pallas kernels for 12%

profile of v9, /device:TPU:1, one launch (start us, length us, event | category | flops | bytes accessed | tf_op | source)
XLA Modules:
  0.0 134.4 jit_solution(457212531195943300)
XLA Ops:
  0.6 0.0 copy-start
  0.7 0.1 pad_add_fusion.refs_0_
  0.7 0.0 copy-start.9
  0.7 2.6 %shard_map.85 = bf16[8,72,1024]{2,1,0:T(8,128)(2,1)} custom-call(s32[4]{0:T(128)S(1)} %pad_add_fusion.refs_0_, bf16[64,1024]{1,0:T(8,128)(2,1)} %refs_1_.1, s32[1,64]{1,0:T(1,128)} %bitcast.11), custom_call_target="tpu_custom_call" | custom-call | bytes 2097152 | tf_op jit(solution)/shard_map/pallas_call | solution.py:74
  3.4 10.9 %all-to-all-start = ((bf16[8,72,1024]{2,1,0:T(8,128)(2,1)}), bf16[8,72,1024]{2,1,0:T(8,128)(2,1)}, u32[]{:S(2)}, u32[]{:S(2)}) async-start(bf16[8,72,1024]{2,1,0:T(8,128)(2,1)} %shard_map.85), calls=%async_computation | async-start | bytes 2359296 | tf_op jit(solution)/shard_map/all_to_all | solution.py:284
  14.3 0.0 copy-done.9
  14.3 0.0 copy-done
  14.3 0.0 copy-start.5
  14.3 2.8 %gather_fusion = bf16[512,1024]{1,0:T(8,128)(2,1)} fusion(bf16[768,1024]{1,0:T(8,128)(2,1)S(1)} %copy-done, s32[1024]{0:T(1024)S(1)} %pad_clamp_fusion), kind=kCustom, calls=%fused_computation | custom fusion | bytes 2099200 | tf_op jit(solution)/shard_map/gather | solution.py:286
  17.1 0.0 copy-done.5
  17.1 1.2 constant_dynamic-slice_fusion
  18.3 3.2 %collective-permute-start = (bf16[256,1024]{1,0:T(8,128)(2,1)S(1)}, bf16[256,1024]{1,0:T(8,128)(2,1)S(1)}, u32[]{:S(2)}, u32[]{:S(2)}) collective-permute-start(bf16[256,1024]{1,0:T(8,128)(2,1)S(1)} %pad_maximum_fusion), channel_id=1, source_target_pairs={{0,1},{1,128},{128,129},{129,256},{256,257},{257,384},{384,385},{3... | collective-permute-start | bytes 1572872 | tf_op jit(solution)/shard_map/ppermute | solution.py:28
  21.6 3.8 %collective-permute-start.1 = (bf16[256,1024]{1,0:T(8,128)(2,1)S(1)}, bf16[256,1024]{1,0:T(8,128)(2,1)S(1)}, u32[]{:S(2)}, u32[]{:S(2)}) collective-permute-start(bf16[256,1024]{1,0:T(8,128)(2,1)S(1)} %pad_maximum_fusion.1), channel_id=1, source_target_pairs={{0,385},{1,0},{128,1},{129,128},{256,129},{257,256},{384,257},{385... | collective-permute-start | bytes 1572872 | tf_op jit(solution)/shard_map/ppermute | solution.py:28
  25.4 9.4 %collective-permute-done.refs_3_.refs_4_ = bf16[256,1024]{1,0:T(8,128)(2,1)S(1)} collective-permute-done((bf16[256,1024]{1,0:T(8,128)(2,1)S(1)}, bf16[256,1024]{1,0:T(8,128)(2,1)S(1)}, u32[]{:S(2)}, u32[]{:S(2)}) %collective-permute-start) | collective-permute-done | bytes 524320 | tf_op jit(solution)/shard_map/ppermute | solution.py:28
  34.9 0.0 copy-start.6
  34.9 3.3 %collective-permute-start.2 = (bf16[256,1024]{1,0:T(8,128)(2,1)S(1)}, bf16[256,1024]{1,0:T(8,128)(2,1)S(1)}, u32[]{:S(2)}, u32[]{:S(2)}) collective-permute-start(bf16[256,1024]{1,0:T(8,128)(2,1)S(1)} %collective-permute-done.refs_3_.refs_4_), channel_id=1, source_target_pairs={{0,16},{16,0},{1,17},{17,1},{2,18},{18,2},{3,19},{19,3},{4,20},{20... | collective-permute-start | bytes 1572872 | tf_op jit(solution)/shard_map/ppermute | solution.py:33
  38.2 0.0 collective-permute-done.1.refs_4_.refs_5_
  38.2 0.0 copy-start.7
  38.2 1.9 %collective-permute-start.3 = (bf16[256,1024]{1,0:T(8,128)(2,1)S(1)}, bf16[256,1024]{1,0:T(8,128)(2,1)}, u32[]{:S(2)}, u32[]{:S(2)}) collective-permute-start(bf16[256,1024]{1,0:T(8,128)(2,1)S(1)} %collective-permute-done.1.refs_4_.refs_5_), channel_id=1, source_target_pairs={{0,16},{16,0},{1,17},{17,1},{2,18},{18,2},{3,19},{19,3},{4,20},{20... | collective-permute-start | bytes 1572872 | tf_op jit(solution)/shard_map/ppermute | solution.py:33
  40.2 0.0 collective-permute-done.2.refs_5_.refs_6_
  40.2 0.0 copy-done.7
  40.2 0.0 copy-start.8
  40.2 0.8 copy-done.8
  41.0 1.2 collective-permute-done.3.refs_6_.refs_7_
  42.2 4.2 %all-to-all-done.refs_1_ = bf16[8,72,1024]{2,1,0:T(8,128)(2,1)} async-done(((bf16[8,72,1024]{2,1,0:T(8,128)(2,1)}), bf16[8,72,1024]{2,1,0:T(8,128)(2,1)}, u32[]{:S(2)}, u32[]{:S(2)}) %all-to-all-start) | async-done | bytes 1179680 | tf_op jit(solution)/shard_map/all_to_all | solution.py:284
  46.4 0.0 copy-done.6
  46.4 5.8 %shard_map.86 = (bf16[512,1024]{1,0:T(8,128)(2,1)S(1)}, bf16[256,1152]{1,0:T(8,128)(2,1)S(1)}, bf16[256,1152]{1,0:T(8,128)(2,1)S(1)}) custom-call(s32[4]{0:T(128)S(1)} %pad_add_fusion.refs_0_, bf16[8,72,1024]{2,1,0:T(8,128)(2,1)} %all-to-all-done.refs_1_, bf16[512,1024]{1,0:T(8,128)(2,1)} %gather_fusion, bf16[256,1024]{1,0:T(8,128)(2,1)} %copy-done.6, ...), custom_call_target="tpu_custom_call" | custom-call | flops 1610612736 | bytes 6291456 | tf_op jit(solution)/shard_map/pallas_call | solution.py:74
  52.2 2.4 %collective-permute-start.7 = (bf16[256,1152]{1,0:T(8,128)(2,1)S(1)}, bf16[256,1152]{1,0:T(8,128)(2,1)S(1)}, u32[]{:S(2)}, u32[]{:S(2)}) collective-permute-start(bf16[256,1152]{1,0:T(8,128)(2,1)S(1)} %get-tuple-element.32), channel_id=1, source_target_pairs={{0,16},{16,0},{1,17},{17,1},{2,18},{18,2},{3,19},{19,3},{4,20},{20... | collective-permute-start | bytes 1769480 | tf_op jit(solution)/shard_map/ppermute | solution.py:33
  54.6 3.6 %shard_map.88 = (bf16[256,1024]{1,0:T(8,128)(2,1)}, f32[8,128]{1,0:T(8,128)S(1)}) custom-call(s32[4]{0:T(128)S(1)} %pad_add_fusion.refs_0_, bf16[512,1024]{1,0:T(8,128)(2,1)S(1)} %get-tuple-element.23.refs_1_, bf16[512,1024]{1,0:T(8,128)(2,1)} %refs_3_.1, bf16[256,1024]{1,0:T(8,128)(2,1)} %copy-done.6, bf16[256,1024]{1,0:T(8,128)(2,1)} %copy-done.7, ...), custom_call_target="tpu_custom_call" | custom-call | flops 536870912 | bytes 3145728 | tf_op jit(solution)/shard_map/pallas_call | solution.py:74
  58.3 2.1 %collective-permute-start.4 = (bf16[256,1024]{1,0:T(8,128)(2,1)}, bf16[256,1024]{1,0:T(8,128)(2,1)}, u32[]{:S(2)}, u32[]{:S(2)}) collective-permute-start(bf16[256,1024]{1,0:T(8,128)(2,1)} %get-tuple-element.24), channel_id=1, source_target_pairs={{0,2},{2,0},{4,6},{6,4},{8,10},{10,8},{12,14},{14,12},{1,3},{3,1},... | collective-permute-start | bytes 1572872 | tf_op jit(solution)/shard_map/ppermute | solution.py:33
  60.4 0.0 collective-permute-done.7.refs_2_
  60.4 1.5 %shard_map.92 = bf16[256,1152]{1,0:T(8,128)(2,1)} custom-call(s32[4]{0:T(128)S(1)} %pad_add_fusion.refs_0_, bf16[256,1152]{1,0:T(8,128)(2,1)S(1)} %get-tuple-element.31.refs_1_, bf16[256,1152]{1,0:T(8,128)(2,1)S(1)} %collective-permute-done.7.refs_2_, f32[8,128]{1,0:T(8,128)S(1)} %get-tuple-element.33.refs_3_), custom_call_target="tpu_custom_call" | custom-call | bytes 2097152 | tf_op jit(solution)/shard_map/pallas_call | solution.py:74
  62.0 9.7 %all-to-all-start.1 = ((bf16[32,8,1152]{2,1,0:T(8,128)(2,1)}), bf16[32,8,1152]{2,1,0:T(8,128)(2,1)S(1)}, u32[]{:S(2)}, u32[]{:S(2)}) async-start(bf16[32,8,1152]{2,1,0:T(8,128)(2,1)} %bitcast.10), calls=%async_computation.1 | async-start | bytes 1179648 | tf_op jit(solution)/shard_map/all_to_all | solution.py:331
  71.7 2.9 %shard_map.87.refs_1_ = bf16[256,1024]{1,0:T(8,128)(2,1)S(1)} custom-call(s32[4]{0:T(128)S(1)} %pad_add_fusion.refs_0_, bf16[512,1024]{1,0:T(8,128)(2,1)S(1)} %get-tuple-element.23.refs_1_, bf16[512,1024]{1,0:T(8,128)(2,1)} %refs_3_.1, bf16[256,1024]{1,0:T(8,128)(2,1)} %copy-done.6, bf16[256,1024]{1,0:T(8,128)(2,1)} %copy-done.7, ...), custom_call_target="tpu_custom_call" | custom-call | flops 68719476736 | bytes 3145728 | tf_op jit(solution)/shard_map/pallas_call | solution.py:74
  74.5 0.0 collective-permute-done.4.refs_2_
  74.5 2.0 %shard_map.89 = (bf16[128,1024]{1,0:T(8,128)(2,1)}, bf16[128,1024]{1,0:T(8,128)(2,1)}, f32[8,128]{1,0:T(8,128)S(1)}) custom-call(s32[4]{0:T(128)S(1)} %pad_add_fusion.refs_0_, bf16[256,1024]{1,0:T(8,128)(2,1)S(1)} %shard_map.87.refs_1_, bf16[256,1024]{1,0:T(8,128)(2,1)} %collective-permute-done.4.refs_2_), custom_call_target="tpu_custom_call" | custom-call | bytes 1048576 | tf_op jit(solution)/shard_map/pallas_call | solution.py:74
  76.5 3.0 %collective-permute-start.5 = (bf16[128,1024]{1,0:T(8,128)(2,1)}, bf16[128,1024]{1,0:T(8,128)(2,1)S(1)}, u32[]{:S(2)}, u32[]{:S(2)}) collective-permute-start(bf16[128,1024]{1,0:T(8,128)(2,1)} %get-tuple-element.26), channel_id=1, source_target_pairs={{0,6},{2,4},{4,2},{6,0},{8,14},{10,12},{12,10},{14,8},{1,7},{3,5},... | collective-permute-start | bytes 786440 | tf_op jit(solution)/shard_map/ppermute | solution.py:33
  79.5 10.1 %all-to-all-done.1.refs_1_ = bf16[32,8,1152]{2,1,0:T(8,128)(2,1)S(1)} async-done(((bf16[32,8,1152]{2,1,0:T(8,128)(2,1)}), bf16[32,8,1152]{2,1,0:T(8,128)(2,1)S(1)}, u32[]{:S(2)}, u32[]{:S(2)}) %all-to-all-start.1) | async-done | bytes 589856 | tf_op jit(solution)/shard_map/all_to_all | solution.py:331
  89.5 0.0 copy-start.4
  89.5 3.1 %shard_map.93 = (bf16[8,8,1024]{2,1,0:T(8,128)(2,1)}, f32[8,1024]{1,0:T(8,128)S(1)}) custom-call(s32[4]{0:T(128)S(1)} %pad_add_fusion.refs_0_, bf16[32,8,1152]{2,1,0:T(8,128)(2,1)S(1)} %all-to-all-done.1.refs_1_, f32[8,128]{1,0:T(8,128)S(1)} %get-tuple-element.34.refs_2_, bf16[512,1024]{1,0:T(8,128)(2,1)} %refs_3_.1, bf16[256,1024]{1,0:T(8,128)(2,1)} %copy-done.6, ...), custom_call_target="tpu_custom_call" | custom-call | flops 68719476736 | bytes 3145728 | tf_op jit(solution)/shard_map/pallas_call | solution.py:74
  92.7 3.4 %all-to-all-start.2 = ((bf16[8,8,1024]{2,1,0:T(8,128)(2,1)}), bf16[8,8,1024]{2,1,0:T(8,128)(2,1)S(1)}, u32[]{:S(2)}, u32[]{:S(2)}) async-start(bf16[8,8,1024]{2,1,0:T(8,128)(2,1)} %get-tuple-element.35), calls=%async_computation.2 | async-start | bytes 262144 | tf_op jit(solution)/shard_map/all_to_all | solution.py:358
  96.1 0.0 collective-permute-done.5.refs_2_
  96.1 0.0 copy-done.4
  96.1 1.3 shard_map.90
  97.4 0.0 copy-start.2
  97.4 0.6 copy-done.2
  98.0 0.0 copy-start.10
  98.0 0.0 copy-start.1
  98.0 0.0 copy-start.3
  98.0 5.7 %all-to-all-done.2.refs_1_ = bf16[8,8,1024]{2,1,0:T(8,128)(2,1)S(1)} async-done(((bf16[8,8,1024]{2,1,0:T(8,128)(2,1)}), bf16[8,8,1024]{2,1,0:T(8,128)(2,1)S(1)}, u32[]{:S(2)}, u32[]{:S(2)}) %all-to-all-start.2) | async-done | bytes 131104 | tf_op jit(solution)/shard_map/all_to_all | solution.py:358
  103.7 1.4 %shard_map.94 = bf16[32,8,1024]{2,1,0:T(8,128)(2,1)} custom-call(s32[4]{0:T(128)S(1)} %pad_add_fusion.refs_0_, bf16[8,8,1024]{2,1,0:T(8,128)(2,1)S(1)} %all-to-all-done.2.refs_1_, f32[8,1024]{1,0:T(8,128)S(1)} %get-tuple-element.36.refs_2_, f32[8,128]{1,0:T(8,128)} %copy-done.2), custom_call_target="tpu_custom_call" | custom-call | bytes 1048576 | tf_op jit(solution)/shard_map/pallas_call | solution.py:74
  105.2 5.1 %all-to-all-start.3 = ((bf16[32,8,1024]{2,1,0:T(8,128)(2,1)}), bf16[32,8,1024]{2,1,0:T(8,128)(2,1)S(1)}, u32[]{:S(2)}, u32[]{:S(2)}) async-start(bf16[32,8,1024]{2,1,0:T(8,128)(2,1)} %shard_map.94), calls=%async_computation.3 | async-start | bytes 1048576 | tf_op jit(solution)/shard_map/all_to_all | solution.py:363
  110.3 0.0 copy-done.10
  110.3 1.9 %collective-permute-start.6 = (bf16[64,1024]{1,0:T(8,128)(2,1)S(1)}, bf16[64,1024]{1,0:T(8,128)(2,1)S(1)}, u32[]{:S(2)}, u32[]{:S(2)}) collective-permute-start(bf16[64,1024]{1,0:T(8,128)(2,1)S(1)} %copy-done.10), channel_id=1, source_target_pairs={{0,14},{2,12},{4,10},{6,8},{8,6},{10,4},{12,2},{14,0},{1,15},{3,13... | collective-permute-start | bytes 393224 | tf_op jit(solution)/shard_map/ppermute | solution.py:33
  112.2 6.5 %collective-permute-done.6.refs_3_ = bf16[64,1024]{1,0:T(8,128)(2,1)S(1)} collective-permute-done((bf16[64,1024]{1,0:T(8,128)(2,1)S(1)}, bf16[64,1024]{1,0:T(8,128)(2,1)S(1)}, u32[]{:S(2)}, u32[]{:S(2)}) %collective-permute-start.6) | collective-permute-done | bytes 131104 | tf_op jit(solution)/shard_map/ppermute | solution.py:33
  118.8 0.0 copy-done.1
  118.8 0.0 copy-done.3
  118.8 1.3 shard_map.91
  120.1 3.8 %all-to-all-done.3 = bf16[32,8,1024]{2,1,0:T(8,128)(2,1)S(1)} async-done(((bf16[32,8,1024]{2,1,0:T(8,128)(2,1)}), bf16[32,8,1024]{2,1,0:T(8,128)(2,1)S(1)}, u32[]{:S(2)}, u32[]{:S(2)}) %all-to-all-start.3) | async-done | bytes 524320 | tf_op jit(solution)/shard_map/all_to_all | solution.py:363
  123.9 0.6 shard_map.95.refs_2_
  124.5 6.8 %collective-permute-start.8 = (bf16[256,1024]{1,0:T(8,128)(2,1)S(1)}, bf16[256,1024]{1,0:T(8,128)(2,1)S(1)}, u32[]{:S(2)}, u32[]{:S(2)}) collective-permute-start(bf16[256,1024]{1,0:T(8,128)(2,1)S(1)} %shard_map.95.refs_2_), channel_id=1, source_target_pairs={{0,16},{16,0},{1,17},{17,1},{2,18},{18,2},{3,19},{19,3},{4,20},{20... | collective-permute-start | bytes 1572872 | tf_op jit(solution)/shard_map/ppermute | solution.py:33
  131.3 0.9 shard_map.96
  132.2 0.6 collective-permute-done.8.refs_2_
  132.8 1.6 %shard_map.97 = (f32[64,512]{1,0:T(8,128)}, bf16[16,1024]{1,0:T(8,128)(2,1)}) custom-call(s32[4]{0:T(128)S(1)} %pad_add_fusion.refs_0_, bf16[64,1024]{1,0:T(8,128)(2,1)S(1)} %get-tuple-element.30.refs_1_, bf16[256,1024]{1,0:T(8,128)(2,1)S(1)} %collective-permute-done.8.refs_2_, bf16[16,512]{1,0:T(8,128)(2,1)S(1)} %get-tuple-element.38.refs_2_.refs_3_, ...), custom_call_target="tpu_custom_call" | custom-call | bytes 1048576 | tf_op jit(solution)/shard_map/pallas_call | solution.py:74
  (4 shorter events, 0.1 us)
Async XLA Ops:
  0.6 13.7 %copy-start = (bf16[768,1024]{1,0:T(8,128)(2,1)S(1)}, bf16[768,1024]{1,0:T(8,128)(2,1)}, u32[]{:S(2)}) copy-start(bf16[768,1024]{1,0:T(8,128)(2,1)} %param.8) | copy-start | bytes 4718596
  0.7 13.5 %copy-start.9 = (s32[512]{0:T(512)S(1)}, s32[512]{0:T(512)}, u32[]{:S(2)}) copy-start(s32[512]{0:T(512)} %param.9) | copy-start | bytes 6148
  3.4 43.0 %all-to-all-start = ((bf16[8,72,1024]{2,1,0:T(8,128)(2,1)}), bf16[8,72,1024]{2,1,0:T(8,128)(2,1)}, u32[]{:S(2)}, u32[]{:S(2)}) async-start(bf16[8,72,1024]{2,1,0:T(8,128)(2,1)} %shard_map.85), calls=%async_computation | async-start | bytes 2359296 | tf_op jit(solution)/shard_map/all_to_all | solution.py:284
  14.3 2.8 %copy-start.5 = (bf16[512,1024]{1,0:T(8,128)(2,1)S(1)}, bf16[512,1024]{1,0:T(8,128)(2,1)}, u32[]{:S(2)}) copy-start(bf16[512,1024]{1,0:T(8,128)(2,1)} %refs_3_.1) | copy-start | bytes 3145732
  18.3 16.5 %collective-permute-start = (bf16[256,1024]{1,0:T(8,128)(2,1)S(1)}, bf16[256,1024]{1,0:T(8,128)(2,1)S(1)}, u32[]{:S(2)}, u32[]{:S(2)}) collective-permute-start(bf16[256,1024]{1,0:T(8,128)(2,1)S(1)} %pad_maximum_fusion), channel_id=1, source_target_pairs={{0,1},{1,128},{128,129},{129,256},{256,257},{257,384},{384,385},{3... | collective-permute-start | bytes 1572872 | tf_op jit(solution)/shard_map/ppermute | solution.py:28
  21.6 16.6 %collective-permute-start.1 = (bf16[256,1024]{1,0:T(8,128)(2,1)S(1)}, bf16[256,1024]{1,0:T(8,128)(2,1)S(1)}, u32[]{:S(2)}, u32[]{:S(2)}) collective-permute-start(bf16[256,1024]{1,0:T(8,128)(2,1)S(1)} %pad_maximum_fusion.1), channel_id=1, source_target_pairs={{0,385},{1,0},{128,1},{129,128},{256,129},{257,256},{384,257},{385... | collective-permute-start | bytes 1572872 | tf_op jit(solution)/shard_map/ppermute | solution.py:28
  34.9 11.6 %copy-start.6 = (bf16[256,1024]{1,0:T(8,128)(2,1)}, bf16[256,1024]{1,0:T(8,128)(2,1)S(1)}, u32[]{:S(2)}) copy-start(bf16[256,1024]{1,0:T(8,128)(2,1)S(1)} %collective-permute-done.refs_3_.refs_4_) | copy-start | bytes 1572868
  34.9 5.3 %collective-permute-start.2 = (bf16[256,1024]{1,0:T(8,128)(2,1)S(1)}, bf16[256,1024]{1,0:T(8,128)(2,1)S(1)}, u32[]{:S(2)}, u32[]{:S(2)}) collective-permute-start(bf16[256,1024]{1,0:T(8,128)(2,1)S(1)} %collective-permute-done.refs_3_.refs_4_), channel_id=1, source_target_pairs={{0,16},{16,0},{1,17},{17,1},{2,18},{18,2},{3,19},{19,3},{4,20},{20... | collective-permute-start | bytes 1572872 | tf_op jit(solution)/shard_map/ppermute | solution.py:33
  38.2 2.0 %copy-start.7 = (bf16[256,1024]{1,0:T(8,128)(2,1)}, bf16[256,1024]{1,0:T(8,128)(2,1)S(1)}, u32[]{:S(2)}) copy-start(bf16[256,1024]{1,0:T(8,128)(2,1)S(1)} %collective-permute-done.1.refs_4_.refs_5_) | copy-start | bytes 1572868
  38.2 3.9 %collective-permute-start.3 = (bf16[256,1024]{1,0:T(8,128)(2,1)S(1)}, bf16[256,1024]{1,0:T(8,128)(2,1)}, u32[]{:S(2)}, u32[]{:S(2)}) collective-permute-start(bf16[256,1024]{1,0:T(8,128)(2,1)S(1)} %collective-permute-done.1.refs_4_.refs_5_), channel_id=1, source_target_pairs={{0,16},{16,0},{1,17},{17,1},{2,18},{18,2},{3,19},{19,3},{4,20},{20... | collective-permute-start | bytes 1572872 | tf_op jit(solution)/shard_map/ppermute | solution.py:33
  40.2 0.8 copy-start.8
  52.2 8.2 %collective-permute-start.7 = (bf16[256,1152]{1,0:T(8,128)(2,1)S(1)}, bf16[256,1152]{1,0:T(8,128)(2,1)S(1)}, u32[]{:S(2)}, u32[]{:S(2)}) collective-permute-start(bf16[256,1152]{1,0:T(8,128)(2,1)S(1)} %get-tuple-element.32), channel_id=1, source_target_pairs={{0,16},{16,0},{1,17},{17,1},{2,18},{18,2},{3,19},{19,3},{4,20},{20... | collective-permute-start | bytes 1769480 | tf_op jit(solution)/shard_map/ppermute | solution.py:33
  58.3 16.2 %collective-permute-start.4 = (bf16[256,1024]{1,0:T(8,128)(2,1)}, bf16[256,1024]{1,0:T(8,128)(2,1)}, u32[]{:S(2)}, u32[]{:S(2)}) collective-permute-start(bf16[256,1024]{1,0:T(8,128)(2,1)} %get-tuple-element.24), channel_id=1, source_target_pairs={{0,2},{2,0},{4,6},{6,4},{8,10},{10,8},{12,14},{14,12},{1,3},{3,1},... | collective-permute-start | bytes 1572872 | tf_op jit(solution)/shard_map/ppermute | solution.py:33
  62.0 27.6 %all-to-all-start.1 = ((bf16[32,8,1152]{2,1,0:T(8,128)(2,1)}), bf16[32,8,1152]{2,1,0:T(8,128)(2,1)S(1)}, u32[]{:S(2)}, u32[]{:S(2)}) async-start(bf16[32,8,1152]{2,1,0:T(8,128)(2,1)} %bitcast.10), calls=%async_computation.1 | async-start | bytes 1179648 | tf_op jit(solution)/shard_map/all_to_all | solution.py:331
  76.5 19.6 %collective-permute-start.5 = (bf16[128,1024]{1,0:T(8,128)(2,1)}, bf16[128,1024]{1,0:T(8,128)(2,1)S(1)}, u32[]{:S(2)}, u32[]{:S(2)}) collective-permute-start(bf16[128,1024]{1,0:T(8,128)(2,1)} %get-tuple-element.26), channel_id=1, source_target_pairs={{0,6},{2,4},{4,2},{6,0},{8,14},{10,12},{12,10},{14,8},{1,7},{3,5},... | collective-permute-start | bytes 786440 | tf_op jit(solution)/shard_map/ppermute | solution.py:33
  89.5 6.6 %copy-start.4 = (bf16[128,1024]{1,0:T(8,128)(2,1)S(1)}, bf16[128,1024]{1,0:T(8,128)(2,1)}, u32[]{:S(2)}) copy-start(bf16[128,1024]{1,0:T(8,128)(2,1)} %get-tuple-element.25.refs_1_) | copy-start | bytes 786436
  92.7 11.0 %all-to-all-start.2 = ((bf16[8,8,1024]{2,1,0:T(8,128)(2,1)}), bf16[8,8,1024]{2,1,0:T(8,128)(2,1)S(1)}, u32[]{:S(2)}, u32[]{:S(2)}) async-start(bf16[8,8,1024]{2,1,0:T(8,128)(2,1)} %get-tuple-element.35), calls=%async_computation.2 | async-start | bytes 262144 | tf_op jit(solution)/shard_map/all_to_all | solution.py:358
  97.4 0.6 copy-start.2
  98.0 12.3 %copy-start.10 = (bf16[64,1024]{1,0:T(8,128)(2,1)S(1)}, bf16[64,1024]{1,0:T(8,128)(2,1)}, u32[]{:S(2)}) copy-start(bf16[64,1024]{1,0:T(8,128)(2,1)} %get-tuple-element.28) | copy-start | bytes 393220
  98.0 20.8 %copy-start.1 = (bf16[64,1024]{1,0:T(8,128)(2,1)S(1)}, bf16[64,1024]{1,0:T(8,128)(2,1)}, u32[]{:S(2)}) copy-start(bf16[64,1024]{1,0:T(8,128)(2,1)} %get-tuple-element.27.refs_2_) | copy-start | bytes 393220
  98.0 20.8 %copy-start.3 = (s32[512]{0:T(512)S(1)}, s32[512]{0:T(512)}, u32[]{:S(2)}) copy-start(s32[512]{0:T(512)} %param.11) | copy-start | bytes 6148
  105.2 18.8 %all-to-all-start.3 = ((bf16[32,8,1024]{2,1,0:T(8,128)(2,1)}), bf16[32,8,1024]{2,1,0:T(8,128)(2,1)S(1)}, u32[]{:S(2)}, u32[]{:S(2)}) async-start(bf16[32,8,1024]{2,1,0:T(8,128)(2,1)} %shard_map.94), calls=%async_computation.3 | async-start | bytes 1048576 | tf_op jit(solution)/shard_map/all_to_all | solution.py:363
  110.3 8.5 %collective-permute-start.6 = (bf16[64,1024]{1,0:T(8,128)(2,1)S(1)}, bf16[64,1024]{1,0:T(8,128)(2,1)S(1)}, u32[]{:S(2)}, u32[]{:S(2)}) collective-permute-start(bf16[64,1024]{1,0:T(8,128)(2,1)S(1)} %copy-done.10), channel_id=1, source_target_pairs={{0,14},{2,12},{4,10},{6,8},{8,6},{10,4},{12,2},{14,0},{1,15},{3,13... | collective-permute-start | bytes 393224 | tf_op jit(solution)/shard_map/ppermute | solution.py:33
  124.5 8.3 %collective-permute-start.8 = (bf16[256,1024]{1,0:T(8,128)(2,1)S(1)}, bf16[256,1024]{1,0:T(8,128)(2,1)S(1)}, u32[]{:S(2)}, u32[]{:S(2)}) collective-permute-start(bf16[256,1024]{1,0:T(8,128)(2,1)S(1)} %shard_map.95.refs_2_), channel_id=1, source_target_pairs={{0,16},{16,0},{1,17},{17,1},{2,18},{18,2},{3,19},{19,3},{4,20},{20... | collective-permute-start | bytes 1572872 | tf_op jit(solution)/shard_map/ppermute | solution.py:33

commit v10 on v9

--- a/solution.py
+++ b/solution.py
@@ -144,7 +144,7 @@
     length = lax.rsqrt(jnp.sum(jnp.square(visitors.astype(f32)), axis=1, keepdims=True) + epsilon) * math.sqrt(width)
     for copy in copies:
         copy.wait()
-    tile = min(256, count)
+    tile = min(512, count)
 
     for at in range(0, count, tile):
         values = spread[:, :rows, :].reshape(points, width)
@@ -168,7 +168,7 @@
     for copy in copies:
         copy.wait()
     token[...] = jnp.zeros_like(token)
-    tile = min(256, leave.shape[1])
+    tile = min(512, leave.shape[1])
     for at in range(0, leave.shape[1], tile):
         leave[:, at : at + tile] = project(place, kernel, maps, LEAVE, rows, at, tile).astype(bf16)
 

time: 135 us -> 134 us (level)
  no operation moved by 1% of the time
where the time goes in v10:
time: 134 us; the launch traced here: 133 us
  starting transfers between devices  57.5 us (43%)
  waiting for transfers between devices  41.7 us (31%)
  Pallas kernels  27.4 us (20%)
  local copies, waits for them, and re-layouts  5.38 us (4%)
    pallas_call x13, Pallas kernels, call(): made(*args[:near], *(pltpu.with_memory_space_constraint(a, pltpu.HBM) for...  27.4 us
    ppermute x7, starting transfers between devices, flip(): return lax.ppermute(value, axis, [(i, i ^ bit) for i in range(size)])  21.5 us
    all_to_all x1, starting transfers between devices, body(): spread = lax.all_to_all(block, 'z', 0, 0)  10.9 us
    all_to_all x1, waiting for transfers between devices, body(): gathered = lax.all_to_all(paired.reshape(peers, share, -1), PLANE, 0, 0)  10.1 us
    all_to_all x1, starting transfers between devices, body(): gathered = lax.all_to_all(paired.reshape(peers, share, -1), PLANE, 0, 0)  9.71 us
    ppermute x2, waiting for transfers between devices, hop(): lax.ppermute(value, axis, [(i, (i + by) % size) for i in range(size)])  9.45 us
    ppermute x7, waiting for transfers between devices, flip(): return lax.ppermute(value, axis, [(i, i ^ bit) for i in range(size)])  8.33 us
    ppermute x2, starting transfers between devices, hop(): lax.ppermute(value, axis, [(i, (i + by) % size) for i in range(size)])  7.02 us
  transfers between devices with their start and end apart: 13, of which 8 were waited for; matrix products, arithmetic and copies ran while one was open for 3% of the time, Pallas kernels for 12%

profile of v10, /device:TPU:1, one launch (start us, length us, event | category | flops | bytes accessed | tf_op | source)
XLA Modules:
  0.0 133.2 jit_solution(16006696852406826408)
XLA Ops:
  0.6 0.0 copy-start
  0.7 0.1 pad_add_fusion.refs_0_
  0.7 0.0 copy-start.9
  0.7 2.6 %shard_map.85 = bf16[8,72,1024]{2,1,0:T(8,128)(2,1)} custom-call(s32[4]{0:T(128)S(1)} %pad_add_fusion.refs_0_, bf16[64,1024]{1,0:T(8,128)(2,1)} %refs_1_.1, s32[1,64]{1,0:T(1,128)} %bitcast.11), custom_call_target="tpu_custom_call" | custom-call | bytes 2097152 | tf_op jit(solution)/shard_map/pallas_call | solution.py:74
  3.4 10.9 %all-to-all-start = ((bf16[8,72,1024]{2,1,0:T(8,128)(2,1)}), bf16[8,72,1024]{2,1,0:T(8,128)(2,1)}, u32[]{:S(2)}, u32[]{:S(2)}) async-start(bf16[8,72,1024]{2,1,0:T(8,128)(2,1)} %shard_map.85), calls=%async_computation | async-start | bytes 2359296 | tf_op jit(solution)/shard_map/all_to_all | solution.py:284
  14.3 0.0 copy-done.9
  14.3 0.0 copy-done
  14.3 0.0 copy-start.5
  14.3 2.8 %gather_fusion = bf16[512,1024]{1,0:T(8,128)(2,1)} fusion(bf16[768,1024]{1,0:T(8,128)(2,1)S(1)} %copy-done, s32[1024]{0:T(1024)S(1)} %pad_clamp_fusion), kind=kCustom, calls=%fused_computation | custom fusion | bytes 2099200 | tf_op jit(solution)/shard_map/gather | solution.py:286
  17.1 0.0 copy-done.5
  17.1 1.2 constant_dynamic-slice_fusion
  18.3 3.2 %collective-permute-start = (bf16[256,1024]{1,0:T(8,128)(2,1)S(1)}, bf16[256,1024]{1,0:T(8,128)(2,1)S(1)}, u32[]{:S(2)}, u32[]{:S(2)}) collective-permute-start(bf16[256,1024]{1,0:T(8,128)(2,1)S(1)} %pad_maximum_fusion), channel_id=1, source_target_pairs={{0,1},{1,128},{128,129},{129,256},{256,257},{257,384},{384,385},{3... | collective-permute-start | bytes 1572872 | tf_op jit(solution)/shard_map/ppermute | solution.py:28
  21.6 3.8 %collective-permute-start.1 = (bf16[256,1024]{1,0:T(8,128)(2,1)S(1)}, bf16[256,1024]{1,0:T(8,128)(2,1)S(1)}, u32[]{:S(2)}, u32[]{:S(2)}) collective-permute-start(bf16[256,1024]{1,0:T(8,128)(2,1)S(1)} %pad_maximum_fusion.1), channel_id=1, source_target_pairs={{0,385},{1,0},{128,1},{129,128},{256,129},{257,256},{384,257},{385... | collective-permute-start | bytes 1572872 | tf_op jit(solution)/shard_map/ppermute | solution.py:28
  25.4 9.4 %collective-permute-done.refs_3_.refs_4_ = bf16[256,1024]{1,0:T(8,128)(2,1)S(1)} collective-permute-done((bf16[256,1024]{1,0:T(8,128)(2,1)S(1)}, bf16[256,1024]{1,0:T(8,128)(2,1)S(1)}, u32[]{:S(2)}, u32[]{:S(2)}) %collective-permute-start) | collective-permute-done | bytes 524320 | tf_op jit(solution)/shard_map/ppermute | solution.py:28
  34.9 0.0 copy-start.6
  34.9 3.3 %collective-permute-start.2 = (bf16[256,1024]{1,0:T(8,128)(2,1)S(1)}, bf16[256,1024]{1,0:T(8,128)(2,1)S(1)}, u32[]{:S(2)}, u32[]{:S(2)}) collective-permute-start(bf16[256,1024]{1,0:T(8,128)(2,1)S(1)} %collective-permute-done.refs_3_.refs_4_), channel_id=1, source_target_pairs={{0,16},{16,0},{1,17},{17,1},{2,18},{18,2},{3,19},{19,3},{4,20},{20... | collective-permute-start | bytes 1572872 | tf_op jit(solution)/shard_map/ppermute | solution.py:33
  38.2 0.0 collective-permute-done.1.refs_4_.refs_5_
  38.2 0.0 copy-start.7
  38.2 1.9 %collective-permute-start.3 = (bf16[256,1024]{1,0:T(8,128)(2,1)S(1)}, bf16[256,1024]{1,0:T(8,128)(2,1)}, u32[]{:S(2)}, u32[]{:S(2)}) collective-permute-start(bf16[256,1024]{1,0:T(8,128)(2,1)S(1)} %collective-permute-done.1.refs_4_.refs_5_), channel_id=1, source_target_pairs={{0,16},{16,0},{1,17},{17,1},{2,18},{18,2},{3,19},{19,3},{4,20},{20... | collective-permute-start | bytes 1572872 | tf_op jit(solution)/shard_map/ppermute | solution.py:33
  40.2 0.0 collective-permute-done.2.refs_5_.refs_6_
  40.2 0.0 copy-done.7
  40.2 0.0 copy-start.8
  40.2 0.8 copy-done.8
  41.0 1.2 collective-permute-done.3.refs_6_.refs_7_
  42.2 4.2 %all-to-all-done.refs_1_ = bf16[8,72,1024]{2,1,0:T(8,128)(2,1)} async-done(((bf16[8,72,1024]{2,1,0:T(8,128)(2,1)}), bf16[8,72,1024]{2,1,0:T(8,128)(2,1)}, u32[]{:S(2)}, u32[]{:S(2)}) %all-to-all-start) | async-done | bytes 1179680 | tf_op jit(solution)/shard_map/all_to_all | solution.py:284
  46.4 0.0 copy-done.6
  46.4 4.7 %shard_map.86 = (bf16[512,1024]{1,0:T(8,128)(2,1)S(1)}, bf16[256,1152]{1,0:T(8,128)(2,1)S(1)}, bf16[256,1152]{1,0:T(8,128)(2,1)S(1)}) custom-call(s32[4]{0:T(128)S(1)} %pad_add_fusion.refs_0_, bf16[8,72,1024]{2,1,0:T(8,128)(2,1)} %all-to-all-done.refs_1_, bf16[512,1024]{1,0:T(8,128)(2,1)} %gather_fusion, bf16[256,1024]{1,0:T(8,128)(2,1)} %copy-done.6, ...), custom_call_target="tpu_custom_call" | custom-call | flops 1610612736 | bytes 6291456 | tf_op jit(solution)/shard_map/pallas_call | solution.py:74
  51.1 2.4 %collective-permute-start.7 = (bf16[256,1152]{1,0:T(8,128)(2,1)S(1)}, bf16[256,1152]{1,0:T(8,128)(2,1)S(1)}, u32[]{:S(2)}, u32[]{:S(2)}) collective-permute-start(bf16[256,1152]{1,0:T(8,128)(2,1)S(1)} %get-tuple-element.32), channel_id=1, source_target_pairs={{0,16},{16,0},{1,17},{17,1},{2,18},{18,2},{3,19},{19,3},{4,20},{20... | collective-permute-start | bytes 1769480 | tf_op jit(solution)/shard_map/ppermute | solution.py:33
  53.5 3.6 %shard_map.88 = (bf16[256,1024]{1,0:T(8,128)(2,1)}, f32[8,128]{1,0:T(8,128)S(1)}) custom-call(s32[4]{0:T(128)S(1)} %pad_add_fusion.refs_0_, bf16[512,1024]{1,0:T(8,128)(2,1)S(1)} %get-tuple-element.23.refs_1_, bf16[512,1024]{1,0:T(8,128)(2,1)} %refs_3_.1, bf16[256,1024]{1,0:T(8,128)(2,1)} %copy-done.6, bf16[256,1024]{1,0:T(8,128)(2,1)} %copy-done.7, ...), custom_call_target="tpu_custom_call" | custom-call | flops 536870912 | bytes 3145728 | tf_op jit(solution)/shard_map/pallas_call | solution.py:74
  57.1 2.1 %collective-permute-start.4 = (bf16[256,1024]{1,0:T(8,128)(2,1)}, bf16[256,1024]{1,0:T(8,128)(2,1)}, u32[]{:S(2)}, u32[]{:S(2)}) collective-permute-start(bf16[256,1024]{1,0:T(8,128)(2,1)} %get-tuple-element.24), channel_id=1, source_target_pairs={{0,2},{2,0},{4,6},{6,4},{8,10},{10,8},{12,14},{14,12},{1,3},{3,1},... | collective-permute-start | bytes 1572872 | tf_op jit(solution)/shard_map/ppermute | solution.py:33
  59.3 0.0 collective-permute-done.7.refs_2_
  59.3 1.5 %shard_map.92 = bf16[256,1152]{1,0:T(8,128)(2,1)} custom-call(s32[4]{0:T(128)S(1)} %pad_add_fusion.refs_0_, bf16[256,1152]{1,0:T(8,128)(2,1)S(1)} %get-tuple-element.31.refs_1_, bf16[256,1152]{1,0:T(8,128)(2,1)S(1)} %collective-permute-done.7.refs_2_, f32[8,128]{1,0:T(8,128)S(1)} %get-tuple-element.33.refs_3_), custom_call_target="tpu_custom_call" | custom-call | bytes 2097152 | tf_op jit(solution)/shard_map/pallas_call | solution.py:74
  60.8 9.7 %all-to-all-start.1 = ((bf16[32,8,1152]{2,1,0:T(8,128)(2,1)}), bf16[32,8,1152]{2,1,0:T(8,128)(2,1)S(1)}, u32[]{:S(2)}, u32[]{:S(2)}) async-start(bf16[32,8,1152]{2,1,0:T(8,128)(2,1)} %bitcast.10), calls=%async_computation.1 | async-start | bytes 1179648 | tf_op jit(solution)/shard_map/all_to_all | solution.py:331
  70.5 2.8 %shard_map.87.refs_1_ = bf16[256,1024]{1,0:T(8,128)(2,1)S(1)} custom-call(s32[4]{0:T(128)S(1)} %pad_add_fusion.refs_0_, bf16[512,1024]{1,0:T(8,128)(2,1)S(1)} %get-tuple-element.23.refs_1_, bf16[512,1024]{1,0:T(8,128)(2,1)} %refs_3_.1, bf16[256,1024]{1,0:T(8,128)(2,1)} %copy-done.6, bf16[256,1024]{1,0:T(8,128)(2,1)} %copy-done.7, ...), custom_call_target="tpu_custom_call" | custom-call | flops 68719476736 | bytes 3145728 | tf_op jit(solution)/shard_map/pallas_call | solution.py:74
  73.3 0.0 collective-permute-done.4.refs_2_
  73.3 2.0 %shard_map.89 = (bf16[128,1024]{1,0:T(8,128)(2,1)}, bf16[128,1024]{1,0:T(8,128)(2,1)}, f32[8,128]{1,0:T(8,128)S(1)}) custom-call(s32[4]{0:T(128)S(1)} %pad_add_fusion.refs_0_, bf16[256,1024]{1,0:T(8,128)(2,1)S(1)} %shard_map.87.refs_1_, bf16[256,1024]{1,0:T(8,128)(2,1)} %collective-permute-done.4.refs_2_), custom_call_target="tpu_custom_call" | custom-call | bytes 1048576 | tf_op jit(solution)/shard_map/pallas_call | solution.py:74
  75.3 3.0 %collective-permute-start.5 = (bf16[128,1024]{1,0:T(8,128)(2,1)}, bf16[128,1024]{1,0:T(8,128)(2,1)S(1)}, u32[]{:S(2)}, u32[]{:S(2)}) collective-permute-start(bf16[128,1024]{1,0:T(8,128)(2,1)} %get-tuple-element.26), channel_id=1, source_target_pairs={{0,6},{2,4},{4,2},{6,0},{8,14},{10,12},{12,10},{14,8},{1,7},{3,5},... | collective-permute-start | bytes 786440 | tf_op jit(solution)/shard_map/ppermute | solution.py:33
  78.3 10.1 %all-to-all-done.1.refs_1_ = bf16[32,8,1152]{2,1,0:T(8,128)(2,1)S(1)} async-done(((bf16[32,8,1152]{2,1,0:T(8,128)(2,1)}), bf16[32,8,1152]{2,1,0:T(8,128)(2,1)S(1)}, u32[]{:S(2)}, u32[]{:S(2)}) %all-to-all-start.1) | async-done | bytes 589856 | tf_op jit(solution)/shard_map/all_to_all | solution.py:331
  88.4 0.0 copy-start.4
  88.4 3.1 %shard_map.93 = (bf16[8,8,1024]{2,1,0:T(8,128)(2,1)}, f32[8,1024]{1,0:T(8,128)S(1)}) custom-call(s32[4]{0:T(128)S(1)} %pad_add_fusion.refs_0_, bf16[32,8,1152]{2,1,0:T(8,128)(2,1)S(1)} %all-to-all-done.1.refs_1_, f32[8,128]{1,0:T(8,128)S(1)} %get-tuple-element.34.refs_2_, bf16[512,1024]{1,0:T(8,128)(2,1)} %refs_3_.1, bf16[256,1024]{1,0:T(8,128)(2,1)} %copy-done.6, ...), custom_call_target="tpu_custom_call" | custom-call | flops 68719476736 | bytes 3145728 | tf_op jit(solution)/shard_map/pallas_call | solution.py:74
  91.5 3.4 %all-to-all-start.2 = ((bf16[8,8,1024]{2,1,0:T(8,128)(2,1)}), bf16[8,8,1024]{2,1,0:T(8,128)(2,1)S(1)}, u32[]{:S(2)}, u32[]{:S(2)}) async-start(bf16[8,8,1024]{2,1,0:T(8,128)(2,1)} %get-tuple-element.35), calls=%async_computation.2 | async-start | bytes 262144 | tf_op jit(solution)/shard_map/all_to_all | solution.py:358
  94.9 0.0 collective-permute-done.5.refs_2_
  94.9 0.0 copy-done.4
  95.0 1.3 shard_map.90
  96.3 0.0 copy-start.2
  96.3 0.6 copy-done.2
  96.8 0.0 copy-start.10
  96.8 0.0 copy-start.1
  96.9 0.0 copy-start.3
  96.9 5.7 %all-to-all-done.2.refs_1_ = bf16[8,8,1024]{2,1,0:T(8,128)(2,1)S(1)} async-done(((bf16[8,8,1024]{2,1,0:T(8,128)(2,1)}), bf16[8,8,1024]{2,1,0:T(8,128)(2,1)S(1)}, u32[]{:S(2)}, u32[]{:S(2)}) %all-to-all-start.2) | async-done | bytes 131104 | tf_op jit(solution)/shard_map/all_to_all | solution.py:358
  102.6 1.4 %shard_map.94 = bf16[32,8,1024]{2,1,0:T(8,128)(2,1)} custom-call(s32[4]{0:T(128)S(1)} %pad_add_fusion.refs_0_, bf16[8,8,1024]{2,1,0:T(8,128)(2,1)S(1)} %all-to-all-done.2.refs_1_, f32[8,1024]{1,0:T(8,128)S(1)} %get-tuple-element.36.refs_2_, f32[8,128]{1,0:T(8,128)} %copy-done.2), custom_call_target="tpu_custom_call" | custom-call | bytes 1048576 | tf_op jit(solution)/shard_map/pallas_call | solution.py:74
  104.0 5.1 %all-to-all-start.3 = ((bf16[32,8,1024]{2,1,0:T(8,128)(2,1)}), bf16[32,8,1024]{2,1,0:T(8,128)(2,1)S(1)}, u32[]{:S(2)}, u32[]{:S(2)}) async-start(bf16[32,8,1024]{2,1,0:T(8,128)(2,1)} %shard_map.94), calls=%async_computation.3 | async-start | bytes 1048576 | tf_op jit(solution)/shard_map/all_to_all | solution.py:363
  109.1 0.0 copy-done.10
  109.1 1.9 %collective-permute-start.6 = (bf16[64,1024]{1,0:T(8,128)(2,1)S(1)}, bf16[64,1024]{1,0:T(8,128)(2,1)S(1)}, u32[]{:S(2)}, u32[]{:S(2)}) collective-permute-start(bf16[64,1024]{1,0:T(8,128)(2,1)S(1)} %copy-done.10), channel_id=1, source_target_pairs={{0,14},{2,12},{4,10},{6,8},{8,6},{10,4},{12,2},{14,0},{1,15},{3,13... | collective-permute-start | bytes 393224 | tf_op jit(solution)/shard_map/ppermute | solution.py:33
  111.1 6.5 %collective-permute-done.6.refs_3_ = bf16[64,1024]{1,0:T(8,128)(2,1)S(1)} collective-permute-done((bf16[64,1024]{1,0:T(8,128)(2,1)S(1)}, bf16[64,1024]{1,0:T(8,128)(2,1)S(1)}, u32[]{:S(2)}, u32[]{:S(2)}) %collective-permute-start.6) | collective-permute-done | bytes 131104 | tf_op jit(solution)/shard_map/ppermute | solution.py:33
  117.6 0.0 copy-done.1
  117.6 0.0 copy-done.3
  117.6 1.3 shard_map.91
  118.9 3.8 %all-to-all-done.3 = bf16[32,8,1024]{2,1,0:T(8,128)(2,1)S(1)} async-done(((bf16[32,8,1024]{2,1,0:T(8,128)(2,1)}), bf16[32,8,1024]{2,1,0:T(8,128)(2,1)S(1)}, u32[]{:S(2)}, u32[]{:S(2)}) %all-to-all-start.3) | async-done | bytes 524320 | tf_op jit(solution)/shard_map/all_to_all | solution.py:363
  122.8 0.6 shard_map.95.refs_2_
  123.3 6.8 %collective-permute-start.8 = (bf16[256,1024]{1,0:T(8,128)(2,1)S(1)}, bf16[256,1024]{1,0:T(8,128)(2,1)S(1)}, u32[]{:S(2)}, u32[]{:S(2)}) collective-permute-start(bf16[256,1024]{1,0:T(8,128)(2,1)S(1)} %shard_map.95.refs_2_), channel_id=1, source_target_pairs={{0,16},{16,0},{1,17},{17,1},{2,18},{18,2},{3,19},{19,3},{4,20},{20... | collective-permute-start | bytes 1572872 | tf_op jit(solution)/shard_map/ppermute | solution.py:33
  130.1 0.9 shard_map.96
  131.0 0.6 collective-permute-done.8.refs_2_
  131.6 1.6 %shard_map.97 = (f32[64,512]{1,0:T(8,128)}, bf16[16,1024]{1,0:T(8,128)(2,1)}) custom-call(s32[4]{0:T(128)S(1)} %pad_add_fusion.refs_0_, bf16[64,1024]{1,0:T(8,128)(2,1)S(1)} %get-tuple-element.30.refs_1_, bf16[256,1024]{1,0:T(8,128)(2,1)S(1)} %collective-permute-done.8.refs_2_, bf16[16,512]{1,0:T(8,128)(2,1)S(1)} %get-tuple-element.38.refs_2_.refs_3_, ...), custom_call_target="tpu_custom_call" | custom-call | bytes 1048576 | tf_op jit(solution)/shard_map/pallas_call | solution.py:74
  (4 shorter events, 0.1 us)
Async XLA Ops:
  0.6 13.7 %copy-start = (bf16[768,1024]{1,0:T(8,128)(2,1)S(1)}, bf16[768,1024]{1,0:T(8,128)(2,1)}, u32[]{:S(2)}) copy-start(bf16[768,1024]{1,0:T(8,128)(2,1)} %param.8) | copy-start | bytes 4718596
  0.7 13.5 %copy-start.9 = (s32[512]{0:T(512)S(1)}, s32[512]{0:T(512)}, u32[]{:S(2)}) copy-start(s32[512]{0:T(512)} %param.9) | copy-start | bytes 6148
  3.4 43.0 %all-to-all-start = ((bf16[8,72,1024]{2,1,0:T(8,128)(2,1)}), bf16[8,72,1024]{2,1,0:T(8,128)(2,1)}, u32[]{:S(2)}, u32[]{:S(2)}) async-start(bf16[8,72,1024]{2,1,0:T(8,128)(2,1)} %shard_map.85), calls=%async_computation | async-start | bytes 2359296 | tf_op jit(solution)/shard_map/all_to_all | solution.py:284
  14.3 2.8 %copy-start.5 = (bf16[512,1024]{1,0:T(8,128)(2,1)S(1)}, bf16[512,1024]{1,0:T(8,128)(2,1)}, u32[]{:S(2)}) copy-start(bf16[512,1024]{1,0:T(8,128)(2,1)} %refs_3_.1) | copy-start | bytes 3145732
  18.3 16.5 %collective-permute-start = (bf16[256,1024]{1,0:T(8,128)(2,1)S(1)}, bf16[256,1024]{1,0:T(8,128)(2,1)S(1)}, u32[]{:S(2)}, u32[]{:S(2)}) collective-permute-start(bf16[256,1024]{1,0:T(8,128)(2,1)S(1)} %pad_maximum_fusion), channel_id=1, source_target_pairs={{0,1},{1,128},{128,129},{129,256},{256,257},{257,384},{384,385},{3... | collective-permute-start | bytes 1572872 | tf_op jit(solution)/shard_map/ppermute | solution.py:28
  21.6 16.6 %collective-permute-start.1 = (bf16[256,1024]{1,0:T(8,128)(2,1)S(1)}, bf16[256,1024]{1,0:T(8,128)(2,1)S(1)}, u32[]{:S(2)}, u32[]{:S(2)}) collective-permute-start(bf16[256,1024]{1,0:T(8,128)(2,1)S(1)} %pad_maximum_fusion.1), channel_id=1, source_target_pairs={{0,385},{1,0},{128,1},{129,128},{256,129},{257,256},{384,257},{385... | collective-permute-start | bytes 1572872 | tf_op jit(solution)/shard_map/ppermute | solution.py:28
  34.9 11.6 %copy-start.6 = (bf16[256,1024]{1,0:T(8,128)(2,1)}, bf16[256,1024]{1,0:T(8,128)(2,1)S(1)}, u32[]{:S(2)}) copy-start(bf16[256,1024]{1,0:T(8,128)(2,1)S(1)} %collective-permute-done.refs_3_.refs_4_) | copy-start | bytes 1572868
  34.9 5.3 %collective-permute-start.2 = (bf16[256,1024]{1,0:T(8,128)(2,1)S(1)}, bf16[256,1024]{1,0:T(8,128)(2,1)S(1)}, u32[]{:S(2)}, u32[]{:S(2)}) collective-permute-start(bf16[256,1024]{1,0:T(8,128)(2,1)S(1)} %collective-permute-done.refs_3_.refs_4_), channel_id=1, source_target_pairs={{0,16},{16,0},{1,17},{17,1},{2,18},{18,2},{3,19},{19,3},{4,20},{20... | collective-permute-start | bytes 1572872 | tf_op jit(solution)/shard_map/ppermute | solution.py:33
  38.2 2.0 %copy-start.7 = (bf16[256,1024]{1,0:T(8,128)(2,1)}, bf16[256,1024]{1,0:T(8,128)(2,1)S(1)}, u32[]{:S(2)}) copy-start(bf16[256,1024]{1,0:T(8,128)(2,1)S(1)} %collective-permute-done.1.refs_4_.refs_5_) | copy-start | bytes 1572868
  38.2 3.9 %collective-permute-start.3 = (bf16[256,1024]{1,0:T(8,128)(2,1)S(1)}, bf16[256,1024]{1,0:T(8,128)(2,1)}, u32[]{:S(2)}, u32[]{:S(2)}) collective-permute-start(bf16[256,1024]{1,0:T(8,128)(2,1)S(1)} %collective-permute-done.1.refs_4_.refs_5_), channel_id=1, source_target_pairs={{0,16},{16,0},{1,17},{17,1},{2,18},{18,2},{3,19},{19,3},{4,20},{20... | collective-permute-start | bytes 1572872 | tf_op jit(solution)/shard_map/ppermute | solution.py:33
  40.2 0.8 copy-start.8
  51.1 8.2 %collective-permute-start.7 = (bf16[256,1152]{1,0:T(8,128)(2,1)S(1)}, bf16[256,1152]{1,0:T(8,128)(2,1)S(1)}, u32[]{:S(2)}, u32[]{:S(2)}) collective-permute-start(bf16[256,1152]{1,0:T(8,128)(2,1)S(1)} %get-tuple-element.32), channel_id=1, source_target_pairs={{0,16},{16,0},{1,17},{17,1},{2,18},{18,2},{3,19},{19,3},{4,20},{20... | collective-permute-start | bytes 1769480 | tf_op jit(solution)/shard_map/ppermute | solution.py:33
  57.1 16.2 %collective-permute-start.4 = (bf16[256,1024]{1,0:T(8,128)(2,1)}, bf16[256,1024]{1,0:T(8,128)(2,1)}, u32[]{:S(2)}, u32[]{:S(2)}) collective-permute-start(bf16[256,1024]{1,0:T(8,128)(2,1)} %get-tuple-element.24), channel_id=1, source_target_pairs={{0,2},{2,0},{4,6},{6,4},{8,10},{10,8},{12,14},{14,12},{1,3},{3,1},... | collective-permute-start | bytes 1572872 | tf_op jit(solution)/shard_map/ppermute | solution.py:33
  60.8 27.6 %all-to-all-start.1 = ((bf16[32,8,1152]{2,1,0:T(8,128)(2,1)}), bf16[32,8,1152]{2,1,0:T(8,128)(2,1)S(1)}, u32[]{:S(2)}, u32[]{:S(2)}) async-start(bf16[32,8,1152]{2,1,0:T(8,128)(2,1)} %bitcast.10), calls=%async_computation.1 | async-start | bytes 1179648 | tf_op jit(solution)/shard_map/all_to_all | solution.py:331
  75.3 19.6 %collective-permute-start.5 = (bf16[128,1024]{1,0:T(8,128)(2,1)}, bf16[128,1024]{1,0:T(8,128)(2,1)S(1)}, u32[]{:S(2)}, u32[]{:S(2)}) collective-permute-start(bf16[128,1024]{1,0:T(8,128)(2,1)} %get-tuple-element.26), channel_id=1, source_target_pairs={{0,6},{2,4},{4,2},{6,0},{8,14},{10,12},{12,10},{14,8},{1,7},{3,5},... | collective-permute-start | bytes 786440 | tf_op jit(solution)/shard_map/ppermute | solution.py:33
  88.4 6.6 %copy-start.4 = (bf16[128,1024]{1,0:T(8,128)(2,1)S(1)}, bf16[128,1024]{1,0:T(8,128)(2,1)}, u32[]{:S(2)}) copy-start(bf16[128,1024]{1,0:T(8,128)(2,1)} %get-tuple-element.25.refs_1_) | copy-start | bytes 786436
  91.5 11.1 %all-to-all-start.2 = ((bf16[8,8,1024]{2,1,0:T(8,128)(2,1)}), bf16[8,8,1024]{2,1,0:T(8,128)(2,1)S(1)}, u32[]{:S(2)}, u32[]{:S(2)}) async-start(bf16[8,8,1024]{2,1,0:T(8,128)(2,1)} %get-tuple-element.35), calls=%async_computation.2 | async-start | bytes 262144 | tf_op jit(solution)/shard_map/all_to_all | solution.py:358
  96.3 0.6 copy-start.2
  96.8 12.3 %copy-start.10 = (bf16[64,1024]{1,0:T(8,128)(2,1)S(1)}, bf16[64,1024]{1,0:T(8,128)(2,1)}, u32[]{:S(2)}) copy-start(bf16[64,1024]{1,0:T(8,128)(2,1)} %get-tuple-element.28) | copy-start | bytes 393220
  96.8 20.8 %copy-start.1 = (bf16[64,1024]{1,0:T(8,128)(2,1)S(1)}, bf16[64,1024]{1,0:T(8,128)(2,1)}, u32[]{:S(2)}) copy-start(bf16[64,1024]{1,0:T(8,128)(2,1)} %get-tuple-element.27.refs_2_) | copy-start | bytes 393220
  96.9 20.8 %copy-start.3 = (s32[512]{0:T(512)S(1)}, s32[512]{0:T(512)}, u32[]{:S(2)}) copy-start(s32[512]{0:T(512)} %param.11) | copy-start | bytes 6148
  104.0 18.7 %all-to-all-start.3 = ((bf16[32,8,1024]{2,1,0:T(8,128)(2,1)}), bf16[32,8,1024]{2,1,0:T(8,128)(2,1)S(1)}, u32[]{:S(2)}, u32[]{:S(2)}) async-start(bf16[32,8,1024]{2,1,0:T(8,128)(2,1)} %shard_map.94), calls=%async_computation.3 | async-start | bytes 1048576 | tf_op jit(solution)/shard_map/all_to_all | solution.py:363
  109.1 8.5 %collective-permute-start.6 = (bf16[64,1024]{1,0:T(8,128)(2,1)S(1)}, bf16[64,1024]{1,0:T(8,128)(2,1)S(1)}, u32[]{:S(2)}, u32[]{:S(2)}) collective-permute-start(bf16[64,1024]{1,0:T(8,128)(2,1)S(1)} %copy-done.10), channel_id=1, source_target_pairs={{0,14},{2,12},{4,10},{6,8},{8,6},{10,4},{12,2},{14,0},{1,15},{3,13... | collective-permute-start | bytes 393224 | tf_op jit(solution)/shard_map/ppermute | solution.py:33
  123.3 8.3 %collective-permute-start.8 = (bf16[256,1024]{1,0:T(8,128)(2,1)S(1)}, bf16[256,1024]{1,0:T(8,128)(2,1)S(1)}, u32[]{:S(2)}, u32[]{:S(2)}) collective-permute-start(bf16[256,1024]{1,0:T(8,128)(2,1)S(1)} %shard_map.95.refs_2_), channel_id=1, source_target_pairs={{0,16},{16,0},{1,17},{17,1},{2,18},{18,2},{3,19},{19,3},{4,20},{20... | collective-permute-start | bytes 1572872 | tf_op jit(solution)/shard_map/ppermute | solution.py:33
